TPU v7x, 32 devices: a whole 2x2x4 slice. The times are simulated.
32 devices in a mesh: grp: 2 (over y), dom: 8 (over z, x), col: 2 (over core).
Axes of the slice: x: 2, y: 2, z: 4, core: 2. Of those that a mesh axis runs over, the one named last changes fastest.
Arguments:
- features: bfloat16 [49152, 128], P(('grp', 'dom', 'col')), parts along dimension 0, may hold values from -6 to 6
- first_weight: bfloat16 [128, 1024], replicated, may hold values from -0.5 to 0.5
- first_bias: float32 [1024], replicated, may hold values from -3 to 3
- second_weight: bfloat16 [1024, 1024], replicated, may hold values from -0.1875 to 0.1875
- second_bias: float32 [1024], replicated, may hold values from -3 to 3
- third_weight: bfloat16 [1024, 172], replicated, may hold values from -0.1875 to 0.1875
- local_tiles: bfloat16 [16, 2, 16, 128, 128], P(('grp', 'dom'), 'col'), parts along dimension 0, may hold values from 0 to 1, as said below
- local_target: int32 [16, 2, 16], P(('grp', 'dom'), 'col'), parts along dimension 0, may hold values from 0 to 23
- local_source: int32 [16, 2, 16], P(('grp', 'dom'), 'col'), parts along dimension 0, may hold values from 0 to 23
- halo_tiles: bfloat16 [16, 2, 16, 128, 128], P(('grp', 'dom'), 'col'), parts along dimension 0, may hold values from 0 to 1, as said below
- halo_target: int32 [16, 2, 16], P(('grp', 'dom'), 'col'), parts along dimension 0, may hold values from 0 to 23
- halo_block: int32 [16, 2, 16], P(('grp', 'dom'), 'col'), parts along dimension 0, may hold values from 0 to 15
- send_rows: int32 [16, 8, 256], P(('grp', 'dom')), parts along dimension 0, may hold values from 0 to 3071
- send_count: int32 [16, 8], P(('grp', 'dom')), parts along dimension 0, may hold values from 0 to 256, as said below
- degree: int32 [49152], P(('grp', 'dom')), parts along dimension 0, may hold values from 2 to 5
- batch_nodes: int32 [16, 256], P(('grp', 'dom')), parts along dimension 0, may hold values from 0 to 3071
- labels: int32 [16, 256], P(('grp', 'dom')), parts along dimension 0, may hold values from 0 to 171
- batch_logits: float32 [16, 256, 172], P(('grp', 'dom')), parts along dimension 0, may hold values from -18 to 350
Outputs:
- first_weight_gradient: float32 [256, 1024], P('grp'), parts along dimension 0
- first_bias_gradient: float32 [2048], P('grp'), parts along dimension 0
- second_weight_gradient: float32 [2048, 1024], P('grp'), parts along dimension 0
- second_bias_gradient: float32 [2048], P('grp'), parts along dimension 0
- third_weight_gradient: float32 [2048, 172], P('grp'), parts along dimension 0
There are 2 independent parts, one for each index of `grp`. A program takes and returns all parts, laid end to end along the dimension named above; an argument that names none is the same for every part. Nothing has to cross between parts.
Inputs may be any that keep to these rules, and one draw needn't show every extreme that they name: `local_tiles`: entries are 0 or 1, the edges between two blocks of nodes. `halo_tiles`: entries are 0 or 1, the edges between two blocks of nodes. `send_count`: some destinations receive 256 live rows from every source partition.
All inputs are finite; a program needn't handle non-finite values.
Results may differ from a plain program's by a relative error of at most 0.013.
Values may be sent and summed in bfloat16 or wider, within the bound.
No kernel may reach another device: no remote copies, remote signals or barrier semaphores. Data moves between devices by JAX's collectives and lax.ppermute only.
A program may use at most 128 MiB of HBM per device.

v0:
```python
import jax
import jax.numpy as jnp
from jax import lax
from jax.sharding import PartitionSpec as P

HOPS = 4


teleport = 0.1


def backward_rows(
    feature_rows, delta_rows, first_weight, first_bias, second_weight, second_bias, third_weight
):
    pre_first = jnp.dot(feature_rows, first_weight, preferred_element_type=jnp.float32) + first_bias
    hidden_first = jax.nn.gelu(pre_first).astype(jnp.bfloat16)
    pre_second = (
        jnp.dot(hidden_first, second_weight, preferred_element_type=jnp.float32) + second_bias
    )
    hidden_second = jax.nn.gelu(pre_second).astype(jnp.bfloat16)
    third_grad = jnp.dot(hidden_second.T, delta_rows, preferred_element_type=jnp.float32)
    back_second = jnp.dot(delta_rows, third_weight.T, preferred_element_type=jnp.float32)
    unused_second, slope_second = jax.vjp(jax.nn.gelu, pre_second)
    second_delta = slope_second(back_second)[0].astype(jnp.bfloat16)
    second_grad = jnp.dot(hidden_first.T, second_delta, preferred_element_type=jnp.float32)
    second_bias_grad = jnp.sum(second_delta.astype(jnp.float32), axis=0)
    back_first = jnp.dot(second_delta, second_weight.T, preferred_element_type=jnp.float32)
    unused_first, slope_first = jax.vjp(jax.nn.gelu, pre_first)
    first_delta = slope_first(back_first)[0].astype(jnp.bfloat16)
    first_grad = jnp.dot(feature_rows.T, first_delta, preferred_element_type=jnp.float32)
    first_bias_grad = jnp.sum(first_delta.astype(jnp.float32), axis=0)
    return (first_grad, first_bias_grad, second_grad, second_bias_grad, third_grad)


def tile_sum(tiles, targets, blocks, block_count):
    product = jnp.einsum("tij,tjc->tic", tiles, blocks, preferred_element_type=jnp.float32)
    empty = jnp.zeros((block_count, tiles.shape[1], product.shape[-1]), jnp.float32)
    return empty.at[targets].add(product)


def shards(
    features,
    first_weight,
    first_bias,
    second_weight,
    second_bias,
    third_weight,
    local_tiles,
    local_target,
    local_source,
    halo_tiles,
    halo_target,
    halo_block,
    send_rows,
    send_count,
    degree,
    batch_nodes,
    labels,
    batch_logits,
):
    node_rows = degree.shape[0]
    classes = batch_logits.shape[-1]
    block_size = local_tiles.shape[-1]
    block_count = node_rows // block_size
    peers = send_rows.shape[1]
    slot_count = send_rows.shape[2]
    cores = lax.axis_size("col")
    core_index = lax.axis_index("col")
    share_rows = node_rows // cores
    row_start = core_index * share_rows
    inv_root = lax.rsqrt(degree.astype(jnp.float32))[:, None]
    keep_rate = 1.0 - teleport
    probs = jax.nn.softmax(batch_logits[0], axis=-1)
    onehot = (labels[0][:, None] == jnp.arange(classes, dtype=jnp.int32)[None, :]).astype(
        jnp.float32
    )
    loss_grad = jnp.zeros((node_rows, classes), jnp.float32).at[batch_nodes[0]].add(probs - onehot)
    my_rows = send_rows[0]
    my_counts = send_count[0]
    zero_value = jnp.zeros((), jnp.bfloat16)
    current = loss_grad
    accrued = teleport * loss_grad
    for hop in range(HOPS):
        scaled = (inv_root * current).astype(jnp.bfloat16)
        half_slots = slot_count // cores
        first_slot = core_index * half_slots
        chosen = lax.dynamic_slice_in_dim(my_rows, first_slot, half_slots, 1)
        slots = first_slot + jnp.arange(half_slots, dtype=jnp.int32)
        live = slots[None, :] < my_counts[:, None]
        outgoing = jnp.where(live[..., None], scaled[chosen], zero_value)
        landed = lax.all_to_all(outgoing, "dom", split_axis=0, concat_axis=0, tiled=True)
        arrived = lax.all_gather(landed, "col", axis=1, tiled=True)
        propagate_arrived = arrived.reshape(peers * slot_count // block_size, block_size, classes)
        own = scaled.reshape(block_count, block_size, classes)
        near = tile_sum(local_tiles[0, 0], local_target[0, 0], own[local_source[0, 0]], block_count)
        far = tile_sum(
            halo_tiles[0, 0], halo_target[0, 0], propagate_arrived[halo_block[0, 0]], block_count
        )
        summed = lax.psum(
            (near + far).reshape(node_rows, classes).astype(jnp.bfloat16), "col"
        ).astype(jnp.float32)
        current = keep_rate * inv_root * summed
        accrued = accrued + (teleport if hop + 1 < HOPS else 1.0) * current
    delta_rows = lax.dynamic_slice_in_dim(accrued, row_start, share_rows, 0)
    delta_value = delta_rows.astype(jnp.bfloat16)
    terms = backward_rows(
        features, delta_value, first_weight, first_bias, second_weight, second_bias, third_weight
    )
    totals = lax.psum((terms[0], terms[1], terms[2], terms[3], terms[4]), ("dom", "col"))
    return (totals[0], totals[1], totals[2], totals[3], totals[4])


def solution(mesh):
    return jax.shard_map(
        shards,
        mesh=mesh,
        in_specs=(
            P(("grp", "dom", "col"), None),
            P(),
            P(),
            P(),
            P(),
            P(),
            P(("grp", "dom"), "col", None, None, None),
            P(("grp", "dom"), "col", None),
            P(("grp", "dom"), "col", None),
            P(("grp", "dom"), "col", None, None, None),
            P(("grp", "dom"), "col", None),
            P(("grp", "dom"), "col", None),
            P(("grp", "dom"), None, None),
            P(("grp", "dom"), None),
            P(("grp", "dom")),
            P(("grp", "dom"), None),
            P(("grp", "dom"), None),
            P(("grp", "dom"), None, None),
        ),
        out_specs=(P("grp", None), P("grp"), P("grp", None), P("grp"), P("grp", None)),
        check_vma=False,
    )
```

profile of v0, /device:TPU:0, one launch (start us, length us, event | category | flops | bytes accessed | tf_op | source)
XLA Modules:
  0.0 507.1 jit_solution(17913557326237743894)
XLA Ops:
  11.8 4.1 scatter_custom_fusion
  15.9 3.5 multiply_convert_fusion.5
  19.4 5.1 %gather_fusion.1 = bf16[1024,172]{1,0:T(8,128)(2,1)S(1)} fusion(bf16[3072,172]{1,0:T(8,128)(2,1)} %multiply_convert_fusion.5, s32[1024]{0:T(1024)S(1)} %fusion.38), kind=kCustom, calls=%fused_computation.1 | custom fusion | bytes 708608 | tf_op jit(solution)/shard_map/gather | solution.py:90
  25.7 7.3 %all-to-all-start = ((bf16[8,128,172]{1,2,0:T(8,128)(2,1)}), bf16[8,128,172]{1,2,0:T(8,128)(2,1)}, u32[]{:S(2)}, u32[]{:S(2)}) async-start(bf16[8,128,172]{1,2,0:T(8,128)(2,1)} %broadcast_select_fusion.3), calls=%async_computation | async-start | bytes 720896 | tf_op jit(solution)/shard_map/all_to_all | solution.py:91
  32.9 2.5 copy.60
  40.6 4.3 scatter_fusion
  45.0 2.5 all_gather.12
  52.9 2.6 gather_fusion.2
  55.5 2.8 convolution_bitcast_fusion.6
  59.8 4.3 scatter_fusion.1
  64.1 3.4 add_convert_fusion.3
  67.6 2.5 copy.84
  70.1 21.8 %all-reduce.8.cloned.1.call-done = bf16[3072,172]{1,0:T(8,128)(2,1)} async-done(((bf16[3072,172]{1,0:T(8,128)(2,1)}), bf16[3072,172]{1,0:T(8,128)(2,1)}) %all-reduce.8.cloned.1.call-update) | async-done | bytes 1056784 | tf_op jit(solution)/shard_map/psum | solution.py:99
  91.9 4.2 convert_multiply_fusion.2
  96.1 6.2 %gather_fusion.4 = bf16[1024,172]{1,0:T(8,128)(2,1)} fusion(bf16[3072,172]{1,0:T(8,128)(2,1)} %get-tuple-element.35, s32[1024]{0:T(1024)S(1)} %fusion.38), kind=kCustom, calls=%fused_computation.4 | custom fusion | bytes 708608 | tf_op jit(solution)/shard_map/gather | solution.py:90
  104.4 5.8 %all-to-all-start.1 = ((bf16[8,128,172]{1,2,0:T(8,128)(2,1)}), bf16[8,128,172]{1,2,0:T(8,128)(2,1)S(1)}, u32[]{:S(2)}, u32[]{:S(2)}) async-start(bf16[8,128,172]{1,2,0:T(8,128)(2,1)} %broadcast_select_fusion.2), calls=%async_computation.1 | async-start | bytes 720896 | tf_op jit(solution)/shard_map/all_to_all | solution.py:91
  110.4 2.5 copy.66
  112.9 2.7 gather_fusion.3
  115.6 2.7 convolution_bitcast_fusion.5
  119.9 4.3 scatter_fusion.2
  124.2 2.3 all_gather.13
  131.8 2.6 gather_fusion.5
  134.5 2.8 convolution_bitcast_fusion.4
  138.8 4.3 scatter_fusion.3
  143.1 3.4 add_convert_fusion.2
  146.5 2.5 copy.70
  149.1 21.8 %all-reduce.10.cloned.1.call-done = bf16[3072,172]{1,0:T(8,128)(2,1)} async-done(((bf16[3072,172]{1,0:T(8,128)(2,1)}), bf16[3072,172]{1,0:T(8,128)(2,1)}) %all-reduce.10.cloned.1.call-update) | async-done | bytes 1056784 | tf_op jit(solution)/shard_map/psum | solution.py:99
  170.9 4.1 convert_multiply_fusion.1
  175.0 6.2 %gather_fusion.7 = bf16[1024,172]{1,0:T(8,128)(2,1)} fusion(bf16[3072,172]{1,0:T(8,128)(2,1)} %get-tuple-element.37, s32[1024]{0:T(1024)S(1)} %fusion.38), kind=kCustom, calls=%fused_computation.7 | custom fusion | bytes 708608 | tf_op jit(solution)/shard_map/gather | solution.py:90
  183.3 5.8 %all-to-all-start.2 = ((bf16[8,128,172]{1,2,0:T(8,128)(2,1)}), bf16[8,128,172]{1,2,0:T(8,128)(2,1)S(1)}, u32[]{:S(2)}, u32[]{:S(2)}) async-start(bf16[8,128,172]{1,2,0:T(8,128)(2,1)} %broadcast_select_fusion.1), calls=%async_computation.2 | async-start | bytes 720896 | tf_op jit(solution)/shard_map/all_to_all | solution.py:91
  189.1 2.5 copy.71
  191.6 2.7 gather_fusion.6
  194.4 2.7 convolution_bitcast_fusion.3
  198.6 4.3 scatter_fusion.4
  203.0 2.5 all_gather.14
  210.8 2.6 gather_fusion.8
  213.5 2.8 convolution_bitcast_fusion.2
  217.7 4.3 scatter_fusion.5
  222.1 3.5 add_convert_fusion.1
  225.5 2.5 copy.75
  228.2 21.7 %all-reduce.12.cloned.1.call-done = bf16[3072,172]{1,0:T(8,128)(2,1)} async-done(((bf16[3072,172]{1,0:T(8,128)(2,1)}), bf16[3072,172]{1,0:T(8,128)(2,1)}) %all-reduce.12.cloned.1.call-update) | async-done | bytes 1056784 | tf_op jit(solution)/shard_map/psum | solution.py:99
  249.9 4.3 multiply_convert_fusion.2
  254.2 6.3 %gather_fusion.10 = bf16[1024,172]{1,0:T(8,128)(2,1)} fusion(bf16[3072,172]{1,0:T(8,128)(2,1)} %get-tuple-element.32, s32[1024]{0:T(1024)S(1)} %fusion.38), kind=kCustom, calls=%fused_computation.10 | custom fusion | bytes 708608 | tf_op jit(solution)/shard_map/gather | solution.py:90
  264.2 5.8 %all-to-all-start.3 = ((bf16[8,128,172]{1,2,0:T(8,128)(2,1)}), bf16[8,128,172]{1,2,0:T(8,128)(2,1)}, u32[]{:S(2)}, u32[]{:S(2)}) async-start(bf16[8,128,172]{1,2,0:T(8,128)(2,1)} %broadcast_select_fusion), calls=%async_computation.3 | async-start | bytes 720896 | tf_op jit(solution)/shard_map/all_to_all | solution.py:91
  270.0 4.6 fusion.50
  274.6 2.5 copy.76
  277.1 2.9 gather_fusion.9
  280.0 2.8 convolution_bitcast_fusion.1
  284.3 4.3 scatter_fusion.6
  288.6 2.5 all_gather.15
  296.5 2.8 gather_fusion.11
  299.3 2.8 convolution_bitcast_fusion
  304.1 3.9 scatter_fusion.7
  308.0 2.5 add_convert_fusion
  312.4 9.7 %fusion.48 = f32[1536,1024]{1,0:T(8,128)} fusion(bf16[1024,1024]{1,0:T(8,128)(2,1)S(1)} %copy-done, f32[1536,1024]{1,0:T(8,128)} %fusion.50, f32[1024]{0:T(1024)S(1)} %copy-done.18), kind=kOutput, calls=%fused_computation.117 | convolution fusion | flops 3236954112 | bytes 14684160 | tf_op jit(solution)/shard_map/dot_general | solution.py:18
  322.0 12.0 %all-reduce.14.cloned.1.call-done = bf16[3072,172]{1,0:T(8,128)(2,1)} async-done(((bf16[3072,172]{1,0:T(8,128)(2,1)}), bf16[3072,172]{1,0:T(8,128)(2,1)}) %all-reduce.14.cloned.1.call-update) | async-done | bytes 1056784 | tf_op jit(solution)/shard_map/psum | solution.py:99
  334.0 3.6 fusion.17
  338.9 3.5 fusion.14
  342.3 5.1 convert_reduce_fusion
  347.4 7.5 %convert_reduce_fusion.1 = (f32[1024]{0:T(1024)S(1)}, bf16[1536,1024]{1,0:T(8,128)(2,1)S(1)}) fusion(f32[1536,1024]{1,0:T(8,128)S(1)} %bitcast.116, f32[1024]{0:T(1024)S(1)} %copy-done.18, bf16[1536,1024]{1,0:T(8,128)(2,1)S(1)} %get-tuple-element.41, bf16[1024,1024]{1,0:T(8,128)(2,1)S(1)} %copy-done), kind=kOutput, calls=%fused_computation.41 | convolution fusion | flops 3257400320 | bytes 14688256 | tf_op jit(solution)/shard_map/dot_general | solution.py:27
  355.0 5.4 %fusion.47 = f32[1024,1024]{1,0:T(8,128)} fusion(bf16[1536,1024]{1,0:T(8,128)(2,1)S(1)} %get-tuple-element.41, f32[1536,1024]{1,0:T(8,128)S(1)} %bitcast.116, f32[1024]{0:T(1024)S(1)} %copy-done.18), kind=kOutput, calls=%fused_computation.116 | convolution fusion | flops 3236954112 | bytes 13635584 | tf_op jit(solution)/shard_map/dot_general | solution.py:25
  362.2 37.0 %all-reduce = (f32[1024]{0:T(1024)}, f32[1024]{0:T(1024)}) all-reduce(f32[1024]{0:T(1024)S(1)} %get-tuple-element.30, f32[1024]{0:T(1024)S(1)} %get-tuple-element.40), channel_id=1, replica_groups=mesh['grp'=2,'dom'=8,'col'=2] {'dom','col'}, use_global_device_ids=true, to_apply=%region_17.18 | all-reduce | flops 2048 | bytes 16384 | tf_op jit(solution)/shard_map/psum | solution.py:109
  399.2 93.2 %all-reduce.16.cloned.1.call-done = (f32[128,1024]{0,1:T(8,128)}, f32[1024,1024]{1,0:T(8,128)}, f32[1024,172]{0,1:T(8,128)}) async-done(((f32[128,1024]{0,1:T(8,128)}, f32[1024,1024]{1,0:T(8,128)}, f32[1024,172]{0,1:T(8,128)}), (f32[128,1024]{0,1:T(8,128)}, f32[1024,1024]{1,0:T(8,128)}, f32[1024,172]{0,1:T(8,128)})) %all-reduce.16.cloned.1.call-update) | async-done | bytes 5423120 | tf_op jit(solution)/shard_map/psum | solution.py:109
  494.4 4.9 copy.102
  (111 shorter events, 59.4 us)
Async XLA Ops:
  7.2 305.2 %copy-start = (bf16[1024,1024]{1,0:T(8,128)(2,1)S(1)}, bf16[1024,1024]{1,0:T(8,128)(2,1)}, u32[]{:S(2)}) copy-start(bf16[1024,1024]{1,0:T(8,128)(2,1)} %param.21) | copy-start | bytes 6291460
  19.4 5.4 %copy-start.13 = (s32[1,8]{1,0:T(1,128)S(1)}, s32[1,8]{1,0:T(1,128)}, u32[]{:S(2)}) copy-start(s32[1,8]{1,0:T(1,128)} %param.31) | copy-start | bytes 100
  24.5 10.9 %copy-start.14 = (s32[1,1,16]{2,1,0:T(1,128)S(1)}, s32[1,1,16]{2,1,0:T(1,128)}, u32[]{:S(2)}) copy-start(s32[1,1,16]{2,1,0:T(1,128)} %param.25) | copy-start | bytes 196
  24.5 10.9 %copy-start.15 = (s32[1,1,16]{2,1,0:T(1,128)S(1)}, s32[1,1,16]{2,1,0:T(1,128)}, u32[]{:S(2)}) copy-start(s32[1,1,16]{2,1,0:T(1,128)} %param.26) | copy-start | bytes 196
  24.8 12.6 %copy-start.1 = (bf16[1,1,16,128,128]{4,3,2,1,0:T(8,128)(2,1)S(1)}, bf16[1,1,16,128,128]{4,3,2,1,0:T(8,128)(2,1)}, u32[]{:S(2)}) copy-start(bf16[1,1,16,128,128]{4,3,2,1,0:T(8,128)(2,1)} %param.24) | copy-start | bytes 1572868
  25.7 19.3 %all-to-all-start = ((bf16[8,128,172]{1,2,0:T(8,128)(2,1)}), bf16[8,128,172]{1,2,0:T(8,128)(2,1)}, u32[]{:S(2)}, u32[]{:S(2)}) async-start(bf16[8,128,172]{1,2,0:T(8,128)(2,1)} %broadcast_select_fusion.3), calls=%async_computation | async-start | bytes 720896 | tf_op jit(solution)/shard_map/all_to_all | solution.py:91
  32.9 59.0 %all-reduce.8.cloned.1.call-start = ((), (), s32[]{:S(2)}) async-start(), calls=%async_computation.4 | async-start | bytes 3145728 | tf_op jit(solution)/shard_map/psum | solution.py:99
  35.5 163.2 %copy-start.7 = (s32[16]{0:T(128)}, s32[16]{0:T(128)S(1)}, u32[]{:S(2)}) copy-start(s32[16]{0:T(128)S(1)} %get-tuple-element.42) | copy-start | bytes 196
  35.5 156.2 %copy-start.10 = (s32[1024]{0:T(1024)}, s32[1024]{0:T(1024)S(1)}, u32[]{:S(2)}) copy-start(s32[1024]{0:T(1024)S(1)} %pad_clamp_fusion.1) | copy-start | bytes 12292
  39.1 5.9 %copy-start.19 = (s32[1,1,16]{2,1,0:T(1,128)S(1)}, s32[1,1,16]{2,1,0:T(1,128)}, u32[]{:S(2)}) copy-start(s32[1,1,16]{2,1,0:T(1,128)} %param.29) | copy-start | bytes 196
  39.1 5.9 %copy-start.20 = (s32[1,1,16]{2,1,0:T(1,128)S(1)}, s32[1,1,16]{2,1,0:T(1,128)}, u32[]{:S(2)}) copy-start(s32[1,1,16]{2,1,0:T(1,128)} %param.28) | copy-start | bytes 196
  44.9 165.9 %copy-start.9 = (s32[1024]{0:T(1024)}, s32[1024]{0:T(1024)S(1)}, u32[]{:S(2)}) copy-start(s32[1024]{0:T(1024)S(1)} %pad_clamp_fusion) | copy-start | bytes 12292
  45.0 172.8 %copy-start.11 = (s32[16]{0:T(128)}, s32[16]{0:T(128)S(1)}, u32[]{:S(2)}) copy-start(s32[16]{0:T(128)S(1)} %fusion.41) | copy-start | bytes 196
  47.5 8.0 %copy-start.2 = (bf16[1,1,16,128,128]{4,3,2,1,0:T(8,128)(2,1)S(1)}, bf16[1,1,16,128,128]{4,3,2,1,0:T(8,128)(2,1)}, u32[]{:S(2)}) copy-start(bf16[1,1,16,128,128]{4,3,2,1,0:T(8,128)(2,1)} %param.27) | copy-start | bytes 1572868
  104.4 19.8 %all-to-all-start.1 = ((bf16[8,128,172]{1,2,0:T(8,128)(2,1)}), bf16[8,128,172]{1,2,0:T(8,128)(2,1)S(1)}, u32[]{:S(2)}, u32[]{:S(2)}) async-start(bf16[8,128,172]{1,2,0:T(8,128)(2,1)} %broadcast_select_fusion.2), calls=%async_computation.1 | async-start | bytes 720896 | tf_op jit(solution)/shard_map/all_to_all | solution.py:91
  110.2 60.7 %all-reduce.10.cloned.1.call-start = ((), (), s32[]{:S(2)}) async-start(), calls=%async_computation.5 | async-start | bytes 3145728 | tf_op jit(solution)/shard_map/psum | solution.py:99
  183.3 19.7 %all-to-all-start.2 = ((bf16[8,128,172]{1,2,0:T(8,128)(2,1)}), bf16[8,128,172]{1,2,0:T(8,128)(2,1)S(1)}, u32[]{:S(2)}, u32[]{:S(2)}) async-start(bf16[8,128,172]{1,2,0:T(8,128)(2,1)} %broadcast_select_fusion.1), calls=%async_computation.2 | async-start | bytes 720896 | tf_op jit(solution)/shard_map/all_to_all | solution.py:91
  189.1 60.8 %all-reduce.12.cloned.1.call-start = ((), (), s32[]{:S(2)}) async-start(), calls=%async_computation.6 | async-start | bytes 3145728 | tf_op jit(solution)/shard_map/psum | solution.py:99
  254.2 15.8 %copy-start.4 = (bf16[1536,128]{1,0:T(8,128)(2,1)S(1)}, bf16[1536,128]{1,0:T(8,128)(2,1)}, u32[]{:S(2)}) copy-start(bf16[1536,128]{1,0:T(8,128)(2,1)} %param.18) | copy-start | bytes 1179652
  264.2 24.4 %all-to-all-start.3 = ((bf16[8,128,172]{1,2,0:T(8,128)(2,1)}), bf16[8,128,172]{1,2,0:T(8,128)(2,1)}, u32[]{:S(2)}, u32[]{:S(2)}) async-start(bf16[8,128,172]{1,2,0:T(8,128)(2,1)} %broadcast_select_fusion), calls=%async_computation.3 | async-start | bytes 720896 | tf_op jit(solution)/shard_map/all_to_all | solution.py:91
  270.0 64.0 %all-reduce.14.cloned.1.call-start = ((), (), s32[]{:S(2)}) async-start(), calls=%async_computation.7 | async-start | bytes 3145728 | tf_op jit(solution)/shard_map/psum | solution.py:99
  277.1 7.2 %copy-start.8 = (s32[16]{0:T(128)S(1)}, s32[16]{0:T(128)}, u32[]{:S(2)}) copy-start(s32[16]{0:T(128)} %copy-done.7) | copy-start | bytes 196
  296.5 7.1 %copy-start.12 = (s32[16]{0:T(128)S(1)}, s32[16]{0:T(128)}, u32[]{:S(2)}) copy-start(s32[16]{0:T(128)} %copy-done.11) | copy-start | bytes 196
  302.0 2.0 copy-start.3
  310.4 1.9 copy-start.18
  312.0 180.3 %all-reduce.16.cloned.1.call-start = ((), (), s32[]{:S(2)}) async-start(), calls=%async_computation.8 | async-start | bytes 10878976 | tf_op jit(solution)/shard_map/psum | solution.py:109
  334.0 3.6 copy-start.17
  334.0 4.9 copy-start.21
  338.9 3.5 copy-start.16
  338.9 8.6 %slice-start = ((s8[6291456]{0:T(1024)(128)(4,1)}), s8[4194304]{0:T(1024)(128)(4,1)S(1)}, s32[]{:S(2)}) async-start(s8[6291456]{0:T(1024)(128)(4,1)} %bitcast.115), calls=%async_computation.9 | async-start | bytes 8388608
  342.3 5.1 %slice-start.1 = ((s8[6291456]{0:T(1024)(128)(4,1)}), s8[2097152]{0:T(1024)(128)(4,1)S(1)}, s32[]{:S(2)}) async-start(s8[6291456]{0:T(1024)(128)(4,1)} %bitcast.115), calls=%async_computation.10 | async-start | bytes 4194304
  354.9 5.4 %copy-start.5 = (bf16[1536,128]{1,0:T(8,128)(2,1)S(1)}, bf16[1536,128]{1,0:T(8,128)(2,1)}, u32[]{:S(2)}) copy-start(bf16[1536,128]{1,0:T(8,128)(2,1)} %param.18) | copy-start | bytes 1179652
  494.4 4.9 copy-start.6
Sparse Core Ops, SparseCore 0:
  70.2 21.6 all-reduce.7
  149.2 21.6 all-reduce.9
  228.2 21.6 all-reduce.11
  312.2 21.7 all-reduce.13
  362.3 130.0 all-reduce.15
where the time goes:
time: 517 us; the launch traced here: 507 us
  waiting for transfers between devices  171 us (33%)
  local copies, waits for them, and re-layouts  113 us (22%)
  other arithmetic  78.4 us (15%)
  matrix products  58.5 us (11%)
  blocking collectives  46.9 us (9%)
  starting transfers between devices  25.2 us (5%)
  between operations  14.5 us (3%)
    psum x1, waiting for transfers between devices, shards(): lax.psum((terms[0], terms[1], terms[2], terms[3], terms[4]), ('dom', 'col'))  93.2 us
    psum x4, waiting for transfers between devices, shards(): lax.psum((near + far).reshape(node_rows, classes).astype(jnp.bfloat16), '...  77.3 us
    psum x1, blocking collectives, shards(): lax.psum((terms[0], terms[1], terms[2], terms[3], terms[4]), ('dom', 'col'))  37 us
    scatter-add x8, other arithmetic, tile_sum(): return empty.at[targets].add(product)  34.2 us
    gather x8, local copies, waits for them, and re-layouts, shards(): outgoing = jnp.where(live[..., None], scaled[chosen], zero_value)  28.6 us
    all_to_all x4, starting transfers between devices, shards(): lax.all_to_all(outgoing, 'dom', split_axis=0, concat_axis=0, tiled=True)  24.6 us
    dot_general x8, matrix products, tile_sum(): jnp.einsum('tij,tjc->tic', tiles, blocks, preferred_element_type=jnp.floa...  21.1 us
    reshape x8, local copies, waits for them, and re-layouts, shards(): arrived.reshape(peers * slot_count // block_size, block_size, classes)  17 us
  transfers between devices with their start and end apart: 9, of which 5 were waited for; matrix products, arithmetic and copies ran while one was open for 13% of the time, Pallas kernels for 0%

commit v1 on v0

v1 whole, which is shorter than its diff:
```python
import functools
import math

import jax
import jax.numpy as jnp
from jax import lax
from jax.experimental import pallas as pl
from jax.experimental.pallas import tpu as pltpu
from jax.sharding import PartitionSpec as P

HOPS = 4
teleport = 0.1
LANES = 128
UNROLL = 16
VMEM_LIMIT = 40 * 1024 * 1024

bf16 = jnp.bfloat16
f32 = jnp.float32


def vmem():
    return pl.BlockSpec(memory_space=pltpu.VMEM)


def smem():
    return pl.BlockSpec(memory_space=pltpu.SMEM)


def params():
    return pltpu.CompilerParams(vmem_limit_bytes=VMEM_LIMIT)


def is_packed(slots, class_half):
    return slots % 64 == 0 and class_half <= 96


def packed_rows(slots, class_half):
    return slots * 3 // 4 if is_packed(slots, class_half) else slots


def gather_rows(v_ref, idx_ref, stage_ref):
    def body(g, carry):
        base = pl.multiple_of(g * UNROLL, UNROLL)
        for u in range(UNROLL):
            stage_ref[pl.ds(base + u, 1), :] = v_ref[pl.ds(idx_ref[base + u], 1), :]
        return carry

    lax.fori_loop(0, stage_ref.shape[0] // UNROLL, body, 0)


def pack_rows(stage_ref, out_ref, slots, class_half):
    peers = out_ref.shape[0]
    if not is_packed(slots, class_half):

        def plain(j, carry):
            base = pl.multiple_of(j * slots, slots)
            out_ref[j] = stage_ref[pl.ds(base, slots), :].astype(bf16)
            return carry

        lax.fori_loop(0, peers, plain, 0)
        return
    half, quarter = slots // 2, slots // 4
    lane_a = lax.broadcasted_iota(jnp.int32, (half, LANES), 1)
    lane_b = lax.broadcasted_iota(jnp.int32, (quarter, LANES), 1) // 32

    def body(j, carry):
        base = pl.multiple_of(j * slots, slots)
        low = stage_ref[pl.ds(base, half), :]
        high = stage_ref[pl.ds(base + half, half), :]
        out_ref[j, 0:half] = jnp.where(lane_a < 64, low, pltpu.roll(high, 64, 1)).astype(bf16)
        parts = (low[:quarter], low[quarter:], high[:quarter], high[quarter:])
        packed = jnp.zeros((quarter, LANES), f32)
        for g in range(4):
            packed = jnp.where(lane_b == g, pltpu.roll(parts[g], (g * 32 - 64) % LANES, 1), packed)
        out_ref[j, half : half + quarter] = packed.astype(bf16)
        return carry

    lax.fori_loop(0, peers, body, 0)


def unpack_rows(recv_ref, rows_ref, slots, class_half):
    peers = recv_ref.shape[0]
    if not is_packed(slots, class_half):

        def plain(j, carry):
            rows_ref[pl.ds(pl.multiple_of(j * slots, slots), slots), :] = recv_ref[j]
            return carry

        lax.fori_loop(0, peers, plain, 0)
        return
    half, quarter = slots // 2, slots // 4
    lane = lax.broadcasted_iota(jnp.int32, (quarter, LANES), 1)

    def body(j, carry):
        base = pl.multiple_of(j * slots, slots)
        wide = recv_ref[j, 0:half].astype(f32)
        narrow = recv_ref[j, half : half + quarter].astype(f32)
        turned = pltpu.roll(wide, 64, 1)
        fronts = (wide[:quarter], wide[quarter:], turned[:quarter], turned[quarter:])
        for g in range(4):
            back = pltpu.roll(narrow, (64 - g * 32) % LANES, 1)
            back = jnp.where(lane < 96, back, 0.0)
            rows_ref[pl.ds(base + g * quarter, quarter), :] = jnp.where(
                lane < 64, fronts[g], back
            ).astype(bf16)
        return carry

    lax.fori_loop(0, peers, body, 0)


def first_kernel(slots, class_half, classes, core_ref, idx_ref, nodes_ref, labels_ref, logits_ref, degree_ref,
                 out_ref, value_ref, accrued_ref, root_ref, wide_ref, diff_ref, v_ref, stage_ref):
    batch = logits_ref.shape[0]
    blocks, block = degree_ref.shape
    rows = blocks * block
    core = core_ref[0]
    wide_ref[...] = jnp.zeros_like(wide_ref)
    logits = logits_ref[...]
    shifted = jnp.exp(logits - jnp.max(logits, axis=-1, keepdims=True))
    wide_ref[:, :classes] = shifted / jnp.sum(shifted, axis=-1, keepdims=True)
    probs = wide_ref[...]
    turned = pltpu.roll(probs, wide_ref.shape[1] - class_half, 1)[:, :LANES]
    lane = lax.broadcasted_iota(jnp.int32, (batch, LANES), 1)
    chosen = jnp.where(core == 0, probs[:, :LANES], turned)
    diff_ref[...] = jnp.where(lane < class_half, chosen, 0.0)
    v_ref[...] = jnp.zeros_like(v_ref)
    lane_row = lax.broadcasted_iota(jnp.int32, (1, LANES), 1)
    inside = lane_row < class_half
    start = core * class_half

    def add_row(i, carry):
        hot = jnp.where((lane_row == labels_ref[i] - start) & inside, 1.0, 0.0)
        at = pl.ds(nodes_ref[i], 1)
        v_ref[at, :] = v_ref[at, :] + (diff_ref[pl.ds(i, 1), :] - hot)
        return carry

    lax.fori_loop(0, batch, add_row, 0, unroll=8)

    def scale(b, carry):
        at = pl.ds(pl.multiple_of(b * block, block), block)
        inv = lax.rsqrt(degree_ref[pl.ds(b, 1), :].astype(f32))
        root = jnp.transpose(jnp.broadcast_to(inv, (block, block)))
        root_ref[at, :] = root
        grad = v_ref[at, :]
        accrued_ref[at, :] = teleport * grad
        scaled = root * grad
        value_ref[at, :] = scaled.astype(bf16)
        v_ref[at, :] = scaled
        return carry

    lax.fori_loop(0, blocks, scale, 0)
    gather_rows(v_ref, idx_ref, stage_ref)
    pack_rows(stage_ref, out_ref, slots, class_half)


def add_tiles(acc_ref, source_ref, tile_refs, meta_ref, target_base, source_base, stride):
    count, block = tile_refs[0].shape[0], tile_refs[0].shape[1]
    for which, tiles in enumerate(tile_refs):
        for t in range(count):
            target = meta_ref[which * stride + target_base + t]
            source = meta_ref[which * stride + source_base + t]
            product = jnp.dot(
                tiles[t],
                source_ref[pl.ds(pl.multiple_of(source * block, block), block), :],
                preferred_element_type=f32,
            )
            at = pl.ds(pl.multiple_of(target * block, block), block)
            acc_ref[at, :] = acc_ref[at, :] + product


def near_kernel(stride, meta_ref, value_ref, own_ref, other_ref, near_ref):
    near_ref[...] = jnp.zeros_like(near_ref)
    count = own_ref.shape[0]
    add_tiles(near_ref, value_ref, (own_ref, other_ref), meta_ref, 0, count, stride)


def far_kernel(slots, class_half, base, stride, last, core_ref, meta_ref, idx_ref, recv_ref, near_ref, own_ref,
               other_ref, root_ref, accrued_ref, *rest):
    if last:
        keep_ref, send_ref, rows_ref, acc_ref = rest
    else:
        out_ref, value_ref, total_ref, rows_ref, acc_ref, stage_ref = rest
    block = own_ref.shape[1]
    count = own_ref.shape[0]
    rows = near_ref.shape[0]
    blocks = rows // block
    unpack_rows(recv_ref, rows_ref, slots, class_half)
    acc_ref[pl.ds(0, rows), :] = near_ref[...]
    add_tiles(acc_ref, rows_ref, (own_ref, other_ref), meta_ref, base, base + count, stride)
    rate = 1.0 - teleport
    if last:
        half_rows = rows // 2
        core = core_ref[0]
        for out, part in ((send_ref, 1 - core), (keep_ref, core)):

            def finish(b, carry, out=out, part=part):
                to = pl.ds(pl.multiple_of(b * block, block), block)
                at = pl.ds(pl.multiple_of(part * half_rows + b * block, block), block)
                current = rate * root_ref[at, :] * acc_ref[at, :]
                out[to, :] = (accrued_ref[at, :] + current).astype(bf16)
                return carry

            lax.fori_loop(0, half_rows // block, finish, 0)
        return
    acc_ref[pl.ds(rows, 8), :] = jnp.zeros((8, LANES), f32)

    def scale(b, carry):
        at = pl.ds(pl.multiple_of(b * block, block), block)
        root = root_ref[at, :]
        current = rate * root * acc_ref[at, :]
        total_ref[at, :] = accrued_ref[at, :] + teleport * current
        scaled = root * current
        value_ref[at, :] = scaled.astype(bf16)
        acc_ref[at, :] = scaled
        return carry

    lax.fori_loop(0, blocks, scale, 0)
    gather_rows(acc_ref, idx_ref, stage_ref)
    pack_rows(stage_ref, out_ref, slots, class_half)


def gelu_parts(x):
    k = math.sqrt(2.0 / math.pi)
    square = x * x
    t = jnp.tanh(x * (k + (k * 0.044715) * square))
    half_up = 0.5 + 0.5 * t
    slope = half_up + (0.5 * x) * (1.0 - t * t) * (k + (3.0 * k * 0.044715) * square)
    return (x * half_up).astype(bf16), slope.astype(bf16)


def swap_cores(x):
    return lax.ppermute(x, "col", [(0, 1), (1, 0)])


def exchange(x, first_step, second_step):
    domains, cores = lax.axis_size("dom"), lax.axis_size("col")
    steps = (first_step, second_step)
    pairs = [
        (d * cores + c, (d ^ steps[c]) * cores + c) for d in range(domains) for c in range(cores)
    ]
    return lax.ppermute(x, ("dom", "col"), pairs)


def halving_steps():
    domains = lax.axis_size("dom")
    bits = [1 << b for b in range(domains.bit_length() - 1)]
    other = list(bits)
    if len(bits) > 1:
        other[0], other[1] = other[1], other[0]
    return list(zip(bits, other))


def split(x, axis):
    half = x.shape[axis] // 2
    return lax.slice_in_dim(x, 0, half, axis=axis), lax.slice_in_dim(x, half, 2 * half, axis=axis)


def sum_over_domains(x):
    me, core = lax.axis_index("dom"), lax.axis_index("col")
    plan = []
    width, depth = x.shape[1], x.shape[0]
    for steps in halving_steps():
        if width > LANES:
            plan.append((steps, 1))
            width //= 2
        else:
            plan.append((steps, 0))
            depth //= 2
    current = x
    bits = []
    for (a, b), axis in plan:
        up = jnp.where(core == 0, me & a, me & b) != 0
        bits.append(up)
        low, high = split(current, axis)
        got = exchange(jnp.where(up, low, high), a, b)
        keep = jnp.where(up, high, low)
        current = (keep.astype(f32) + got.astype(f32)).astype(bf16)
    for ((a, b), axis), up in zip(plan[::-1], bits[::-1]):
        got = exchange(current, a, b)
        current = jnp.where(
            up,
            jnp.concatenate([got, current], axis),
            jnp.concatenate([current, got], axis),
        )
    return current


def shards(
    features,
    first_weight,
    first_bias,
    second_weight,
    second_bias,
    third_weight,
    local_tiles,
    local_target,
    local_source,
    halo_tiles,
    halo_target,
    halo_block,
    send_rows,
    send_count,
    degree,
    batch_nodes,
    labels,
    batch_logits,
):
    rows = degree.shape[0]
    classes = batch_logits.shape[-1]
    batch = batch_logits.shape[1]
    block = local_tiles.shape[-1]
    blocks = rows // block
    peers, slots = send_rows.shape[1], send_rows.shape[2]
    hidden = second_weight.shape[0]
    class_half = (classes // 2 + 7) // 8 * 8
    core = lax.axis_index("col").astype(jnp.int32)
    core_arg = core.reshape(1)
    packed = packed_rows(slots, class_half)
    local_count, halo_count = local_tiles.shape[2], halo_tiles.shape[2]

    meta_own = jnp.concatenate([local_target[0, 0], local_source[0, 0], halo_target[0, 0], halo_block[0, 0]])
    stride = meta_own.shape[0]
    meta = jnp.concatenate([meta_own, swap_cores(meta_own)])
    own_local, own_halo = local_tiles[0, 0], halo_tiles[0, 0]
    other_local, other_halo = swap_cores(own_local), swap_cores(own_halo)

    live = jnp.arange(slots, dtype=jnp.int32)[None, :] < send_count[0][:, None]
    idx = jnp.where(live, send_rows[0], rows).reshape(-1)

    out_type = jax.ShapeDtypeStruct((peers, packed, LANES), bf16)
    value_type = jax.ShapeDtypeStruct((rows, LANES), bf16)
    wide_type = jax.ShapeDtypeStruct((rows, LANES), f32)
    half_type = jax.ShapeDtypeStruct((rows // 2, LANES), bf16)
    stage = pltpu.VMEM((peers * slots, LANES), f32)

    out, value, accrued, root = pl.pallas_call(
        functools.partial(first_kernel, slots, class_half, classes),
        out_shape=(out_type, value_type, wide_type, wide_type),
        in_specs=[smem(), smem(), smem(), smem(), vmem(), vmem()],
        out_specs=(vmem(), vmem(), vmem(), vmem()),
        scratch_shapes=[
            pltpu.VMEM((batch, 2 * LANES), f32),
            pltpu.VMEM((batch, LANES), f32),
            pltpu.VMEM((rows + 8, LANES), f32),
            stage,
        ],
        compiler_params=params(),
        name="first",
    )(core_arg, idx, batch_nodes[0], labels[0], batch_logits[0], degree.reshape(blocks, block))

    near_call = pl.pallas_call(
        functools.partial(near_kernel, stride),
        out_shape=wide_type,
        in_specs=[smem(), vmem(), vmem(), vmem()],
        out_specs=vmem(),
        compiler_params=params(),
        cost_estimate=pl.CostEstimate(flops=4 * local_count * block**3, bytes_accessed=4 * 2**20, transcendentals=0),
        name="near",
    )

    x = features
    for hop in range(HOPS):
        last = hop + 1 == HOPS
        landed = lax.all_to_all(out, "dom", split_axis=0, concat_axis=0, tiled=True)
        near = near_call(meta, value, own_local, other_local)
        if hop == 0:
            x, _ = lax.optimization_barrier((x, value))
            pre_first = jnp.dot(x, first_weight, preferred_element_type=f32) + first_bias
            hidden_first, slope_first = gelu_parts(pre_first)
        if hop == 1:
            hidden_first, _ = lax.optimization_barrier((hidden_first, value))
            pre_second = jnp.dot(hidden_first, second_weight, preferred_element_type=f32) + second_bias
            hidden_second, slope_second = gelu_parts(pre_second)
        scratch = [pltpu.VMEM((peers * slots, LANES), bf16), pltpu.VMEM((rows + 8, LANES), f32)]
        result = pl.pallas_call(
            functools.partial(far_kernel, slots, class_half, 2 * local_count, stride, last),
            out_shape=(half_type, half_type) if last else (out_type, value_type, wide_type),
            in_specs=[smem(), smem(), smem()] + [vmem()] * 6,
            out_specs=(vmem(), vmem()) if last else (vmem(), vmem(), vmem()),
            scratch_shapes=scratch if last else scratch + [stage],
            compiler_params=params(),
            name="far_last" if last else "far",
        )(core_arg, meta, idx, landed, near, own_halo, other_halo, root, accrued)
        if last:
            keep, send = result
        else:
            out, value, accrued = result

    got = swap_cores(send)
    delta = jnp.concatenate([keep, got], axis=1)
    low = jnp.pad(third_weight[:, :class_half], ((0, 0), (0, LANES - class_half)))
    high = jnp.pad(third_weight[:, class_half:], ((0, 0), (0, LANES - classes + class_half)))
    third = jnp.where(core == 0, jnp.concatenate([low, high], 1), jnp.concatenate([high, low], 1))

    def contract(a, b):
        return lax.dot_general(a, b, (((0,), (0,)), ((), ())), preferred_element_type=f32)

    third_grad = contract(delta, hidden_second).astype(bf16)
    back_second = lax.dot_general(delta, third, (((1,), (1,)), ((), ())), preferred_element_type=f32)
    second_delta = (slope_second.astype(f32) * back_second).astype(bf16)
    second_grad = contract(hidden_first, second_delta).astype(bf16)
    second_bias_grad = jnp.sum(second_delta.astype(f32), axis=0).astype(bf16)
    back_first = lax.dot_general(
        second_delta, second_weight, (((1,), (1,)), ((), ())), preferred_element_type=f32
    )
    first_delta = (slope_first.astype(f32) * back_first).astype(bf16)
    first_grad = contract(x, first_delta).astype(bf16)
    first_bias_grad = jnp.sum(first_delta.astype(f32), axis=0).astype(bf16)

    feat = first_grad.shape[0]
    parts = hidden // 2, feat // 2, class_half
    used = sum(parts) + 1
    domains = lax.axis_size("dom")
    column_splits = (hidden // LANES).bit_length() - 1
    grain = 8 * max(1, domains >> column_splits)
    total_rows = -(-used // grain) * grain

    def bundle(part, third_part, bias_row):
        second_rows = lax.dynamic_slice_in_dim(second_grad, part * parts[0], parts[0], 0)
        first_rows = lax.dynamic_slice_in_dim(first_grad, part * parts[1], parts[1], 0)
        bias = jnp.broadcast_to(bias_row[None], (total_rows - used + 1, hidden))
        return jnp.concatenate([second_rows, first_rows, third_part[:class_half], bias], 0)

    is_first = core == 0
    keep_rows = bundle(core, third_grad[:LANES], jnp.where(is_first, first_bias_grad, second_bias_grad))
    send_rows_ = bundle(1 - core, third_grad[LANES:], jnp.where(is_first, second_bias_grad, first_bias_grad))
    got_rows = swap_cores(send_rows_)
    mine = sum_over_domains((keep_rows.astype(f32) + got_rows.astype(f32)).astype(bf16))
    theirs = swap_cores(mine)
    low = jnp.where(is_first, mine, theirs).astype(f32)
    high = jnp.where(is_first, theirs, mine).astype(f32)
    a, b, c = parts[0], parts[0] + parts[1], used - 1
    return (
        jnp.concatenate([low[a:b], high[a:b]], 0),
        low[c],
        jnp.concatenate([low[:a], high[:a]], 0),
        high[c],
        jnp.concatenate([low[b:c], high[b : b + classes - class_half]], 0).T,
    )


def solution(mesh):
    return jax.shard_map(
        shards,
        mesh=mesh,
        in_specs=(
            P(("grp", "dom", "col"), None),
            P(),
            P(),
            P(),
            P(),
            P(),
            P(("grp", "dom"), "col", None, None, None),
            P(("grp", "dom"), "col", None),
            P(("grp", "dom"), "col", None),
            P(("grp", "dom"), "col", None, None, None),
            P(("grp", "dom"), "col", None),
            P(("grp", "dom"), "col", None),
            P(("grp", "dom"), None, None),
            P(("grp", "dom"), None),
            P(("grp", "dom")),
            P(("grp", "dom"), None),
            P(("grp", "dom"), None),
            P(("grp", "dom"), None, None),
        ),
        out_specs=(P("grp", None), P("grp"), P("grp", None), P("grp"), P("grp", None)),
        check_vma=False,
    )
```

time: 517 us -> 230 us (0.44); the launches traced: 507 us -> 228 us
  waiting for transfers between devices: 171 us -> 67.6 us
  other arithmetic: 78.4 us -> 15.7 us
  local copies, waits for them, and re-layouts: 113 us -> 54.6 us
  blocking collectives: 46.9 us -> 0 us
  Pallas kernels: 0 us -> 32.2 us
  matrix products: 58.5 us -> 28.1 us
  between operations: 14.5 us -> 1.2 us
    psum x5 -> x0, waiting for transfers between devices: 171 us -> none  [the longest x1 93.2 us: shards(): lax.psum((terms[0], terms[1], terms[2], terms[3], terms[4]), ('dom', 'col'))]
    ppermute x0 -> x12, waiting for transfers between devices: none -> 54.6 us  [the longest x6 47.2 us: exchange(): return lax.ppermute(x, ('dom', 'col'), pairs)]
    gather x16 -> x0, local copies, waits for them, and re-layouts: 49.5 us -> none  [the longest x8 28.6 us: shards(): outgoing = jnp.where(live[..., None], scaled[chosen], zero_value)]
    scatter-add x9 -> x0, other arithmetic: 38.3 us -> none  [the longest x8 34.2 us: tile_sum(): return empty.at[targets].add(product)]
    psum x1 -> x0, blocking collectives: 37 us -> none  [shards(): lax.psum((terms[0], terms[1], terms[2], terms[3], terms[4]), ('dom', 'col'))]
    unnamed x52 -> x109, local copies, waits for them, and re-layouts: 10.9 us -> 46.1 us
    pallas_call x0 -> x9, Pallas kernels: none -> 32.2 us  [the longest x4 18.5 us: shards(): pl.pallas_call(functools.partial(far_kernel, slots, class_half, 2 * local...]
    dot_general x15 -> x7, matrix products: 58.5 us -> 28.1 us  [the longest x3 6.95 us: contract(): lax.dot_general(a, b, (((0,), (0,)), ((), ())), preferred_element_type=f32)]
  transfers between devices with their start and end apart: 9 -> 16, of which waited for: 5 -> 12; matrix products, arithmetic and copies ran while one was open for 13% -> 7% of each run, Pallas kernels for 0% -> 3%
where the time goes in v1:
time: 230 us; the launch traced here: 228 us
  waiting for transfers between devices  67.6 us (29%)
  local copies, waits for them, and re-layouts  54.6 us (24%)
  Pallas kernels  32.2 us (14%)
  starting transfers between devices  28.6 us (12%)
  matrix products  28.1 us (12%)
  other arithmetic  15.7 us (7%)
    ppermute x6, waiting for transfers between devices, exchange(): return lax.ppermute(x, ('dom', 'col'), pairs)  47.2 us
    unnamed x109, local copies, waits for them, and re-layouts  46.1 us
    pallas_call x4, Pallas kernels, shards(): pl.pallas_call(functools.partial(far_kernel, slots, class_half, 2 * local...  18.5 us
    all_to_all x4, starting transfers between devices, shards(): landed = lax.all_to_all(out, 'dom', split_axis=0, concat_axis=0, tiled=True)  18.2 us
    all_to_all x4, waiting for transfers between devices, shards(): landed = lax.all_to_all(out, 'dom', split_axis=0, concat_axis=0, tiled=True)  13 us
    ppermute x6, starting transfers between devices, exchange(): return lax.ppermute(x, ('dom', 'col'), pairs)  9.22 us
    pallas_call x1, Pallas kernels, shards(): pl.pallas_call(functools.partial(first_kernel, slots, class_half, classes...  7.44 us
    ppermute x6, waiting for transfers between devices, swap_cores(): return lax.ppermute(x, 'col', [(0, 1), (1, 0)])  7.34 us
  transfers between devices with their start and end apart: 16, of which 12 were waited for; matrix products, arithmetic and copies ran while one was open for 7% of the time, Pallas kernels for 3%

profile of v1, /device:TPU:0, one launch (start us, length us, event | category | flops | bytes accessed | tf_op | source)
XLA Modules:
  0.0 228.0 jit_solution(553437859023075760)
XLA Ops:
  5.4 7.4 %first.1 = (bf16[8,192,128]{2,1,0:T(8,128)(2,1)S(1)}, bf16[3072,128]{1,0:T(8,128)(2,1)S(1)}, f32[3072,128]{1,0:T(8,128)S(1)}, f32[3072,128]{1,0:T(8,128)S(1)}) custom-call(s32[1]{0:T(128)} %bitcast.core_ref, s32[2048]{0:T(1024)S(1)} %broadcast_select_fusion.3.idx_ref, s32[256]{0:T(256)S(1)} %bitcast.42, s32[256]{0:T(256)S(1)} %bitcast.43, ...), custom_call_target="tpu_custom_call" | custom-call | tf_op jit(solution)/shard_map/first/pallas_call | solution.py:336
  12.9 1.2 copy-done.1
  14.1 1.2 copy-done.21
  16.9 7.3 %all-to-all-start = ((bf16[8,192,128]{2,1,0:T(8,128)(2,1)}), bf16[8,192,128]{2,1,0:T(8,128)(2,1)S(1)}, u32[]{:S(2)}, u32[]{:S(2)}) async-start(bf16[8,192,128]{2,1,0:T(8,128)(2,1)} %copy-done.36), calls=%async_computation | async-start | bytes 786432 | tf_op jit(solution)/shard_map/all_to_all | solution.py:364
  25.5 1.3 collective-permute-done
  29.7 1.6 near.4.near_ref
  31.3 1.1 copy-done.13
  32.4 3.4 %all-to-all-done.recv_ref = bf16[8,192,128]{2,1,0:T(8,128)(2,1)S(1)} async-done(((bf16[8,192,128]{2,1,0:T(8,128)(2,1)}), bf16[8,192,128]{2,1,0:T(8,128)(2,1)S(1)}, u32[]{:S(2)}, u32[]{:S(2)}) %all-to-all-start) | async-done | bytes 393248 | tf_op jit(solution)/shard_map/all_to_all | solution.py:364
  35.8 1.4 copy-done.2
  37.2 1.4 copy-done.14
  38.6 1.4 copy-done.22
  40.1 5.4 %far.3 = (bf16[8,192,128]{2,1,0:T(8,128)(2,1)S(1)}, bf16[3072,128]{1,0:T(8,128)(2,1)S(1)}, f32[3072,128]{1,0:T(8,128)S(1)}) custom-call(s32[1]{0:T(128)} %bitcast.core_ref, s32[128]{0:T(128)S(1)} %concatenate.50.meta_ref, s32[2048]{0:T(1024)S(1)} %broadcast_select_fusion.3.idx_ref, bf16[8,192,128]{2,1,0:T(8,128)(2,1)S(1)} %all-to-all-done.recv_ref, ...), custom_call_target="tpu_custom_call" | custom-call | tf_op jit(solution)/shard_map/far/pallas_call | solution.py:375
  45.5 1.1 copy-done.25
  48.2 3.6 %all-to-all-start.1 = ((bf16[8,192,128]{2,1,0:T(8,128)(2,1)}), bf16[8,192,128]{2,1,0:T(8,128)(2,1)S(1)}, u32[]{:S(2)}, u32[]{:S(2)}) async-start(bf16[8,192,128]{2,1,0:T(8,128)(2,1)} %copy-done.38), calls=%async_computation.1 | async-start | bytes 786432 | tf_op jit(solution)/shard_map/all_to_all | solution.py:364
  54.0 1.6 near.5.near_ref
  55.6 1.1 copy-done.15
  56.8 6.7 %all-to-all-done.1.recv_ref = bf16[8,192,128]{2,1,0:T(8,128)(2,1)S(1)} async-done(((bf16[8,192,128]{2,1,0:T(8,128)(2,1)}), bf16[8,192,128]{2,1,0:T(8,128)(2,1)S(1)}, u32[]{:S(2)}, u32[]{:S(2)}) %all-to-all-start.1) | async-done | bytes 393248 | tf_op jit(solution)/shard_map/all_to_all | solution.py:364
  63.4 1.4 copy-done.3
  64.9 1.4 copy-done.16
  66.3 1.4 copy-done.26
  67.7 5.4 %far.4 = (bf16[8,192,128]{2,1,0:T(8,128)(2,1)S(1)}, bf16[3072,128]{1,0:T(8,128)(2,1)S(1)}, f32[3072,128]{1,0:T(8,128)S(1)}) custom-call(s32[1]{0:T(128)} %bitcast.core_ref, s32[128]{0:T(128)S(1)} %concatenate.50.meta_ref, s32[2048]{0:T(1024)S(1)} %broadcast_select_fusion.3.idx_ref, bf16[8,192,128]{2,1,0:T(8,128)(2,1)S(1)} %all-to-all-done.1.recv_ref, ...), custom_call_target="tpu_custom_call" | custom-call | tf_op jit(solution)/shard_map/far/pallas_call | solution.py:375
  73.1 1.1 copy-done.19
  75.8 3.6 %all-to-all-start.2 = ((bf16[8,192,128]{2,1,0:T(8,128)(2,1)}), bf16[8,192,128]{2,1,0:T(8,128)(2,1)S(1)}, u32[]{:S(2)}, u32[]{:S(2)}) async-start(bf16[8,192,128]{2,1,0:T(8,128)(2,1)} %copy-done.35), calls=%async_computation.2 | async-start | bytes 786432 | tf_op jit(solution)/shard_map/all_to_all | solution.py:364
  79.5 1.6 slice.60
  81.1 1.6 pad.9
  84.9 1.6 near.6.near_ref
  86.5 1.1 copy-done.17
  87.7 2.9 %all-to-all-done.2.recv_ref = bf16[8,192,128]{2,1,0:T(8,128)(2,1)S(1)} async-done(((bf16[8,192,128]{2,1,0:T(8,128)(2,1)}), bf16[8,192,128]{2,1,0:T(8,128)(2,1)S(1)}, u32[]{:S(2)}, u32[]{:S(2)}) %all-to-all-start.2) | async-done | bytes 393248 | tf_op jit(solution)/shard_map/all_to_all | solution.py:364
  90.6 1.4 copy-done.4
  92.0 1.4 copy-done.18
  93.4 1.4 copy-done.20
  94.8 5.4 %far.5 = (bf16[8,192,128]{2,1,0:T(8,128)(2,1)S(1)}, bf16[3072,128]{1,0:T(8,128)(2,1)S(1)}, f32[3072,128]{1,0:T(8,128)S(1)}) custom-call(s32[1]{0:T(128)} %bitcast.core_ref, s32[128]{0:T(128)S(1)} %concatenate.50.meta_ref, s32[2048]{0:T(1024)S(1)} %broadcast_select_fusion.3.idx_ref, bf16[8,192,128]{2,1,0:T(8,128)(2,1)S(1)} %all-to-all-done.2.recv_ref, ...), custom_call_target="tpu_custom_call" | custom-call | tf_op jit(solution)/shard_map/far/pallas_call | solution.py:375
  100.2 1.1 copy-done.23
  103.0 3.7 %all-to-all-start.3 = ((bf16[8,192,128]{2,1,0:T(8,128)(2,1)}), bf16[8,192,128]{2,1,0:T(8,128)(2,1)S(1)}, u32[]{:S(2)}, u32[]{:S(2)}) async-start(bf16[8,192,128]{2,1,0:T(8,128)(2,1)} %copy-done.37), calls=%async_computation.3 | async-start | bytes 786432 | tf_op jit(solution)/shard_map/all_to_all | solution.py:364
  106.7 1.7 slice_select_fusion
  108.4 6.9 %multiply_convert_fusion.3 = (bf16[1536,1024]{1,0:T(8,128)(2,1)}, f32[1536,1024]{1,0:T(8,128)}) fusion(f32[1024]{0:T(1024)} %param.20, bf16[1536,128]{1,0:T(8,128)(2,1)} %param.18, bf16[128,1024]{1,0:T(8,128)(2,1)} %param.19), kind=kOutput, calls=%fused_computation.8 | convolution fusion | flops 416808960 | bytes 10096640 | tf_op jit(solution)/shard_map/dot_general | solution.py:368
  115.4 1.6 near.7.near_ref
  118.1 1.4 copy-done.5
  119.5 1.4 copy-done.12
  120.9 1.4 copy-done.24
  122.3 2.3 %far_last.1 = (bf16[1536,128]{1,0:T(8,128)(2,1)S(1)}, bf16[1536,128]{1,0:T(8,128)(2,1)S(1)}) custom-call(s32[1]{0:T(128)} %bitcast.core_ref, s32[128]{0:T(128)S(1)} %concatenate.50.meta_ref, s32[2048]{0:T(1024)S(1)} %broadcast_select_fusion.3.idx_ref, bf16[8,192,128]{2,1,0:T(8,128)(2,1)S(1)} %all-to-all-done.3.recv_ref, f32[3072,128]{1,0:T(8,128)S(1)} %copy-done.12, ...), custom_call_target="tpu_custom_call" | custom-call | tf_op jit(solution)/shard_map/far_last/pallas_call | solution.py:375
  124.8 3.5 %fusion.15 = f32[1536,1024]{1,0:T(8,128)S(1)} fusion(bf16[1536,1024]{1,0:T(8,128)(2,1)S(1)} %copy-done.50, bf16[1024,1024]{1,0:T(8,128)(2,1)S(1)} %copy-done), kind=kOutput, calls=%fused_computation.58 | convolution fusion | flops 3221225472 | bytes 11534336 | tf_op jit(solution)/shard_map/dot_general | solution.py:372
  128.6 2.4 %fusion.1 = bf16[256,1024]{1,0:T(8,128)(2,1)S(1)} fusion(bf16[1536,256]{1,0:T(8,128)(2,1)S(1)} %constant_dynamic-update-slice_fusion, f32[1536,1024]{1,0:T(8,128)S(1)} %fusion.15, f32[1024]{0:T(1024)S(1)} %copy-done.48), kind=kOutput, calls=%fused_computation.21 | convolution fusion | flops 819724288 | bytes 7606272 | tf_op jit(solution)/shard_map/dot_general | solution.py:396
  131.7 4.1 %fusion.14 = (bf16[1024]{0:T(1024)(128)(2,1)S(1)}, bf16[1536,1024]{1,0:T(8,128)(2,1)S(1)}) fusion(bf16[1536,256]{1,0:T(8,128)(2,1)S(1)} %constant_dynamic-update-slice_fusion, bf16[1024,128]{0,1:T(8,128)(2,1)S(1)} %copy-done.46, bf16[1024,128]{0,1:T(8,128)(2,1)S(1)} %copy-done.45, pred[]{:T(512)S(6)} %eq.2, f32[1536,1024]{1,0:T(8,128)S(1)} %fusion.15, ...), kind=kOutput, calls=%fused_computation.57 | convolution fusion | flops 839121920 | bytes 10754049 | tf_op jit(solution)/shard_map/dot_general | solution.py:399
  135.8 3.9 %convolution_convert_fusion = bf16[1024,1024]{1,0:T(8,128)(2,1)S(1)} fusion(bf16[1536,1024]{1,0:T(8,128)(2,1)S(1)} %copy-done.50, bf16[1536,1024]{1,0:T(8,128)(2,1)S(1)} %get-tuple-element.54), kind=kOutput, calls=%fused_computation.15 | convolution fusion | flops 3222274048 | bytes 8388608 | tf_op jit(solution)/shard_map/dot_general | solution.py:396
  139.8 6.6 %fusion.13 = (bf16[1024]{0:T(1024)(128)(2,1)S(1)}, bf16[1536,1024]{1,0:T(8,128)(2,1)S(1)}) fusion(bf16[1536,1024]{1,0:T(8,128)(2,1)S(1)} %get-tuple-element.54, bf16[1024,1024]{1,0:T(8,128)(2,1)S(1)} %copy-done, f32[1536,1024]{1,0:T(8,128)S(1)} %bitcast.58, f32[1024]{0:T(1024)S(1)} %copy-done.49), kind=kOutput, calls=%fused_computation.56 | convolution fusion | flops 3252681728 | bytes 14686208 | tf_op jit(solution)/shard_map/dot_general | solution.py:403
  147.0 1.2 constant_dynamic-slice_fusion.3
  148.9 1.2 pad_maximum_fusion.1
  150.5 3.0 %collective-permute-done.4 = bf16[672,1024]{1,0:T(8,128)(2,1)S(1)} collective-permute-done((bf16[672,1024]{1,0:T(8,128)(2,1)}, bf16[672,1024]{1,0:T(8,128)(2,1)S(1)}, u32[]{:S(2)}, u32[]{:S(2)}) %collective-permute-start.4) | collective-permute-done | bytes 1376288 | tf_op jit(solution)/shard_map/ppermute | solution.py:232
  154.6 2.3 %add_convert_fusion.2 = bf16[672,1024]{1,0:T(8,128)(2,1)S(1)} fusion(bf16[672,1024]{1,0:T(8,128)(2,1)} %copy-done.43, bf16[8,1024]{1,0:T(8,128)(2,1)S(1)} %broadcast_in_dim.9, bf16[88,1024]{1,0:T(8,128)(2,1)} %get-tuple-element.43, bf16[64,1024]{1,0:T(8,128)(2,1)} %get-tuple-element.45, bf16[512,1024]{1,0:T(8,128)(2,1)} %get-tuple-element.41), kind=kLoop, calls=%fused_computation.14 | loop fusion | flops 7569408 | bytes 4128768 | tf_op jit(solution)/shard_map/convert_element_type | solution.py:428
  157.8 2.0 collective-permute-start.5
  159.8 9.3 %collective-permute-done.5 = bf16[672,512]{1,0:T(8,128)(2,1)} collective-permute-done((bf16[672,512]{1,0:T(8,128)(2,1)}, bf16[672,512]{1,0:T(8,128)(2,1)}, u32[]{:S(2)}, u32[]{:S(2)}) %collective-permute-start.5) | collective-permute-done | bytes 688160 | tf_op jit(solution)/shard_map/ppermute | solution.py:241
  169.1 1.4 add_convert_fusion.3
  171.3 2.1 collective-permute-start.6
  173.4 5.2 %collective-permute-done.6 = bf16[672,256]{1,0:T(8,128)(2,1)S(1)} collective-permute-done((bf16[672,256]{1,0:T(8,128)(2,1)S(1)}, bf16[672,256]{1,0:T(8,128)(2,1)S(1)}, u32[]{:S(2)}, u32[]{:S(2)}) %collective-permute-start.6) | collective-permute-done | bytes 344096 | tf_op jit(solution)/shard_map/ppermute | solution.py:241
  178.6 1.2 add_convert_fusion.4
  179.9 3.0 %collective-permute-start.7 = (bf16[672,128]{1,0:T(8,128)(2,1)S(1)}, bf16[672,128]{1,0:T(8,128)(2,1)S(1)}, u32[]{:S(2)}, u32[]{:S(2)}) collective-permute-start(bf16[672,128]{1,0:T(8,128)(2,1)S(1)} %broadcast_select_fusion.2), channel_id=1, source_target_pairs={{0,8},{1,9},{2,10},{3,11},{4,12},{5,13},{6,14},{7,15},{8,0},{9,1},... | collective-permute-start | bytes 516104 | tf_op jit(solution)/shard_map/ppermute | solution.py:241
  182.8 6.9 %collective-permute-done.7 = bf16[672,128]{1,0:T(8,128)(2,1)S(1)} collective-permute-done((bf16[672,128]{1,0:T(8,128)(2,1)S(1)}, bf16[672,128]{1,0:T(8,128)(2,1)S(1)}, u32[]{:S(2)}, u32[]{:S(2)}) %collective-permute-start.7) | collective-permute-done | bytes 172064 | tf_op jit(solution)/shard_map/ppermute | solution.py:241
  189.9 9.6 %collective-permute-done.8 = bf16[672,128]{1,0:T(8,128)(2,1)S(1)} collective-permute-done((bf16[672,128]{1,0:T(8,128)(2,1)S(1)}, bf16[672,128]{1,0:T(8,128)(2,1)S(1)}, u32[]{:S(2)}, u32[]{:S(2)}) %collective-permute-start.8) | collective-permute-done | bytes 172064 | tf_op jit(solution)/shard_map/ppermute | solution.py:241
  199.7 7.2 %collective-permute-done.9 = bf16[672,256]{1,0:T(8,128)(2,1)S(1)} collective-permute-done((bf16[672,256]{1,0:T(8,128)(2,1)S(1)}, bf16[672,256]{1,0:T(8,128)(2,1)S(1)}, u32[]{:S(2)}, u32[]{:S(2)}) %collective-permute-start.9) | collective-permute-done | bytes 344096 | tf_op jit(solution)/shard_map/ppermute | solution.py:241
  207.1 2.0 collective-permute-start.10
  209.2 9.0 %collective-permute-done.10 = bf16[672,512]{1,0:T(8,128)(2,1)S(1)} collective-permute-done((bf16[672,512]{1,0:T(8,128)(2,1)S(1)}, bf16[672,512]{1,0:T(8,128)(2,1)S(1)}, u32[]{:S(2)}, u32[]{:S(2)}) %collective-permute-start.10) | collective-permute-done | bytes 688160 | tf_op jit(solution)/shard_map/ppermute | solution.py:241
  218.6 3.1 %collective-permute-done.11 = bf16[672,1024]{1,0:T(8,128)(2,1)S(1)} collective-permute-done((bf16[672,1024]{1,0:T(8,128)(2,1)S(1)}, bf16[672,1024]{1,0:T(8,128)(2,1)S(1)}, u32[]{:S(2)}, u32[]{:S(2)}) %collective-permute-start.11) | collective-permute-done | bytes 1376288 | tf_op jit(solution)/shard_map/ppermute | solution.py:232
  224.7 2.3 %pad_maximum_fusion = f32[1024,1024]{1,0:T(8,128)} fusion(f32[512,1024]{1,0:T(8,128)S(1)} %slice.89, f32[512,1024]{1,0:T(8,128)S(1)} %slice.88), kind=kLoop, calls=%fused_computation.12 | loop fusion | flops 1048576 | bytes 8388608 | tf_op jit(solution)/shard_map/concatenate | solution.py:436
  (132 shorter events, 31.6 us)
Async XLA Ops:
  0.6 124.1 %copy-start = (bf16[1024,1024]{1,0:T(8,128)(2,1)S(1)}, bf16[1024,1024]{1,0:T(8,128)(2,1)}, u32[]{:S(2)}) copy-start(bf16[1024,1024]{1,0:T(8,128)(2,1)} %param.21) | copy-start | bytes 6291460
  0.6 35.2 %copy-start.6 = (bf16[1,1,16,128,128]{4,3,2,1,0:T(8,128)(2,1)S(1)}, bf16[1,1,16,128,128]{4,3,2,1,0:T(8,128)(2,1)}, u32[]{:S(2)}) copy-start(bf16[1,1,16,128,128]{4,3,2,1,0:T(8,128)(2,1)} %param.27) | copy-start | bytes 1572868
  12.9 1.2 copy-start.1
  14.1 1.2 copy-start.21
  15.3 0.9 copy-start.29
  16.1 0.7 copy-start.36
  16.9 18.9 %all-to-all-start = ((bf16[8,192,128]{2,1,0:T(8,128)(2,1)}), bf16[8,192,128]{2,1,0:T(8,128)(2,1)S(1)}, u32[]{:S(2)}, u32[]{:S(2)}) async-start(bf16[8,192,128]{2,1,0:T(8,128)(2,1)} %copy-done.36), calls=%async_computation | async-start | bytes 786432 | tf_op jit(solution)/shard_map/all_to_all | solution.py:364
  24.1 3.4 %collective-permute-start.1 = (bf16[16,128,128]{2,1,0:T(8,128)(2,1)}, bf16[16,128,128]{2,1,0:T(8,128)(2,1)}, u32[]{:S(2)}, u32[]{:S(2)}) collective-permute-start(bf16[16,128,128]{2,1,0:T(8,128)(2,1)} %bitcast.35), channel_id=1, source_target_pairs={{0,1},{1,0},{2,3},{3,2},{4,5},{5,4},{6,7},{7,6},{8,9},{9,8},{10,11... | collective-permute-start | bytes 1572872 | tf_op jit(solution)/shard_map/ppermute | solution.py:232
  24.1 8.3 %collective-permute-start.2 = (bf16[16,128,128]{2,1,0:T(8,128)(2,1)}, bf16[16,128,128]{2,1,0:T(8,128)(2,1)S(1)}, u32[]{:S(2)}, u32[]{:S(2)}) collective-permute-start(bf16[16,128,128]{2,1,0:T(8,128)(2,1)} %bitcast.30), channel_id=1, source_target_pairs={{0,1},{1,0},{2,3},{3,2},{4,5},{5,4},{6,7},{7,6},{8,9},{9,8},{10,11... | collective-permute-start | bytes 1572872 | tf_op jit(solution)/shard_map/ppermute | solution.py:232
  25.4 1.3 collective-permute-start
  27.5 1.0 copy-start.7
  28.6 1.1 copy-start.30
  31.3 1.1 copy-start.13
  35.8 1.4 copy-start.2
  37.2 1.4 copy-start.14
  38.6 1.4 copy-start.22
  45.4 1.2 copy-start.25
  46.6 0.9 copy-start.33
  47.5 0.7 copy-start.38
  48.2 15.2 %all-to-all-start.1 = ((bf16[8,192,128]{2,1,0:T(8,128)(2,1)}), bf16[8,192,128]{2,1,0:T(8,128)(2,1)S(1)}, u32[]{:S(2)}, u32[]{:S(2)}) async-start(bf16[8,192,128]{2,1,0:T(8,128)(2,1)} %copy-done.38), calls=%async_computation.1 | async-start | bytes 786432 | tf_op jit(solution)/shard_map/all_to_all | solution.py:364
  51.9 1.0 copy-start.8
  52.9 1.1 copy-start.34
  55.6 1.1 copy-start.15
  63.4 1.4 copy-start.3
  64.8 1.4 copy-start.16
  66.3 1.4 copy-start.26
  73.1 1.2 copy-start.19
  74.2 0.9 copy-start.27
  75.8 14.8 %all-to-all-start.2 = ((bf16[8,192,128]{2,1,0:T(8,128)(2,1)}), bf16[8,192,128]{2,1,0:T(8,128)(2,1)S(1)}, u32[]{:S(2)}, u32[]{:S(2)}) async-start(bf16[8,192,128]{2,1,0:T(8,128)(2,1)} %copy-done.35), calls=%async_computation.2 | async-start | bytes 786432 | tf_op jit(solution)/shard_map/all_to_all | solution.py:364
  82.8 1.0 copy-start.9
  83.8 1.1 copy-start.28
  86.5 1.1 copy-start.17
  90.6 1.4 copy-start.4
  92.0 1.4 copy-start.18
  93.4 1.4 copy-start.20
  94.8 11.9 %copy-start.47 = (pred[128]{0:T(512)(128)(4,1)S(1)}, pred[128]{0:T(512)(128)(4,1)}, u32[]{:S(2)}) copy-start(pred[128]{0:T(512)(128)(4,1)} %constant.37.clone.1) | copy-start | bytes 388
  100.2 1.1 copy-start.23
  101.4 0.9 copy-start.31
  103.0 15.1 %all-to-all-start.3 = ((bf16[8,192,128]{2,1,0:T(8,128)(2,1)}), bf16[8,192,128]{2,1,0:T(8,128)(2,1)S(1)}, u32[]{:S(2)}, u32[]{:S(2)}) async-start(bf16[8,192,128]{2,1,0:T(8,128)(2,1)} %copy-done.37), calls=%async_computation.3 | async-start | bytes 786432 | tf_op jit(solution)/shard_map/all_to_all | solution.py:364
  108.4 6.9 %copy-start.10 = (bf16[1,1,16,128,128]{4,3,2,1,0:T(8,128)(2,1)S(1)}, bf16[1,1,16,128,128]{4,3,2,1,0:T(8,128)(2,1)}, u32[]{:S(2)}) copy-start(bf16[1,1,16,128,128]{4,3,2,1,0:T(8,128)(2,1)} %param.24) | copy-start | bytes 1572868
  108.4 6.9 %copy-start.32 = (bf16[3072,128]{1,0:T(8,128)(2,1)S(1)}, bf16[3072,128]{1,0:T(8,128)(2,1)}, u32[]{:S(2)}) copy-start(bf16[3072,128]{1,0:T(8,128)(2,1)} %copy-done.31) | copy-start | bytes 2359300
  117.0 1.1 copy-start.11
  118.1 1.4 copy-start.5
  119.5 1.4 copy-start.12
  120.9 1.4 copy-start.24
  122.3 2.5 %copy-start.50 = (bf16[1536,1024]{1,0:T(8,128)(2,1)S(1)}, bf16[1536,1024]{1,0:T(8,128)(2,1)}, u32[]{:S(2)}) copy-start(bf16[1536,1024]{1,0:T(8,128)(2,1)} %get-tuple-element.28) | copy-start | bytes 9437188
  124.7 3.8 %copy-start.48 = (f32[1024]{0:T(1024)S(1)}, f32[1024]{0:T(1024)}, u32[]{:S(2)}) copy-start(f32[1024]{0:T(1024)} %param.22) | copy-start | bytes 12292
  124.7 3.7 %collective-permute-start.3 = (bf16[1536,128]{1,0:T(8,128)(2,1)S(1)}, bf16[1536,128]{1,0:T(8,128)(2,1)S(1)}, u32[]{:S(2)}, u32[]{:S(2)}) collective-permute-start(bf16[1536,128]{1,0:T(8,128)(2,1)S(1)} %get-tuple-element.38), channel_id=1, source_target_pairs={{0,1},{1,0},{2,3},{3,2},{4,5},{5,4},{6,7},{7,6},{8,9},{9,8},{10,11... | collective-permute-start | bytes 1179656 | tf_op jit(solution)/shard_map/ppermute | solution.py:232
  128.5 3.2 %copy-start.45 = (bf16[1024,128]{0,1:T(8,128)(2,1)S(1)}, bf16[1024,128]{0,1:T(8,128)(2,1)}, u32[]{:S(2)}) copy-start(bf16[1024,128]{0,1:T(8,128)(2,1)} %slice_select_fusion) | copy-start | bytes 786436
  128.5 3.2 %copy-start.46 = (bf16[1024,128]{0,1:T(8,128)(2,1)S(1)}, bf16[1024,128]{0,1:T(8,128)(2,1)}, u32[]{:S(2)}) copy-start(bf16[1024,128]{0,1:T(8,128)(2,1)} %pad.9) | copy-start | bytes 786436
  128.5 11.2 %slice-start = ((s8[6291456]{0:T(1024)(128)(4,1)}), s8[4194304]{0:T(1024)(128)(4,1)S(1)}, s32[]{:S(2)}) async-start(s8[6291456]{0:T(1024)(128)(4,1)} %bitcast.57), calls=%async_computation.4 | async-start | bytes 8388608
  131.7 8.1 %slice-start.1 = ((s8[6291456]{0:T(1024)(128)(4,1)}), s8[2097152]{0:T(1024)(128)(4,1)S(1)}, s32[]{:S(2)}) async-start(s8[6291456]{0:T(1024)(128)(4,1)} %bitcast.57), calls=%async_computation.5 | async-start | bytes 4194304
  135.8 4.0 %copy-start.49 = (f32[1024]{0:T(1024)S(1)}, f32[1024]{0:T(1024)}, u32[]{:S(2)}) copy-start(f32[1024]{0:T(1024)} %param.20) | copy-start | bytes 12292
  139.8 6.6 %copy-start.44 = (bf16[1536,128]{1,0:T(8,128)(2,1)S(1)}, bf16[1536,128]{1,0:T(8,128)(2,1)}, u32[]{:S(2)}) copy-start(bf16[1536,128]{1,0:T(8,128)(2,1)} %param.18) | copy-start | bytes 1179652
  150.0 3.5 %collective-permute-start.4 = (bf16[672,1024]{1,0:T(8,128)(2,1)}, bf16[672,1024]{1,0:T(8,128)(2,1)S(1)}, u32[]{:S(2)}, u32[]{:S(2)}) collective-permute-start(bf16[672,1024]{1,0:T(8,128)(2,1)} %pad_maximum_fusion.1), channel_id=1, source_target_pairs={{0,1},{1,0},{2,3},{3,2},{4,5},{5,4},{6,7},{7,6},{8,9},{9,8},{10,11... | collective-permute-start | bytes 4128776 | tf_op jit(solution)/shard_map/ppermute | solution.py:232
  153.5 1.1 copy-start.43
  157.8 11.3 %collective-permute-start.5 = (bf16[672,512]{1,0:T(8,128)(2,1)}, bf16[672,512]{1,0:T(8,128)(2,1)}, u32[]{:S(2)}, u32[]{:S(2)}) collective-permute-start(bf16[672,512]{1,0:T(8,128)(2,1)} %broadcast_select_fusion), channel_id=1, source_target_pairs={{0,2},{1,5},{2,0},{3,7},{4,6},{5,1},{6,4},{7,3},{8,10},{9,13},{10,... | collective-permute-start | bytes 2064392 | tf_op jit(solution)/shard_map/ppermute | solution.py:241
  170.4 0.8 copy-start.42
  171.3 7.3 %collective-permute-start.6 = (bf16[672,256]{1,0:T(8,128)(2,1)S(1)}, bf16[672,256]{1,0:T(8,128)(2,1)S(1)}, u32[]{:S(2)}, u32[]{:S(2)}) collective-permute-start(bf16[672,256]{1,0:T(8,128)(2,1)S(1)} %broadcast_select_fusion.1), channel_id=1, source_target_pairs={{0,4},{1,3},{2,6},{3,1},{4,0},{5,7},{6,2},{7,5},{8,12},{9,11},{10,... | collective-permute-start | bytes 1032200 | tf_op jit(solution)/shard_map/ppermute | solution.py:241
  179.9 9.9 %collective-permute-start.7 = (bf16[672,128]{1,0:T(8,128)(2,1)S(1)}, bf16[672,128]{1,0:T(8,128)(2,1)S(1)}, u32[]{:S(2)}, u32[]{:S(2)}) collective-permute-start(bf16[672,128]{1,0:T(8,128)(2,1)S(1)} %broadcast_select_fusion.2), channel_id=1, source_target_pairs={{0,8},{1,9},{2,10},{3,11},{4,12},{5,13},{6,14},{7,15},{8,0},{9,1},... | collective-permute-start | bytes 516104 | tf_op jit(solution)/shard_map/ppermute | solution.py:241
  189.8 9.7 %collective-permute-start.8 = (bf16[672,128]{1,0:T(8,128)(2,1)S(1)}, bf16[672,128]{1,0:T(8,128)(2,1)S(1)}, u32[]{:S(2)}, u32[]{:S(2)}) collective-permute-start(bf16[672,128]{1,0:T(8,128)(2,1)S(1)} %add_convert_fusion.5), channel_id=1, source_target_pairs={{0,8},{1,9},{2,10},{3,11},{4,12},{5,13},{6,14},{7,15},{8,0},{9,1},... | collective-permute-start | bytes 516104 | tf_op jit(solution)/shard_map/ppermute | solution.py:241
  199.6 7.3 %collective-permute-start.9 = (bf16[672,256]{1,0:T(8,128)(2,1)S(1)}, bf16[672,256]{1,0:T(8,128)(2,1)S(1)}, u32[]{:S(2)}, u32[]{:S(2)}) collective-permute-start(bf16[672,256]{1,0:T(8,128)(2,1)S(1)} %maximum_select_fusion.4), channel_id=1, source_target_pairs={{0,4},{1,3},{2,6},{3,1},{4,0},{5,7},{6,2},{7,5},{8,12},{9,11},{10,... | collective-permute-start | bytes 1032200 | tf_op jit(solution)/shard_map/ppermute | solution.py:241
  207.1 11.0 %collective-permute-start.10 = (bf16[672,512]{1,0:T(8,128)(2,1)S(1)}, bf16[672,512]{1,0:T(8,128)(2,1)S(1)}, u32[]{:S(2)}, u32[]{:S(2)}) collective-permute-start(bf16[672,512]{1,0:T(8,128)(2,1)S(1)} %maximum_select_fusion.1), channel_id=1, source_target_pairs={{0,2},{1,5},{2,0},{3,7},{4,6},{5,1},{6,4},{7,3},{8,10},{9,13},{10,... | collective-permute-start | bytes 2064392 | tf_op jit(solution)/shard_map/ppermute | solution.py:241
  218.5 3.2 %collective-permute-start.11 = (bf16[672,1024]{1,0:T(8,128)(2,1)S(1)}, bf16[672,1024]{1,0:T(8,128)(2,1)S(1)}, u32[]{:S(2)}, u32[]{:S(2)}) collective-permute-start(bf16[672,1024]{1,0:T(8,128)(2,1)S(1)} %maximum_select_fusion), channel_id=1, source_target_pairs={{0,1},{1,0},{2,3},{3,2},{4,5},{5,4},{6,7},{7,6},{8,9},{9,8},{10,11... | collective-permute-start | bytes 4128776 | tf_op jit(solution)/shard_map/ppermute | solution.py:232
  (5 other events, 3.6 us)

commit v2 on v1

--- a/solution.py
+++ b/solution.py
@@ -12,7 +12,7 @@
 teleport = 0.1
 LANES = 128
 UNROLL = 16
-VMEM_LIMIT = 40 * 1024 * 1024
+VMEM_LIMIT = 60 * 1024 * 1024
 
 bf16 = jnp.bfloat16
 f32 = jnp.float32
@@ -26,6 +26,10 @@
     return pl.BlockSpec(memory_space=pltpu.SMEM)
 
 
+def hbm():
+    return pl.BlockSpec(memory_space=pltpu.HBM)
+
+
 def params():
     return pltpu.CompilerParams(vmem_limit_bytes=VMEM_LIMIT)
 
@@ -38,44 +42,47 @@
     return slots * 3 // 4 if is_packed(slots, class_half) else slots
 
 
-def gather_rows(v_ref, idx_ref, stage_ref):
-    def body(g, carry):
-        base = pl.multiple_of(g * UNROLL, UNROLL)
-        for u in range(UNROLL):
-            stage_ref[pl.ds(base + u, 1), :] = v_ref[pl.ds(idx_ref[base + u], 1), :]
-        return carry
-
-    lax.fori_loop(0, stage_ref.shape[0] // UNROLL, body, 0)
-
-
-def pack_rows(stage_ref, out_ref, slots, class_half):
-    peers = out_ref.shape[0]
-    if not is_packed(slots, class_half):
-
-        def plain(j, carry):
-            base = pl.multiple_of(j * slots, slots)
-            out_ref[j] = stage_ref[pl.ds(base, slots), :].astype(bf16)
+def send_packed(v_ref, idx_ref, stage_ref, packed_ref, out_ref, sems, class_half):
+    peers, slots = idx_ref.shape
+
+    def gather(j):
+        def body(g, carry):
+            base = pl.multiple_of(g * UNROLL, UNROLL)
+            for u in range(UNROLL):
+                stage_ref[pl.ds(base + u, 1), :] = v_ref[pl.ds(idx_ref[j, base + u], 1), :]
             return carry
 
-        lax.fori_loop(0, peers, plain, 0)
-        return
+        lax.fori_loop(0, slots // UNROLL, body, 0)
+
     half, quarter = slots // 2, slots // 4
     lane_a = lax.broadcasted_iota(jnp.int32, (half, LANES), 1)
     lane_b = lax.broadcasted_iota(jnp.int32, (quarter, LANES), 1) // 32
 
-    def body(j, carry):
-        base = pl.multiple_of(j * slots, slots)
-        low = stage_ref[pl.ds(base, half), :]
-        high = stage_ref[pl.ds(base + half, half), :]
-        out_ref[j, 0:half] = jnp.where(lane_a < 64, low, pltpu.roll(high, 64, 1)).astype(bf16)
-        parts = (low[:quarter], low[quarter:], high[:quarter], high[quarter:])
-        packed = jnp.zeros((quarter, LANES), f32)
-        for g in range(4):
-            packed = jnp.where(lane_b == g, pltpu.roll(parts[g], (g * 32 - 64) % LANES, 1), packed)
-        out_ref[j, half : half + quarter] = packed.astype(bf16)
+    def peer(j, carry):
+        gather(j)
+        if is_packed(slots, class_half):
+            low = stage_ref[0:half, :]
+            high = stage_ref[half : 2 * half, :]
+            packed_ref[j, 0:half] = jnp.where(lane_a < 64, low, pltpu.roll(high, 64, 1)).astype(bf16)
+            parts = (low[:quarter], low[quarter:], high[:quarter], high[quarter:])
+            narrow = jnp.zeros((quarter, LANES), f32)
+            for g in range(4):
+                narrow = jnp.where(lane_b == g, pltpu.roll(parts[g], (g * 32 - 64) % LANES, 1), narrow)
+            packed_ref[j, half : half + quarter] = narrow.astype(bf16)
+        else:
+            packed_ref[j] = stage_ref[...].astype(bf16)
+        pltpu.make_async_copy(packed_ref.at[j], out_ref.at[j], sems.at[j]).start()
         return carry
 
-    lax.fori_loop(0, peers, body, 0)
+    lax.fori_loop(0, peers, peer, 0)
+
+
+def wait_packed(packed_ref, out_ref, sems):
+    def peer(j, carry):
+        pltpu.make_async_copy(packed_ref.at[j], out_ref.at[j], sems.at[j]).wait()
+        return carry
+
+    lax.fori_loop(0, packed_ref.shape[0], peer, 0)
 
 
 def unpack_rows(recv_ref, rows_ref, slots, class_half):
@@ -108,21 +115,38 @@
     lax.fori_loop(0, peers, body, 0)
 
 
-def first_kernel(slots, class_half, classes, core_ref, idx_ref, nodes_ref, labels_ref, logits_ref, degree_ref,
-                 out_ref, value_ref, accrued_ref, root_ref, wide_ref, diff_ref, v_ref, stage_ref):
-    batch = logits_ref.shape[0]
+def root_columns(degree_ref, function):
+    blocks, block = degree_ref.shape
+    values = function(degree_ref[...].astype(f32))
+    return jnp.transpose(jnp.concatenate([values, jnp.zeros((block - blocks, block), f32)], 0))
+
+
+def over_lanes(columns, b):
+    return jnp.broadcast_to(columns[:, b : b + 1], columns.shape)
+
+
+def first_kernel(class_half, core_ref, count_ref, nodes_ref, labels_ref, rows_ref, logits_ref, degree_ref,
+                 out_ref, value_ref, idx_ref, wide_ref, diff_ref, v_ref, stage_ref, packed_ref, value_v, idx_v, idx_s,
+                 sems, own_sems):
+    classes, batch = logits_ref.shape
+    peers, slots = rows_ref.shape
     blocks, block = degree_ref.shape
     rows = blocks * block
     core = core_ref[0]
+    slot = lax.broadcasted_iota(jnp.int32, (1, slots), 1)
+    for j in range(peers):
+        idx_v[j : j + 1, :] = jnp.where(slot < count_ref[j], rows_ref[j : j + 1, :], rows)
+    to_smem = pltpu.make_async_copy(idx_v, idx_s, own_sems.at[0])
+    to_smem.start()
+    to_hbm = pltpu.make_async_copy(idx_v, idx_ref, own_sems.at[1])
+    to_hbm.start()
+    logits = logits_ref[...]
+    shifted = jnp.exp(logits - jnp.max(logits, axis=0, keepdims=True))
     wide_ref[...] = jnp.zeros_like(wide_ref)
-    logits = logits_ref[...]
-    shifted = jnp.exp(logits - jnp.max(logits, axis=-1, keepdims=True))
-    wide_ref[:, :classes] = shifted / jnp.sum(shifted, axis=-1, keepdims=True)
-    probs = wide_ref[...]
-    turned = pltpu.roll(probs, wide_ref.shape[1] - class_half, 1)[:, :LANES]
+    wide_ref[0:classes, :] = shifted / jnp.sum(shifted, axis=0, keepdims=True)
+    chosen = wide_ref[pl.ds(pl.multiple_of(core * class_half, 8), LANES), :]
     lane = lax.broadcasted_iota(jnp.int32, (batch, LANES), 1)
-    chosen = jnp.where(core == 0, probs[:, :LANES], turned)
-    diff_ref[...] = jnp.where(lane < class_half, chosen, 0.0)
+    diff_ref[...] = jnp.where(lane < class_half, jnp.transpose(chosen), 0.0)
     v_ref[...] = jnp.zeros_like(v_ref)
     lane_row = lax.broadcasted_iota(jnp.int32, (1, LANES), 1)
     inside = lane_row < class_half
@@ -135,22 +159,19 @@
         return carry
 
     lax.fori_loop(0, batch, add_row, 0, unroll=8)
-
-    def scale(b, carry):
-        at = pl.ds(pl.multiple_of(b * block, block), block)
-        inv = lax.rsqrt(degree_ref[pl.ds(b, 1), :].astype(f32))
-        root = jnp.transpose(jnp.broadcast_to(inv, (block, block)))
-        root_ref[at, :] = root
-        grad = v_ref[at, :]
-        accrued_ref[at, :] = teleport * grad
-        scaled = root * grad
-        value_ref[at, :] = scaled.astype(bf16)
+    roots = root_columns(degree_ref, lax.rsqrt)
+    for b in range(blocks):
+        at = slice(b * block, (b + 1) * block)
+        scaled = over_lanes(roots, b) * v_ref[at, :]
+        value_v[at, :] = scaled.astype(bf16)
         v_ref[at, :] = scaled
-        return carry
-
-    lax.fori_loop(0, blocks, scale, 0)
-    gather_rows(v_ref, idx_ref, stage_ref)
-    pack_rows(stage_ref, out_ref, slots, class_half)
+    value_copy = pltpu.make_async_copy(value_v, value_ref, own_sems.at[2])
+    value_copy.start()
+    to_smem.wait()
+    send_packed(v_ref, idx_s, stage_ref, packed_ref, out_ref, sems, class_half)
+    to_hbm.wait()
+    value_copy.wait()
+    wait_packed(packed_ref, out_ref, sems)
 
 
 def add_tiles(acc_ref, source_ref, tile_refs, meta_ref, target_base, source_base, stride):
@@ -168,55 +189,113 @@
             acc_ref[at, :] = acc_ref[at, :] + product
 
 
-def near_kernel(stride, meta_ref, value_ref, own_ref, other_ref, near_ref):
-    near_ref[...] = jnp.zeros_like(near_ref)
+def near_kernel(stride, last, meta_ref, degree_ref, own_ref, other_ref, *rest):
     count = own_ref.shape[0]
-    add_tiles(near_ref, value_ref, (own_ref, other_ref), meta_ref, 0, count, stride)
-
-
-def far_kernel(slots, class_half, base, stride, last, core_ref, meta_ref, idx_ref, recv_ref, near_ref, own_ref,
-               other_ref, root_ref, accrued_ref, *rest):
+    values = 1 if not last else HOPS
+    value_refs, rest = rest[:values], rest[values:]
+    near_ref, value_vs, own_v, other_v, acc_ref, sems = rest
+    copies = [pltpu.make_async_copy(value_refs[i], value_vs.at[i], sems.at[i]) for i in range(values)]
+    copies.append(pltpu.make_async_copy(own_ref, own_v, sems.at[HOPS]))
+    copies.append(pltpu.make_async_copy(other_ref, other_v, sems.at[HOPS + 1]))
+    for copy in copies:
+        copy.start()
+    blocks, block = degree_ref.shape
+    if not last:
+        acc_ref[...] = jnp.zeros_like(acc_ref)
+    for copy in copies:
+        copy.wait()
     if last:
-        keep_ref, send_ref, rows_ref, acc_ref = rest
+        columns = root_columns(degree_ref, lambda degree: (teleport / (1.0 - teleport)) * degree)
+        for b in range(blocks):
+            at = slice(b * block, (b + 1) * block)
+            total = value_vs[0, at, :].astype(f32)
+            for i in range(1, values):
+                total = total + value_vs[i, at, :].astype(f32)
+            acc_ref[at, :] = over_lanes(columns, b) * total
+    add_tiles(acc_ref, value_vs.at[0], (own_v, other_v), meta_ref, 0, count, stride)
+    out = pltpu.make_async_copy(acc_ref, near_ref, sems.at[HOPS + 2])
+    out.start()
+    out.wait()
+
+
+def far_kernel(class_half, base, stride, last, core_ref, meta_ref, idx_ref, degree_ref, recv_ref, own_ref,
+               other_ref, near_ref, *rest):
+    if last:
+        keep_ref, send_ref, rows_ref, acc_ref, own_sems = rest
     else:
-        out_ref, value_ref, total_ref, rows_ref, acc_ref, stage_ref = rest
-    block = own_ref.shape[1]
-    count = own_ref.shape[0]
-    rows = near_ref.shape[0]
-    blocks = rows // block
+        out_ref, value_ref, rows_ref, acc_ref, stage_ref, packed_ref, value_v, sems, own_sems = rest
+    count, block = own_ref.shape[0], own_ref.shape[1]
+    slots = idx_ref.shape[1]
+    blocks = degree_ref.shape[0]
+    rows = blocks * block
+    near_copy = pltpu.make_async_copy(near_ref, acc_ref.at[pl.ds(0, rows)], own_sems.at[0])
+    near_copy.start()
+    roots = root_columns(degree_ref, lax.rsqrt)
     unpack_rows(recv_ref, rows_ref, slots, class_half)
-    acc_ref[pl.ds(0, rows), :] = near_ref[...]
+    near_copy.wait()
     add_tiles(acc_ref, rows_ref, (own_ref, other_ref), meta_ref, base, base + count, stride)
     rate = 1.0 - teleport
     if last:
-        half_rows = rows // 2
+        half_blocks = blocks // 2
         core = core_ref[0]
-        for out, part in ((send_ref, 1 - core), (keep_ref, core)):
-
-            def finish(b, carry, out=out, part=part):
-                to = pl.ds(pl.multiple_of(b * block, block), block)
-                at = pl.ds(pl.multiple_of(part * half_rows + b * block, block), block)
-                current = rate * root_ref[at, :] * acc_ref[at, :]
-                out[to, :] = (accrued_ref[at, :] + current).astype(bf16)
-                return carry
-
-            lax.fori_loop(0, half_rows // block, finish, 0)
+        for b in range(half_blocks):
+            to = slice(b * block, (b + 1) * block)
+            outs = []
+            for b_at in (b, half_blocks + b):
+                at = slice(b_at * block, (b_at + 1) * block)
+                outs.append((rate * over_lanes(roots, b_at) * acc_ref[at, :]).astype(bf16))
+            keep_ref[to, :] = jnp.where(core == 0, outs[0], outs[1])
+            send_ref[to, :] = jnp.where(core == 0, outs[1], outs[0])
         return
     acc_ref[pl.ds(rows, 8), :] = jnp.zeros((8, LANES), f32)
-
-    def scale(b, carry):
-        at = pl.ds(pl.multiple_of(b * block, block), block)
-        root = root_ref[at, :]
-        current = rate * root * acc_ref[at, :]
-        total_ref[at, :] = accrued_ref[at, :] + teleport * current
-        scaled = root * current
-        value_ref[at, :] = scaled.astype(bf16)
+    for b in range(blocks):
+        at = slice(b * block, (b + 1) * block)
+        root = over_lanes(roots, b)
+        scaled = (rate * root * root) * acc_ref[at, :]
+        value_v[at, :] = scaled.astype(bf16)
         acc_ref[at, :] = scaled
+    value_copy = pltpu.make_async_copy(value_v, value_ref, own_sems.at[1])
+    value_copy.start()
+    send_packed(acc_ref, idx_ref, stage_ref, packed_ref, out_ref, sems, class_half)
+    value_copy.wait()
+    wait_packed(packed_ref, out_ref, sems)
+
+
+def forward_kernel(x_ref, weight_ref, bias_ref, hidden_ref, slope_ref):
+    width = min(256, weight_ref.shape[1])
+
+    def body(j, carry):
+        at = pl.ds(pl.multiple_of(j * width, width), width)
+        pre = jnp.dot(x_ref[...], weight_ref[:, at], preferred_element_type=f32) + bias_ref[:, at]
+        hidden, slope = gelu_parts(pre)
+        hidden_ref[:, at] = hidden
+        slope_ref[:, at] = slope
         return carry
 
-    lax.fori_loop(0, blocks, scale, 0)
-    gather_rows(acc_ref, idx_ref, stage_ref)
-    pack_rows(stage_ref, out_ref, slots, class_half)
+    lax.fori_loop(0, weight_ref.shape[1] // width, body, 0)
+
+
+def forward_layer(x, weight, bias, name):
+    rows, depth = x.shape
+    width = weight.shape[1]
+    step = 256 if rows % 256 == 0 else rows
+    kind = jax.ShapeDtypeStruct((rows, width), bf16)
+    return pl.pallas_call(
+        forward_kernel,
+        grid=(rows // step,),
+        out_shape=(kind, kind),
+        in_specs=[
+            pl.BlockSpec((step, depth), lambda i: (i, 0)),
+            pl.BlockSpec((depth, width), lambda i: (0, 0)),
+            pl.BlockSpec((1, width), lambda i: (0, 0)),
+        ],
+        out_specs=(pl.BlockSpec((step, width), lambda i: (i, 0)), pl.BlockSpec((step, width), lambda i: (i, 0))),
+        compiler_params=params(),
+        cost_estimate=pl.CostEstimate(
+            flops=2 * rows * depth * width + 20 * rows * width, bytes_accessed=8 * 2**20, transcendentals=rows * width
+        ),
+        name=name,
+    )(x, weight, bias.reshape(1, width))
 
 
 def gelu_parts(x):
@@ -324,67 +403,84 @@
     own_local, own_halo = local_tiles[0, 0], halo_tiles[0, 0]
     other_local, other_halo = swap_cores(own_local), swap_cores(own_halo)
 
-    live = jnp.arange(slots, dtype=jnp.int32)[None, :] < send_count[0][:, None]
-    idx = jnp.where(live, send_rows[0], rows).reshape(-1)
-
+    degree_blocks = degree.reshape(blocks, block)
     out_type = jax.ShapeDtypeStruct((peers, packed, LANES), bf16)
     value_type = jax.ShapeDtypeStruct((rows, LANES), bf16)
-    wide_type = jax.ShapeDtypeStruct((rows, LANES), f32)
     half_type = jax.ShapeDtypeStruct((rows // 2, LANES), bf16)
-    stage = pltpu.VMEM((peers * slots, LANES), f32)
-
-    out, value, accrued, root = pl.pallas_call(
-        functools.partial(first_kernel, slots, class_half, classes),
-        out_shape=(out_type, value_type, wide_type, wide_type),
-        in_specs=[smem(), smem(), smem(), smem(), vmem(), vmem()],
-        out_specs=(vmem(), vmem(), vmem(), vmem()),
+    acc = pltpu.VMEM((rows + 8, LANES), f32)
+    sending = [
+        pltpu.VMEM((slots, LANES), f32),
+        pltpu.VMEM((peers, packed, LANES), bf16),
+        pltpu.VMEM((rows, LANES), bf16),
+    ]
+    peer_sems = pltpu.SemaphoreType.DMA((peers,))
+
+    out, value, idx = pl.pallas_call(
+        functools.partial(first_kernel, class_half),
+        out_shape=(out_type, value_type, jax.ShapeDtypeStruct((peers, slots), jnp.int32)),
+        in_specs=[smem()] * 4 + [vmem()] * 3,
+        out_specs=(hbm(), hbm(), hbm()),
         scratch_shapes=[
-            pltpu.VMEM((batch, 2 * LANES), f32),
+            pltpu.VMEM((2 * LANES, batch), f32),
             pltpu.VMEM((batch, LANES), f32),
-            pltpu.VMEM((rows + 8, LANES), f32),
-            stage,
+            acc,
+            *sending,
+            pltpu.VMEM((peers, slots), jnp.int32),
+            pltpu.SMEM((peers, slots), jnp.int32),
+            peer_sems,
+            pltpu.SemaphoreType.DMA((3,)),
         ],
         compiler_params=params(),
         name="first",
-    )(core_arg, idx, batch_nodes[0], labels[0], batch_logits[0], degree.reshape(blocks, block))
-
-    near_call = pl.pallas_call(
-        functools.partial(near_kernel, stride),
-        out_shape=wide_type,
-        in_specs=[smem(), vmem(), vmem(), vmem()],
-        out_specs=vmem(),
-        compiler_params=params(),
-        cost_estimate=pl.CostEstimate(flops=4 * local_count * block**3, bytes_accessed=4 * 2**20, transcendentals=0),
-        name="near",
-    )
-
-    x = features
+    )(core_arg, send_count[0], batch_nodes[0], labels[0], send_rows[0], batch_logits[0].T, degree_blocks)
+
+    values = []
     for hop in range(HOPS):
         last = hop + 1 == HOPS
+        values.insert(0, value)
         landed = lax.all_to_all(out, "dom", split_axis=0, concat_axis=0, tiled=True)
-        near = near_call(meta, value, own_local, other_local)
+        near_values = values if last else values[:1]
+        near = pl.pallas_call(
+            functools.partial(near_kernel, stride, last),
+            out_shape=jax.ShapeDtypeStruct((rows, LANES), f32),
+            in_specs=[smem(), vmem(), hbm(), hbm()] + [hbm()] * len(near_values),
+            out_specs=hbm(),
+            scratch_shapes=[
+                pltpu.VMEM((len(near_values), rows, LANES), bf16),
+                pltpu.VMEM((local_count, block, block), bf16),
+                pltpu.VMEM((local_count, block, block), bf16),
+                pltpu.VMEM((rows, LANES), f32),
+                pltpu.SemaphoreType.DMA((HOPS + 3,)),
+            ],
+            compiler_params=params(),
+            cost_estimate=pl.CostEstimate(
+                flops=4 * local_count * block**3, bytes_accessed=4 * 2**20, transcendentals=0
+            ),
+            name="near_last" if last else "near",
+        )(meta, degree_blocks, own_local, other_local, *near_values)
         if hop == 0:
-            x, _ = lax.optimization_barrier((x, value))
-            pre_first = jnp.dot(x, first_weight, preferred_element_type=f32) + first_bias
-            hidden_first, slope_first = gelu_parts(pre_first)
+            x, _ = lax.optimization_barrier((features, value))
+            hidden_first, slope_first = forward_layer(x, first_weight, first_bias, "forward_one")
+            near, hidden_first, slope_first = lax.optimization_barrier((near, hidden_first, slope_first))
         if hop == 1:
-            hidden_first, _ = lax.optimization_barrier((hidden_first, value))
-            pre_second = jnp.dot(hidden_first, second_weight, preferred_element_type=f32) + second_bias
-            hidden_second, slope_second = gelu_parts(pre_second)
-        scratch = [pltpu.VMEM((peers * slots, LANES), bf16), pltpu.VMEM((rows + 8, LANES), f32)]
+            tied, _ = lax.optimization_barrier((hidden_first, value))
+            hidden_second, slope_second = forward_layer(tied, second_weight, second_bias, "forward_two")
+            near, hidden_second, slope_second = lax.optimization_barrier((near, hidden_second, slope_second))
         result = pl.pallas_call(
-            functools.partial(far_kernel, slots, class_half, 2 * local_count, stride, last),
-            out_shape=(half_type, half_type) if last else (out_type, value_type, wide_type),
-            in_specs=[smem(), smem(), smem()] + [vmem()] * 6,
-            out_specs=(vmem(), vmem()) if last else (vmem(), vmem(), vmem()),
-            scratch_shapes=scratch if last else scratch + [stage],
+            functools.partial(far_kernel, class_half, 2 * local_count, stride, last),
+            out_shape=(half_type, half_type) if last else (out_type, value_type),
+            in_specs=[smem(), smem(), smem()] + [vmem()] * 4 + [hbm()],
+            out_specs=(vmem(), vmem()) if last else (hbm(), hbm()),
+            scratch_shapes=[pltpu.VMEM((peers * slots, LANES), bf16), acc]
+            + ([] if last else sending + [peer_sems])
+            + [pltpu.SemaphoreType.DMA((2,))],
             compiler_params=params(),
             name="far_last" if last else "far",
-        )(core_arg, meta, idx, landed, near, own_halo, other_halo, root, accrued)
+        )(core_arg, meta, idx, degree_blocks, landed, own_halo, other_halo, near)
         if last:
             keep, send = result
         else:
-            out, value, accrued = result
+            out, value = result
 
     got = swap_cores(send)
     delta = jnp.concatenate([keep, got], axis=1)

time: 230 us -> 221 us (0.961)
  Pallas kernels: 32.2 us -> 85.1 us
  local copies, waits for them, and re-layouts: 54.6 us -> 11.7 us
  matrix products: 28.1 us -> 12.4 us
  other arithmetic: 15.7 us -> 9.67 us
  waiting for transfers between devices: 67.6 us -> 71.1 us
    pallas_call x9 -> x11, Pallas kernels: 32.2 us -> 85.1 us  [the longest x4 36.4 us: shards(): pl.pallas_call(functools.partial(far_kernel, class_half, 2 * local_count,...]
    unnamed x109 -> x38, local copies, waits for them, and re-layouts: 46.1 us -> 8.94 us
    dot_general x2 -> x0, matrix products: 10.5 us -> none  [the longest x1 6.93 us: shards(): jnp.dot(x, first_weight, preferred_element_type=f32) + first_bias]
    all_to_all x4, starting transfers between devices: 18.2 us -> 22.9 us  [shards(): landed = lax.all_to_all(out, 'dom', split_axis=0, concat_axis=0, tiled=True)]
    ppermute x6, starting transfers between devices: 9.22 us -> 5.32 us  [exchange(): return lax.ppermute(x, ('dom', 'col'), pairs)]
    dot_general x1, matrix products: 6.56 us -> 3.62 us  [shards(): lax.dot_general(second_delta, second_weight, (((1,), (1,)), ((), ())), pr...]
  transfers between devices with their start and end apart: 16 -> 16, of which waited for: 12 -> 11; matrix products, arithmetic and copies ran while one was open for 7% -> 1% of each run, Pallas kernels for 3% -> 18%
where the time goes in v2:
time: 221 us; the launch traced here: 220 us
  Pallas kernels  85.1 us (39%)
  waiting for transfers between devices  71.1 us (32%)
  starting transfers between devices  29.1 us (13%)
  matrix products  12.4 us (6%)
  local copies, waits for them, and re-layouts  11.7 us (5%)
  other arithmetic  9.67 us (4%)
    ppermute x6, waiting for transfers between devices, exchange(): return lax.ppermute(x, ('dom', 'col'), pairs)  49.5 us
    pallas_call x4, Pallas kernels, shards(): pl.pallas_call(functools.partial(far_kernel, class_half, 2 * local_count,...  36.4 us
    all_to_all x4, starting transfers between devices, shards(): landed = lax.all_to_all(out, 'dom', split_axis=0, concat_axis=0, tiled=True)  22.9 us
    pallas_call x2, Pallas kernels, forward_layer(): pl.pallas_call(forward_kernel, grid=(rows // step,), out_shape=(kind, kin...  22.4 us
    pallas_call x4, Pallas kernels, shards(): pl.pallas_call(functools.partial(near_kernel, stride, last), out_shape=ja...  16.5 us
    all_to_all x4, waiting for transfers between devices, shards(): landed = lax.all_to_all(out, 'dom', split_axis=0, concat_axis=0, tiled=True)  14.5 us
    pallas_call x1, Pallas kernels, shards(): pl.pallas_call(functools.partial(first_kernel, class_half), out_shape=(ou...  9.75 us
    unnamed x38, local copies, waits for them, and re-layouts  8.94 us
  transfers between devices with their start and end apart: 16, of which 11 were waited for; matrix products, arithmetic and copies ran while one was open for 1% of the time, Pallas kernels for 18%

profile of v2, /device:TPU:0, one launch (start us, length us, event | category | flops | bytes accessed | tf_op | source)
XLA Modules:
  0.0 220.2 jit_solution(6194313826078078654)
XLA Ops:
  0.7 1.6 copy.25
  2.3 9.7 %first.1 = (bf16[8,192,128]{2,1,0:T(8,128)(2,1)}, bf16[3072,128]{1,0:T(8,128)(2,1)}, s32[8,256]{1,0:T(8,128)}) custom-call(s32[1]{0:T(128)} %bitcast.6.core_ref, s32[8]{0:T(128)} %bitcast.64, s32[256]{0:T(256)} %bitcast.62, s32[256]{0:T(256)} %bitcast.63, s32[8,256]{1,0:T(8,128)} %bitcast.51, f32[172,256]{1,0:T(8,128)} %bitcast.50, s32[24,128]{1,0:T(8,128)} %bitcast.41), custom_call_target="tpu_custom_call" | custom-call | tf_op jit(solution)/shard_map/first/pallas_call | solution.py:418
  12.1 7.3 %all-to-all-start = ((bf16[8,192,128]{2,1,0:T(8,128)(2,1)}), bf16[8,192,128]{2,1,0:T(8,128)(2,1)S(1)}, u32[]{:S(2)}, u32[]{:S(2)}) async-start(bf16[8,192,128]{2,1,0:T(8,128)(2,1)} %get-tuple-element.34), calls=%async_computation | async-start | bytes 786432 | tf_op jit(solution)/shard_map/all_to_all | solution.py:441
  19.3 0.5 collective-permute-start.2
  19.8 0.8 pad_add_fusion
  20.7 9.4 %forward_one.1 = (bf16[1536,1024]{1,0:T(8,128)(2,1)}, bf16[1536,1024]{1,0:T(8,128)(2,1)}) custom-call(bf16[1536,128]{1,0:T(8,128)(2,1)} %x_ref, bf16[128,1024]{1,0:T(8,128)(2,1)} %weight_ref.2, f32[1,1024]{1,0:T(1,128)} %bitcast.65), custom_call_target="tpu_custom_call" | custom-call | flops 434110464 | bytes 8388608 | tf_op jit(solution)/shard_map/forward_one/pallas_call | solution.py:283
  30.1 0.6 concatenate.50.meta_ref
  30.7 0.8 copy-done.1
  31.5 3.8 %near.3.near_ref = f32[3072,128]{1,0:T(8,128)} custom-call(s32[128]{0:T(128)} %concatenate.50.meta_ref, s32[24,128]{1,0:T(8,128)} %bitcast.42, bf16[16,128,128]{2,1,0:T(8,128)(2,1)} %bitcast.37, bf16[16,128,128]{2,1,0:T(8,128)(2,1)} %copy-done.1, bf16[3072,128]{1,0:T(8,128)(2,1)} %get-tuple-element.28.rest_0_.rest_3_), custom_call_target="tpu_custom_call" | custom-call | flops 134217728 | bytes 4194304 | tf_op jit(solution)/shard_map/near/pallas_call | solution.py:443
  35.4 0.8 copy-done
  36.2 0.2 copy-done.4
  36.4 10.6 %far.3 = (bf16[8,192,128]{2,1,0:T(8,128)(2,1)}, bf16[3072,128]{1,0:T(8,128)(2,1)}) custom-call(s32[1]{0:T(128)} %bitcast.6.core_ref, s32[128]{0:T(128)} %concatenate.50.meta_ref, s32[8,256]{1,0:T(8,128)} %get-tuple-element.33.idx_ref, s32[24,128]{1,0:T(8,128)} %bitcast.43, bf16[8,192,128]{2,1,0:T(8,128)(2,1)} %copy-done.4, bf16[16,128,128]{2,1,0:T(8,128)(2,1)} %bitcast.32, ...), custom_call_target="tpu_custom_call" | custom-call | tf_op jit(solution)/shard_map/far/pallas_call | solution.py:469
  47.0 6.0 %all-to-all-start.1 = ((bf16[8,192,128]{2,1,0:T(8,128)(2,1)}), bf16[8,192,128]{2,1,0:T(8,128)(2,1)S(1)}, u32[]{:S(2)}, u32[]{:S(2)}) async-start(bf16[8,192,128]{2,1,0:T(8,128)(2,1)} %get-tuple-element.41), calls=%async_computation.1 | async-start | bytes 786432 | tf_op jit(solution)/shard_map/all_to_all | solution.py:441
  53.0 3.8 %near.4.near_ref = f32[3072,128]{1,0:T(8,128)} custom-call(s32[128]{0:T(128)} %concatenate.50.meta_ref, s32[24,128]{1,0:T(8,128)} %bitcast.44, bf16[16,128,128]{2,1,0:T(8,128)(2,1)} %bitcast.38, bf16[16,128,128]{2,1,0:T(8,128)(2,1)} %copy-done.1, bf16[3072,128]{1,0:T(8,128)(2,1)} %get-tuple-element.36.rest_0_.rest_2_), custom_call_target="tpu_custom_call" | custom-call | flops 134217728 | bytes 4194304 | tf_op jit(solution)/shard_map/near/pallas_call | solution.py:443
  56.8 13.0 %forward_two.1 = (bf16[1536,1024]{1,0:T(8,128)(2,1)}, bf16[1536,1024]{1,0:T(8,128)(2,1)}) custom-call(bf16[1536,1024]{1,0:T(8,128)(2,1)} %get-tuple-element.37.x_ref, bf16[1024,1024]{1,0:T(8,128)(2,1)} %weight_ref.3, f32[1,1024]{1,0:T(1,128)} %bitcast.66), custom_call_target="tpu_custom_call" | custom-call | flops 3252682752 | bytes 8388608 | tf_op jit(solution)/shard_map/forward_two/pallas_call | solution.py:283
  69.8 0.7 copy-done.5
  70.6 10.6 %far.4 = (bf16[8,192,128]{2,1,0:T(8,128)(2,1)}, bf16[3072,128]{1,0:T(8,128)(2,1)}) custom-call(s32[1]{0:T(128)} %bitcast.6.core_ref, s32[128]{0:T(128)} %concatenate.50.meta_ref, s32[8,256]{1,0:T(8,128)} %get-tuple-element.33.idx_ref, s32[24,128]{1,0:T(8,128)} %bitcast.45, bf16[8,192,128]{2,1,0:T(8,128)(2,1)} %copy-done.5, bf16[16,128,128]{2,1,0:T(8,128)(2,1)} %bitcast.33, ...), custom_call_target="tpu_custom_call" | custom-call | tf_op jit(solution)/shard_map/far/pallas_call | solution.py:469
  81.2 6.0 %all-to-all-start.2 = ((bf16[8,192,128]{2,1,0:T(8,128)(2,1)}), bf16[8,192,128]{2,1,0:T(8,128)(2,1)S(1)}, u32[]{:S(2)}, u32[]{:S(2)}) async-start(bf16[8,192,128]{2,1,0:T(8,128)(2,1)} %get-tuple-element.43), calls=%async_computation.2 | async-start | bytes 786432 | tf_op jit(solution)/shard_map/all_to_all | solution.py:441
  87.2 3.8 %near.5.near_ref = f32[3072,128]{1,0:T(8,128)} custom-call(s32[128]{0:T(128)} %concatenate.50.meta_ref, s32[24,128]{1,0:T(8,128)} %bitcast.46, bf16[16,128,128]{2,1,0:T(8,128)(2,1)} %bitcast.39, bf16[16,128,128]{2,1,0:T(8,128)(2,1)} %copy-done.1, bf16[3072,128]{1,0:T(8,128)(2,1)} %get-tuple-element.44.rest_0_.rest_1_), custom_call_target="tpu_custom_call" | custom-call | flops 134217728 | bytes 4194304 | tf_op jit(solution)/shard_map/near/pallas_call | solution.py:443
  91.1 7.9 %all-to-all-done.2.recv_ref = bf16[8,192,128]{2,1,0:T(8,128)(2,1)S(1)} async-done(((bf16[8,192,128]{2,1,0:T(8,128)(2,1)}), bf16[8,192,128]{2,1,0:T(8,128)(2,1)S(1)}, u32[]{:S(2)}, u32[]{:S(2)}) %all-to-all-start.2) | async-done | bytes 393248 | tf_op jit(solution)/shard_map/all_to_all | solution.py:441
  99.0 0.8 copy-done.6
  99.8 10.6 %far.5 = (bf16[8,192,128]{2,1,0:T(8,128)(2,1)}, bf16[3072,128]{1,0:T(8,128)(2,1)}) custom-call(s32[1]{0:T(128)} %bitcast.6.core_ref, s32[128]{0:T(128)} %concatenate.50.meta_ref, s32[8,256]{1,0:T(8,128)} %get-tuple-element.33.idx_ref, s32[24,128]{1,0:T(8,128)} %bitcast.47, bf16[8,192,128]{2,1,0:T(8,128)(2,1)} %copy-done.6, bf16[16,128,128]{2,1,0:T(8,128)(2,1)} %bitcast.34, ...), custom_call_target="tpu_custom_call" | custom-call | tf_op jit(solution)/shard_map/far/pallas_call | solution.py:469
  110.4 3.7 %all-to-all-start.3 = ((bf16[8,192,128]{2,1,0:T(8,128)(2,1)}), bf16[8,192,128]{2,1,0:T(8,128)(2,1)S(1)}, u32[]{:S(2)}, u32[]{:S(2)}) async-start(bf16[8,192,128]{2,1,0:T(8,128)(2,1)} %get-tuple-element.45), calls=%async_computation.3 | async-start | bytes 786432 | tf_op jit(solution)/shard_map/all_to_all | solution.py:441
  114.1 5.0 %near_last.1.near_ref = f32[3072,128]{1,0:T(8,128)} custom-call(s32[128]{0:T(128)} %concatenate.50.meta_ref, s32[24,128]{1,0:T(8,128)} %bitcast.48, bf16[16,128,128]{2,1,0:T(8,128)(2,1)} %bitcast.40, bf16[16,128,128]{2,1,0:T(8,128)(2,1)} %copy-done.1, bf16[3072,128]{1,0:T(8,128)(2,1)} %get-tuple-element.46.rest_0_, ...), custom_call_target="tpu_custom_call" | custom-call | flops 134217728 | bytes 4194304 | tf_op jit(solution)/shard_map/near_last/pallas_call | solution.py:443
  119.1 6.6 %all-to-all-done.3.recv_ref = bf16[8,192,128]{2,1,0:T(8,128)(2,1)S(1)} async-done(((bf16[8,192,128]{2,1,0:T(8,128)(2,1)}), bf16[8,192,128]{2,1,0:T(8,128)(2,1)S(1)}, u32[]{:S(2)}, u32[]{:S(2)}) %all-to-all-start.3) | async-done | bytes 393248 | tf_op jit(solution)/shard_map/all_to_all | solution.py:441
  125.8 0.7 copy-done.3
  126.5 4.5 %far_last.1 = (bf16[1536,128]{1,0:T(8,128)(2,1)}, bf16[1536,128]{1,0:T(8,128)(2,1)}) custom-call(s32[1]{0:T(128)} %bitcast.6.core_ref, s32[128]{0:T(128)} %concatenate.50.meta_ref, s32[8,256]{1,0:T(8,128)} %get-tuple-element.33.idx_ref, s32[24,128]{1,0:T(8,128)} %bitcast.49, bf16[8,192,128]{2,1,0:T(8,128)(2,1)} %copy-done.3, bf16[16,128,128]{2,1,0:T(8,128)(2,1)} %bitcast.35, ...), custom_call_target="tpu_custom_call" | custom-call | tf_op jit(solution)/shard_map/far_last/pallas_call | solution.py:469
  131.2 1.1 constant_dynamic-update-slice_fusion.1
  132.3 0.7 collective-permute-done.3
  133.2 3.1 %fusion.10 = (bf16[1024]{0:T(1024)(128)(2,1)S(1)}, bf16[1536,1024]{1,0:T(8,128)(2,1)S(1)}) fusion(bf16[1536,256]{1,0:T(8,128)(2,1)S(1)} %constant_dynamic-update-slice_fusion, bf16[1024,128]{0,1:T(8,128)(2,1)S(1)} %pad.9, bf16[1024,128]{0,1:T(8,128)(2,1)S(1)} %slice_select_fusion, pred[]{:T(512)S(6)} %eq.2, bf16[1536,1024]{1,0:T(8,128)(2,1)} %get-tuple-element.40), kind=kOutput, calls=%fused_computation.43 | convolution fusion | flops 813956096 | bytes 7604225 | tf_op jit(solution)/shard_map/dot_general | solution.py:495
  136.3 3.9 %convolution_convert_fusion = bf16[1024,1024]{1,0:T(8,128)(2,1)S(1)} fusion(bf16[1536,1024]{1,0:T(8,128)(2,1)S(1)} %copy-done.17, bf16[1536,1024]{1,0:T(8,128)(2,1)S(1)} %get-tuple-element.64), kind=kOutput, calls=%fused_computation.4 | convolution fusion | flops 3222274048 | bytes 8388608 | tf_op jit(solution)/shard_map/dot_general | solution.py:492
  140.3 3.6 %fusion.8 = (bf16[1024]{0:T(1024)(128)(2,1)S(1)}, f32[1536,1024]{1,0:T(8,128)S(1)}) fusion(bf16[1536,1024]{1,0:T(8,128)(2,1)S(1)} %copy-done.2, bf16[1536,1024]{1,0:T(8,128)(2,1)S(1)} %get-tuple-element.64, bf16[1024,1024]{1,0:T(8,128)(2,1)S(1)} %copy-done.15), kind=kOutput, calls=%fused_computation.41 | convolution fusion | flops 3227515904 | bytes 14682112 | tf_op jit(solution)/shard_map/dot_general | solution.py:499
  143.9 0.7 convolution_convert_fusion.2
  144.7 1.1 copy-done.16
  145.8 1.0 convolution_convert_fusion.1
  146.8 0.2 constant_dynamic-slice_fusion.3
  147.1 1.2 pad_maximum_fusion.1
  148.3 0.1 collective-permute-start.4
  148.4 3.2 %collective-permute-done.4 = bf16[672,1024]{1,0:T(8,128)(2,1)S(1)} collective-permute-done((bf16[672,1024]{1,0:T(8,128)(2,1)}, bf16[672,1024]{1,0:T(8,128)(2,1)S(1)}, u32[]{:S(2)}, u32[]{:S(2)}) %collective-permute-start.4) | collective-permute-done | bytes 1376288 | tf_op jit(solution)/shard_map/ppermute | solution.py:311
  151.6 1.1 copy-done.7
  152.7 1.9 add_convert_fusion
  154.7 1.5 collective-permute-start.5
  156.2 9.5 %collective-permute-done.5 = bf16[672,512]{1,0:T(8,128)(2,1)S(1)} collective-permute-done((bf16[672,512]{1,0:T(8,128)(2,1)S(1)}, bf16[672,512]{1,0:T(8,128)(2,1)S(1)}, u32[]{:S(2)}, u32[]{:S(2)}) %collective-permute-start.5) | collective-permute-done | bytes 688160 | tf_op jit(solution)/shard_map/ppermute | solution.py:320
  165.7 0.3 add_convert_fusion.1
  166.0 1.0 collective-permute-start.6
  167.0 6.3 %collective-permute-done.6 = bf16[672,256]{1,0:T(8,128)(2,1)S(1)} collective-permute-done((bf16[672,256]{1,0:T(8,128)(2,1)S(1)}, bf16[672,256]{1,0:T(8,128)(2,1)S(1)}, u32[]{:S(2)}, u32[]{:S(2)}) %collective-permute-start.6) | collective-permute-done | bytes 344096 | tf_op jit(solution)/shard_map/ppermute | solution.py:320
  173.3 0.1 add_convert_fusion.2
  173.5 0.9 collective-permute-start.7
  174.4 8.5 %collective-permute-done.7 = bf16[672,128]{1,0:T(8,128)(2,1)S(1)} collective-permute-done((bf16[672,128]{1,0:T(8,128)(2,1)S(1)}, bf16[672,128]{1,0:T(8,128)(2,1)S(1)}, u32[]{:S(2)}, u32[]{:S(2)}) %collective-permute-start.7) | collective-permute-done | bytes 172064 | tf_op jit(solution)/shard_map/ppermute | solution.py:320
  183.0 8.7 %collective-permute-done.8 = bf16[672,128]{1,0:T(8,128)(2,1)S(1)} collective-permute-done((bf16[672,128]{1,0:T(8,128)(2,1)S(1)}, bf16[672,128]{1,0:T(8,128)(2,1)S(1)}, u32[]{:S(2)}, u32[]{:S(2)}) %collective-permute-start.8) | collective-permute-done | bytes 172064 | tf_op jit(solution)/shard_map/ppermute | solution.py:320
  191.9 7.2 %collective-permute-done.9 = bf16[672,256]{1,0:T(8,128)(2,1)S(1)} collective-permute-done((bf16[672,256]{1,0:T(8,128)(2,1)S(1)}, bf16[672,256]{1,0:T(8,128)(2,1)S(1)}, u32[]{:S(2)}, u32[]{:S(2)}) %collective-permute-start.9) | collective-permute-done | bytes 344096 | tf_op jit(solution)/shard_map/ppermute | solution.py:320
  199.2 0.2 maximum_select_fusion.1
  199.3 1.8 collective-permute-start.10
  201.2 9.2 %collective-permute-done.10 = bf16[672,512]{1,0:T(8,128)(2,1)S(1)} collective-permute-done((bf16[672,512]{1,0:T(8,128)(2,1)S(1)}, bf16[672,512]{1,0:T(8,128)(2,1)S(1)}, u32[]{:S(2)}, u32[]{:S(2)}) %collective-permute-start.10) | collective-permute-done | bytes 688160 | tf_op jit(solution)/shard_map/ppermute | solution.py:320
  210.3 0.4 maximum_select_fusion
  210.8 3.1 %collective-permute-done.11 = bf16[672,1024]{1,0:T(8,128)(2,1)S(1)} collective-permute-done((bf16[672,1024]{1,0:T(8,128)(2,1)S(1)}, bf16[672,1024]{1,0:T(8,128)(2,1)S(1)}, u32[]{:S(2)}, u32[]{:S(2)}) %collective-permute-start.11) | collective-permute-done | bytes 1376288 | tf_op jit(solution)/shard_map/ppermute | solution.py:311
  213.9 0.4 select_convert_fusion.1
  214.3 0.2 slice.88
  214.6 0.2 slice.89
  214.9 0.6 slice.87
  215.5 0.6 slice.90
  216.1 0.9 maximum_bitcast_fusion
  217.0 2.3 %pad_maximum_fusion = f32[1024,1024]{1,0:T(8,128)} fusion(f32[512,1024]{1,0:T(8,128)S(1)} %slice.89, f32[512,1024]{1,0:T(8,128)S(1)} %slice.88), kind=kLoop, calls=%fused_computation.2 | loop fusion | flops 1048576 | bytes 8388608 | tf_op jit(solution)/shard_map/concatenate | solution.py:532
  219.3 0.8 pad_maximum_fusion.2
  (58 shorter events, 1.2 us)
Async XLA Ops:
  0.6 29.5 %copy-start.10 = (s32[1,1,16]{2,1,0:T(1,128)S(1)}, s32[1,1,16]{2,1,0:T(1,128)}, u32[]{:S(2)}) copy-start(s32[1,1,16]{2,1,0:T(1,128)} %param.25) | copy-start | bytes 196
  0.6 29.5 %copy-start.11 = (s32[1,1,16]{2,1,0:T(1,128)S(1)}, s32[1,1,16]{2,1,0:T(1,128)}, u32[]{:S(2)}) copy-start(s32[1,1,16]{2,1,0:T(1,128)} %param.26) | copy-start | bytes 196
  0.7 29.5 %copy-start.12 = (s32[1,1,16]{2,1,0:T(1,128)S(1)}, s32[1,1,16]{2,1,0:T(1,128)}, u32[]{:S(2)}) copy-start(s32[1,1,16]{2,1,0:T(1,128)} %param.28) | copy-start | bytes 196
  0.7 29.5 %copy-start.13 = (s32[1,1,16]{2,1,0:T(1,128)S(1)}, s32[1,1,16]{2,1,0:T(1,128)}, u32[]{:S(2)}) copy-start(s32[1,1,16]{2,1,0:T(1,128)} %param.29) | copy-start | bytes 196
  12.1 23.4 %all-to-all-start = ((bf16[8,192,128]{2,1,0:T(8,128)(2,1)}), bf16[8,192,128]{2,1,0:T(8,128)(2,1)S(1)}, u32[]{:S(2)}, u32[]{:S(2)}) async-start(bf16[8,192,128]{2,1,0:T(8,128)(2,1)} %get-tuple-element.34), calls=%async_computation | async-start | bytes 786432 | tf_op jit(solution)/shard_map/all_to_all | solution.py:441
  19.3 11.4 %collective-permute-start.1 = (bf16[16,128,128]{2,1,0:T(8,128)(2,1)}, bf16[16,128,128]{2,1,0:T(8,128)(2,1)S(1)}, u32[]{:S(2)}, u32[]{:S(2)}) collective-permute-start(bf16[16,128,128]{2,1,0:T(8,128)(2,1)} %bitcast.36), channel_id=1, source_target_pairs={{0,1},{1,0},{2,3},{3,2},{4,5},{5,4},{6,7},{7,6},{8,9},{9,8},{10,11... | collective-permute-start | bytes 1572872 | tf_op jit(solution)/shard_map/ppermute | solution.py:311
  19.3 16.1 %collective-permute-start.2 = (bf16[16,128,128]{2,1,0:T(8,128)(2,1)}, bf16[16,128,128]{2,1,0:T(8,128)(2,1)S(1)}, u32[]{:S(2)}, u32[]{:S(2)}) collective-permute-start(bf16[16,128,128]{2,1,0:T(8,128)(2,1)} %bitcast.31), channel_id=1, source_target_pairs={{0,1},{1,0},{2,3},{3,2},{4,5},{5,4},{6,7},{7,6},{8,9},{9,8},{10,11... | collective-permute-start | bytes 1572872 | tf_op jit(solution)/shard_map/ppermute | solution.py:311
  20.6 9.5 %collective-permute-start = (s32[64]{0:T(128)S(1)}, s32[64]{0:T(128)S(1)}, u32[]{:S(2)}, u32[]{:S(2)}) collective-permute-start(s32[64]{0:T(128)S(1)} %pad_add_fusion), channel_id=1, source_target_pairs={{0,1},{1,0},{2,3},{3,2},{4,5},{5,4},{6,7},{7,6},{8,9},{9,8},{10,11... | collective-permute-start | bytes 776 | tf_op jit(solution)/shard_map/ppermute | solution.py:311
  30.7 0.8 copy-start.1
  35.4 0.8 copy-start
  35.4 0.9 copy-start.4
  47.0 22.8 %all-to-all-start.1 = ((bf16[8,192,128]{2,1,0:T(8,128)(2,1)}), bf16[8,192,128]{2,1,0:T(8,128)(2,1)S(1)}, u32[]{:S(2)}, u32[]{:S(2)}) async-start(bf16[8,192,128]{2,1,0:T(8,128)(2,1)} %get-tuple-element.41), calls=%async_computation.1 | async-start | bytes 786432 | tf_op jit(solution)/shard_map/all_to_all | solution.py:441
  69.8 0.7 copy-start.5
  81.2 17.8 %all-to-all-start.2 = ((bf16[8,192,128]{2,1,0:T(8,128)(2,1)}), bf16[8,192,128]{2,1,0:T(8,128)(2,1)S(1)}, u32[]{:S(2)}, u32[]{:S(2)}) async-start(bf16[8,192,128]{2,1,0:T(8,128)(2,1)} %get-tuple-element.43), calls=%async_computation.2 | async-start | bytes 786432 | tf_op jit(solution)/shard_map/all_to_all | solution.py:441
  91.1 23.0 %slice-start = ((bf16[1024,172]{0,1:T(8,128)(2,1)}), bf16[1024,84]{0,1:T(8,128)(2,1)S(1)}, s32[]{:S(2)}) async-start(bf16[1024,172]{0,1:T(8,128)(2,1)} %param.23), calls=%async_computation.4 | async-start | bytes 360448 | tf_op jit(solution)/shard_map/slice | solution.py:488
  99.0 0.8 copy-start.6
  110.4 15.3 %all-to-all-start.3 = ((bf16[8,192,128]{2,1,0:T(8,128)(2,1)}), bf16[8,192,128]{2,1,0:T(8,128)(2,1)S(1)}, u32[]{:S(2)}, u32[]{:S(2)}) async-start(bf16[8,192,128]{2,1,0:T(8,128)(2,1)} %get-tuple-element.45), calls=%async_computation.3 | async-start | bytes 786432 | tf_op jit(solution)/shard_map/all_to_all | solution.py:441
  119.1 12.0 %copy-start.8 = (bf16[1024,172]{0,1:T(8,128)(2,1)S(1)}, bf16[1024,172]{0,1:T(8,128)(2,1)}, u32[]{:S(2)}) copy-start(bf16[1024,172]{0,1:T(8,128)(2,1)} %param.23) | copy-start | bytes 1056772
  119.1 12.0 %copy-start.14 = (pred[128]{0:T(512)(128)(4,1)S(1)}, pred[128]{0:T(512)(128)(4,1)}, u32[]{:S(2)}) copy-start(pred[128]{0:T(512)(128)(4,1)} %constant.25.clone.1) | copy-start | bytes 388
  125.8 0.7 copy-start.3
  131.1 2.0 collective-permute-start.3
  133.2 3.1 %copy-start.17 = (bf16[1536,1024]{1,0:T(8,128)(2,1)S(1)}, bf16[1536,1024]{1,0:T(8,128)(2,1)}, u32[]{:S(2)}) copy-start(bf16[1536,1024]{1,0:T(8,128)(2,1)} %get-tuple-element.37.x_ref) | copy-start | bytes 9437188
  136.3 3.9 %copy-start.2 = (bf16[1536,1024]{1,0:T(8,128)(2,1)S(1)}, bf16[1536,1024]{1,0:T(8,128)(2,1)}, u32[]{:S(2)}) copy-start(bf16[1536,1024]{1,0:T(8,128)(2,1)} %get-tuple-element.49) | copy-start | bytes 9437188
  136.3 3.9 %copy-start.15 = (bf16[1024,1024]{1,0:T(8,128)(2,1)S(1)}, bf16[1024,1024]{1,0:T(8,128)(2,1)}, u32[]{:S(2)}) copy-start(bf16[1024,1024]{1,0:T(8,128)(2,1)} %weight_ref.3) | copy-start | bytes 6291460
  140.2 3.6 %copy-start.9 = (bf16[1536,128]{1,0:T(8,128)(2,1)S(1)}, bf16[1536,128]{1,0:T(8,128)(2,1)}, u32[]{:S(2)}) copy-start(bf16[1536,128]{1,0:T(8,128)(2,1)} %x_ref) | copy-start | bytes 1179652
  143.9 1.9 copy-start.16
  148.3 3.3 %collective-permute-start.4 = (bf16[672,1024]{1,0:T(8,128)(2,1)}, bf16[672,1024]{1,0:T(8,128)(2,1)S(1)}, u32[]{:S(2)}, u32[]{:S(2)}) collective-permute-start(bf16[672,1024]{1,0:T(8,128)(2,1)} %pad_maximum_fusion.1), channel_id=1, source_target_pairs={{0,1},{1,0},{2,3},{3,2},{4,5},{5,4},{6,7},{7,6},{8,9},{9,8},{10,11... | collective-permute-start | bytes 4128776 | tf_op jit(solution)/shard_map/ppermute | solution.py:311
  151.6 1.1 copy-start.7
  154.7 11.0 %collective-permute-start.5 = (bf16[672,512]{1,0:T(8,128)(2,1)S(1)}, bf16[672,512]{1,0:T(8,128)(2,1)S(1)}, u32[]{:S(2)}, u32[]{:S(2)}) collective-permute-start(bf16[672,512]{1,0:T(8,128)(2,1)S(1)} %broadcast_select_fusion), channel_id=1, source_target_pairs={{0,2},{1,5},{2,0},{3,7},{4,6},{5,1},{6,4},{7,3},{8,10},{9,13},{10,... | collective-permute-start | bytes 2064392 | tf_op jit(solution)/shard_map/ppermute | solution.py:320
  166.0 7.3 %collective-permute-start.6 = (bf16[672,256]{1,0:T(8,128)(2,1)S(1)}, bf16[672,256]{1,0:T(8,128)(2,1)S(1)}, u32[]{:S(2)}, u32[]{:S(2)}) collective-permute-start(bf16[672,256]{1,0:T(8,128)(2,1)S(1)} %broadcast_select_fusion.1), channel_id=1, source_target_pairs={{0,4},{1,3},{2,6},{3,1},{4,0},{5,7},{6,2},{7,5},{8,12},{9,11},{10,... | collective-permute-start | bytes 1032200 | tf_op jit(solution)/shard_map/ppermute | solution.py:320
  173.5 9.4 %collective-permute-start.7 = (bf16[672,128]{1,0:T(8,128)(2,1)S(1)}, bf16[672,128]{1,0:T(8,128)(2,1)S(1)}, u32[]{:S(2)}, u32[]{:S(2)}) collective-permute-start(bf16[672,128]{1,0:T(8,128)(2,1)S(1)} %broadcast_select_fusion.2), channel_id=1, source_target_pairs={{0,8},{1,9},{2,10},{3,11},{4,12},{5,13},{6,14},{7,15},{8,0},{9,1},... | collective-permute-start | bytes 516104 | tf_op jit(solution)/shard_map/ppermute | solution.py:320
  182.9 8.8 %collective-permute-start.8 = (bf16[672,128]{1,0:T(8,128)(2,1)S(1)}, bf16[672,128]{1,0:T(8,128)(2,1)S(1)}, u32[]{:S(2)}, u32[]{:S(2)}) collective-permute-start(bf16[672,128]{1,0:T(8,128)(2,1)S(1)} %add_convert_fusion.3), channel_id=1, source_target_pairs={{0,8},{1,9},{2,10},{3,11},{4,12},{5,13},{6,14},{7,15},{8,0},{9,1},... | collective-permute-start | bytes 516104 | tf_op jit(solution)/shard_map/ppermute | solution.py:320
  191.9 7.3 %collective-permute-start.9 = (bf16[672,256]{1,0:T(8,128)(2,1)S(1)}, bf16[672,256]{1,0:T(8,128)(2,1)S(1)}, u32[]{:S(2)}, u32[]{:S(2)}) collective-permute-start(bf16[672,256]{1,0:T(8,128)(2,1)S(1)} %maximum_select_fusion.6), channel_id=1, source_target_pairs={{0,4},{1,3},{2,6},{3,1},{4,0},{5,7},{6,2},{7,5},{8,12},{9,11},{10,... | collective-permute-start | bytes 1032200 | tf_op jit(solution)/shard_map/ppermute | solution.py:320
  199.3 11.0 %collective-permute-start.10 = (bf16[672,512]{1,0:T(8,128)(2,1)S(1)}, bf16[672,512]{1,0:T(8,128)(2,1)S(1)}, u32[]{:S(2)}, u32[]{:S(2)}) collective-permute-start(bf16[672,512]{1,0:T(8,128)(2,1)S(1)} %maximum_select_fusion.1), channel_id=1, source_target_pairs={{0,2},{1,5},{2,0},{3,7},{4,6},{5,1},{6,4},{7,3},{8,10},{9,13},{10,... | collective-permute-start | bytes 2064392 | tf_op jit(solution)/shard_map/ppermute | solution.py:320
  210.8 3.2 %collective-permute-start.11 = (bf16[672,1024]{1,0:T(8,128)(2,1)S(1)}, bf16[672,1024]{1,0:T(8,128)(2,1)S(1)}, u32[]{:S(2)}, u32[]{:S(2)}) collective-permute-start(bf16[672,1024]{1,0:T(8,128)(2,1)S(1)} %maximum_select_fusion), channel_id=1, source_target_pairs={{0,1},{1,0},{2,3},{3,2},{4,5},{5,4},{6,7},{7,6},{8,9},{9,8},{10,11... | collective-permute-start | bytes 4128776 | tf_op jit(solution)/shard_map/ppermute | solution.py:311

commit v3 on v2

--- a/solution.py
+++ b/solution.py
@@ -42,27 +42,31 @@
     return slots * 3 // 4 if is_packed(slots, class_half) else slots
 
 
-def send_packed(v_ref, idx_ref, stage_ref, packed_ref, out_ref, sems, class_half):
-    peers, slots = idx_ref.shape
-
-    def gather(j):
-        def body(g, carry):
-            base = pl.multiple_of(g * UNROLL, UNROLL)
+def send_packed(v_ref, count_ref, idx_ref, stage_ref, packed_ref, out_ref, sems, slots, class_half):
+    peers = packed_ref.shape[0]
+
+    def gather(j, carry):
+        first = j * slots
+
+        def body(g, inner):
+            base = pl.multiple_of(first + g * UNROLL, UNROLL)
             for u in range(UNROLL):
-                stage_ref[pl.ds(base + u, 1), :] = v_ref[pl.ds(idx_ref[j, base + u], 1), :]
-            return carry
-
-        lax.fori_loop(0, slots // UNROLL, body, 0)
-
+                stage_ref[pl.ds(base + u, 1), :] = v_ref[pl.ds(idx_ref[base + u], 1), :]
+            return inner
+
+        return lax.fori_loop(0, (count_ref[j] + (UNROLL - 1)) // UNROLL, body, carry)
+
+    lax.fori_loop(0, peers, gather, 0)
     half, quarter = slots // 2, slots // 4
+    row = lax.broadcasted_iota(jnp.int32, (slots, LANES), 0)
     lane_a = lax.broadcasted_iota(jnp.int32, (half, LANES), 1)
     lane_b = lax.broadcasted_iota(jnp.int32, (quarter, LANES), 1) // 32
 
     def peer(j, carry):
-        gather(j)
+        base = pl.multiple_of(j * slots, slots)
+        taken = jnp.where(row < count_ref[j], stage_ref[pl.ds(base, slots), :], 0.0)
         if is_packed(slots, class_half):
-            low = stage_ref[0:half, :]
-            high = stage_ref[half : 2 * half, :]
+            low, high = taken[:half], taken[half:]
             packed_ref[j, 0:half] = jnp.where(lane_a < 64, low, pltpu.roll(high, 64, 1)).astype(bf16)
             parts = (low[:quarter], low[quarter:], high[:quarter], high[quarter:])
             narrow = jnp.zeros((quarter, LANES), f32)
@@ -70,7 +74,7 @@
                 narrow = jnp.where(lane_b == g, pltpu.roll(parts[g], (g * 32 - 64) % LANES, 1), narrow)
             packed_ref[j, half : half + quarter] = narrow.astype(bf16)
         else:
-            packed_ref[j] = stage_ref[...].astype(bf16)
+            packed_ref[j] = taken.astype(bf16)
         pltpu.make_async_copy(packed_ref.at[j], out_ref.at[j], sems.at[j]).start()
         return carry
 
@@ -125,37 +129,25 @@
     return jnp.broadcast_to(columns[:, b : b + 1], columns.shape)
 
 
-def first_kernel(class_half, core_ref, count_ref, nodes_ref, labels_ref, rows_ref, logits_ref, degree_ref,
-                 out_ref, value_ref, idx_ref, wide_ref, diff_ref, v_ref, stage_ref, packed_ref, value_v, idx_v, idx_s,
-                 sems, own_sems):
+def first_kernel(slots, class_half, core_ref, count_ref, idx_ref, nodes_ref, labels_ref, logits_ref, degree_ref,
+                 out_ref, value_ref, wide_ref, diff_ref, v_ref, stage_ref, packed_ref, value_v, sems, own_sems):
     classes, batch = logits_ref.shape
-    peers, slots = rows_ref.shape
     blocks, block = degree_ref.shape
-    rows = blocks * block
     core = core_ref[0]
-    slot = lax.broadcasted_iota(jnp.int32, (1, slots), 1)
-    for j in range(peers):
-        idx_v[j : j + 1, :] = jnp.where(slot < count_ref[j], rows_ref[j : j + 1, :], rows)
-    to_smem = pltpu.make_async_copy(idx_v, idx_s, own_sems.at[0])
-    to_smem.start()
-    to_hbm = pltpu.make_async_copy(idx_v, idx_ref, own_sems.at[1])
-    to_hbm.start()
     logits = logits_ref[...]
     shifted = jnp.exp(logits - jnp.max(logits, axis=0, keepdims=True))
+    hot = lax.broadcasted_iota(jnp.int32, (classes, batch), 0) == labels_ref[...]
+    probs = shifted / jnp.sum(shifted, axis=0, keepdims=True)
     wide_ref[...] = jnp.zeros_like(wide_ref)
-    wide_ref[0:classes, :] = shifted / jnp.sum(shifted, axis=0, keepdims=True)
+    wide_ref[0:classes, :] = probs - jnp.where(hot, 1.0, 0.0)
     chosen = wide_ref[pl.ds(pl.multiple_of(core * class_half, 8), LANES), :]
     lane = lax.broadcasted_iota(jnp.int32, (batch, LANES), 1)
     diff_ref[...] = jnp.where(lane < class_half, jnp.transpose(chosen), 0.0)
     v_ref[...] = jnp.zeros_like(v_ref)
-    lane_row = lax.broadcasted_iota(jnp.int32, (1, LANES), 1)
-    inside = lane_row < class_half
-    start = core * class_half
 
     def add_row(i, carry):
-        hot = jnp.where((lane_row == labels_ref[i] - start) & inside, 1.0, 0.0)
         at = pl.ds(nodes_ref[i], 1)
-        v_ref[at, :] = v_ref[at, :] + (diff_ref[pl.ds(i, 1), :] - hot)
+        v_ref[at, :] = v_ref[at, :] + diff_ref[pl.ds(i, 1), :]
         return carry
 
     lax.fori_loop(0, batch, add_row, 0, unroll=8)
@@ -165,11 +157,9 @@
         scaled = over_lanes(roots, b) * v_ref[at, :]
         value_v[at, :] = scaled.astype(bf16)
         v_ref[at, :] = scaled
-    value_copy = pltpu.make_async_copy(value_v, value_ref, own_sems.at[2])
+    value_copy = pltpu.make_async_copy(value_v, value_ref, own_sems.at[0])
     value_copy.start()
-    to_smem.wait()
-    send_packed(v_ref, idx_s, stage_ref, packed_ref, out_ref, sems, class_half)
-    to_hbm.wait()
+    send_packed(v_ref, count_ref, idx_ref, stage_ref, packed_ref, out_ref, sems, slots, class_half)
     value_copy.wait()
     wait_packed(packed_ref, out_ref, sems)
 
@@ -218,22 +208,29 @@
     out.wait()
 
 
-def far_kernel(class_half, base, stride, last, core_ref, meta_ref, idx_ref, degree_ref, recv_ref, own_ref,
-               other_ref, near_ref, *rest):
+def far_kernel(slots, class_half, base, stride, last, core_ref, meta_ref, count_ref, idx_ref, degree_ref, recv_ref,
+               own_ref, other_ref, near_ref, *rest):
     if last:
-        keep_ref, send_ref, rows_ref, acc_ref, own_sems = rest
+        keep_ref, send_ref, recv_v, own_v, other_v, rows_ref, acc_ref, own_sems = rest
     else:
-        out_ref, value_ref, rows_ref, acc_ref, stage_ref, packed_ref, value_v, sems, own_sems = rest
+        (out_ref, value_ref, recv_v, own_v, other_v, rows_ref, acc_ref, stage_ref, packed_ref, value_v, sems,
+         own_sems) = rest
     count, block = own_ref.shape[0], own_ref.shape[1]
-    slots = idx_ref.shape[1]
     blocks = degree_ref.shape[0]
-    rows = blocks * block
-    near_copy = pltpu.make_async_copy(near_ref, acc_ref.at[pl.ds(0, rows)], own_sems.at[0])
-    near_copy.start()
+    copies = [
+        pltpu.make_async_copy(recv_ref, recv_v, own_sems.at[0]),
+        pltpu.make_async_copy(near_ref, acc_ref, own_sems.at[1]),
+        pltpu.make_async_copy(own_ref, own_v, own_sems.at[2]),
+        pltpu.make_async_copy(other_ref, other_v, own_sems.at[3]),
+    ]
+    for copy in copies:
+        copy.start()
     roots = root_columns(degree_ref, lax.rsqrt)
-    unpack_rows(recv_ref, rows_ref, slots, class_half)
-    near_copy.wait()
-    add_tiles(acc_ref, rows_ref, (own_ref, other_ref), meta_ref, base, base + count, stride)
+    copies[0].wait()
+    unpack_rows(recv_v, rows_ref, slots, class_half)
+    for copy in copies[1:]:
+        copy.wait()
+    add_tiles(acc_ref, rows_ref, (own_v, other_v), meta_ref, base, base + count, stride)
     rate = 1.0 - teleport
     if last:
         half_blocks = blocks // 2
@@ -247,21 +244,21 @@
             keep_ref[to, :] = jnp.where(core == 0, outs[0], outs[1])
             send_ref[to, :] = jnp.where(core == 0, outs[1], outs[0])
         return
-    acc_ref[pl.ds(rows, 8), :] = jnp.zeros((8, LANES), f32)
     for b in range(blocks):
         at = slice(b * block, (b + 1) * block)
         root = over_lanes(roots, b)
         scaled = (rate * root * root) * acc_ref[at, :]
         value_v[at, :] = scaled.astype(bf16)
         acc_ref[at, :] = scaled
-    value_copy = pltpu.make_async_copy(value_v, value_ref, own_sems.at[1])
+    value_copy = pltpu.make_async_copy(value_v, value_ref, own_sems.at[4])
     value_copy.start()
-    send_packed(acc_ref, idx_ref, stage_ref, packed_ref, out_ref, sems, class_half)
+    send_packed(acc_ref, count_ref, idx_ref, stage_ref, packed_ref, out_ref, sems, slots, class_half)
     value_copy.wait()
     wait_packed(packed_ref, out_ref, sems)
 
 
-def forward_kernel(x_ref, weight_ref, bias_ref, hidden_ref, slope_ref):
+def forward_kernel(x_ref, weight_ref, bias_ref, *rest):
+    hidden_ref, slope_ref = rest[-2:]
     width = min(256, weight_ref.shape[1])
 
     def body(j, carry):
@@ -275,27 +272,34 @@
     lax.fori_loop(0, weight_ref.shape[1] // width, body, 0)
 
 
-def forward_layer(x, weight, bias, name):
+def forward_layer(x, weight, bias, part, parts, earlier, name):
     rows, depth = x.shape
     width = weight.shape[1]
-    step = 256 if rows % 256 == 0 else rows
+    step = 256 if rows % (256 * parts) == 0 else rows // parts
+    steps = rows // step // parts
+    first = part * steps
     kind = jax.ShapeDtypeStruct((rows, width), bf16)
+    block = pl.BlockSpec((step, width), lambda i: (first + i, 0))
     return pl.pallas_call(
         forward_kernel,
-        grid=(rows // step,),
+        grid=(steps,),
         out_shape=(kind, kind),
         in_specs=[
-            pl.BlockSpec((step, depth), lambda i: (i, 0)),
+            pl.BlockSpec((step, depth), lambda i: (first + i, 0)),
             pl.BlockSpec((depth, width), lambda i: (0, 0)),
             pl.BlockSpec((1, width), lambda i: (0, 0)),
-        ],
-        out_specs=(pl.BlockSpec((step, width), lambda i: (i, 0)), pl.BlockSpec((step, width), lambda i: (i, 0))),
+        ]
+        + [hbm()] * len(earlier),
+        out_specs=(block, block),
+        input_output_aliases={3 + i: i for i in range(len(earlier))},
         compiler_params=params(),
         cost_estimate=pl.CostEstimate(
-            flops=2 * rows * depth * width + 20 * rows * width, bytes_accessed=8 * 2**20, transcendentals=rows * width
+            flops=(2 * rows * depth * width + 20 * rows * width) // parts,
+            bytes_accessed=8 * 2**20 // parts,
+            transcendentals=rows * width // parts,
         ),
         name=name,
-    )(x, weight, bias.reshape(1, width))
+    )(x, weight, bias.reshape(1, width), *earlier)
 
 
 def gelu_parts(x):
@@ -407,32 +411,32 @@
     out_type = jax.ShapeDtypeStruct((peers, packed, LANES), bf16)
     value_type = jax.ShapeDtypeStruct((rows, LANES), bf16)
     half_type = jax.ShapeDtypeStruct((rows // 2, LANES), bf16)
-    acc = pltpu.VMEM((rows + 8, LANES), f32)
+    acc = pltpu.VMEM((rows, LANES), f32)
     sending = [
-        pltpu.VMEM((slots, LANES), f32),
+        pltpu.VMEM((peers * slots, LANES), f32),
         pltpu.VMEM((peers, packed, LANES), bf16),
         pltpu.VMEM((rows, LANES), bf16),
     ]
     peer_sems = pltpu.SemaphoreType.DMA((peers,))
 
-    out, value, idx = pl.pallas_call(
-        functools.partial(first_kernel, class_half),
-        out_shape=(out_type, value_type, jax.ShapeDtypeStruct((peers, slots), jnp.int32)),
+    idx = send_rows[0].reshape(-1)
+    counts = send_count[0]
+    out, value = pl.pallas_call(
+        functools.partial(first_kernel, slots, class_half),
+        out_shape=(out_type, value_type),
         in_specs=[smem()] * 4 + [vmem()] * 3,
-        out_specs=(hbm(), hbm(), hbm()),
+        out_specs=(hbm(), hbm()),
         scratch_shapes=[
             pltpu.VMEM((2 * LANES, batch), f32),
             pltpu.VMEM((batch, LANES), f32),
             acc,
             *sending,
-            pltpu.VMEM((peers, slots), jnp.int32),
-            pltpu.SMEM((peers, slots), jnp.int32),
             peer_sems,
-            pltpu.SemaphoreType.DMA((3,)),
+            pltpu.SemaphoreType.DMA((1,)),
         ],
         compiler_params=params(),
         name="first",
-    )(core_arg, send_count[0], batch_nodes[0], labels[0], send_rows[0], batch_logits[0].T, degree_blocks)
+    )(core_arg, counts, idx, batch_nodes[0], labels, batch_logits[0].T, degree_blocks)
 
     values = []
     for hop in range(HOPS):
@@ -460,28 +464,37 @@
         )(meta, degree_blocks, own_local, other_local, *near_values)
         if hop == 0:
             x, _ = lax.optimization_barrier((features, value))
-            hidden_first, slope_first = forward_layer(x, first_weight, first_bias, "forward_one")
+            hidden_first, slope_first = forward_layer(x, first_weight, first_bias, 0, 1, (), "forward_one")
             near, hidden_first, slope_first = lax.optimization_barrier((near, hidden_first, slope_first))
-        if hop == 1:
+        if hop in (1, 2):
             tied, _ = lax.optimization_barrier((hidden_first, value))
-            hidden_second, slope_second = forward_layer(tied, second_weight, second_bias, "forward_two")
-            near, hidden_second, slope_second = lax.optimization_barrier((near, hidden_second, slope_second))
+            second = forward_layer(
+                tied, second_weight, second_bias, hop - 1, 2, () if hop == 1 else second, "forward_two"
+            )
+            near, *second = lax.optimization_barrier((near, *second))
         result = pl.pallas_call(
-            functools.partial(far_kernel, class_half, 2 * local_count, stride, last),
+            functools.partial(far_kernel, slots, class_half, 2 * local_count, stride, last),
             out_shape=(half_type, half_type) if last else (out_type, value_type),
-            in_specs=[smem(), smem(), smem()] + [vmem()] * 4 + [hbm()],
+            in_specs=[smem()] * 4 + [vmem()] + [hbm()] * 4,
             out_specs=(vmem(), vmem()) if last else (hbm(), hbm()),
-            scratch_shapes=[pltpu.VMEM((peers * slots, LANES), bf16), acc]
+            scratch_shapes=[
+                pltpu.VMEM((peers, packed, LANES), bf16),
+                pltpu.VMEM((halo_count, block, block), bf16),
+                pltpu.VMEM((halo_count, block, block), bf16),
+                pltpu.VMEM((peers * slots, LANES), bf16),
+                acc,
+            ]
             + ([] if last else sending + [peer_sems])
-            + [pltpu.SemaphoreType.DMA((2,))],
+            + [pltpu.SemaphoreType.DMA((5,))],
             compiler_params=params(),
             name="far_last" if last else "far",
-        )(core_arg, meta, idx, degree_blocks, landed, own_halo, other_halo, near)
+        )(core_arg, meta, counts, idx, degree_blocks, landed, own_halo, other_halo, near)
         if last:
             keep, send = result
         else:
             out, value = result
 
+    hidden_second, slope_second = second
     got = swap_cores(send)
     delta = jnp.concatenate([keep, got], axis=1)
     low = jnp.pad(third_weight[:, :class_half], ((0, 0), (0, LANES - class_half)))

time: 221 us -> 202 us (0.914)
  Pallas kernels: 85.1 us -> 69.8 us
  waiting for transfers between devices: 71.1 us -> 61.4 us
  local copies, waits for them, and re-layouts: 11.7 us -> 15.1 us
  starting transfers between devices: 29.1 us -> 31.5 us
    pallas_call x7 -> x8, Pallas kernels: 68.6 us -> 53.2 us  [the longest x3 25.2 us: forward_layer(): pl.pallas_call(forward_kernel, grid=(steps,), out_shape=(kind, kind), in_...]
    all_to_all x4, waiting for transfers between devices: 14.5 us -> 6.03 us  [shards(): landed = lax.all_to_all(out, 'dom', split_axis=0, concat_axis=0, tiled=True)]
    unnamed x38 -> x41, local copies, waits for them, and re-layouts: 8.94 us -> 11.7 us
  transfers between devices with their start and end apart: 16 -> 16, of which waited for: 11 -> 11; matrix products, arithmetic and copies ran while one was open for 1% -> 2% of each run, Pallas kernels for 18% -> 21%
where the time goes in v3:
time: 202 us; the launch traced here: 200 us
  Pallas kernels  69.8 us (35%)
  waiting for transfers between devices  61.4 us (30%)
  starting transfers between devices  31.5 us (16%)
  local copies, waits for them, and re-layouts  15.1 us (7%)
  other arithmetic  10.6 us (5%)
  matrix products  10.3 us (5%)
    ppermute x6, waiting for transfers between devices, exchange(): return lax.ppermute(x, ('dom', 'col'), pairs)  49.3 us
    pallas_call x3, Pallas kernels, forward_layer(): pl.pallas_call(forward_kernel, grid=(steps,), out_shape=(kind, kind), in_...  25.2 us
    all_to_all x4, starting transfers between devices, shards(): landed = lax.all_to_all(out, 'dom', split_axis=0, concat_axis=0, tiled=True)  24.6 us
    pallas_call x4, Pallas kernels, shards(): pl.pallas_call(functools.partial(far_kernel, slots, class_half, 2 * local...  22.8 us
    pallas_call x4, Pallas kernels, shards(): pl.pallas_call(functools.partial(near_kernel, stride, last), out_shape=ja...  16.6 us
    unnamed x41, local copies, waits for them, and re-layouts  11.7 us
    ppermute x6, waiting for transfers between devices, swap_cores(): return lax.ppermute(x, 'col', [(0, 1), (1, 0)])  6.09 us
    all_to_all x4, waiting for transfers between devices, shards(): landed = lax.all_to_all(out, 'dom', split_axis=0, concat_axis=0, tiled=True)  6.03 us
  transfers between devices with their start and end apart: 16, of which 11 were waited for; matrix products, arithmetic and copies ran while one was open for 2% of the time, Pallas kernels for 21%

profile of v3, /device:TPU:0, one launch (start us, length us, event | category | flops | bytes accessed | tf_op | source)
XLA Modules:
  0.0 200.0 jit_solution(5748213500439297967)
XLA Ops:
  0.7 1.3 copy.26
  2.0 1.6 copy.28
  3.6 5.2 %first.1 = (bf16[8,192,128]{2,1,0:T(8,128)(2,1)}, bf16[3072,128]{1,0:T(8,128)(2,1)}) custom-call(s32[1]{0:T(128)} %bitcast.6.core_ref, s32[8]{0:T(128)} %bitcast.56, s32[2048]{0:T(1024)} %bitcast.51, s32[256]{0:T(256)} %bitcast.74, s32[1,256]{1,0:T(1,128)} %labels_ref.1, f32[172,256]{1,0:T(8,128)} %bitcast.50, s32[24,128]{1,0:T(8,128)} %bitcast.41), custom_call_target="tpu_custom_call" | custom-call | tf_op jit(solution)/shard_map/first/pallas_call | solution.py:424
  8.9 7.2 %all-to-all-start = ((bf16[8,192,128]{2,1,0:T(8,128)(2,1)}), bf16[8,192,128]{2,1,0:T(8,128)(2,1)S(1)}, u32[]{:S(2)}, u32[]{:S(2)}) async-start(bf16[8,192,128]{2,1,0:T(8,128)(2,1)} %get-tuple-element.38), calls=%async_computation | async-start | bytes 786432 | tf_op jit(solution)/shard_map/all_to_all | solution.py:445
  16.1 0.5 collective-permute-start.2
  16.6 0.8 pad_add_fusion
  17.5 9.4 %forward_one.1 = (bf16[1536,1024]{1,0:T(8,128)(2,1)}, bf16[1536,1024]{1,0:T(8,128)(2,1)}) custom-call(bf16[1536,128]{1,0:T(8,128)(2,1)} %x_ref, bf16[128,1024]{1,0:T(8,128)(2,1)} %weight_ref.3, f32[1,1024]{1,0:T(1,128)} %bitcast.75), custom_call_target="tpu_custom_call" | custom-call | flops 434110464 | bytes 8388608 | tf_op jit(solution)/shard_map/forward_one/pallas_call | solution.py:283
  26.9 0.6 concatenate.50.meta_ref
  27.5 0.8 copy-done.1
  28.3 3.8 %near.3.near_ref = f32[3072,128]{1,0:T(8,128)} custom-call(s32[128]{0:T(128)} %concatenate.50.meta_ref, s32[24,128]{1,0:T(8,128)} %bitcast.42, bf16[16,128,128]{2,1,0:T(8,128)(2,1)} %bitcast.37, bf16[16,128,128]{2,1,0:T(8,128)(2,1)} %copy-done.1, bf16[3072,128]{1,0:T(8,128)(2,1)} %get-tuple-element.33.rest_0_.rest_3_), custom_call_target="tpu_custom_call" | custom-call | flops 134217728 | bytes 4194304 | tf_op jit(solution)/shard_map/near/pallas_call | solution.py:447
  32.2 0.8 copy-done
  33.0 0.8 copy-done.8
  33.8 6.1 %far.3 = (bf16[8,192,128]{2,1,0:T(8,128)(2,1)}, bf16[3072,128]{1,0:T(8,128)(2,1)}) custom-call(s32[1]{0:T(128)} %bitcast.6.core_ref, s32[128]{0:T(128)} %concatenate.50.meta_ref, s32[8]{0:T(128)} %bitcast.57, s32[2048]{0:T(1024)} %bitcast.52, s32[24,128]{1,0:T(8,128)} %bitcast.43, bf16[8,192,128]{2,1,0:T(8,128)(2,1)} %copy-done.8, ...), custom_call_target="tpu_custom_call" | custom-call | tf_op jit(solution)/shard_map/far/pallas_call | solution.py:475
  39.9 5.9 %all-to-all-start.1 = ((bf16[8,192,128]{2,1,0:T(8,128)(2,1)}), bf16[8,192,128]{2,1,0:T(8,128)(2,1)S(1)}, u32[]{:S(2)}, u32[]{:S(2)}) async-start(bf16[8,192,128]{2,1,0:T(8,128)(2,1)} %get-tuple-element.40), calls=%async_computation.1 | async-start | bytes 786432 | tf_op jit(solution)/shard_map/all_to_all | solution.py:445
  45.8 3.8 %near.4.near_ref = f32[3072,128]{1,0:T(8,128)} custom-call(s32[128]{0:T(128)} %concatenate.50.meta_ref, s32[24,128]{1,0:T(8,128)} %bitcast.44, bf16[16,128,128]{2,1,0:T(8,128)(2,1)} %bitcast.38, bf16[16,128,128]{2,1,0:T(8,128)(2,1)} %copy-done.1, bf16[3072,128]{1,0:T(8,128)(2,1)} %get-tuple-element.41.rest_0_.rest_2_), custom_call_target="tpu_custom_call" | custom-call | flops 134217728 | bytes 4194304 | tf_op jit(solution)/shard_map/near/pallas_call | solution.py:447
  49.7 7.9 %forward_two.2 = (bf16[1536,1024]{1,0:T(8,128)(2,1)}, bf16[1536,1024]{1,0:T(8,128)(2,1)}) custom-call(bf16[1536,1024]{1,0:T(8,128)(2,1)} %get-tuple-element.47.x_ref, bf16[1024,1024]{1,0:T(8,128)(2,1)} %weight_ref.5, f32[1,1024]{1,0:T(1,128)} %bitcast.62), custom_call_target="tpu_custom_call" | custom-call | flops 1626341376 | bytes 4194304 | tf_op jit(solution)/shard_map/forward_two/pallas_call | solution.py:283
  57.6 0.6 all-to-all-done.1.recv_ref
  58.1 0.8 copy-done.10
  58.9 6.1 %far.4 = (bf16[8,192,128]{2,1,0:T(8,128)(2,1)}, bf16[3072,128]{1,0:T(8,128)(2,1)}) custom-call(s32[1]{0:T(128)} %bitcast.6.core_ref, s32[128]{0:T(128)} %concatenate.50.meta_ref, s32[8]{0:T(128)} %bitcast.58, s32[2048]{0:T(1024)} %bitcast.53, s32[24,128]{1,0:T(8,128)} %bitcast.45, bf16[8,192,128]{2,1,0:T(8,128)(2,1)} %copy-done.10, ...), custom_call_target="tpu_custom_call" | custom-call | tf_op jit(solution)/shard_map/far/pallas_call | solution.py:475
  65.0 5.4 %all-to-all-start.2 = ((bf16[8,192,128]{2,1,0:T(8,128)(2,1)}), bf16[8,192,128]{2,1,0:T(8,128)(2,1)S(1)}, u32[]{:S(2)}, u32[]{:S(2)}) async-start(bf16[8,192,128]{2,1,0:T(8,128)(2,1)} %get-tuple-element.53), calls=%async_computation.2 | async-start | bytes 786432 | tf_op jit(solution)/shard_map/all_to_all | solution.py:445
  70.4 3.8 %near.5.near_ref = f32[3072,128]{1,0:T(8,128)} custom-call(s32[128]{0:T(128)} %concatenate.50.meta_ref, s32[24,128]{1,0:T(8,128)} %bitcast.46, bf16[16,128,128]{2,1,0:T(8,128)(2,1)} %bitcast.39, bf16[16,128,128]{2,1,0:T(8,128)(2,1)} %copy-done.1, bf16[3072,128]{1,0:T(8,128)(2,1)} %get-tuple-element.46.rest_0_.rest_1_), custom_call_target="tpu_custom_call" | custom-call | flops 134217728 | bytes 4194304 | tf_op jit(solution)/shard_map/near/pallas_call | solution.py:447
  74.3 7.9 %forward_two.3 = (bf16[1536,1024]{1,0:T(8,128)(2,1)}, bf16[1536,1024]{1,0:T(8,128)(2,1)}) custom-call(bf16[1536,1024]{1,0:T(8,128)(2,1)} %get-tuple-element.47.x_ref, bf16[1024,1024]{1,0:T(8,128)(2,1)} %weight_ref.5, f32[1,1024]{1,0:T(1,128)} %bitcast.63, ...), custom_call_target="tpu_custom_call", output_to_operand_aliasing={{0}: (3, {}), {1}: (4, {})} | custom-call | flops 1626341376 | bytes 4194304 | tf_op jit(solution)/shard_map/forward_two/pallas_call | solution.py:283
  82.2 0.8 copy-done.9
  83.0 6.1 %far.5 = (bf16[8,192,128]{2,1,0:T(8,128)(2,1)}, bf16[3072,128]{1,0:T(8,128)(2,1)}) custom-call(s32[1]{0:T(128)} %bitcast.6.core_ref, s32[128]{0:T(128)} %concatenate.50.meta_ref, s32[8]{0:T(128)} %bitcast.59, s32[2048]{0:T(1024)} %bitcast.54, s32[24,128]{1,0:T(8,128)} %bitcast.47, bf16[8,192,128]{2,1,0:T(8,128)(2,1)} %copy-done.9, ...), custom_call_target="tpu_custom_call" | custom-call | tf_op jit(solution)/shard_map/far/pallas_call | solution.py:475
  89.1 5.9 %all-to-all-start.3 = ((bf16[8,192,128]{2,1,0:T(8,128)(2,1)}), bf16[8,192,128]{2,1,0:T(8,128)(2,1)S(1)}, u32[]{:S(2)}, u32[]{:S(2)}) async-start(bf16[8,192,128]{2,1,0:T(8,128)(2,1)} %get-tuple-element.55), calls=%async_computation.3 | async-start | bytes 786432 | tf_op jit(solution)/shard_map/all_to_all | solution.py:445
  95.0 0.7 pad.9
  95.8 5.1 %near_last.1.near_ref = f32[3072,128]{1,0:T(8,128)} custom-call(s32[128]{0:T(128)} %concatenate.50.meta_ref, s32[24,128]{1,0:T(8,128)} %bitcast.48, bf16[16,128,128]{2,1,0:T(8,128)(2,1)} %bitcast.40, bf16[16,128,128]{2,1,0:T(8,128)(2,1)} %copy-done.1, bf16[3072,128]{1,0:T(8,128)(2,1)} %get-tuple-element.56.rest_0_, ...), custom_call_target="tpu_custom_call" | custom-call | flops 134217728 | bytes 4194304 | tf_op jit(solution)/shard_map/near_last/pallas_call | solution.py:447
  100.9 5.4 %all-to-all-done.3.recv_ref = bf16[8,192,128]{2,1,0:T(8,128)(2,1)S(1)} async-done(((bf16[8,192,128]{2,1,0:T(8,128)(2,1)}), bf16[8,192,128]{2,1,0:T(8,128)(2,1)S(1)}, u32[]{:S(2)}, u32[]{:S(2)}) %all-to-all-start.3) | async-done | bytes 393248 | tf_op jit(solution)/shard_map/all_to_all | solution.py:445
  106.3 0.7 copy-done.7
  107.0 4.5 %far_last.1 = (bf16[1536,128]{1,0:T(8,128)(2,1)}, bf16[1536,128]{1,0:T(8,128)(2,1)}) custom-call(s32[1]{0:T(128)} %bitcast.6.core_ref, s32[128]{0:T(128)} %concatenate.50.meta_ref, s32[8]{0:T(128)} %bitcast.60, s32[2048]{0:T(1024)} %bitcast.55, s32[24,128]{1,0:T(8,128)} %bitcast.49, bf16[8,192,128]{2,1,0:T(8,128)(2,1)} %copy-done.7, ...), custom_call_target="tpu_custom_call" | custom-call | tf_op jit(solution)/shard_map/far_last/pallas_call | solution.py:475
  111.7 1.0 slice_select_fusion
  112.7 1.1 constant_dynamic-update-slice_fusion.1
  113.9 1.1 fusion.10
  115.0 0.8 copy-done.3
  115.8 3.9 %convolution_convert_fusion = bf16[1024,1024]{1,0:T(8,128)(2,1)S(1)} fusion(bf16[1536,1024]{1,0:T(8,128)(2,1)S(1)} %copy-done.3, bf16[1536,1024]{1,0:T(8,128)(2,1)S(1)} %get-tuple-element.74), kind=kOutput, calls=%fused_computation.4 | convolution fusion | flops 3222274048 | bytes 8388608 | tf_op jit(solution)/shard_map/dot_general | solution.py:505
  119.7 3.6 %fusion.8 = (bf16[1024]{0:T(1024)(128)(2,1)S(1)}, f32[1536,1024]{1,0:T(8,128)S(1)}) fusion(bf16[1536,1024]{1,0:T(8,128)(2,1)S(1)} %copy-done.2, bf16[1536,1024]{1,0:T(8,128)(2,1)S(1)} %get-tuple-element.74, bf16[1024,1024]{1,0:T(8,128)(2,1)S(1)} %copy-done.6), kind=kOutput, calls=%fused_computation.41 | convolution fusion | flops 3227515904 | bytes 14682112 | tf_op jit(solution)/shard_map/dot_general | solution.py:512
  123.4 0.7 convolution_convert_fusion.2
  124.1 1.1 copy-done.4
  125.3 1.0 convolution_convert_fusion.1
  126.6 1.2 pad_maximum_fusion.1
  127.7 0.5 collective-permute-start.4
  128.2 3.0 %collective-permute-done.4 = bf16[672,1024]{1,0:T(8,128)(2,1)S(1)} collective-permute-done((bf16[672,1024]{1,0:T(8,128)(2,1)}, bf16[672,1024]{1,0:T(8,128)(2,1)S(1)}, u32[]{:S(2)}, u32[]{:S(2)}) %collective-permute-start.4) | collective-permute-done | bytes 1376288 | tf_op jit(solution)/shard_map/ppermute | solution.py:315
  131.2 1.1 copy-done.11
  132.3 1.9 add_convert_fusion
  134.3 1.5 collective-permute-start.5
  135.8 9.5 %collective-permute-done.5 = bf16[672,512]{1,0:T(8,128)(2,1)S(1)} collective-permute-done((bf16[672,512]{1,0:T(8,128)(2,1)S(1)}, bf16[672,512]{1,0:T(8,128)(2,1)S(1)}, u32[]{:S(2)}, u32[]{:S(2)}) %collective-permute-start.5) | collective-permute-done | bytes 688160 | tf_op jit(solution)/shard_map/ppermute | solution.py:324
  145.3 0.3 add_convert_fusion.1
  145.6 1.0 collective-permute-start.6
  146.6 6.4 %collective-permute-done.6 = bf16[672,256]{1,0:T(8,128)(2,1)S(1)} collective-permute-done((bf16[672,256]{1,0:T(8,128)(2,1)S(1)}, bf16[672,256]{1,0:T(8,128)(2,1)S(1)}, u32[]{:S(2)}, u32[]{:S(2)}) %collective-permute-start.6) | collective-permute-done | bytes 344096 | tf_op jit(solution)/shard_map/ppermute | solution.py:324
  153.1 1.0 collective-permute-start.7
  154.1 8.6 %collective-permute-done.7 = bf16[672,128]{1,0:T(8,128)(2,1)S(1)} collective-permute-done((bf16[672,128]{1,0:T(8,128)(2,1)S(1)}, bf16[672,128]{1,0:T(8,128)(2,1)S(1)}, u32[]{:S(2)}, u32[]{:S(2)}) %collective-permute-start.7) | collective-permute-done | bytes 172064 | tf_op jit(solution)/shard_map/ppermute | solution.py:324
  162.8 8.7 %collective-permute-done.8 = bf16[672,128]{1,0:T(8,128)(2,1)S(1)} collective-permute-done((bf16[672,128]{1,0:T(8,128)(2,1)S(1)}, bf16[672,128]{1,0:T(8,128)(2,1)S(1)}, u32[]{:S(2)}, u32[]{:S(2)}) %collective-permute-start.8) | collective-permute-done | bytes 172064 | tf_op jit(solution)/shard_map/ppermute | solution.py:324
  171.7 7.2 %collective-permute-done.9 = bf16[672,256]{1,0:T(8,128)(2,1)S(1)} collective-permute-done((bf16[672,256]{1,0:T(8,128)(2,1)S(1)}, bf16[672,256]{1,0:T(8,128)(2,1)S(1)}, u32[]{:S(2)}, u32[]{:S(2)}) %collective-permute-start.9) | collective-permute-done | bytes 344096 | tf_op jit(solution)/shard_map/ppermute | solution.py:324
  179.1 2.1 %collective-permute-start.10 = (bf16[672,512]{1,0:T(8,128)(2,1)S(1)}, bf16[672,512]{1,0:T(8,128)(2,1)S(1)}, u32[]{:S(2)}, u32[]{:S(2)}) collective-permute-start(bf16[672,512]{1,0:T(8,128)(2,1)S(1)} %maximum_select_fusion.1), channel_id=1, source_target_pairs={{0,2},{1,5},{2,0},{3,7},{4,6},{5,1},{6,4},{7,3},{8,10},{9,13},{10,... | collective-permute-start | bytes 2064392 | tf_op jit(solution)/shard_map/ppermute | solution.py:324
  181.2 8.9 %collective-permute-done.10 = bf16[672,512]{1,0:T(8,128)(2,1)S(1)} collective-permute-done((bf16[672,512]{1,0:T(8,128)(2,1)S(1)}, bf16[672,512]{1,0:T(8,128)(2,1)S(1)}, u32[]{:S(2)}, u32[]{:S(2)}) %collective-permute-start.10) | collective-permute-done | bytes 688160 | tf_op jit(solution)/shard_map/ppermute | solution.py:324
  190.1 0.4 maximum_select_fusion
  190.6 3.1 %collective-permute-done.11 = bf16[672,1024]{1,0:T(8,128)(2,1)S(1)} collective-permute-done((bf16[672,1024]{1,0:T(8,128)(2,1)S(1)}, bf16[672,1024]{1,0:T(8,128)(2,1)S(1)}, u32[]{:S(2)}, u32[]{:S(2)}) %collective-permute-start.11) | collective-permute-done | bytes 1376288 | tf_op jit(solution)/shard_map/ppermute | solution.py:315
  193.7 0.4 select_convert_fusion.1
  194.1 0.2 slice.88
  194.7 0.6 slice.87
  195.3 0.6 slice.90
  195.9 0.9 maximum_bitcast_fusion
  196.8 2.3 %pad_maximum_fusion = f32[1024,1024]{1,0:T(8,128)} fusion(f32[512,1024]{1,0:T(8,128)S(1)} %slice.89, f32[512,1024]{1,0:T(8,128)S(1)} %slice.88), kind=kLoop, calls=%fused_computation.2 | loop fusion | flops 1048576 | bytes 8388608 | tf_op jit(solution)/shard_map/concatenate | solution.py:545
  199.1 0.8 pad_maximum_fusion.2
  (62 shorter events, 1.8 us)
Async XLA Ops:
  0.6 26.3 %copy-start.14 = (s32[1,1,16]{2,1,0:T(1,128)S(1)}, s32[1,1,16]{2,1,0:T(1,128)}, u32[]{:S(2)}) copy-start(s32[1,1,16]{2,1,0:T(1,128)} %param.25) | copy-start | bytes 196
  0.6 26.3 %copy-start.15 = (s32[1,1,16]{2,1,0:T(1,128)S(1)}, s32[1,1,16]{2,1,0:T(1,128)}, u32[]{:S(2)}) copy-start(s32[1,1,16]{2,1,0:T(1,128)} %param.26) | copy-start | bytes 196
  0.7 26.2 %copy-start.16 = (s32[1,1,16]{2,1,0:T(1,128)S(1)}, s32[1,1,16]{2,1,0:T(1,128)}, u32[]{:S(2)}) copy-start(s32[1,1,16]{2,1,0:T(1,128)} %param.28) | copy-start | bytes 196
  0.7 26.2 %copy-start.17 = (s32[1,1,16]{2,1,0:T(1,128)S(1)}, s32[1,1,16]{2,1,0:T(1,128)}, u32[]{:S(2)}) copy-start(s32[1,1,16]{2,1,0:T(1,128)} %param.29) | copy-start | bytes 196
  8.9 23.3 %all-to-all-start = ((bf16[8,192,128]{2,1,0:T(8,128)(2,1)}), bf16[8,192,128]{2,1,0:T(8,128)(2,1)S(1)}, u32[]{:S(2)}, u32[]{:S(2)}) async-start(bf16[8,192,128]{2,1,0:T(8,128)(2,1)} %get-tuple-element.38), calls=%async_computation | async-start | bytes 786432 | tf_op jit(solution)/shard_map/all_to_all | solution.py:445
  16.1 11.4 %collective-permute-start.1 = (bf16[16,128,128]{2,1,0:T(8,128)(2,1)}, bf16[16,128,128]{2,1,0:T(8,128)(2,1)S(1)}, u32[]{:S(2)}, u32[]{:S(2)}) collective-permute-start(bf16[16,128,128]{2,1,0:T(8,128)(2,1)} %bitcast.36), channel_id=1, source_target_pairs={{0,1},{1,0},{2,3},{3,2},{4,5},{5,4},{6,7},{7,6},{8,9},{9,8},{10,11... | collective-permute-start | bytes 1572872 | tf_op jit(solution)/shard_map/ppermute | solution.py:315
  16.1 16.1 %collective-permute-start.2 = (bf16[16,128,128]{2,1,0:T(8,128)(2,1)}, bf16[16,128,128]{2,1,0:T(8,128)(2,1)S(1)}, u32[]{:S(2)}, u32[]{:S(2)}) collective-permute-start(bf16[16,128,128]{2,1,0:T(8,128)(2,1)} %bitcast.31), channel_id=1, source_target_pairs={{0,1},{1,0},{2,3},{3,2},{4,5},{5,4},{6,7},{7,6},{8,9},{9,8},{10,11... | collective-permute-start | bytes 1572872 | tf_op jit(solution)/shard_map/ppermute | solution.py:315
  17.4 9.5 %collective-permute-start = (s32[64]{0:T(128)S(1)}, s32[64]{0:T(128)S(1)}, u32[]{:S(2)}, u32[]{:S(2)}) collective-permute-start(s32[64]{0:T(128)S(1)} %pad_add_fusion), channel_id=1, source_target_pairs={{0,1},{1,0},{2,3},{3,2},{4,5},{5,4},{6,7},{7,6},{8,9},{9,8},{10,11... | collective-permute-start | bytes 776 | tf_op jit(solution)/shard_map/ppermute | solution.py:315
  27.5 0.8 copy-start.1
  32.2 0.8 copy-start
  33.0 0.8 copy-start.8
  39.9 18.3 %all-to-all-start.1 = ((bf16[8,192,128]{2,1,0:T(8,128)(2,1)}), bf16[8,192,128]{2,1,0:T(8,128)(2,1)S(1)}, u32[]{:S(2)}, u32[]{:S(2)}) async-start(bf16[8,192,128]{2,1,0:T(8,128)(2,1)} %get-tuple-element.40), calls=%async_computation.1 | async-start | bytes 786432 | tf_op jit(solution)/shard_map/all_to_all | solution.py:445
  58.1 0.8 copy-start.10
  65.0 17.2 %all-to-all-start.2 = ((bf16[8,192,128]{2,1,0:T(8,128)(2,1)}), bf16[8,192,128]{2,1,0:T(8,128)(2,1)S(1)}, u32[]{:S(2)}, u32[]{:S(2)}) async-start(bf16[8,192,128]{2,1,0:T(8,128)(2,1)} %get-tuple-element.53), calls=%async_computation.2 | async-start | bytes 786432 | tf_op jit(solution)/shard_map/all_to_all | solution.py:445
  82.2 12.9 %slice-start = ((bf16[1024,172]{0,1:T(8,128)(2,1)}), bf16[1024,84]{0,1:T(8,128)(2,1)S(1)}, s32[]{:S(2)}) async-start(bf16[1024,172]{0,1:T(8,128)(2,1)} %param.23), calls=%async_computation.4 | async-start | bytes 360448 | tf_op jit(solution)/shard_map/slice | solution.py:501
  82.2 0.8 copy-start.9
  89.1 17.2 %all-to-all-start.3 = ((bf16[8,192,128]{2,1,0:T(8,128)(2,1)}), bf16[8,192,128]{2,1,0:T(8,128)(2,1)S(1)}, u32[]{:S(2)}, u32[]{:S(2)}) async-start(bf16[8,192,128]{2,1,0:T(8,128)(2,1)} %get-tuple-element.55), calls=%async_computation.3 | async-start | bytes 786432 | tf_op jit(solution)/shard_map/all_to_all | solution.py:445
  95.8 15.9 %copy-start.18 = (pred[128]{0:T(512)(128)(4,1)S(1)}, pred[128]{0:T(512)(128)(4,1)}, u32[]{:S(2)}) copy-start(pred[128]{0:T(512)(128)(4,1)} %constant.25.clone.1) | copy-start | bytes 388
  100.8 13.0 %copy-start.5 = (bf16[1536,1024]{1,0:T(8,128)(2,1)S(1)}, bf16[1536,1024]{1,0:T(8,128)(2,1)}, u32[]{:S(2)}) copy-start(bf16[1536,1024]{1,0:T(8,128)(2,1)} %get-tuple-element.52) | copy-start | bytes 9437188
  106.3 0.7 copy-start.7
  107.0 6.9 %copy-start.13 = (bf16[1024,128]{0,1:T(8,128)(2,1)S(1)}, bf16[1024,128]{0,1:T(8,128)(2,1)}, u32[]{:S(2)}) copy-start(bf16[1024,128]{0,1:T(8,128)(2,1)} %pad.9) | copy-start | bytes 786436
  111.6 2.2 %collective-permute-start.3 = (bf16[1536,128]{1,0:T(8,128)(2,1)}, bf16[1536,128]{1,0:T(8,128)(2,1)S(1)}, u32[]{:S(2)}, u32[]{:S(2)}) collective-permute-start(bf16[1536,128]{1,0:T(8,128)(2,1)} %get-tuple-element.58), channel_id=1, source_target_pairs={{0,1},{1,0},{2,3},{3,2},{4,5},{5,4},{6,7},{7,6},{8,9},{9,8},{10,11... | collective-permute-start | bytes 1179656 | tf_op jit(solution)/shard_map/ppermute | solution.py:315
  113.9 1.9 copy-start.3
  115.8 3.9 %copy-start.2 = (bf16[1536,1024]{1,0:T(8,128)(2,1)S(1)}, bf16[1536,1024]{1,0:T(8,128)(2,1)}, u32[]{:S(2)}) copy-start(bf16[1536,1024]{1,0:T(8,128)(2,1)} %get-tuple-element.59) | copy-start | bytes 9437188
  115.8 3.9 %copy-start.6 = (bf16[1024,1024]{1,0:T(8,128)(2,1)S(1)}, bf16[1024,1024]{1,0:T(8,128)(2,1)}, u32[]{:S(2)}) copy-start(bf16[1024,1024]{1,0:T(8,128)(2,1)} %weight_ref.5) | copy-start | bytes 6291460
  119.7 3.6 %copy-start.12 = (bf16[1536,128]{1,0:T(8,128)(2,1)S(1)}, bf16[1536,128]{1,0:T(8,128)(2,1)}, u32[]{:S(2)}) copy-start(bf16[1536,128]{1,0:T(8,128)(2,1)} %x_ref) | copy-start | bytes 1179652
  123.4 1.9 copy-start.4
  127.7 3.5 %collective-permute-start.4 = (bf16[672,1024]{1,0:T(8,128)(2,1)}, bf16[672,1024]{1,0:T(8,128)(2,1)S(1)}, u32[]{:S(2)}, u32[]{:S(2)}) collective-permute-start(bf16[672,1024]{1,0:T(8,128)(2,1)} %pad_maximum_fusion.1), channel_id=1, source_target_pairs={{0,1},{1,0},{2,3},{3,2},{4,5},{5,4},{6,7},{7,6},{8,9},{9,8},{10,11... | collective-permute-start | bytes 4128776 | tf_op jit(solution)/shard_map/ppermute | solution.py:315
  131.2 1.1 copy-start.11
  134.3 11.0 %collective-permute-start.5 = (bf16[672,512]{1,0:T(8,128)(2,1)S(1)}, bf16[672,512]{1,0:T(8,128)(2,1)S(1)}, u32[]{:S(2)}, u32[]{:S(2)}) collective-permute-start(bf16[672,512]{1,0:T(8,128)(2,1)S(1)} %broadcast_select_fusion), channel_id=1, source_target_pairs={{0,2},{1,5},{2,0},{3,7},{4,6},{5,1},{6,4},{7,3},{8,10},{9,13},{10,... | collective-permute-start | bytes 2064392 | tf_op jit(solution)/shard_map/ppermute | solution.py:324
  145.6 7.3 %collective-permute-start.6 = (bf16[672,256]{1,0:T(8,128)(2,1)S(1)}, bf16[672,256]{1,0:T(8,128)(2,1)S(1)}, u32[]{:S(2)}, u32[]{:S(2)}) collective-permute-start(bf16[672,256]{1,0:T(8,128)(2,1)S(1)} %broadcast_select_fusion.1), channel_id=1, source_target_pairs={{0,4},{1,3},{2,6},{3,1},{4,0},{5,7},{6,2},{7,5},{8,12},{9,11},{10,... | collective-permute-start | bytes 1032200 | tf_op jit(solution)/shard_map/ppermute | solution.py:324
  153.1 9.6 %collective-permute-start.7 = (bf16[672,128]{1,0:T(8,128)(2,1)S(1)}, bf16[672,128]{1,0:T(8,128)(2,1)S(1)}, u32[]{:S(2)}, u32[]{:S(2)}) collective-permute-start(bf16[672,128]{1,0:T(8,128)(2,1)S(1)} %broadcast_select_fusion.2), channel_id=1, source_target_pairs={{0,8},{1,9},{2,10},{3,11},{4,12},{5,13},{6,14},{7,15},{8,0},{9,1},... | collective-permute-start | bytes 516104 | tf_op jit(solution)/shard_map/ppermute | solution.py:324
  162.8 8.8 %collective-permute-start.8 = (bf16[672,128]{1,0:T(8,128)(2,1)S(1)}, bf16[672,128]{1,0:T(8,128)(2,1)S(1)}, u32[]{:S(2)}, u32[]{:S(2)}) collective-permute-start(bf16[672,128]{1,0:T(8,128)(2,1)S(1)} %add_convert_fusion.3), channel_id=1, source_target_pairs={{0,8},{1,9},{2,10},{3,11},{4,12},{5,13},{6,14},{7,15},{8,0},{9,1},... | collective-permute-start | bytes 516104 | tf_op jit(solution)/shard_map/ppermute | solution.py:324
  171.6 7.3 %collective-permute-start.9 = (bf16[672,256]{1,0:T(8,128)(2,1)S(1)}, bf16[672,256]{1,0:T(8,128)(2,1)S(1)}, u32[]{:S(2)}, u32[]{:S(2)}) collective-permute-start(bf16[672,256]{1,0:T(8,128)(2,1)S(1)} %maximum_select_fusion.6), channel_id=1, source_target_pairs={{0,4},{1,3},{2,6},{3,1},{4,0},{5,7},{6,2},{7,5},{8,12},{9,11},{10,... | collective-permute-start | bytes 1032200 | tf_op jit(solution)/shard_map/ppermute | solution.py:324
  179.1 11.0 %collective-permute-start.10 = (bf16[672,512]{1,0:T(8,128)(2,1)S(1)}, bf16[672,512]{1,0:T(8,128)(2,1)S(1)}, u32[]{:S(2)}, u32[]{:S(2)}) collective-permute-start(bf16[672,512]{1,0:T(8,128)(2,1)S(1)} %maximum_select_fusion.1), channel_id=1, source_target_pairs={{0,2},{1,5},{2,0},{3,7},{4,6},{5,1},{6,4},{7,3},{8,10},{9,13},{10,... | collective-permute-start | bytes 2064392 | tf_op jit(solution)/shard_map/ppermute | solution.py:324
  190.5 3.2 %collective-permute-start.11 = (bf16[672,1024]{1,0:T(8,128)(2,1)S(1)}, bf16[672,1024]{1,0:T(8,128)(2,1)S(1)}, u32[]{:S(2)}, u32[]{:S(2)}) collective-permute-start(bf16[672,1024]{1,0:T(8,128)(2,1)S(1)} %maximum_select_fusion), channel_id=1, source_target_pairs={{0,1},{1,0},{2,3},{3,2},{4,5},{5,4},{6,7},{7,6},{8,9},{9,8},{10,11... | collective-permute-start | bytes 4128776 | tf_op jit(solution)/shard_map/ppermute | solution.py:315

commit v4 on v3

--- a/solution.py
+++ b/solution.py
@@ -257,41 +257,75 @@
     wait_packed(packed_ref, out_ref, sems)
 
 
-def forward_kernel(x_ref, weight_ref, bias_ref, *rest):
-    hidden_ref, slope_ref = rest[-2:]
-    width = min(256, weight_ref.shape[1])
-
-    def body(j, carry):
-        at = pl.ds(pl.multiple_of(j * width, width), width)
-        pre = jnp.dot(x_ref[...], weight_ref[:, at], preferred_element_type=f32) + bias_ref[:, at]
-        hidden, slope = gelu_parts(pre)
-        hidden_ref[:, at] = hidden
-        slope_ref[:, at] = slope
-        return carry
-
-    lax.fori_loop(0, weight_ref.shape[1] // width, body, 0)
-
-
-def forward_layer(x, weight, bias, part, parts, earlier, name):
+def forward_kernel(first_row, chunk, turn_depth, turn_hidden, core_ref, bias_ref, x_ref, weight_ref, *rest):
+    hidden_ref, slope_ref, x_v, weight_v, hidden_v, slope_v, sems, out_sems = rest[-8:]
+    core = core_ref[0]
+    rows, depth = x_v.shape
+    width = weight_v.shape[1]
+    step = min(256, width // 2)
+    copies = [pltpu.make_async_copy(x_ref.at[pl.ds(first_row, rows)], x_v, sems.at[0])]
+    if turn_depth:
+        half = depth // 2
+        for i in range(2):
+            source = pl.multiple_of((core ^ i) * half, half)
+            copies.append(
+                pltpu.make_async_copy(
+                    weight_ref.at[pl.ds(source, half)], weight_v.at[pl.ds(i * half, half)], sems.at[1 + i]
+                )
+            )
+    else:
+        copies.append(pltpu.make_async_copy(weight_ref, weight_v, sems.at[1]))
+    for copy in copies:
+        copy.start()
+    for copy in copies:
+        copy.wait()
+    outs = []
+    for c in range(rows // chunk):
+        here = slice(c * chunk, (c + 1) * chunk)
+
+        def body(j, carry, here=here):
+            start = pl.multiple_of(j * step, step)
+            at = pl.ds(start, step)
+            pre = jnp.dot(x_v[here, :], weight_v[:, at], preferred_element_type=f32) + bias_ref[:, at]
+            hidden, slope = gelu_parts(pre)
+            slope_v[here, at] = slope
+            if turn_hidden:
+                turned = lax.rem(start + core * (width // 2), width)
+                hidden_v[here, pl.ds(pl.multiple_of(turned, step), step)] = hidden
+            else:
+                hidden_v[here, at] = hidden
+            return carry
+
+        lax.fori_loop(0, width // step, body, 0)
+        to = pl.ds(first_row + c * chunk, chunk)
+        for k, (source, target) in enumerate(((hidden_v, hidden_ref), (slope_v, slope_ref))):
+            out = pltpu.make_async_copy(source.at[pl.ds(c * chunk, chunk)], target.at[to], out_sems.at[2 * c + k])
+            out.start()
+            outs.append(out)
+    for out in outs:
+        out.wait()
+
+
+def forward_layer(core_arg, x, weight, bias, part, parts, turn_depth, turn_hidden, earlier, name):
     rows, depth = x.shape
     width = weight.shape[1]
-    step = 256 if rows % (256 * parts) == 0 else rows // parts
-    steps = rows // step // parts
-    first = part * steps
+    own = rows // parts
+    chunk = 256 if own % 256 == 0 else own
     kind = jax.ShapeDtypeStruct((rows, width), bf16)
-    block = pl.BlockSpec((step, width), lambda i: (first + i, 0))
     return pl.pallas_call(
-        forward_kernel,
-        grid=(steps,),
+        functools.partial(forward_kernel, part * own, chunk, turn_depth, turn_hidden),
         out_shape=(kind, kind),
-        in_specs=[
-            pl.BlockSpec((step, depth), lambda i: (first + i, 0)),
-            pl.BlockSpec((depth, width), lambda i: (0, 0)),
-            pl.BlockSpec((1, width), lambda i: (0, 0)),
-        ]
-        + [hbm()] * len(earlier),
-        out_specs=(block, block),
-        input_output_aliases={3 + i: i for i in range(len(earlier))},
+        in_specs=[smem(), vmem(), hbm(), hbm()] + [hbm()] * len(earlier),
+        out_specs=(hbm(), hbm()),
+        scratch_shapes=[
+            pltpu.VMEM((own, depth), bf16),
+            pltpu.VMEM((depth, width), bf16),
+            pltpu.VMEM((own, width), bf16),
+            pltpu.VMEM((own, width), bf16),
+            pltpu.SemaphoreType.DMA((3,)),
+            pltpu.SemaphoreType.DMA((2 * (own // chunk),)),
+        ],
+        input_output_aliases={4 + i: i for i in range(len(earlier))},
         compiler_params=params(),
         cost_estimate=pl.CostEstimate(
             flops=(2 * rows * depth * width + 20 * rows * width) // parts,
@@ -299,7 +333,59 @@
             transcendentals=rows * width // parts,
         ),
         name=name,
-    )(x, weight, bias.reshape(1, width), *earlier)
+    )(core_arg, bias.reshape(1, width), x, weight, *earlier)
+
+
+def finish_kernel(class_half, core_ref, mine_one, theirs_one, mine_two, theirs_two, first_ref, first_bias_ref,
+                  second_ref, second_bias_ref, third_ref, mine_v, theirs_v, wide_v, sems, out_sems):
+    one, two = mine_one.shape[0], mine_two.shape[0]
+    hidden = second_ref.shape[0]
+    feat = first_ref.shape[0]
+    classes = third_ref.shape[0]
+    half, feat_half = hidden // 2, feat // 2
+    copies = []
+    for i, (source, target) in enumerate(((mine_one, mine_v), (theirs_one, theirs_v))):
+        copies.append(pltpu.make_async_copy(source, target.at[pl.ds(0, one)], sems.at[i]))
+    for i, (source, target) in enumerate(((mine_two, mine_v), (theirs_two, theirs_v))):
+        copies.append(pltpu.make_async_copy(source, target.at[pl.ds(one, two)], sems.at[2 + i]))
+    for copy in copies:
+        copy.start()
+    is_first = core_ref[0] == 0
+
+    def both(start, count):
+        mine = mine_v[start : start + count, :].astype(f32)
+        theirs = theirs_v[start : start + count, :].astype(f32)
+        return jnp.where(is_first, mine, theirs), jnp.where(is_first, theirs, mine)
+
+    step = math.gcd(one, half)
+    outs = []
+    for start in range(0, half, step):
+        if start == 0:
+            copies[0].wait()
+            copies[1].wait()
+        if start == one:
+            copies[2].wait()
+            copies[3].wait()
+        low, high = both(start, step)
+        for k, value in enumerate((low, high)):
+            at = k * half + start
+            wide_v[at : at + step, :] = value
+            out = pltpu.make_async_copy(
+                wide_v.at[pl.ds(at, step)], second_ref.at[pl.ds(at, step)], out_sems.at[2 * (start // step) + k]
+            )
+            out.start()
+            outs.append(out)
+    low, high = both(half, feat_half)
+    first_ref[0:feat_half, :] = low
+    first_ref[feat_half:feat, :] = high
+    low, high = both(half + feat_half, class_half)
+    third_ref[0:class_half, :] = low
+    third_ref[class_half:classes, :] = high[: classes - class_half]
+    low, high = both(half + feat_half + class_half, 8)
+    first_bias_ref[...] = low[:1]
+    second_bias_ref[...] = high[:1]
+    for out in outs:
+        out.wait()
 
 
 def gelu_parts(x):
@@ -464,14 +550,23 @@
         )(meta, degree_blocks, own_local, other_local, *near_values)
         if hop == 0:
             x, _ = lax.optimization_barrier((features, value))
-            hidden_first, slope_first = forward_layer(x, first_weight, first_bias, 0, 1, (), "forward_one")
+            hidden_first, slope_first = forward_layer(
+                core_arg, x, first_weight, first_bias, 0, 1, False, True, (), "forward_one"
+            )
             near, hidden_first, slope_first = lax.optimization_barrier((near, hidden_first, slope_first))
         if hop in (1, 2):
             tied, _ = lax.optimization_barrier((hidden_first, value))
             second = forward_layer(
-                tied, second_weight, second_bias, hop - 1, 2, () if hop == 1 else second, "forward_two"
+                core_arg, tied, second_weight, second_bias, hop - 1, 2, True, False, () if hop == 1 else second,
+                "forward_two",
             )
             near, *second = lax.optimization_barrier((near, *second))
+        if last:
+            tied, _ = lax.optimization_barrier((third_weight, value))
+            low = jnp.pad(tied[:, :class_half], ((0, 0), (0, LANES - class_half)))
+            high = jnp.pad(tied[:, class_half:], ((0, 0), (0, LANES - classes + class_half)))
+            third = jnp.where(core == 0, jnp.concatenate([low, high], 1), jnp.concatenate([high, low], 1))
+            near, third = lax.optimization_barrier((near, third))
         result = pl.pallas_call(
             functools.partial(far_kernel, slots, class_half, 2 * local_count, stride, last),
             out_shape=(half_type, half_type) if last else (out_type, value_type),
@@ -497,55 +592,79 @@
     hidden_second, slope_second = second
     got = swap_cores(send)
     delta = jnp.concatenate([keep, got], axis=1)
-    low = jnp.pad(third_weight[:, :class_half], ((0, 0), (0, LANES - class_half)))
-    high = jnp.pad(third_weight[:, class_half:], ((0, 0), (0, LANES - classes + class_half)))
-    third = jnp.where(core == 0, jnp.concatenate([low, high], 1), jnp.concatenate([high, low], 1))
 
     def contract(a, b):
-        return lax.dot_general(a, b, (((0,), (0,)), ((), ())), preferred_element_type=f32)
-
-    third_grad = contract(delta, hidden_second).astype(bf16)
+        return lax.dot_general(a, b, (((0,), (0,)), ((), ())), preferred_element_type=f32).astype(bf16)
+
+    half, feat = hidden // 2, x.shape[1]
+    lead = half // 4 * 3
     back_second = lax.dot_general(delta, third, (((1,), (1,)), ((), ())), preferred_element_type=f32)
     second_delta = (slope_second.astype(f32) * back_second).astype(bf16)
-    second_grad = contract(hidden_first, second_delta).astype(bf16)
     second_bias_grad = jnp.sum(second_delta.astype(f32), axis=0).astype(bf16)
+    send_lead = contract(hidden_first[:, half : half + lead], second_delta)
+    got_lead = swap_cores(send_lead)
+    keep_lead = contract(hidden_first[:, :lead], second_delta)
+    send_tail = contract(hidden_first[:, half + lead :], second_delta)
+    keep_tail = contract(hidden_first[:, lead:half], second_delta)
+    third_grad = contract(delta, hidden_second)
     back_first = lax.dot_general(
         second_delta, second_weight, (((1,), (1,)), ((), ())), preferred_element_type=f32
     )
     first_delta = (slope_first.astype(f32) * back_first).astype(bf16)
-    first_grad = contract(x, first_delta).astype(bf16)
+    first_grad = contract(x, first_delta)
     first_bias_grad = jnp.sum(first_delta.astype(f32), axis=0).astype(bf16)
 
-    feat = first_grad.shape[0]
-    parts = hidden // 2, feat // 2, class_half
-    used = sum(parts) + 1
+    is_first = core == 0
     domains = lax.axis_size("dom")
     column_splits = (hidden // LANES).bit_length() - 1
     grain = 8 * max(1, domains >> column_splits)
-    total_rows = -(-used // grain) * grain
-
-    def bundle(part, third_part, bias_row):
-        second_rows = lax.dynamic_slice_in_dim(second_grad, part * parts[0], parts[0], 0)
-        first_rows = lax.dynamic_slice_in_dim(first_grad, part * parts[1], parts[1], 0)
-        bias = jnp.broadcast_to(bias_row[None], (total_rows - used + 1, hidden))
-        return jnp.concatenate([second_rows, first_rows, third_part[:class_half], bias], 0)
-
-    is_first = core == 0
-    keep_rows = bundle(core, third_grad[:LANES], jnp.where(is_first, first_bias_grad, second_bias_grad))
-    send_rows_ = bundle(1 - core, third_grad[LANES:], jnp.where(is_first, second_bias_grad, first_bias_grad))
-    got_rows = swap_cores(send_rows_)
-    mine = sum_over_domains((keep_rows.astype(f32) + got_rows.astype(f32)).astype(bf16))
-    theirs = swap_cores(mine)
-    low = jnp.where(is_first, mine, theirs).astype(f32)
-    high = jnp.where(is_first, theirs, mine).astype(f32)
-    a, b, c = parts[0], parts[0] + parts[1], used - 1
-    return (
-        jnp.concatenate([low[a:b], high[a:b]], 0),
-        low[c],
-        jnp.concatenate([low[:a], high[:a]], 0),
-        high[c],
-        jnp.concatenate([low[b:c], high[b : b + classes - class_half]], 0).T,
+    used = half - lead + feat // 2 + class_half
+    tail_rows = -(-(used + 1) // grain) * grain
+    low_first, high_first = first_grad[: feat // 2], first_grad[feat // 2 :]
+
+    def bundle(tail, first_rows, third_rows, bias_row):
+        bias = jnp.broadcast_to(bias_row[None], (tail_rows - used, hidden))
+        return jnp.concatenate([tail, first_rows, third_rows[:class_half], bias], 0)
+
+    keep_rest = bundle(
+        keep_tail,
+        jnp.where(is_first, low_first, high_first),
+        third_grad[:LANES],
+        jnp.where(is_first, first_bias_grad, second_bias_grad),
     )
+    send_rest = bundle(
+        send_tail,
+        jnp.where(is_first, high_first, low_first),
+        third_grad[LANES:],
+        jnp.where(is_first, second_bias_grad, first_bias_grad),
+    )
+    got_rest = swap_cores(send_rest)
+    mine_lead = sum_over_domains((keep_lead.astype(f32) + got_lead.astype(f32)).astype(bf16))
+    mine_rest = sum_over_domains((keep_rest.astype(f32) + got_rest.astype(f32)).astype(bf16))
+    theirs_lead, theirs_rest = swap_cores(mine_lead), swap_cores(mine_rest)
+    rows_all = lead + tail_rows
+    first_out, first_bias_out, second_out, second_bias_out, third_out = pl.pallas_call(
+        functools.partial(finish_kernel, class_half),
+        out_shape=(
+            jax.ShapeDtypeStruct((feat, hidden), f32),
+            jax.ShapeDtypeStruct((1, hidden), f32),
+            jax.ShapeDtypeStruct((hidden, hidden), f32),
+            jax.ShapeDtypeStruct((1, hidden), f32),
+            jax.ShapeDtypeStruct((classes, hidden), f32),
+        ),
+        in_specs=[smem()] + [hbm()] * 4,
+        out_specs=(vmem(), vmem(), hbm(), vmem(), vmem()),
+        scratch_shapes=[
+            pltpu.VMEM((rows_all, hidden), bf16),
+            pltpu.VMEM((rows_all, hidden), bf16),
+            pltpu.VMEM((hidden, hidden), f32),
+            pltpu.SemaphoreType.DMA((4,)),
+            pltpu.SemaphoreType.DMA((2 * (half // math.gcd(lead, half)),)),
+        ],
+        compiler_params=params(),
+        name="finish",
+    )(core_arg, mine_lead, theirs_lead, mine_rest, theirs_rest)
+    return first_out, first_bias_out.reshape(hidden), second_out, second_bias_out.reshape(hidden), third_out.T
 
 
 def solution(mesh):

time: 202 us -> 194 us (0.960)
  waiting for transfers between devices: 61.4 us -> 47 us
  Pallas kernels: 69.8 us -> 77.1 us
  other arithmetic: 10.6 us -> 4.52 us
  starting transfers between devices: 31.5 us -> 37 us
    ppermute x6 -> x12, waiting for transfers between devices: 49.3 us -> 40.1 us  [exchange(): return lax.ppermute(x, ('dom', 'col'), pairs)]
    pallas_call x3 -> x4, Pallas kernels: 25.2 us -> 32.4 us  [the longest x3 27.8 us: forward_layer(): pl.pallas_call(functools.partial(forward_kernel, part * own, chunk, turn_...]
    ppermute x6 -> x12, starting transfers between devices: 5.67 us -> 10.2 us  [exchange(): return lax.ppermute(x, ('dom', 'col'), pairs)]
    concatenate x3 -> x1, other arithmetic: 4.33 us -> 0.04 us  [bundle(): return jnp.concatenate([tail, first_rows, third_rows[:class_half], bias], 0)]
    ppermute x6 -> x8, waiting for transfers between devices: 6.09 us -> 2.85 us  [swap_cores(): return lax.ppermute(x, 'col', [(0, 1), (1, 0)])]
    convert_element_type x2 -> x1, other arithmetic: 2.27 us -> 0.22 us  [shards(): (keep_rest.astype(f32) + got_rest.astype(f32)).astype(bf16)]
    unnamed x41 -> x45, local copies, waits for them, and re-layouts: 11.7 us -> 12.7 us
    dot_general x3 -> x6, matrix products: 5.64 us -> 5.79 us  [contract(): lax.dot_general(a, b, (((0,), (0,)), ((), ())), preferred_element_type=f32)]
  transfers between devices with their start and end apart: 16 -> 24, of which waited for: 11 -> 14; matrix products, arithmetic and copies ran while one was open for 2% -> 5% of each run, Pallas kernels for 21% -> 23%
where the time goes in v4:
time: 194 us; the launch traced here: 192 us
  Pallas kernels  77.1 us (40%)
  waiting for transfers between devices  47 us (24%)
  starting transfers between devices  37 us (19%)
  local copies, waits for them, and re-layouts  13.5 us (7%)
  matrix products  11.6 us (6%)
  other arithmetic  4.52 us (2%)
    ppermute x12, waiting for transfers between devices, exchange(): return lax.ppermute(x, ('dom', 'col'), pairs)  40.1 us
    pallas_call x3, Pallas kernels, forward_layer(): pl.pallas_call(functools.partial(forward_kernel, part * own, chunk, turn_...  27.8 us
    all_to_all x4, starting transfers between devices, shards(): landed = lax.all_to_all(out, 'dom', split_axis=0, concat_axis=0, tiled=True)  25.3 us
    pallas_call x4, Pallas kernels, shards(): pl.pallas_call(functools.partial(far_kernel, slots, class_half, 2 * local...  22.8 us
    pallas_call x4, Pallas kernels, shards(): pl.pallas_call(functools.partial(near_kernel, stride, last), out_shape=ja...  16.5 us
    unnamed x45, local copies, waits for them, and re-layouts  12.7 us
    ppermute x12, starting transfers between devices, exchange(): return lax.ppermute(x, ('dom', 'col'), pairs)  10.2 us
    dot_general x6, matrix products, contract(): lax.dot_general(a, b, (((0,), (0,)), ((), ())), preferred_element_type=f32)  5.79 us
  transfers between devices with their start and end apart: 24, of which 14 were waited for; matrix products, arithmetic and copies ran while one was open for 5% of the time, Pallas kernels for 23%

profile of v4, /device:TPU:0, one launch (start us, length us, event | category | flops | bytes accessed | tf_op | source)
XLA Modules:
  0.0 192.2 jit_solution(161243681145744003)
XLA Ops:
  0.7 1.3 copy.26
  2.0 1.6 copy.28
  3.6 5.3 %first.1 = (bf16[8,192,128]{2,1,0:T(8,128)(2,1)}, bf16[3072,128]{1,0:T(8,128)(2,1)}) custom-call(s32[1]{0:T(128)} %bitcast.core_ref, s32[8]{0:T(128)} %bitcast.58, s32[2048]{0:T(1024)} %bitcast.53, s32[256]{0:T(256)} %bitcast.74, s32[1,256]{1,0:T(1,128)} %labels_ref.1, f32[172,256]{1,0:T(8,128)} %bitcast.52, s32[24,128]{1,0:T(8,128)} %bitcast.43), custom_call_target="tpu_custom_call" | custom-call | tf_op jit(solution)/shard_map/first/pallas_call | solution.py:510
  8.9 7.3 %all-to-all-start = ((bf16[8,192,128]{2,1,0:T(8,128)(2,1)}), bf16[8,192,128]{2,1,0:T(8,128)(2,1)S(1)}, u32[]{:S(2)}, u32[]{:S(2)}) async-start(bf16[8,192,128]{2,1,0:T(8,128)(2,1)} %get-tuple-element.46), calls=%async_computation | async-start | bytes 786432 | tf_op jit(solution)/shard_map/all_to_all | solution.py:531
  16.2 0.5 collective-permute-start.2
  16.7 0.8 pad_add_fusion
  17.5 10.1 %forward_one.1 = (bf16[1536,1024]{1,0:T(8,128)(2,1)}, bf16[1536,1024]{1,0:T(8,128)(2,1)}) custom-call(s32[1]{0:T(128)} %bitcast.core_ref, f32[1,1024]{1,0:T(1,128)} %bitcast.76, bf16[1536,128]{1,0:T(8,128)(2,1)} %x_ref, bf16[128,1024]{1,0:T(8,128)(2,1)} %weight_ref.3), custom_call_target="tpu_custom_call" | custom-call | flops 434110464 | bytes 8388608 | tf_op jit(solution)/shard_map/forward_one/pallas_call | solution.py:315
  27.7 0.6 concatenate.59.meta_ref
  28.3 0.8 copy-done.2
  29.1 3.8 %near.3.near_ref = f32[3072,128]{1,0:T(8,128)} custom-call(s32[128]{0:T(128)} %concatenate.59.meta_ref, s32[24,128]{1,0:T(8,128)} %bitcast.44, bf16[16,128,128]{2,1,0:T(8,128)(2,1)} %bitcast.39, bf16[16,128,128]{2,1,0:T(8,128)(2,1)} %copy-done.2, bf16[3072,128]{1,0:T(8,128)(2,1)} %get-tuple-element.41.rest_0_.rest_3_), custom_call_target="tpu_custom_call" | custom-call | flops 134217728 | bytes 4194304 | tf_op jit(solution)/shard_map/near/pallas_call | solution.py:533
  33.0 0.8 copy-done.1
  33.8 0.8 copy-done.9
  34.5 6.1 %far.3 = (bf16[8,192,128]{2,1,0:T(8,128)(2,1)}, bf16[3072,128]{1,0:T(8,128)(2,1)}) custom-call(s32[1]{0:T(128)} %bitcast.core_ref, s32[128]{0:T(128)} %concatenate.59.meta_ref, s32[8]{0:T(128)} %bitcast.59, s32[2048]{0:T(1024)} %bitcast.54, s32[24,128]{1,0:T(8,128)} %bitcast.45, bf16[8,192,128]{2,1,0:T(8,128)(2,1)} %copy-done.9, ...), custom_call_target="tpu_custom_call" | custom-call | tf_op jit(solution)/shard_map/far/pallas_call | solution.py:570
  40.6 6.0 %all-to-all-start.1 = ((bf16[8,192,128]{2,1,0:T(8,128)(2,1)}), bf16[8,192,128]{2,1,0:T(8,128)(2,1)S(1)}, u32[]{:S(2)}, u32[]{:S(2)}) async-start(bf16[8,192,128]{2,1,0:T(8,128)(2,1)} %get-tuple-element.48), calls=%async_computation.1 | async-start | bytes 786432 | tf_op jit(solution)/shard_map/all_to_all | solution.py:531
  46.6 3.8 %near.4.near_ref = f32[3072,128]{1,0:T(8,128)} custom-call(s32[128]{0:T(128)} %concatenate.59.meta_ref, s32[24,128]{1,0:T(8,128)} %bitcast.46, bf16[16,128,128]{2,1,0:T(8,128)(2,1)} %bitcast.40, bf16[16,128,128]{2,1,0:T(8,128)(2,1)} %copy-done.2, bf16[3072,128]{1,0:T(8,128)(2,1)} %get-tuple-element.49.rest_0_.rest_2_), custom_call_target="tpu_custom_call" | custom-call | flops 134217728 | bytes 4194304 | tf_op jit(solution)/shard_map/near/pallas_call | solution.py:533
  50.4 8.9 %forward_two.2 = (bf16[1536,1024]{1,0:T(8,128)(2,1)}, bf16[1536,1024]{1,0:T(8,128)(2,1)}) custom-call(s32[1]{0:T(128)} %bitcast.core_ref, f32[1,1024]{1,0:T(1,128)} %bitcast.64, bf16[1536,1024]{1,0:T(8,128)(2,1)} %get-tuple-element.55.x_ref, bf16[1024,1024]{1,0:T(8,128)(2,1)} %weight_ref.5), custom_call_target="tpu_custom_call" | custom-call | flops 1626341376 | bytes 4194304 | tf_op jit(solution)/shard_map/forward_two/pallas_call | solution.py:315
  59.3 0.7 copy-done.12
  60.1 6.1 %far.4 = (bf16[8,192,128]{2,1,0:T(8,128)(2,1)}, bf16[3072,128]{1,0:T(8,128)(2,1)}) custom-call(s32[1]{0:T(128)} %bitcast.core_ref, s32[128]{0:T(128)} %concatenate.59.meta_ref, s32[8]{0:T(128)} %bitcast.60, s32[2048]{0:T(1024)} %bitcast.55, s32[24,128]{1,0:T(8,128)} %bitcast.47, bf16[8,192,128]{2,1,0:T(8,128)(2,1)} %copy-done.12, ...), custom_call_target="tpu_custom_call" | custom-call | tf_op jit(solution)/shard_map/far/pallas_call | solution.py:570
  66.2 6.0 %all-to-all-start.2 = ((bf16[8,192,128]{2,1,0:T(8,128)(2,1)}), bf16[8,192,128]{2,1,0:T(8,128)(2,1)S(1)}, u32[]{:S(2)}, u32[]{:S(2)}) async-start(bf16[8,192,128]{2,1,0:T(8,128)(2,1)} %get-tuple-element.61), calls=%async_computation.2 | async-start | bytes 786432 | tf_op jit(solution)/shard_map/all_to_all | solution.py:531
  72.2 3.8 %near.5.near_ref = f32[3072,128]{1,0:T(8,128)} custom-call(s32[128]{0:T(128)} %concatenate.59.meta_ref, s32[24,128]{1,0:T(8,128)} %bitcast.48, bf16[16,128,128]{2,1,0:T(8,128)(2,1)} %bitcast.41, bf16[16,128,128]{2,1,0:T(8,128)(2,1)} %copy-done.2, bf16[3072,128]{1,0:T(8,128)(2,1)} %get-tuple-element.54.rest_0_.rest_1_), custom_call_target="tpu_custom_call" | custom-call | flops 134217728 | bytes 4194304 | tf_op jit(solution)/shard_map/near/pallas_call | solution.py:533
  76.1 8.8 %forward_two.3 = (bf16[1536,1024]{1,0:T(8,128)(2,1)}, bf16[1536,1024]{1,0:T(8,128)(2,1)}) custom-call(s32[1]{0:T(128)} %bitcast.core_ref, f32[1,1024]{1,0:T(1,128)} %bitcast.65, bf16[1536,1024]{1,0:T(8,128)(2,1)} %get-tuple-element.55.x_ref, bf16[1024,1024]{1,0:T(8,128)(2,1)} %weight_ref.5, ...), custom_call_target="tpu_custom_call", output_to_operand_aliasing={{0}: (4, {}), {1}: (5, {})} | custom-call | flops 1626341376 | bytes 4194304 | tf_op jit(solution)/shard_map/forward_two/pallas_call | solution.py:315
  84.9 0.7 copy-done.11
  85.7 6.1 %far.5 = (bf16[8,192,128]{2,1,0:T(8,128)(2,1)}, bf16[3072,128]{1,0:T(8,128)(2,1)}) custom-call(s32[1]{0:T(128)} %bitcast.core_ref, s32[128]{0:T(128)} %concatenate.59.meta_ref, s32[8]{0:T(128)} %bitcast.61, s32[2048]{0:T(1024)} %bitcast.56, s32[24,128]{1,0:T(8,128)} %bitcast.49, bf16[8,192,128]{2,1,0:T(8,128)(2,1)} %copy-done.11, ...), custom_call_target="tpu_custom_call" | custom-call | tf_op jit(solution)/shard_map/far/pallas_call | solution.py:570
  91.8 6.0 %all-to-all-start.3 = ((bf16[8,192,128]{2,1,0:T(8,128)(2,1)}), bf16[8,192,128]{2,1,0:T(8,128)(2,1)S(1)}, u32[]{:S(2)}, u32[]{:S(2)}) async-start(bf16[8,192,128]{2,1,0:T(8,128)(2,1)} %get-tuple-element.63), calls=%async_computation.3 | async-start | bytes 786432 | tf_op jit(solution)/shard_map/all_to_all | solution.py:531
  97.9 5.0 %near_last.1.near_ref = f32[3072,128]{1,0:T(8,128)} custom-call(s32[128]{0:T(128)} %concatenate.59.meta_ref, s32[24,128]{1,0:T(8,128)} %bitcast.50, bf16[16,128,128]{2,1,0:T(8,128)(2,1)} %bitcast.42, bf16[16,128,128]{2,1,0:T(8,128)(2,1)} %copy-done.2, bf16[3072,128]{1,0:T(8,128)(2,1)} %get-tuple-element.64.rest_0_, ...), custom_call_target="tpu_custom_call" | custom-call | flops 134217728 | bytes 4194304 | tf_op jit(solution)/shard_map/near_last/pallas_call | solution.py:533
  102.9 1.2 slice_select_fusion
  104.1 0.9 maximum_select_fusion.2
  105.0 4.1 %all-to-all-done.3.recv_ref = bf16[8,192,128]{2,1,0:T(8,128)(2,1)S(1)} async-done(((bf16[8,192,128]{2,1,0:T(8,128)(2,1)}), bf16[8,192,128]{2,1,0:T(8,128)(2,1)S(1)}, u32[]{:S(2)}, u32[]{:S(2)}) %all-to-all-start.3) | async-done | bytes 393248 | tf_op jit(solution)/shard_map/all_to_all | solution.py:531
  109.1 0.7 copy-done.10
  109.8 4.6 %far_last.1 = (bf16[1536,128]{1,0:T(8,128)(2,1)}, bf16[1536,128]{1,0:T(8,128)(2,1)}) custom-call(s32[1]{0:T(128)} %bitcast.core_ref, s32[128]{0:T(128)} %concatenate.59.meta_ref, s32[8]{0:T(128)} %bitcast.62, s32[2048]{0:T(1024)} %bitcast.57, s32[24,128]{1,0:T(8,128)} %bitcast.51, bf16[8,192,128]{2,1,0:T(8,128)(2,1)} %copy-done.10, ...), custom_call_target="tpu_custom_call" | custom-call | tf_op jit(solution)/shard_map/far_last/pallas_call | solution.py:570
  114.5 1.1 constant_dynamic-update-slice_fusion.1
  115.5 0.8 collective-permute-done.3
  116.5 2.2 %fusion.5 = (bf16[1024]{0:T(1024)(128)(2,1)S(1)}, bf16[1536,1024]{1,0:T(8,128)(2,1)S(1)}) fusion(bf16[1536,1024]{1,0:T(8,128)(2,1)S(1)} %copy-done, bf16[1536,256]{1,0:T(8,128)(2,1)S(1)} %constant_dynamic-update-slice_fusion, bf16[1024,256]{0,1:T(8,128)(2,1)} %maximum_select_fusion.2), kind=kOutput, calls=%fused_computation.44 | convolution fusion | flops 811596800 | bytes 7604224 | tf_op jit(solution)/shard_map/dot_general | solution.py:601
  118.8 0.6 convolution_convert_fusion.3
  119.4 1.4 copy-done.4
  120.7 3.6 %fusion.4 = (bf16[1024]{0:T(1024)(128)(2,1)S(1)}, f32[1536,1024]{1,0:T(8,128)S(1)}) fusion(bf16[1536,1024]{1,0:T(8,128)(2,1)S(1)} %copy-done.4, bf16[1536,1024]{1,0:T(8,128)(2,1)S(1)} %get-tuple-element.78, bf16[1024,1024]{1,0:T(8,128)(2,1)S(1)} %copy-done.8), kind=kOutput, calls=%fused_computation.43 | convolution fusion | flops 3227515904 | bytes 14682112 | tf_op jit(solution)/shard_map/dot_general | solution.py:610
  124.4 0.7 convolution_convert_fusion.4
  125.2 1.1 copy-done.6
  126.3 1.0 convolution_convert_fusion.2
  127.6 1.4 convolution_convert_fusion
  129.0 0.4 collective-permute-start.4
  129.4 0.6 convolution_convert_fusion.5
  130.4 1.5 collective-permute-start.13
  131.9 1.4 add_convert_fusion
  133.3 1.0 collective-permute-start.5
  134.3 2.8 %collective-permute-done.13 = bf16[288,512]{1,0:T(8,128)(2,1)S(1)} collective-permute-done((bf16[288,512]{1,0:T(8,128)(2,1)S(1)}, bf16[288,512]{1,0:T(8,128)(2,1)S(1)}, u32[]{:S(2)}, u32[]{:S(2)}) %collective-permute-start.13) | collective-permute-done | bytes 294944 | tf_op jit(solution)/shard_map/ppermute | solution.py:410
  137.3 4.1 %collective-permute-done.5 = bf16[384,512]{1,0:T(8,128)(2,1)S(1)} collective-permute-done((bf16[384,512]{1,0:T(8,128)(2,1)S(1)}, bf16[384,512]{1,0:T(8,128)(2,1)S(1)}, u32[]{:S(2)}, u32[]{:S(2)}) %collective-permute-start.5) | collective-permute-done | bytes 393248 | tf_op jit(solution)/shard_map/ppermute | solution.py:410
  141.5 0.9 collective-permute-start.6
  142.5 1.2 collective-permute-start.14
  143.7 3.6 %collective-permute-done.6 = bf16[384,256]{1,0:T(8,128)(2,1)S(1)} collective-permute-done((bf16[384,256]{1,0:T(8,128)(2,1)S(1)}, bf16[384,256]{1,0:T(8,128)(2,1)S(1)}, u32[]{:S(2)}, u32[]{:S(2)}) %collective-permute-start.6) | collective-permute-done | bytes 196640 | tf_op jit(solution)/shard_map/ppermute | solution.py:410
  147.4 1.0 collective-permute-start.7
  148.4 0.5 collective-permute-done.14
  148.9 5.1 %collective-permute-done.7 = bf16[384,128]{1,0:T(8,128)(2,1)S(1)} collective-permute-done((bf16[384,128]{1,0:T(8,128)(2,1)S(1)}, bf16[384,128]{1,0:T(8,128)(2,1)S(1)}, u32[]{:S(2)}, u32[]{:S(2)}) %collective-permute-start.7) | collective-permute-done | bytes 98336 | tf_op jit(solution)/shard_map/ppermute | solution.py:410
  154.2 3.0 %collective-permute-start.15 = (bf16[288,128]{1,0:T(8,128)(2,1)S(1)}, bf16[288,128]{1,0:T(8,128)(2,1)S(1)}, u32[]{:S(2)}, u32[]{:S(2)}) collective-permute-start(bf16[288,128]{1,0:T(8,128)(2,1)S(1)} %broadcast_select_fusion.7), channel_id=1, source_target_pairs={{0,8},{1,9},{2,10},{3,11},{4,12},{5,13},{6,14},{7,15},{8,0},{9,1},... | collective-permute-start | bytes 221192 | tf_op jit(solution)/shard_map/ppermute | solution.py:410
  157.1 4.5 %collective-permute-done.8 = bf16[384,128]{1,0:T(8,128)(2,1)S(1)} collective-permute-done((bf16[384,128]{1,0:T(8,128)(2,1)S(1)}, bf16[384,128]{1,0:T(8,128)(2,1)S(1)}, u32[]{:S(2)}, u32[]{:S(2)}) %collective-permute-start.8) | collective-permute-done | bytes 98336 | tf_op jit(solution)/shard_map/ppermute | solution.py:410
  161.8 1.4 collective-permute-done.15
  163.3 7.0 %collective-permute-done.9 = bf16[384,256]{1,0:T(8,128)(2,1)S(1)} collective-permute-done((bf16[384,256]{1,0:T(8,128)(2,1)S(1)}, bf16[384,256]{1,0:T(8,128)(2,1)S(1)}, u32[]{:S(2)}, u32[]{:S(2)}) %collective-permute-start.9) | collective-permute-done | bytes 196640 | tf_op jit(solution)/shard_map/ppermute | solution.py:410
  170.6 5.9 %collective-permute-done.17 = bf16[288,256]{1,0:T(8,128)(2,1)S(1)} collective-permute-done((bf16[288,256]{1,0:T(8,128)(2,1)S(1)}, bf16[288,256]{1,0:T(8,128)(2,1)S(1)}, u32[]{:S(2)}, u32[]{:S(2)}) %collective-permute-start.17) | collective-permute-done | bytes 147488 | tf_op jit(solution)/shard_map/ppermute | solution.py:410
  176.7 1.3 collective-permute-start.18
  178.5 4.9 %collective-permute-done.18 = bf16[288,512]{1,0:T(8,128)(2,1)S(1)} collective-permute-done((bf16[288,512]{1,0:T(8,128)(2,1)S(1)}, bf16[288,512]{1,0:T(8,128)(2,1)S(1)}, u32[]{:S(2)}, u32[]{:S(2)}) %collective-permute-start.18) | collective-permute-done | bytes 294944 | tf_op jit(solution)/shard_map/ppermute | solution.py:410
  183.7 2.0 %collective-permute-done.19.theirs_two = bf16[288,1024]{1,0:T(8,128)(2,1)S(1)} collective-permute-done((bf16[288,1024]{1,0:T(8,128)(2,1)S(1)}, bf16[288,1024]{1,0:T(8,128)(2,1)S(1)}, u32[]{:S(2)}, u32[]{:S(2)}) %collective-permute-start.19) | collective-permute-done | bytes 589856 | tf_op jit(solution)/shard_map/ppermute | solution.py:401
  185.7 0.8 copy-done.14
  186.5 0.9 copy-done.13
  187.4 4.6 %finish.1 = (f32[128,1024]{1,0:T(8,128)}, f32[1,1024]{1,0:T(1,128)}, f32[1024,1024]{1,0:T(8,128)}, f32[1,1024]{1,0:T(1,128)}, f32[172,1024]{1,0:T(8,128)}) custom-call(s32[1]{0:T(128)} %bitcast.core_ref, bf16[384,1024]{1,0:T(8,128)(2,1)} %copy-done.5, bf16[384,1024]{1,0:T(8,128)(2,1)} %copy-done.13, bf16[288,1024]{1,0:T(8,128)(2,1)} %copy-done.7, ...), custom_call_target="tpu_custom_call" | custom-call | tf_op jit(solution)/shard_map/finish/pallas_call | solution.py:646
  (83 shorter events, 3.0 us)
Async XLA Ops:
  0.6 27.0 %copy-start.16 = (s32[1,1,16]{2,1,0:T(1,128)S(1)}, s32[1,1,16]{2,1,0:T(1,128)}, u32[]{:S(2)}) copy-start(s32[1,1,16]{2,1,0:T(1,128)} %param.25) | copy-start | bytes 196
  0.6 27.0 %copy-start.17 = (s32[1,1,16]{2,1,0:T(1,128)S(1)}, s32[1,1,16]{2,1,0:T(1,128)}, u32[]{:S(2)}) copy-start(s32[1,1,16]{2,1,0:T(1,128)} %param.26) | copy-start | bytes 196
  0.7 27.0 %copy-start.18 = (s32[1,1,16]{2,1,0:T(1,128)S(1)}, s32[1,1,16]{2,1,0:T(1,128)}, u32[]{:S(2)}) copy-start(s32[1,1,16]{2,1,0:T(1,128)} %param.28) | copy-start | bytes 196
  0.7 27.0 %copy-start.19 = (s32[1,1,16]{2,1,0:T(1,128)S(1)}, s32[1,1,16]{2,1,0:T(1,128)}, u32[]{:S(2)}) copy-start(s32[1,1,16]{2,1,0:T(1,128)} %param.29) | copy-start | bytes 196
  8.9 24.1 %all-to-all-start = ((bf16[8,192,128]{2,1,0:T(8,128)(2,1)}), bf16[8,192,128]{2,1,0:T(8,128)(2,1)S(1)}, u32[]{:S(2)}, u32[]{:S(2)}) async-start(bf16[8,192,128]{2,1,0:T(8,128)(2,1)} %get-tuple-element.46), calls=%async_computation | async-start | bytes 786432 | tf_op jit(solution)/shard_map/all_to_all | solution.py:531
  16.1 12.2 %collective-permute-start.1 = (bf16[16,128,128]{2,1,0:T(8,128)(2,1)}, bf16[16,128,128]{2,1,0:T(8,128)(2,1)S(1)}, u32[]{:S(2)}, u32[]{:S(2)}) collective-permute-start(bf16[16,128,128]{2,1,0:T(8,128)(2,1)} %bitcast.38), channel_id=1, source_target_pairs={{0,1},{1,0},{2,3},{3,2},{4,5},{5,4},{6,7},{7,6},{8,9},{9,8},{10,11... | collective-permute-start | bytes 1572872 | tf_op jit(solution)/shard_map/ppermute | solution.py:401
  16.2 16.8 %collective-permute-start.2 = (bf16[16,128,128]{2,1,0:T(8,128)(2,1)}, bf16[16,128,128]{2,1,0:T(8,128)(2,1)S(1)}, u32[]{:S(2)}, u32[]{:S(2)}) collective-permute-start(bf16[16,128,128]{2,1,0:T(8,128)(2,1)} %bitcast.33), channel_id=1, source_target_pairs={{0,1},{1,0},{2,3},{3,2},{4,5},{5,4},{6,7},{7,6},{8,9},{9,8},{10,11... | collective-permute-start | bytes 1572872 | tf_op jit(solution)/shard_map/ppermute | solution.py:401
  17.4 10.2 %collective-permute-start = (s32[64]{0:T(128)S(1)}, s32[64]{0:T(128)S(1)}, u32[]{:S(2)}, u32[]{:S(2)}) collective-permute-start(s32[64]{0:T(128)S(1)} %pad_add_fusion), channel_id=1, source_target_pairs={{0,1},{1,0},{2,3},{3,2},{4,5},{5,4},{6,7},{7,6},{8,9},{9,8},{10,11... | collective-permute-start | bytes 776 | tf_op jit(solution)/shard_map/ppermute | solution.py:401
  28.3 0.8 copy-start.2
  33.0 0.8 copy-start.1
  33.8 0.8 copy-start.9
  40.6 18.7 %all-to-all-start.1 = ((bf16[8,192,128]{2,1,0:T(8,128)(2,1)}), bf16[8,192,128]{2,1,0:T(8,128)(2,1)S(1)}, u32[]{:S(2)}, u32[]{:S(2)}) async-start(bf16[8,192,128]{2,1,0:T(8,128)(2,1)} %get-tuple-element.48), calls=%async_computation.1 | async-start | bytes 786432 | tf_op jit(solution)/shard_map/all_to_all | solution.py:531
  59.3 0.8 copy-start.12
  66.2 18.7 %all-to-all-start.2 = ((bf16[8,192,128]{2,1,0:T(8,128)(2,1)}), bf16[8,192,128]{2,1,0:T(8,128)(2,1)S(1)}, u32[]{:S(2)}, u32[]{:S(2)}) async-start(bf16[8,192,128]{2,1,0:T(8,128)(2,1)} %get-tuple-element.61), calls=%async_computation.2 | async-start | bytes 786432 | tf_op jit(solution)/shard_map/all_to_all | solution.py:531
  84.9 12.9 %slice-start = ((bf16[1024,172]{0,1:T(8,128)(2,1)}), bf16[1024,84]{0,1:T(8,128)(2,1)S(1)}, s32[]{:S(2)}) async-start(bf16[1024,172]{0,1:T(8,128)(2,1)} %param.23), calls=%async_computation.4 | async-start | bytes 360448 | tf_op jit(solution)/shard_map/slice | solution.py:567
  84.9 0.8 copy-start.11
  91.8 17.3 %all-to-all-start.3 = ((bf16[8,192,128]{2,1,0:T(8,128)(2,1)}), bf16[8,192,128]{2,1,0:T(8,128)(2,1)S(1)}, u32[]{:S(2)}, u32[]{:S(2)}) async-start(bf16[8,192,128]{2,1,0:T(8,128)(2,1)} %get-tuple-element.63), calls=%async_computation.3 | async-start | bytes 786432 | tf_op jit(solution)/shard_map/all_to_all | solution.py:531
  97.8 5.0 %copy-start.20 = (pred[128]{0:T(512)(128)(4,1)S(1)}, pred[128]{0:T(512)(128)(4,1)}, u32[]{:S(2)}) copy-start(pred[128]{0:T(512)(128)(4,1)} %constant.21.clone.1) | copy-start | bytes 388
  102.9 13.6 %copy-start = (bf16[1536,1024]{1,0:T(8,128)(2,1)S(1)}, bf16[1536,1024]{1,0:T(8,128)(2,1)}, u32[]{:S(2)}) copy-start(bf16[1536,1024]{1,0:T(8,128)(2,1)} %get-tuple-element.60) | copy-start | bytes 9437188
  109.1 0.7 copy-start.10
  114.4 2.0 %collective-permute-start.3 = (bf16[1536,128]{1,0:T(8,128)(2,1)}, bf16[1536,128]{1,0:T(8,128)(2,1)S(1)}, u32[]{:S(2)}, u32[]{:S(2)}) collective-permute-start(bf16[1536,128]{1,0:T(8,128)(2,1)} %get-tuple-element.68), channel_id=1, source_target_pairs={{0,1},{1,0},{2,3},{3,2},{4,5},{5,4},{6,7},{7,6},{8,9},{9,8},{10,11... | collective-permute-start | bytes 1179656 | tf_op jit(solution)/shard_map/ppermute | solution.py:401
  116.5 2.3 %copy-start.3 = (bf16[1536,1024]{1,0:T(8,128)(2,1)S(1)}, bf16[1536,1024]{1,0:T(8,128)(2,1)}, u32[]{:S(2)}) copy-start(bf16[1536,1024]{1,0:T(8,128)(2,1)} %get-tuple-element.55.x_ref) | copy-start | bytes 9437188
  116.5 2.9 %copy-start.8 = (bf16[1024,1024]{1,0:T(8,128)(2,1)S(1)}, bf16[1024,1024]{1,0:T(8,128)(2,1)}, u32[]{:S(2)}) copy-start(bf16[1024,1024]{1,0:T(8,128)(2,1)} %weight_ref.5) | copy-start | bytes 6291460
  118.7 2.0 %copy-start.4 = (bf16[1536,1024]{1,0:T(8,128)(2,1)S(1)}, bf16[1536,1024]{1,0:T(8,128)(2,1)}, u32[]{:S(2)}) copy-start(bf16[1536,1024]{1,0:T(8,128)(2,1)} %get-tuple-element.70) | copy-start | bytes 9437188
  120.7 3.6 %copy-start.15 = (bf16[1536,128]{1,0:T(8,128)(2,1)S(1)}, bf16[1536,128]{1,0:T(8,128)(2,1)}, u32[]{:S(2)}) copy-start(bf16[1536,128]{1,0:T(8,128)(2,1)} %x_ref) | copy-start | bytes 1179652
  124.4 1.9 copy-start.6
  127.4 2.7 %collective-permute-start.12 = (bf16[288,1024]{1,0:T(8,128)(2,1)S(1)}, bf16[288,1024]{1,0:T(8,128)(2,1)S(1)}, u32[]{:S(2)}, u32[]{:S(2)}) collective-permute-start(bf16[288,1024]{1,0:T(8,128)(2,1)S(1)} %pad_maximum_fusion), channel_id=1, source_target_pairs={{0,1},{1,0},{2,3},{3,2},{4,5},{5,4},{6,7},{7,6},{8,9},{9,8},{10,11... | collective-permute-start | bytes 1769480 | tf_op jit(solution)/shard_map/ppermute | solution.py:401
  129.0 2.9 %collective-permute-start.4 = (bf16[384,1024]{1,0:T(8,128)(2,1)S(1)}, bf16[384,1024]{1,0:T(8,128)(2,1)S(1)}, u32[]{:S(2)}, u32[]{:S(2)}) collective-permute-start(bf16[384,1024]{1,0:T(8,128)(2,1)S(1)} %convolution_convert_fusion), channel_id=1, source_target_pairs={{0,1},{1,0},{2,3},{3,2},{4,5},{5,4},{6,7},{7,6},{8,9},{9,8},{10,11... | collective-permute-start | bytes 2359304 | tf_op jit(solution)/shard_map/ppermute | solution.py:401
  130.4 6.8 %collective-permute-start.13 = (bf16[288,512]{1,0:T(8,128)(2,1)S(1)}, bf16[288,512]{1,0:T(8,128)(2,1)S(1)}, u32[]{:S(2)}, u32[]{:S(2)}) collective-permute-start(bf16[288,512]{1,0:T(8,128)(2,1)S(1)} %broadcast_select_fusion.1), channel_id=1, source_target_pairs={{0,2},{1,5},{2,0},{3,7},{4,6},{5,1},{6,4},{7,3},{8,10},{9,13},{10,... | collective-permute-start | bytes 884744 | tf_op jit(solution)/shard_map/ppermute | solution.py:410
  133.3 8.0 %collective-permute-start.5 = (bf16[384,512]{1,0:T(8,128)(2,1)S(1)}, bf16[384,512]{1,0:T(8,128)(2,1)S(1)}, u32[]{:S(2)}, u32[]{:S(2)}) collective-permute-start(bf16[384,512]{1,0:T(8,128)(2,1)S(1)} %broadcast_select_fusion), channel_id=1, source_target_pairs={{0,2},{1,5},{2,0},{3,7},{4,6},{5,1},{6,4},{7,3},{8,10},{9,13},{10,... | collective-permute-start | bytes 1179656 | tf_op jit(solution)/shard_map/ppermute | solution.py:410
  141.5 5.7 %collective-permute-start.6 = (bf16[384,256]{1,0:T(8,128)(2,1)S(1)}, bf16[384,256]{1,0:T(8,128)(2,1)S(1)}, u32[]{:S(2)}, u32[]{:S(2)}) collective-permute-start(bf16[384,256]{1,0:T(8,128)(2,1)S(1)} %broadcast_select_fusion.2), channel_id=1, source_target_pairs={{0,4},{1,3},{2,6},{3,1},{4,0},{5,7},{6,2},{7,5},{8,12},{9,11},{10,... | collective-permute-start | bytes 589832 | tf_op jit(solution)/shard_map/ppermute | solution.py:410
  142.5 6.3 %collective-permute-start.14 = (bf16[288,256]{1,0:T(8,128)(2,1)S(1)}, bf16[288,256]{1,0:T(8,128)(2,1)S(1)}, u32[]{:S(2)}, u32[]{:S(2)}) collective-permute-start(bf16[288,256]{1,0:T(8,128)(2,1)S(1)} %broadcast_select_fusion.3), channel_id=1, source_target_pairs={{0,4},{1,3},{2,6},{3,1},{4,0},{5,7},{6,2},{7,5},{8,12},{9,11},{10,... | collective-permute-start | bytes 442376 | tf_op jit(solution)/shard_map/ppermute | solution.py:410
  147.4 6.6 %collective-permute-start.7 = (bf16[384,128]{1,0:T(8,128)(2,1)S(1)}, bf16[384,128]{1,0:T(8,128)(2,1)S(1)}, u32[]{:S(2)}, u32[]{:S(2)}) collective-permute-start(bf16[384,128]{1,0:T(8,128)(2,1)S(1)} %broadcast_select_fusion.6), channel_id=1, source_target_pairs={{0,8},{1,9},{2,10},{3,11},{4,12},{5,13},{6,14},{7,15},{8,0},{9,1},... | collective-permute-start | bytes 294920 | tf_op jit(solution)/shard_map/ppermute | solution.py:410
  154.1 7.6 %collective-permute-start.8 = (bf16[384,128]{1,0:T(8,128)(2,1)S(1)}, bf16[384,128]{1,0:T(8,128)(2,1)S(1)}, u32[]{:S(2)}, u32[]{:S(2)}) collective-permute-start(bf16[384,128]{1,0:T(8,128)(2,1)S(1)} %add_convert_fusion.6), channel_id=1, source_target_pairs={{0,8},{1,9},{2,10},{3,11},{4,12},{5,13},{6,14},{7,15},{8,0},{9,1},... | collective-permute-start | bytes 294920 | tf_op jit(solution)/shard_map/ppermute | solution.py:410
  154.2 9.0 %collective-permute-start.15 = (bf16[288,128]{1,0:T(8,128)(2,1)S(1)}, bf16[288,128]{1,0:T(8,128)(2,1)S(1)}, u32[]{:S(2)}, u32[]{:S(2)}) collective-permute-start(bf16[288,128]{1,0:T(8,128)(2,1)S(1)} %broadcast_select_fusion.7), channel_id=1, source_target_pairs={{0,8},{1,9},{2,10},{3,11},{4,12},{5,13},{6,14},{7,15},{8,0},{9,1},... | collective-permute-start | bytes 221192 | tf_op jit(solution)/shard_map/ppermute | solution.py:410
  161.7 8.6 %collective-permute-start.9 = (bf16[384,256]{1,0:T(8,128)(2,1)S(1)}, bf16[384,256]{1,0:T(8,128)(2,1)S(1)}, u32[]{:S(2)}, u32[]{:S(2)}) collective-permute-start(bf16[384,256]{1,0:T(8,128)(2,1)S(1)} %maximum_select_fusion.5), channel_id=1, source_target_pairs={{0,4},{1,3},{2,6},{3,1},{4,0},{5,7},{6,2},{7,5},{8,12},{9,11},{10,... | collective-permute-start | bytes 589832 | tf_op jit(solution)/shard_map/ppermute | solution.py:410
  163.2 7.3 %collective-permute-start.16 = (bf16[288,128]{1,0:T(8,128)(2,1)S(1)}, bf16[288,128]{1,0:T(8,128)(2,1)S(1)}, u32[]{:S(2)}, u32[]{:S(2)}) collective-permute-start(bf16[288,128]{1,0:T(8,128)(2,1)S(1)} %add_convert_fusion.7), channel_id=1, source_target_pairs={{0,8},{1,9},{2,10},{3,11},{4,12},{5,13},{6,14},{7,15},{8,0},{9,1},... | collective-permute-start | bytes 221192 | tf_op jit(solution)/shard_map/ppermute | solution.py:410
  170.4 7.8 %collective-permute-start.10 = (bf16[384,512]{1,0:T(8,128)(2,1)S(1)}, bf16[384,512]{1,0:T(8,128)(2,1)S(1)}, u32[]{:S(2)}, u32[]{:S(2)}) collective-permute-start(bf16[384,512]{1,0:T(8,128)(2,1)S(1)} %maximum_select_fusion.3), channel_id=1, source_target_pairs={{0,2},{1,5},{2,0},{3,7},{4,6},{5,1},{6,4},{7,3},{8,10},{9,13},{10,... | collective-permute-start | bytes 1179656 | tf_op jit(solution)/shard_map/ppermute | solution.py:410
  170.5 6.0 %collective-permute-start.17 = (bf16[288,256]{1,0:T(8,128)(2,1)S(1)}, bf16[288,256]{1,0:T(8,128)(2,1)S(1)}, u32[]{:S(2)}, u32[]{:S(2)}) collective-permute-start(bf16[288,256]{1,0:T(8,128)(2,1)S(1)} %maximum_select_fusion.6), channel_id=1, source_target_pairs={{0,4},{1,3},{2,6},{3,1},{4,0},{5,7},{6,2},{7,5},{8,12},{9,11},{10,... | collective-permute-start | bytes 442376 | tf_op jit(solution)/shard_map/ppermute | solution.py:410
  176.7 6.8 %collective-permute-start.18 = (bf16[288,512]{1,0:T(8,128)(2,1)S(1)}, bf16[288,512]{1,0:T(8,128)(2,1)S(1)}, u32[]{:S(2)}, u32[]{:S(2)}) collective-permute-start(bf16[288,512]{1,0:T(8,128)(2,1)S(1)} %maximum_select_fusion.4), channel_id=1, source_target_pairs={{0,2},{1,5},{2,0},{3,7},{4,6},{5,1},{6,4},{7,3},{8,10},{9,13},{10,... | collective-permute-start | bytes 884744 | tf_op jit(solution)/shard_map/ppermute | solution.py:410
  178.5 7.3 %copy-start.5 = (bf16[384,1024]{1,0:T(8,128)(2,1)}, bf16[384,1024]{1,0:T(8,128)(2,1)S(1)}, u32[]{:S(2)}) copy-start(bf16[384,1024]{1,0:T(8,128)(2,1)S(1)} %maximum_select_fusion.mine_one) | copy-start | bytes 2359300
  178.5 7.3 %collective-permute-start.11 = (bf16[384,1024]{1,0:T(8,128)(2,1)S(1)}, bf16[384,1024]{1,0:T(8,128)(2,1)S(1)}, u32[]{:S(2)}, u32[]{:S(2)}) collective-permute-start(bf16[384,1024]{1,0:T(8,128)(2,1)S(1)} %maximum_select_fusion.mine_one), channel_id=1, source_target_pairs={{0,1},{1,0},{2,3},{3,2},{4,5},{5,4},{6,7},{7,6},{8,9},{9,8},{10,11... | collective-permute-start | bytes 2359304 | tf_op jit(solution)/shard_map/ppermute | solution.py:401
  183.6 2.1 %copy-start.7 = (bf16[288,1024]{1,0:T(8,128)(2,1)}, bf16[288,1024]{1,0:T(8,128)(2,1)S(1)}, u32[]{:S(2)}) copy-start(bf16[288,1024]{1,0:T(8,128)(2,1)S(1)} %maximum_select_fusion.1.mine_two) | copy-start | bytes 1769476
  183.7 2.1 %collective-permute-start.19 = (bf16[288,1024]{1,0:T(8,128)(2,1)S(1)}, bf16[288,1024]{1,0:T(8,128)(2,1)S(1)}, u32[]{:S(2)}, u32[]{:S(2)}) collective-permute-start(bf16[288,1024]{1,0:T(8,128)(2,1)S(1)} %maximum_select_fusion.1.mine_two), channel_id=1, source_target_pairs={{0,1},{1,0},{2,3},{3,2},{4,5},{5,4},{6,7},{7,6},{8,9},{9,8},{10,11... | collective-permute-start | bytes 1769480 | tf_op jit(solution)/shard_map/ppermute | solution.py:401
  185.7 0.8 copy-start.14
  186.5 0.9 copy-start.13

commit v5 on v4

--- a/solution.py
+++ b/solution.py
@@ -129,12 +129,24 @@
     return jnp.broadcast_to(columns[:, b : b + 1], columns.shape)
 
 
-def first_kernel(slots, class_half, core_ref, count_ref, idx_ref, nodes_ref, labels_ref, logits_ref, degree_ref,
-                 out_ref, value_ref, wide_ref, diff_ref, v_ref, stage_ref, packed_ref, value_v, sems, own_sems):
-    classes, batch = logits_ref.shape
+def first_kernel(class_half, core_ref, count_ref, nodes_ref, rows_ref, labels_ref, logits_ref, degree_ref,
+                 out_ref, value_ref, wide_ref, diff_ref, v_ref, stage_ref, packed_ref, value_v, idx_ref, idx_sems,
+                 sems, own_sems):
+    classes, unused, batch = logits_ref.shape
+    peers = packed_ref.shape[0]
+    slots = stage_ref.shape[0] // peers
+    flat = []
+    if rows_ref.ndim == 1:
+        idx_ref = rows_ref
+    else:
+        for j in range(peers):
+            to = idx_ref.at[pl.ds(j * slots, slots)]
+            flat.append(pltpu.make_async_copy(rows_ref.at[j], to, idx_sems.at[j]))
+    for copy in flat:
+        copy.start()
     blocks, block = degree_ref.shape
     core = core_ref[0]
-    logits = logits_ref[...]
+    logits = logits_ref[...].reshape(classes, batch)
     shifted = jnp.exp(logits - jnp.max(logits, axis=0, keepdims=True))
     hot = lax.broadcasted_iota(jnp.int32, (classes, batch), 0) == labels_ref[...]
     probs = shifted / jnp.sum(shifted, axis=0, keepdims=True)
@@ -159,6 +171,8 @@
         v_ref[at, :] = scaled
     value_copy = pltpu.make_async_copy(value_v, value_ref, own_sems.at[0])
     value_copy.start()
+    for copy in flat:
+        copy.wait()
     send_packed(v_ref, count_ref, idx_ref, stage_ref, packed_ref, out_ref, sems, slots, class_half)
     value_copy.wait()
     wait_packed(packed_ref, out_ref, sems)
@@ -257,117 +271,26 @@
     wait_packed(packed_ref, out_ref, sems)
 
 
-def forward_kernel(first_row, chunk, turn_depth, turn_hidden, core_ref, bias_ref, x_ref, weight_ref, *rest):
-    hidden_ref, slope_ref, x_v, weight_v, hidden_v, slope_v, sems, out_sems = rest[-8:]
-    core = core_ref[0]
-    rows, depth = x_v.shape
-    width = weight_v.shape[1]
-    step = min(256, width // 2)
-    copies = [pltpu.make_async_copy(x_ref.at[pl.ds(first_row, rows)], x_v, sems.at[0])]
-    if turn_depth:
-        half = depth // 2
-        for i in range(2):
-            source = pl.multiple_of((core ^ i) * half, half)
-            copies.append(
-                pltpu.make_async_copy(
-                    weight_ref.at[pl.ds(source, half)], weight_v.at[pl.ds(i * half, half)], sems.at[1 + i]
-                )
-            )
-    else:
-        copies.append(pltpu.make_async_copy(weight_ref, weight_v, sems.at[1]))
-    for copy in copies:
-        copy.start()
-    for copy in copies:
-        copy.wait()
-    outs = []
-    for c in range(rows // chunk):
-        here = slice(c * chunk, (c + 1) * chunk)
-
-        def body(j, carry, here=here):
-            start = pl.multiple_of(j * step, step)
-            at = pl.ds(start, step)
-            pre = jnp.dot(x_v[here, :], weight_v[:, at], preferred_element_type=f32) + bias_ref[:, at]
-            hidden, slope = gelu_parts(pre)
-            slope_v[here, at] = slope
-            if turn_hidden:
-                turned = lax.rem(start + core * (width // 2), width)
-                hidden_v[here, pl.ds(pl.multiple_of(turned, step), step)] = hidden
-            else:
-                hidden_v[here, at] = hidden
-            return carry
-
-        lax.fori_loop(0, width // step, body, 0)
-        to = pl.ds(first_row + c * chunk, chunk)
-        for k, (source, target) in enumerate(((hidden_v, hidden_ref), (slope_v, slope_ref))):
-            out = pltpu.make_async_copy(source.at[pl.ds(c * chunk, chunk)], target.at[to], out_sems.at[2 * c + k])
-            out.start()
-            outs.append(out)
-    for out in outs:
-        out.wait()
-
-
-def forward_layer(core_arg, x, weight, bias, part, parts, turn_depth, turn_hidden, earlier, name):
-    rows, depth = x.shape
-    width = weight.shape[1]
-    own = rows // parts
-    chunk = 256 if own % 256 == 0 else own
-    kind = jax.ShapeDtypeStruct((rows, width), bf16)
-    return pl.pallas_call(
-        functools.partial(forward_kernel, part * own, chunk, turn_depth, turn_hidden),
-        out_shape=(kind, kind),
-        in_specs=[smem(), vmem(), hbm(), hbm()] + [hbm()] * len(earlier),
-        out_specs=(hbm(), hbm()),
-        scratch_shapes=[
-            pltpu.VMEM((own, depth), bf16),
-            pltpu.VMEM((depth, width), bf16),
-            pltpu.VMEM((own, width), bf16),
-            pltpu.VMEM((own, width), bf16),
-            pltpu.SemaphoreType.DMA((3,)),
-            pltpu.SemaphoreType.DMA((2 * (own // chunk),)),
-        ],
-        input_output_aliases={4 + i: i for i in range(len(earlier))},
-        compiler_params=params(),
-        cost_estimate=pl.CostEstimate(
-            flops=(2 * rows * depth * width + 20 * rows * width) // parts,
-            bytes_accessed=8 * 2**20 // parts,
-            transcendentals=rows * width // parts,
-        ),
-        name=name,
-    )(core_arg, bias.reshape(1, width), x, weight, *earlier)
-
-
 def finish_kernel(class_half, core_ref, mine_one, theirs_one, mine_two, theirs_two, first_ref, first_bias_ref,
-                  second_ref, second_bias_ref, third_ref, mine_v, theirs_v, wide_v, sems, out_sems):
-    one, two = mine_one.shape[0], mine_two.shape[0]
+                  second_ref, second_bias_ref, third_ref, wide_v, out_sems):
+    one = mine_one.shape[0]
     hidden = second_ref.shape[0]
     feat = first_ref.shape[0]
     classes = third_ref.shape[0]
     half, feat_half = hidden // 2, feat // 2
-    copies = []
-    for i, (source, target) in enumerate(((mine_one, mine_v), (theirs_one, theirs_v))):
-        copies.append(pltpu.make_async_copy(source, target.at[pl.ds(0, one)], sems.at[i]))
-    for i, (source, target) in enumerate(((mine_two, mine_v), (theirs_two, theirs_v))):
-        copies.append(pltpu.make_async_copy(source, target.at[pl.ds(one, two)], sems.at[2 + i]))
-    for copy in copies:
-        copy.start()
     is_first = core_ref[0] == 0
 
     def both(start, count):
-        mine = mine_v[start : start + count, :].astype(f32)
-        theirs = theirs_v[start : start + count, :].astype(f32)
+        mine_ref, theirs_ref = (mine_one, theirs_one) if start < one else (mine_two, theirs_two)
+        at = start if start < one else start - one
+        mine = mine_ref[at : at + count, :].astype(f32)
+        theirs = theirs_ref[at : at + count, :].astype(f32)
         return jnp.where(is_first, mine, theirs), jnp.where(is_first, theirs, mine)
 
     step = math.gcd(one, half)
     outs = []
     for start in range(0, half, step):
-        if start == 0:
-            copies[0].wait()
-            copies[1].wait()
-        if start == one:
-            copies[2].wait()
-            copies[3].wait()
-        low, high = both(start, step)
-        for k, value in enumerate((low, high)):
+        for k, value in enumerate(both(start, step)):
             at = k * half + start
             wide_v[at : at + step, :] = value
             out = pltpu.make_async_copy(
@@ -375,15 +298,17 @@
             )
             out.start()
             outs.append(out)
-    low, high = both(half, feat_half)
-    first_ref[0:feat_half, :] = low
-    first_ref[feat_half:feat, :] = high
     low, high = both(half + feat_half, class_half)
     third_ref[0:class_half, :] = low
     third_ref[class_half:classes, :] = high[: classes - class_half]
-    low, high = both(half + feat_half + class_half, 8)
-    first_bias_ref[...] = low[:1]
-    second_bias_ref[...] = high[:1]
+    firsts = both(half, feat_half)
+    biases = both(half + feat_half + class_half, 8)
+    for k in range(2):
+        at = slice(k * half, (k + 1) * half)
+        first_ref[0:feat_half, at] = firsts[k][:, :half]
+        first_ref[feat_half:feat, at] = firsts[k][:, half:]
+        first_bias_ref[:, at] = biases[k][:1, :half]
+        second_bias_ref[:, at] = biases[k][:1, half:]
     for out in outs:
         out.wait()
 
@@ -505,24 +430,32 @@
     ]
     peer_sems = pltpu.SemaphoreType.DMA((peers,))
 
-    idx = send_rows[0].reshape(-1)
     counts = send_count[0]
+    whole_tiles = slots % LANES == 0
+    first_rows = send_rows[0] if whole_tiles else send_rows[0].reshape(-1)
     out, value = pl.pallas_call(
-        functools.partial(first_kernel, slots, class_half),
+        functools.partial(first_kernel, class_half),
         out_shape=(out_type, value_type),
-        in_specs=[smem()] * 4 + [vmem()] * 3,
+        in_specs=[smem()] * 3 + [vmem() if whole_tiles else smem()] + [vmem()] * 3,
         out_specs=(hbm(), hbm()),
         scratch_shapes=[
             pltpu.VMEM((2 * LANES, batch), f32),
             pltpu.VMEM((batch, LANES), f32),
             acc,
             *sending,
+            pltpu.SMEM((peers * slots,), jnp.int32),
+            peer_sems,
             peer_sems,
             pltpu.SemaphoreType.DMA((1,)),
         ],
         compiler_params=params(),
         name="first",
-    )(core_arg, counts, idx, batch_nodes[0], labels, batch_logits[0].T, degree_blocks)
+    )(core_arg, counts, batch_nodes[0], first_rows, labels, jnp.transpose(batch_logits, (2, 0, 1)), degree_blocks)
+    idx = lax.optimization_barrier((send_rows, value))[0].reshape(-1)
+
+    def turn(array, axis):
+        low, high = split(array, axis)
+        return jnp.where(core == 0, array, jnp.concatenate([high, low], axis))
 
     values = []
     for hop in range(HOPS):
@@ -549,18 +482,21 @@
             name="near_last" if last else "near",
         )(meta, degree_blocks, own_local, other_local, *near_values)
         if hop == 0:
-            x, _ = lax.optimization_barrier((features, value))
-            hidden_first, slope_first = forward_layer(
-                core_arg, x, first_weight, first_bias, 0, 1, False, True, (), "forward_one"
+            x, first_w, second_w, _ = lax.optimization_barrier((features, first_weight, second_weight, value))
+            pre_first = jnp.dot(x, turn(first_w, 1), preferred_element_type=f32) + turn(first_bias, 0)
+            hidden_first, slope_first = gelu_parts(pre_first)
+            second_turned = turn(second_w, 0)
+            near, hidden_first, slope_first, second_turned = lax.optimization_barrier(
+                (near, hidden_first, slope_first, second_turned)
             )
-            near, hidden_first, slope_first = lax.optimization_barrier((near, hidden_first, slope_first))
-        if hop in (1, 2):
+        if hop == 1:
             tied, _ = lax.optimization_barrier((hidden_first, value))
-            second = forward_layer(
-                core_arg, tied, second_weight, second_bias, hop - 1, 2, True, False, () if hop == 1 else second,
-                "forward_two",
-            )
-            near, *second = lax.optimization_barrier((near, *second))
+            pre_second = jnp.dot(tied, second_turned, preferred_element_type=f32)
+            near, pre_second = lax.optimization_barrier((near, pre_second))
+        if hop == 2:
+            tied, _ = lax.optimization_barrier((pre_second, value))
+            hidden_second, slope_second = gelu_parts(tied + second_bias)
+            near, hidden_second, slope_second = lax.optimization_barrier((near, hidden_second, slope_second))
         if last:
             tied, _ = lax.optimization_barrier((third_weight, value))
             low = jnp.pad(tied[:, :class_half], ((0, 0), (0, LANES - class_half)))
@@ -589,7 +525,6 @@
         else:
             out, value = result
 
-    hidden_second, slope_second = second
     got = swap_cores(send)
     delta = jnp.concatenate([keep, got], axis=1)
 
@@ -608,7 +543,7 @@
     keep_tail = contract(hidden_first[:, lead:half], second_delta)
     third_grad = contract(delta, hidden_second)
     back_first = lax.dot_general(
-        second_delta, second_weight, (((1,), (1,)), ((), ())), preferred_element_type=f32
+        second_delta, second_turned, (((1,), (1,)), ((), ())), preferred_element_type=f32
     )
     first_delta = (slope_first.astype(f32) * back_first).astype(bf16)
     first_grad = contract(x, first_delta)
@@ -620,29 +555,21 @@
     grain = 8 * max(1, domains >> column_splits)
     used = half - lead + feat // 2 + class_half
     tail_rows = -(-(used + 1) // grain) * grain
-    low_first, high_first = first_grad[: feat // 2], first_grad[feat // 2 :]
-
-    def bundle(tail, first_rows, third_rows, bias_row):
+
+    def bundle(part, tail, third_rows, bias_half):
+        at = slice(part * half, (part + 1) * half)
+        first_rows = jnp.concatenate([first_grad[: feat // 2, at], first_grad[feat // 2 :, at]], 1)
+        bias_row = jnp.concatenate([first_bias_grad[at], bias_half])
         bias = jnp.broadcast_to(bias_row[None], (tail_rows - used, hidden))
         return jnp.concatenate([tail, first_rows, third_rows[:class_half], bias], 0)
 
-    keep_rest = bundle(
-        keep_tail,
-        jnp.where(is_first, low_first, high_first),
-        third_grad[:LANES],
-        jnp.where(is_first, first_bias_grad, second_bias_grad),
-    )
-    send_rest = bundle(
-        send_tail,
-        jnp.where(is_first, high_first, low_first),
-        third_grad[LANES:],
-        jnp.where(is_first, second_bias_grad, first_bias_grad),
-    )
+    low_bias, high_bias = split(second_bias_grad, 0)
+    keep_rest = bundle(0, keep_tail, third_grad[:LANES], jnp.where(is_first, low_bias, high_bias))
+    send_rest = bundle(1, send_tail, third_grad[LANES:], jnp.where(is_first, high_bias, low_bias))
     got_rest = swap_cores(send_rest)
     mine_lead = sum_over_domains((keep_lead.astype(f32) + got_lead.astype(f32)).astype(bf16))
     mine_rest = sum_over_domains((keep_rest.astype(f32) + got_rest.astype(f32)).astype(bf16))
     theirs_lead, theirs_rest = swap_cores(mine_lead), swap_cores(mine_rest)
-    rows_all = lead + tail_rows
     first_out, first_bias_out, second_out, second_bias_out, third_out = pl.pallas_call(
         functools.partial(finish_kernel, class_half),
         out_shape=(
@@ -652,16 +579,13 @@
             jax.ShapeDtypeStruct((1, hidden), f32),
             jax.ShapeDtypeStruct((classes, hidden), f32),
         ),
-        in_specs=[smem()] + [hbm()] * 4,
+        in_specs=[smem()] + [vmem()] * 4,
         out_specs=(vmem(), vmem(), hbm(), vmem(), vmem()),
         scratch_shapes=[
-            pltpu.VMEM((rows_all, hidden), bf16),
-            pltpu.VMEM((rows_all, hidden), bf16),
             pltpu.VMEM((hidden, hidden), f32),
-            pltpu.SemaphoreType.DMA((4,)),
             pltpu.SemaphoreType.DMA((2 * (half // math.gcd(lead, half)),)),
         ],
-        compiler_params=params(),
+        compiler_params=pltpu.CompilerParams(vmem_limit_bytes=24 * 1024 * 1024),
         name="finish",
     )(core_arg, mine_lead, theirs_lead, mine_rest, theirs_rest)
     return first_out, first_bias_out.reshape(hidden), second_out, second_bias_out.reshape(hidden), third_out.T

time: 194 us -> 183 us (0.943)
  Pallas kernels: 77.1 us -> 48.9 us
  matrix products: 11.6 us -> 25.8 us
  other arithmetic: 4.52 us -> 13.4 us
  waiting for transfers between devices: 47 us -> 41.7 us
    pallas_call x4 -> x1, Pallas kernels: 33.1 us -> 5.77 us  [shards(): pl.pallas_call(functools.partial(first_kernel, class_half), out_shape=(ou...]
    dot_general x1 -> x3, matrix products: 3.62 us -> 17.8 us  [the longest x1 7.27 us: shards(): pre_second = jnp.dot(tied, second_turned, preferred_element_type=f32)]
    convert_element_type x0 -> x1, other arithmetic: none -> 6.75 us  [gelu_parts(): return ((x * half_up).astype(bf16), slope.astype(bf16))]
    unnamed x45 -> x36, local copies, waits for them, and re-layouts: 12.7 us -> 6.56 us
    ppermute x12, waiting for transfers between devices: 40.1 us -> 37.2 us  [exchange(): return lax.ppermute(x, ('dom', 'col'), pairs)]
    all_to_all x4, waiting for transfers between devices: 4.06 us -> 1.58 us  [shards(): landed = lax.all_to_all(out, 'dom', split_axis=0, concat_axis=0, tiled=True)]
    ppermute x12, starting transfers between devices: 10.2 us -> 12.5 us  [exchange(): return lax.ppermute(x, ('dom', 'col'), pairs)]
    slice x0 -> x5, local copies, waits for them, and re-layouts: none -> 1.96 us  [the longest x3 1.93 us: split(): lax.slice_in_dim(x, half, 2 * half, axis=axis)]
  transfers between devices with their start and end apart: 24 -> 24, of which waited for: 14 -> 13; matrix products, arithmetic and copies ran while one was open for 5% -> 19% of each run, Pallas kernels for 23% -> 12%
where the time goes in v5:
time: 183 us; the launch traced here: 182 us
  Pallas kernels  48.9 us (27%)
  waiting for transfers between devices  41.7 us (23%)
  starting transfers between devices  38.8 us (21%)
  matrix products  25.8 us (14%)
  other arithmetic  13.4 us (7%)
  local copies, waits for them, and re-layouts  11.8 us (6%)
    ppermute x12, waiting for transfers between devices, exchange(): return lax.ppermute(x, ('dom', 'col'), pairs)  37.2 us
    all_to_all x4, starting transfers between devices, shards(): landed = lax.all_to_all(out, 'dom', split_axis=0, concat_axis=0, tiled=True)  25 us
    pallas_call x4, Pallas kernels, shards(): pl.pallas_call(functools.partial(far_kernel, slots, class_half, 2 * local...  23.4 us
    pallas_call x4, Pallas kernels, shards(): pl.pallas_call(functools.partial(near_kernel, stride, last), out_shape=ja...  16.5 us
    ppermute x12, starting transfers between devices, exchange(): return lax.ppermute(x, ('dom', 'col'), pairs)  12.5 us
    dot_general x1, matrix products, shards(): pre_second = jnp.dot(tied, second_turned, preferred_element_type=f32)  7.27 us
    dot_general x1, matrix products, shards(): jnp.dot(x, turn(first_w, 1), preferred_element_type=f32)  6.9 us
    convert_element_type x1, other arithmetic, gelu_parts(): return ((x * half_up).astype(bf16), slope.astype(bf16))  6.75 us
  transfers between devices with their start and end apart: 24, of which 13 were waited for; matrix products, arithmetic and copies ran while one was open for 19% of the time, Pallas kernels for 12%

profile of v5, /device:TPU:0, one launch (start us, length us, event | category | flops | bytes accessed | tf_op | source)
XLA Modules:
  0.0 181.8 jit_solution(2696504855937098520)
XLA Ops:
  0.6 1.3 pad_add_fusion
  2.0 0.5 collective-permute-start
  2.5 5.8 %first.1 = (bf16[8,192,128]{2,1,0:T(8,128)(2,1)}, bf16[3072,128]{1,0:T(8,128)(2,1)}) custom-call(s32[1]{0:T(128)} %bitcast.core_ref, s32[8]{0:T(128)} %bitcast.57, s32[256]{0:T(256)} %bitcast.70, s32[8,256]{1,0:T(8,128)} %bitcast.55, s32[1,256]{1,0:T(1,128)} %labels_ref.1, f32[172,1,256]{2,1,0:T(1,128)} %bitcast.54, s32[24,128]{1,0:T(8,128)} %bitcast.41), custom_call_target="tpu_custom_call" | custom-call | tf_op jit(solution)/shard_map/first/pallas_call | solution.py:436
  8.3 7.2 %all-to-all-start = ((bf16[8,192,128]{2,1,0:T(8,128)(2,1)}), bf16[8,192,128]{2,1,0:T(8,128)(2,1)}, u32[]{:S(2)}, u32[]{:S(2)}) async-start(bf16[8,192,128]{2,1,0:T(8,128)(2,1)} %get-tuple-element.44), calls=%async_computation | async-start | bytes 786432 | tf_op jit(solution)/shard_map/all_to_all | solution.py:464
  15.5 1.0 fusion.14
  16.5 0.8 fusion.15
  17.2 0.7 maximum_select_fusion.10
  17.9 6.9 %add_convert_fusion.1 = (bf16[1536,1024]{1,0:T(8,128)(2,1)}, bf16[1536,1024]{1,0:T(8,128)(2,1)}) fusion(f32[1024]{0:T(1024)S(1)} %maximum_select_fusion.10, bf16[1536,128]{1,0:T(8,128)(2,1)S(1)} %copy-done, bf16[128,1024]{1,0:T(8,128)(2,1)} %param.19, bf16[128,512]{1,0:T(8,128)(2,1)S(1)} %get-tuple-element.86, bf16[128,512]{1,0:T(8,128)(2,1)S(1)} %get-tuple-element.85, ...), kind=kOutput, calls=%fused_computation.7 | convolution fusion | flops 431620096 | bytes 7213057 | tf_op jit(solution)/shard_map/dot_general | solution.py:486
  25.1 1.0 maximum_select_fusion
  26.1 0.7 copy.23
  26.8 1.2 concatenate.80.meta_ref
  28.0 0.8 copy-done.3
  28.8 3.8 %near.3.near_ref = f32[3072,128]{1,0:T(8,128)} custom-call(s32[128]{0:T(128)} %concatenate.80.meta_ref, s32[24,128]{1,0:T(8,128)} %bitcast.42, bf16[16,128,128]{2,1,0:T(8,128)(2,1)} %bitcast.37, bf16[16,128,128]{2,1,0:T(8,128)(2,1)} %copy-done.3, bf16[3072,128]{1,0:T(8,128)(2,1)} %get-tuple-element.38.rest_0_.rest_3_), custom_call_target="tpu_custom_call" | custom-call | flops 134217728 | bytes 4194304 | tf_op jit(solution)/shard_map/near/pallas_call | solution.py:466
  32.6 0.8 copy-done.2
  33.4 6.3 %far.3 = (bf16[8,192,128]{2,1,0:T(8,128)(2,1)}, bf16[3072,128]{1,0:T(8,128)(2,1)}) custom-call(s32[1]{0:T(128)} %bitcast.core_ref, s32[128]{0:T(128)} %concatenate.80.meta_ref, s32[8]{0:T(128)} %bitcast.58, s32[2048]{0:T(1024)} %bitcast.50, s32[24,128]{1,0:T(8,128)} %bitcast.43, bf16[8,192,128]{2,1,0:T(8,128)(2,1)} %all-to-all-done.recv_ref, ...), custom_call_target="tpu_custom_call" | custom-call | tf_op jit(solution)/shard_map/far/pallas_call | solution.py:506
  39.7 5.9 %all-to-all-start.1 = ((bf16[8,192,128]{2,1,0:T(8,128)(2,1)}), bf16[8,192,128]{2,1,0:T(8,128)(2,1)S(1)}, u32[]{:S(2)}, u32[]{:S(2)}) async-start(bf16[8,192,128]{2,1,0:T(8,128)(2,1)} %get-tuple-element.46), calls=%async_computation.1 | async-start | bytes 786432 | tf_op jit(solution)/shard_map/all_to_all | solution.py:464
  45.7 3.8 %near.4.near_ref = f32[3072,128]{1,0:T(8,128)} custom-call(s32[128]{0:T(128)} %concatenate.80.meta_ref, s32[24,128]{1,0:T(8,128)} %bitcast.44, bf16[16,128,128]{2,1,0:T(8,128)(2,1)} %bitcast.38, bf16[16,128,128]{2,1,0:T(8,128)(2,1)} %copy-done.3, bf16[3072,128]{1,0:T(8,128)(2,1)} %get-tuple-element.47.rest_0_.rest_2_), custom_call_target="tpu_custom_call" | custom-call | flops 134217728 | bytes 4194304 | tf_op jit(solution)/shard_map/near/pallas_call | solution.py:466
  49.5 7.3 %fusion.17 = f32[1536,1024]{1,0:T(8,128)} fusion(bf16[1536,1024]{1,0:T(8,128)(2,1)} %get-tuple-element.48, bf16[1024,1024]{1,0:T(8,128)(2,1)S(1)} %maximum_select_fusion), kind=kOutput, calls=%fused_computation.68 | convolution fusion | flops 3221225472 | bytes 11534336 | tf_op jit(solution)/shard_map/dot_general | solution.py:494
  56.8 0.7 copy-done.8
  57.5 6.3 %far.4 = (bf16[8,192,128]{2,1,0:T(8,128)(2,1)}, bf16[3072,128]{1,0:T(8,128)(2,1)}) custom-call(s32[1]{0:T(128)} %bitcast.core_ref, s32[128]{0:T(128)} %concatenate.80.meta_ref, s32[8]{0:T(128)} %bitcast.59, s32[2048]{0:T(1024)} %bitcast.51, s32[24,128]{1,0:T(8,128)} %bitcast.45, bf16[8,192,128]{2,1,0:T(8,128)(2,1)} %copy-done.8, ...), custom_call_target="tpu_custom_call" | custom-call | tf_op jit(solution)/shard_map/far/pallas_call | solution.py:506
  63.9 5.9 %all-to-all-start.2 = ((bf16[8,192,128]{2,1,0:T(8,128)(2,1)}), bf16[8,192,128]{2,1,0:T(8,128)(2,1)}, u32[]{:S(2)}, u32[]{:S(2)}) async-start(bf16[8,192,128]{2,1,0:T(8,128)(2,1)} %get-tuple-element.55), calls=%async_computation.2 | async-start | bytes 786432 | tf_op jit(solution)/shard_map/all_to_all | solution.py:464
  69.8 3.8 %near.5.near_ref = f32[3072,128]{1,0:T(8,128)} custom-call(s32[128]{0:T(128)} %concatenate.80.meta_ref, s32[24,128]{1,0:T(8,128)} %bitcast.46, bf16[16,128,128]{2,1,0:T(8,128)(2,1)} %bitcast.39, bf16[16,128,128]{2,1,0:T(8,128)(2,1)} %copy-done.3, bf16[3072,128]{1,0:T(8,128)(2,1)} %get-tuple-element.51.rest_0_.rest_1_), custom_call_target="tpu_custom_call" | custom-call | flops 134217728 | bytes 4194304 | tf_op jit(solution)/shard_map/near/pallas_call | solution.py:466
  73.7 6.8 %add_convert_fusion = (bf16[1536,1024]{1,0:T(8,128)(2,1)S(1)}, bf16[1536,1024]{1,0:T(8,128)(2,1)}) fusion(f32[1536,1024]{1,0:T(8,128)} %fusion.17, f32[1024]{0:T(1024)S(1)} %copy-done.11), kind=kLoop, calls=%fused_computation.2 | loop fusion | flops 28311552 | bytes 12587008 | tf_op jit(solution)/shard_map/convert_element_type | solution.py:322
  80.4 6.3 %far.5 = (bf16[8,192,128]{2,1,0:T(8,128)(2,1)}, bf16[3072,128]{1,0:T(8,128)(2,1)}) custom-call(s32[1]{0:T(128)} %bitcast.core_ref, s32[128]{0:T(128)} %concatenate.80.meta_ref, s32[8]{0:T(128)} %bitcast.60, s32[2048]{0:T(1024)} %bitcast.52, s32[24,128]{1,0:T(8,128)} %bitcast.47, bf16[8,192,128]{2,1,0:T(8,128)(2,1)} %all-to-all-done.2.recv_ref, ...), custom_call_target="tpu_custom_call" | custom-call | tf_op jit(solution)/shard_map/far/pallas_call | solution.py:506
  86.8 5.9 %all-to-all-start.3 = ((bf16[8,192,128]{2,1,0:T(8,128)(2,1)}), bf16[8,192,128]{2,1,0:T(8,128)(2,1)}, u32[]{:S(2)}, u32[]{:S(2)}) async-start(bf16[8,192,128]{2,1,0:T(8,128)(2,1)} %get-tuple-element.57), calls=%async_computation.3 | async-start | bytes 786432 | tf_op jit(solution)/shard_map/all_to_all | solution.py:464
  92.7 0.9 slice.115
  93.7 5.0 %near_last.1.near_ref = f32[3072,128]{1,0:T(8,128)} custom-call(s32[128]{0:T(128)} %concatenate.80.meta_ref, s32[24,128]{1,0:T(8,128)} %bitcast.48, bf16[16,128,128]{2,1,0:T(8,128)(2,1)} %bitcast.40, bf16[16,128,128]{2,1,0:T(8,128)(2,1)} %copy-done.3, bf16[3072,128]{1,0:T(8,128)(2,1)} %get-tuple-element.58.rest_0_, ...), custom_call_target="tpu_custom_call" | custom-call | flops 134217728 | bytes 4194304 | tf_op jit(solution)/shard_map/near_last/pallas_call | solution.py:466
  98.7 1.0 slice_select_fusion
  99.8 0.9 maximum_select_fusion.3
  100.7 1.6 all-to-all-done.3.recv_ref
  102.3 4.4 %far_last.1 = (bf16[1536,128]{1,0:T(8,128)(2,1)}, bf16[1536,128]{1,0:T(8,128)(2,1)}) custom-call(s32[1]{0:T(128)} %bitcast.core_ref, s32[128]{0:T(128)} %concatenate.80.meta_ref, s32[8]{0:T(128)} %bitcast.61, s32[2048]{0:T(1024)} %bitcast.53, s32[24,128]{1,0:T(8,128)} %bitcast.49, bf16[8,192,128]{2,1,0:T(8,128)(2,1)} %all-to-all-done.3.recv_ref, ...), custom_call_target="tpu_custom_call" | custom-call | tf_op jit(solution)/shard_map/far_last/pallas_call | solution.py:506
  106.8 1.1 constant_dynamic-update-slice_fusion.1
  107.8 1.0 collective-permute-done.3
  108.8 1.1 constant_dynamic-update-slice_fusion
  109.9 2.2 %fusion.10 = (bf16[1024]{0:T(1024)(128)(2,1)S(1)}, bf16[1536,1024]{1,0:T(8,128)(2,1)S(1)}) fusion(bf16[1536,1024]{1,0:T(8,128)(2,1)S(1)} %get-tuple-element.54, bf16[1536,256]{1,0:T(8,128)(2,1)S(1)} %constant_dynamic-update-slice_fusion, bf16[1024,256]{0,1:T(8,128)(2,1)} %maximum_select_fusion.3), kind=kOutput, calls=%fused_computation.61 | convolution fusion | flops 811596800 | bytes 7604224 | tf_op jit(solution)/shard_map/dot_general | solution.py:536
  112.2 0.6 convolution_convert_fusion.3
  112.8 1.4 copy-done.4
  114.1 3.6 %fusion.9 = (bf16[1024]{0:T(1024)(128)(2,1)S(1)}, f32[1536,1024]{1,0:T(8,128)S(1)}) fusion(bf16[1536,1024]{1,0:T(8,128)(2,1)S(1)} %copy-done.4, bf16[1536,1024]{1,0:T(8,128)(2,1)S(1)} %get-tuple-element.72, bf16[1024,1024]{1,0:T(8,128)(2,1)S(1)} %copy-done.7), kind=kOutput, calls=%fused_computation.60 | convolution fusion | flops 3227515904 | bytes 14682112 | tf_op jit(solution)/shard_map/dot_general | solution.py:545
  117.8 0.8 convolution_convert_fusion.4
  118.6 1.1 copy-done.5
  119.7 1.0 convolution_convert_fusion.2
  121.0 1.4 convolution_convert_fusion
  122.9 0.6 convolution_convert_fusion.5
  123.8 1.5 collective-permute-start.13
  125.3 1.4 add_convert_fusion.2
  126.8 1.0 collective-permute-start.5
  127.8 2.8 %collective-permute-done.13 = bf16[288,512]{1,0:T(8,128)(2,1)S(1)} collective-permute-done((bf16[288,512]{1,0:T(8,128)(2,1)S(1)}, bf16[288,512]{1,0:T(8,128)(2,1)S(1)}, u32[]{:S(2)}, u32[]{:S(2)}) %collective-permute-start.13) | collective-permute-done | bytes 294944 | tf_op jit(solution)/shard_map/ppermute | solution.py:335
  130.7 4.1 %collective-permute-done.5 = bf16[384,512]{1,0:T(8,128)(2,1)S(1)} collective-permute-done((bf16[384,512]{1,0:T(8,128)(2,1)S(1)}, bf16[384,512]{1,0:T(8,128)(2,1)S(1)}, u32[]{:S(2)}, u32[]{:S(2)}) %collective-permute-start.5) | collective-permute-done | bytes 393248 | tf_op jit(solution)/shard_map/ppermute | solution.py:335
  135.0 1.0 collective-permute-start.6
  136.0 1.2 collective-permute-start.14
  137.2 3.6 %collective-permute-done.6 = bf16[384,256]{1,0:T(8,128)(2,1)S(1)} collective-permute-done((bf16[384,256]{1,0:T(8,128)(2,1)S(1)}, bf16[384,256]{1,0:T(8,128)(2,1)S(1)}, u32[]{:S(2)}, u32[]{:S(2)}) %collective-permute-start.6) | collective-permute-done | bytes 196640 | tf_op jit(solution)/shard_map/ppermute | solution.py:335
  140.8 1.4 collective-permute-start.7
  142.4 5.1 %collective-permute-done.7 = bf16[384,128]{1,0:T(8,128)(2,1)S(1)} collective-permute-done((bf16[384,128]{1,0:T(8,128)(2,1)S(1)}, bf16[384,128]{1,0:T(8,128)(2,1)S(1)}, u32[]{:S(2)}, u32[]{:S(2)}) %collective-permute-start.7) | collective-permute-done | bytes 98336 | tf_op jit(solution)/shard_map/ppermute | solution.py:335
  147.5 0.5 collective-permute-start.8
  148.0 2.6 %collective-permute-start.15 = (bf16[288,128]{1,0:T(8,128)(2,1)S(1)}, bf16[288,128]{1,0:T(8,128)(2,1)S(1)}, u32[]{:S(2)}, u32[]{:S(2)}) collective-permute-start(bf16[288,128]{1,0:T(8,128)(2,1)S(1)} %broadcast_select_fusion.5), channel_id=1, source_target_pairs={{0,8},{1,9},{2,10},{3,11},{4,12},{5,13},{6,14},{7,15},{8,0},{9,1},... | collective-permute-start | bytes 221192 | tf_op jit(solution)/shard_map/ppermute | solution.py:335
  150.6 3.2 %collective-permute-done.8 = bf16[384,128]{1,0:T(8,128)(2,1)S(1)} collective-permute-done((bf16[384,128]{1,0:T(8,128)(2,1)S(1)}, bf16[384,128]{1,0:T(8,128)(2,1)S(1)}, u32[]{:S(2)}, u32[]{:S(2)}) %collective-permute-start.8) | collective-permute-done | bytes 98336 | tf_op jit(solution)/shard_map/ppermute | solution.py:335
  153.9 2.2 %collective-permute-done.15 = bf16[288,128]{1,0:T(8,128)(2,1)S(1)} collective-permute-done((bf16[288,128]{1,0:T(8,128)(2,1)S(1)}, bf16[288,128]{1,0:T(8,128)(2,1)S(1)}, u32[]{:S(2)}, u32[]{:S(2)}) %collective-permute-start.15) | collective-permute-done | bytes 73760 | tf_op jit(solution)/shard_map/ppermute | solution.py:335
  156.3 6.0 %collective-permute-done.9 = bf16[384,256]{1,0:T(8,128)(2,1)S(1)} collective-permute-done((bf16[384,256]{1,0:T(8,128)(2,1)S(1)}, bf16[384,256]{1,0:T(8,128)(2,1)S(1)}, u32[]{:S(2)}, u32[]{:S(2)}) %collective-permute-start.9) | collective-permute-done | bytes 196640 | tf_op jit(solution)/shard_map/ppermute | solution.py:335
  162.4 1.5 collective-permute-start.10
  164.0 5.2 %collective-permute-done.17 = bf16[288,256]{1,0:T(8,128)(2,1)S(1)} collective-permute-done((bf16[288,256]{1,0:T(8,128)(2,1)S(1)}, bf16[288,256]{1,0:T(8,128)(2,1)S(1)}, u32[]{:S(2)}, u32[]{:S(2)}) %collective-permute-start.17) | collective-permute-done | bytes 147488 | tf_op jit(solution)/shard_map/ppermute | solution.py:335
  169.4 1.5 collective-permute-start.18
  171.3 5.0 %collective-permute-done.18 = bf16[288,512]{1,0:T(8,128)(2,1)S(1)} collective-permute-done((bf16[288,512]{1,0:T(8,128)(2,1)S(1)}, bf16[288,512]{1,0:T(8,128)(2,1)S(1)}, u32[]{:S(2)}, u32[]{:S(2)}) %collective-permute-start.18) | collective-permute-done | bytes 294944 | tf_op jit(solution)/shard_map/ppermute | solution.py:335
  176.5 2.0 %collective-permute-done.19.theirs_two = bf16[288,1024]{1,0:T(8,128)(2,1)S(1)} collective-permute-done((bf16[288,1024]{1,0:T(8,128)(2,1)S(1)}, bf16[288,1024]{1,0:T(8,128)(2,1)S(1)}, u32[]{:S(2)}, u32[]{:S(2)}) %collective-permute-start.19) | collective-permute-done | bytes 589856 | tf_op jit(solution)/shard_map/ppermute | solution.py:326
  178.4 3.2 %finish.1 = (f32[128,1024]{1,0:T(8,128)}, f32[1,1024]{1,0:T(1,128)}, f32[1024,1024]{1,0:T(8,128)}, f32[1,1024]{1,0:T(1,128)}, f32[172,1024]{1,0:T(8,128)}) custom-call(s32[1]{0:T(128)} %bitcast.core_ref, bf16[384,1024]{1,0:T(8,128)(2,1)S(1)} %maximum_select_fusion.1.mine_one, bf16[384,1024]{1,0:T(8,128)(2,1)S(1)} %collective-permute-done.11.theirs_one, ...), custom_call_target="tpu_custom_call" | custom-call | tf_op jit(solution)/shard_map/finish/pallas_call | solution.py:573
  (81 shorter events, 3.2 us)
Async XLA Ops:
  0.6 17.3 %copy-start = (bf16[1536,128]{1,0:T(8,128)(2,1)S(1)}, bf16[1536,128]{1,0:T(8,128)(2,1)}, u32[]{:S(2)}) copy-start(bf16[1536,128]{1,0:T(8,128)(2,1)} %param.18) | copy-start | bytes 1179652
  2.0 24.8 %collective-permute-start = (s32[64]{0:T(128)}, s32[64]{0:T(128)}, u32[]{:S(2)}, u32[]{:S(2)}) collective-permute-start(s32[64]{0:T(128)} %pad_add_fusion), channel_id=1, source_target_pairs={{0,1},{1,0},{2,3},{3,2},{4,5},{5,4},{6,7},{7,6},{8,9},{9,8},{10,11... | collective-permute-start | bytes 776 | tf_op jit(solution)/shard_map/ppermute | solution.py:326
  2.4 25.5 %collective-permute-start.1 = (bf16[16,128,128]{2,1,0:T(8,128)(2,1)}, bf16[16,128,128]{2,1,0:T(8,128)(2,1)S(1)}, u32[]{:S(2)}, u32[]{:S(2)}) collective-permute-start(bf16[16,128,128]{2,1,0:T(8,128)(2,1)} %bitcast.36), channel_id=1, source_target_pairs={{0,1},{1,0},{2,3},{3,2},{4,5},{5,4},{6,7},{7,6},{8,9},{9,8},{10,11... | collective-permute-start | bytes 1572872 | tf_op jit(solution)/shard_map/ppermute | solution.py:326
  8.3 24.3 %all-to-all-start = ((bf16[8,192,128]{2,1,0:T(8,128)(2,1)}), bf16[8,192,128]{2,1,0:T(8,128)(2,1)}, u32[]{:S(2)}, u32[]{:S(2)}) async-start(bf16[8,192,128]{2,1,0:T(8,128)(2,1)} %get-tuple-element.44), calls=%async_computation | async-start | bytes 786432 | tf_op jit(solution)/shard_map/all_to_all | solution.py:464
  15.5 17.1 %collective-permute-start.2 = (bf16[16,128,128]{2,1,0:T(8,128)(2,1)}, bf16[16,128,128]{2,1,0:T(8,128)(2,1)S(1)}, u32[]{:S(2)}, u32[]{:S(2)}) collective-permute-start(bf16[16,128,128]{2,1,0:T(8,128)(2,1)} %bitcast.31), channel_id=1, source_target_pairs={{0,1},{1,0},{2,3},{3,2},{4,5},{5,4},{6,7},{7,6},{8,9},{9,8},{10,11... | collective-permute-start | bytes 1572872 | tf_op jit(solution)/shard_map/ppermute | solution.py:326
  17.9 6.9 %copy-start.1 = (bf16[1024,1024]{1,0:T(8,128)(2,1)S(1)}, bf16[1024,1024]{1,0:T(8,128)(2,1)}, u32[]{:S(2)}) copy-start(bf16[1024,1024]{1,0:T(8,128)(2,1)} %param.21) | copy-start | bytes 6291460
  25.0 1.1 copy-start.10
  25.0 1.7 copy-start.12
  25.0 1.7 copy-start.13
  25.0 1.7 copy-start.14
  25.1 1.7 copy-start.15
  26.1 30.7 %copy-start.6 = (bf16[1024,1024]{1,0:T(8,128)(2,1)}, bf16[1024,1024]{1,0:T(8,128)(2,1)S(1)}, u32[]{:S(2)}) copy-start(bf16[1024,1024]{1,0:T(8,128)(2,1)S(1)} %maximum_select_fusion) | copy-start | bytes 6291460
  28.0 0.8 copy-start.3
  32.6 0.8 copy-start.2
  39.7 17.0 %all-to-all-start.1 = ((bf16[8,192,128]{2,1,0:T(8,128)(2,1)}), bf16[8,192,128]{2,1,0:T(8,128)(2,1)S(1)}, u32[]{:S(2)}, u32[]{:S(2)}) async-start(bf16[8,192,128]{2,1,0:T(8,128)(2,1)} %get-tuple-element.46), calls=%async_computation.1 | async-start | bytes 786432 | tf_op jit(solution)/shard_map/all_to_all | solution.py:464
  56.8 16.9 %copy-start.11 = (f32[1024]{0:T(1024)S(1)}, f32[1024]{0:T(1024)}, u32[]{:S(2)}) copy-start(f32[1024]{0:T(1024)} %param.22) | copy-start | bytes 12292
  56.8 0.8 copy-start.8
  63.9 16.5 %all-to-all-start.2 = ((bf16[8,192,128]{2,1,0:T(8,128)(2,1)}), bf16[8,192,128]{2,1,0:T(8,128)(2,1)}, u32[]{:S(2)}, u32[]{:S(2)}) async-start(bf16[8,192,128]{2,1,0:T(8,128)(2,1)} %get-tuple-element.55), calls=%async_computation.2 | async-start | bytes 786432 | tf_op jit(solution)/shard_map/all_to_all | solution.py:464
  86.8 15.5 %all-to-all-start.3 = ((bf16[8,192,128]{2,1,0:T(8,128)(2,1)}), bf16[8,192,128]{2,1,0:T(8,128)(2,1)}, u32[]{:S(2)}, u32[]{:S(2)}) async-start(bf16[8,192,128]{2,1,0:T(8,128)(2,1)} %get-tuple-element.57), calls=%async_computation.3 | async-start | bytes 786432 | tf_op jit(solution)/shard_map/all_to_all | solution.py:464
  93.6 5.1 %copy-start.16 = (pred[128]{0:T(512)(128)(4,1)S(1)}, pred[128]{0:T(512)(128)(4,1)}, u32[]{:S(2)}) copy-start(pred[128]{0:T(512)(128)(4,1)} %constant.31.clone.1) | copy-start | bytes 388
  106.7 2.1 %collective-permute-start.3 = (bf16[1536,128]{1,0:T(8,128)(2,1)}, bf16[1536,128]{1,0:T(8,128)(2,1)}, u32[]{:S(2)}, u32[]{:S(2)}) collective-permute-start(bf16[1536,128]{1,0:T(8,128)(2,1)} %get-tuple-element.62), channel_id=1, source_target_pairs={{0,1},{1,0},{2,3},{3,2},{4,5},{5,4},{6,7},{7,6},{8,9},{9,8},{10,11... | collective-permute-start | bytes 1179656 | tf_op jit(solution)/shard_map/ppermute | solution.py:326
  109.9 2.3 %copy-start.9 = (bf16[1536,1024]{1,0:T(8,128)(2,1)S(1)}, bf16[1536,1024]{1,0:T(8,128)(2,1)}, u32[]{:S(2)}) copy-start(bf16[1536,1024]{1,0:T(8,128)(2,1)} %get-tuple-element.48) | copy-start | bytes 9437188
  109.9 2.9 %copy-start.7 = (bf16[1024,1024]{1,0:T(8,128)(2,1)S(1)}, bf16[1024,1024]{1,0:T(8,128)(2,1)}, u32[]{:S(2)}) copy-start(bf16[1024,1024]{1,0:T(8,128)(2,1)} %copy-done.6) | copy-start | bytes 6291460
  112.1 2.0 %copy-start.4 = (bf16[1536,1024]{1,0:T(8,128)(2,1)S(1)}, bf16[1536,1024]{1,0:T(8,128)(2,1)}, u32[]{:S(2)}) copy-start(bf16[1536,1024]{1,0:T(8,128)(2,1)} %get-tuple-element.64) | copy-start | bytes 9437188
  117.8 1.9 %copy-start.5 = (bf16[1536,1024]{1,0:T(8,128)(2,1)S(1)}, bf16[1536,1024]{1,0:T(8,128)(2,1)}, u32[]{:S(2)}) copy-start(bf16[1536,1024]{1,0:T(8,128)(2,1)} %get-tuple-element.65) | copy-start | bytes 9437188
  120.8 2.7 %collective-permute-start.12 = (bf16[288,1024]{1,0:T(8,128)(2,1)S(1)}, bf16[288,1024]{1,0:T(8,128)(2,1)S(1)}, u32[]{:S(2)}, u32[]{:S(2)}) collective-permute-start(bf16[288,1024]{1,0:T(8,128)(2,1)S(1)} %pad_maximum_fusion), channel_id=1, source_target_pairs={{0,1},{1,0},{2,3},{3,2},{4,5},{5,4},{6,7},{7,6},{8,9},{9,8},{10,11... | collective-permute-start | bytes 1769480 | tf_op jit(solution)/shard_map/ppermute | solution.py:326
  122.4 2.9 %collective-permute-start.4 = (bf16[384,1024]{1,0:T(8,128)(2,1)S(1)}, bf16[384,1024]{1,0:T(8,128)(2,1)S(1)}, u32[]{:S(2)}, u32[]{:S(2)}) collective-permute-start(bf16[384,1024]{1,0:T(8,128)(2,1)S(1)} %convolution_convert_fusion), channel_id=1, source_target_pairs={{0,1},{1,0},{2,3},{3,2},{4,5},{5,4},{6,7},{7,6},{8,9},{9,8},{10,11... | collective-permute-start | bytes 2359304 | tf_op jit(solution)/shard_map/ppermute | solution.py:326
  123.8 6.8 %collective-permute-start.13 = (bf16[288,512]{1,0:T(8,128)(2,1)S(1)}, bf16[288,512]{1,0:T(8,128)(2,1)S(1)}, u32[]{:S(2)}, u32[]{:S(2)}) collective-permute-start(bf16[288,512]{1,0:T(8,128)(2,1)S(1)} %broadcast_select_fusion.1), channel_id=1, source_target_pairs={{0,2},{1,5},{2,0},{3,7},{4,6},{5,1},{6,4},{7,3},{8,10},{9,13},{10,... | collective-permute-start | bytes 884744 | tf_op jit(solution)/shard_map/ppermute | solution.py:335
  126.8 8.0 %collective-permute-start.5 = (bf16[384,512]{1,0:T(8,128)(2,1)S(1)}, bf16[384,512]{1,0:T(8,128)(2,1)S(1)}, u32[]{:S(2)}, u32[]{:S(2)}) collective-permute-start(bf16[384,512]{1,0:T(8,128)(2,1)S(1)} %broadcast_select_fusion), channel_id=1, source_target_pairs={{0,2},{1,5},{2,0},{3,7},{4,6},{5,1},{6,4},{7,3},{8,10},{9,13},{10,... | collective-permute-start | bytes 1179656 | tf_op jit(solution)/shard_map/ppermute | solution.py:335
  135.0 5.7 %collective-permute-start.6 = (bf16[384,256]{1,0:T(8,128)(2,1)S(1)}, bf16[384,256]{1,0:T(8,128)(2,1)S(1)}, u32[]{:S(2)}, u32[]{:S(2)}) collective-permute-start(bf16[384,256]{1,0:T(8,128)(2,1)S(1)} %broadcast_select_fusion.2), channel_id=1, source_target_pairs={{0,4},{1,3},{2,6},{3,1},{4,0},{5,7},{6,2},{7,5},{8,12},{9,11},{10,... | collective-permute-start | bytes 589832 | tf_op jit(solution)/shard_map/ppermute | solution.py:335
  136.0 6.3 %collective-permute-start.14 = (bf16[288,256]{1,0:T(8,128)(2,1)S(1)}, bf16[288,256]{1,0:T(8,128)(2,1)S(1)}, u32[]{:S(2)}, u32[]{:S(2)}) collective-permute-start(bf16[288,256]{1,0:T(8,128)(2,1)S(1)} %broadcast_select_fusion.3), channel_id=1, source_target_pairs={{0,4},{1,3},{2,6},{3,1},{4,0},{5,7},{6,2},{7,5},{8,12},{9,11},{10,... | collective-permute-start | bytes 442376 | tf_op jit(solution)/shard_map/ppermute | solution.py:335
  140.8 6.6 %collective-permute-start.7 = (bf16[384,128]{1,0:T(8,128)(2,1)S(1)}, bf16[384,128]{1,0:T(8,128)(2,1)S(1)}, u32[]{:S(2)}, u32[]{:S(2)}) collective-permute-start(bf16[384,128]{1,0:T(8,128)(2,1)S(1)} %broadcast_select_fusion.4), channel_id=1, source_target_pairs={{0,8},{1,9},{2,10},{3,11},{4,12},{5,13},{6,14},{7,15},{8,0},{9,1},... | collective-permute-start | bytes 294920 | tf_op jit(solution)/shard_map/ppermute | solution.py:335
  147.5 6.2 %collective-permute-start.8 = (bf16[384,128]{1,0:T(8,128)(2,1)S(1)}, bf16[384,128]{1,0:T(8,128)(2,1)S(1)}, u32[]{:S(2)}, u32[]{:S(2)}) collective-permute-start(bf16[384,128]{1,0:T(8,128)(2,1)S(1)} %add_convert_fusion.8), channel_id=1, source_target_pairs={{0,8},{1,9},{2,10},{3,11},{4,12},{5,13},{6,14},{7,15},{8,0},{9,1},... | collective-permute-start | bytes 294920 | tf_op jit(solution)/shard_map/ppermute | solution.py:335
  148.0 8.1 %collective-permute-start.15 = (bf16[288,128]{1,0:T(8,128)(2,1)S(1)}, bf16[288,128]{1,0:T(8,128)(2,1)S(1)}, u32[]{:S(2)}, u32[]{:S(2)}) collective-permute-start(bf16[288,128]{1,0:T(8,128)(2,1)S(1)} %broadcast_select_fusion.5), channel_id=1, source_target_pairs={{0,8},{1,9},{2,10},{3,11},{4,12},{5,13},{6,14},{7,15},{8,0},{9,1},... | collective-permute-start | bytes 221192 | tf_op jit(solution)/shard_map/ppermute | solution.py:335
  153.8 8.5 %collective-permute-start.9 = (bf16[384,256]{1,0:T(8,128)(2,1)S(1)}, bf16[384,256]{1,0:T(8,128)(2,1)S(1)}, u32[]{:S(2)}, u32[]{:S(2)}) collective-permute-start(bf16[384,256]{1,0:T(8,128)(2,1)S(1)} %maximum_select_fusion.8), channel_id=1, source_target_pairs={{0,4},{1,3},{2,6},{3,1},{4,0},{5,7},{6,2},{7,5},{8,12},{9,11},{10,... | collective-permute-start | bytes 589832 | tf_op jit(solution)/shard_map/ppermute | solution.py:335
  156.1 7.8 %collective-permute-start.16 = (bf16[288,128]{1,0:T(8,128)(2,1)S(1)}, bf16[288,128]{1,0:T(8,128)(2,1)S(1)}, u32[]{:S(2)}, u32[]{:S(2)}) collective-permute-start(bf16[288,128]{1,0:T(8,128)(2,1)S(1)} %add_convert_fusion.9), channel_id=1, source_target_pairs={{0,8},{1,9},{2,10},{3,11},{4,12},{5,13},{6,14},{7,15},{8,0},{9,1},... | collective-permute-start | bytes 221192 | tf_op jit(solution)/shard_map/ppermute | solution.py:335
  162.4 8.6 %collective-permute-start.10 = (bf16[384,512]{1,0:T(8,128)(2,1)S(1)}, bf16[384,512]{1,0:T(8,128)(2,1)S(1)}, u32[]{:S(2)}, u32[]{:S(2)}) collective-permute-start(bf16[384,512]{1,0:T(8,128)(2,1)S(1)} %maximum_select_fusion.4), channel_id=1, source_target_pairs={{0,2},{1,5},{2,0},{3,7},{4,6},{5,1},{6,4},{7,3},{8,10},{9,13},{10,... | collective-permute-start | bytes 1179656 | tf_op jit(solution)/shard_map/ppermute | solution.py:335
  164.0 5.3 %collective-permute-start.17 = (bf16[288,256]{1,0:T(8,128)(2,1)S(1)}, bf16[288,256]{1,0:T(8,128)(2,1)S(1)}, u32[]{:S(2)}, u32[]{:S(2)}) collective-permute-start(bf16[288,256]{1,0:T(8,128)(2,1)S(1)} %maximum_select_fusion.9), channel_id=1, source_target_pairs={{0,4},{1,3},{2,6},{3,1},{4,0},{5,7},{6,2},{7,5},{8,12},{9,11},{10,... | collective-permute-start | bytes 442376 | tf_op jit(solution)/shard_map/ppermute | solution.py:335
  169.4 6.8 %collective-permute-start.18 = (bf16[288,512]{1,0:T(8,128)(2,1)S(1)}, bf16[288,512]{1,0:T(8,128)(2,1)S(1)}, u32[]{:S(2)}, u32[]{:S(2)}) collective-permute-start(bf16[288,512]{1,0:T(8,128)(2,1)S(1)} %maximum_select_fusion.5), channel_id=1, source_target_pairs={{0,2},{1,5},{2,0},{3,7},{4,6},{5,1},{6,4},{7,3},{8,10},{9,13},{10,... | collective-permute-start | bytes 884744 | tf_op jit(solution)/shard_map/ppermute | solution.py:335
  171.2 7.3 %collective-permute-start.11 = (bf16[384,1024]{1,0:T(8,128)(2,1)S(1)}, bf16[384,1024]{1,0:T(8,128)(2,1)S(1)}, u32[]{:S(2)}, u32[]{:S(2)}) collective-permute-start(bf16[384,1024]{1,0:T(8,128)(2,1)S(1)} %maximum_select_fusion.1.mine_one), channel_id=1, source_target_pairs={{0,1},{1,0},{2,3},{3,2},{4,5},{5,4},{6,7},{7,6},{8,9},{9,8},{10,11... | collective-permute-start | bytes 2359304 | tf_op jit(solution)/shard_map/ppermute | solution.py:326
  176.4 2.1 %collective-permute-start.19 = (bf16[288,1024]{1,0:T(8,128)(2,1)S(1)}, bf16[288,1024]{1,0:T(8,128)(2,1)S(1)}, u32[]{:S(2)}, u32[]{:S(2)}) collective-permute-start(bf16[288,1024]{1,0:T(8,128)(2,1)S(1)} %maximum_select_fusion.2.mine_two), channel_id=1, source_target_pairs={{0,1},{1,0},{2,3},{3,2},{4,5},{5,4},{6,7},{7,6},{8,9},{9,8},{10,11... | collective-permute-start | bytes 1769480 | tf_op jit(solution)/shard_map/ppermute | solution.py:326

commit v6 on v5

--- a/solution.py
+++ b/solution.py
@@ -197,49 +197,58 @@
     count = own_ref.shape[0]
     values = 1 if not last else HOPS
     value_refs, rest = rest[:values], rest[values:]
-    near_ref, value_vs, own_v, other_v, acc_ref, sems = rest
+    near_ref, value_vs, own_v, other_v, acc_ref, near_v, sems = rest
     copies = [pltpu.make_async_copy(value_refs[i], value_vs.at[i], sems.at[i]) for i in range(values)]
     copies.append(pltpu.make_async_copy(own_ref, own_v, sems.at[HOPS]))
     copies.append(pltpu.make_async_copy(other_ref, other_v, sems.at[HOPS + 1]))
     for copy in copies:
         copy.start()
     blocks, block = degree_ref.shape
-    if not last:
-        acc_ref[...] = jnp.zeros_like(acc_ref)
+    acc_ref[...] = jnp.zeros_like(acc_ref)
     for copy in copies:
         copy.wait()
-    if last:
-        columns = root_columns(degree_ref, lambda degree: (teleport / (1.0 - teleport)) * degree)
-        for b in range(blocks):
-            at = slice(b * block, (b + 1) * block)
+    add_tiles(acc_ref, value_vs.at[0], (own_v, other_v), meta_ref, 0, count, stride)
+    columns = root_columns(degree_ref, lambda degree: (teleport / (1.0 - teleport)) * degree) if last else None
+    outs = []
+    parts = 4 if blocks % 4 == 0 else 1
+    for b in range(blocks):
+        at = slice(b * block, (b + 1) * block)
+        near = acc_ref[at, :]
+        if last:
             total = value_vs[0, at, :].astype(f32)
             for i in range(1, values):
                 total = total + value_vs[i, at, :].astype(f32)
-            acc_ref[at, :] = over_lanes(columns, b) * total
-    add_tiles(acc_ref, value_vs.at[0], (own_v, other_v), meta_ref, 0, count, stride)
-    out = pltpu.make_async_copy(acc_ref, near_ref, sems.at[HOPS + 2])
-    out.start()
-    out.wait()
+            near = near + over_lanes(columns, b) * total
+        near_v[at, :] = near.astype(bf16)
+        if (b + 1) % (blocks // parts) == 0:
+            part = (b + 1) // (blocks // parts) - 1
+            span = blocks // parts * block
+            here = pl.ds(part * span, span)
+            outs.append(pltpu.make_async_copy(near_v.at[here], near_ref.at[here], sems.at[HOPS + 2 + part]))
+            outs[-1].start()
+    for out in outs:
+        out.wait()
 
 
 def far_kernel(slots, class_half, base, stride, last, core_ref, meta_ref, count_ref, idx_ref, degree_ref, recv_ref,
                own_ref, other_ref, near_ref, *rest):
     if last:
-        keep_ref, send_ref, recv_v, own_v, other_v, rows_ref, acc_ref, own_sems = rest
+        keep_ref, send_ref, recv_v, own_v, other_v, near_v, rows_ref, acc_ref, own_sems = rest
     else:
-        (out_ref, value_ref, recv_v, own_v, other_v, rows_ref, acc_ref, stage_ref, packed_ref, value_v, sems,
+        (out_ref, value_ref, recv_v, own_v, other_v, near_v, rows_ref, acc_ref, stage_ref, packed_ref, value_v, sems,
          own_sems) = rest
     count, block = own_ref.shape[0], own_ref.shape[1]
     blocks = degree_ref.shape[0]
     copies = [
         pltpu.make_async_copy(recv_ref, recv_v, own_sems.at[0]),
-        pltpu.make_async_copy(near_ref, acc_ref, own_sems.at[1]),
-        pltpu.make_async_copy(own_ref, own_v, own_sems.at[2]),
-        pltpu.make_async_copy(other_ref, other_v, own_sems.at[3]),
+        pltpu.make_async_copy(own_ref, own_v, own_sems.at[1]),
+        pltpu.make_async_copy(other_ref, other_v, own_sems.at[2]),
+        pltpu.make_async_copy(near_ref, near_v, own_sems.at[3]),
     ]
     for copy in copies:
         copy.start()
     roots = root_columns(degree_ref, lax.rsqrt)
+    acc_ref[...] = jnp.zeros_like(acc_ref)
     copies[0].wait()
     unpack_rows(recv_v, rows_ref, slots, class_half)
     for copy in copies[1:]:
@@ -254,14 +263,14 @@
             outs = []
             for b_at in (b, half_blocks + b):
                 at = slice(b_at * block, (b_at + 1) * block)
-                outs.append((rate * over_lanes(roots, b_at) * acc_ref[at, :]).astype(bf16))
+                outs.append((rate * over_lanes(roots, b_at) * (acc_ref[at, :] + near_v[at, :].astype(f32))).astype(bf16))
             keep_ref[to, :] = jnp.where(core == 0, outs[0], outs[1])
             send_ref[to, :] = jnp.where(core == 0, outs[1], outs[0])
         return
     for b in range(blocks):
         at = slice(b * block, (b + 1) * block)
         root = over_lanes(roots, b)
-        scaled = (rate * root * root) * acc_ref[at, :]
+        scaled = (rate * root * root) * (acc_ref[at, :] + near_v[at, :].astype(f32))
         value_v[at, :] = scaled.astype(bf16)
         acc_ref[at, :] = scaled
     value_copy = pltpu.make_async_copy(value_v, value_ref, own_sems.at[4])
@@ -349,27 +358,27 @@
     return lax.slice_in_dim(x, 0, half, axis=axis), lax.slice_in_dim(x, half, 2 * half, axis=axis)
 
 
-def sum_over_domains(x):
+def halving_plan(shape):
     me, core = lax.axis_index("dom"), lax.axis_index("col")
-    plan = []
-    width, depth = x.shape[1], x.shape[0]
-    for steps in halving_steps():
-        if width > LANES:
-            plan.append((steps, 1))
-            width //= 2
-        else:
-            plan.append((steps, 0))
-            depth //= 2
-    current = x
-    bits = []
-    for (a, b), axis in plan:
-        up = jnp.where(core == 0, me & a, me & b) != 0
-        bits.append(up)
-        low, high = split(current, axis)
-        got = exchange(jnp.where(up, low, high), a, b)
-        keep = jnp.where(up, high, low)
+    plan, width = [], shape[1]
+    for a, b in halving_steps():
+        plan.append((a, b, 1 if width > LANES else 0, jnp.where(core == 0, me & a, me & b) != 0))
+        width = width // 2 if width > LANES else width
+    return plan
+
+
+def halves_of(x, step):
+    low, high = split(x, step[2])
+    return jnp.where(step[3], high, low), jnp.where(step[3], low, high)
+
+
+def sum_over_domains(keep, send, plan):
+    for i, (a, b, axis, up) in enumerate(plan):
+        got = exchange(send, a, b)
         current = (keep.astype(f32) + got.astype(f32)).astype(bf16)
-    for ((a, b), axis), up in zip(plan[::-1], bits[::-1]):
+        if i + 1 < len(plan):
+            keep, send = halves_of(current, plan[i + 1])
+    for a, b, axis, up in plan[::-1]:
         got = exchange(current, a, b)
         current = jnp.where(
             up,
@@ -412,12 +421,7 @@
     packed = packed_rows(slots, class_half)
     local_count, halo_count = local_tiles.shape[2], halo_tiles.shape[2]
 
-    meta_own = jnp.concatenate([local_target[0, 0], local_source[0, 0], halo_target[0, 0], halo_block[0, 0]])
-    stride = meta_own.shape[0]
-    meta = jnp.concatenate([meta_own, swap_cores(meta_own)])
-    own_local, own_halo = local_tiles[0, 0], halo_tiles[0, 0]
-    other_local, other_halo = swap_cores(own_local), swap_cores(own_halo)
-
+    stride = 2 * (local_count + halo_count)
     degree_blocks = degree.reshape(blocks, block)
     out_type = jax.ShapeDtypeStruct((peers, packed, LANES), bf16)
     value_type = jax.ShapeDtypeStruct((rows, LANES), bf16)
@@ -451,7 +455,14 @@
         compiler_params=params(),
         name="first",
     )(core_arg, counts, batch_nodes[0], first_rows, labels, jnp.transpose(batch_logits, (2, 0, 1)), degree_blocks)
-    idx = lax.optimization_barrier((send_rows, value))[0].reshape(-1)
+    tied_rows, *lists, _ = lax.optimization_barrier(
+        (send_rows, local_target, local_source, halo_target, halo_block, value)
+    )
+    idx = tied_rows.reshape(-1)
+    meta_own = jnp.concatenate([part[0, 0] for part in lists])
+    meta = jnp.concatenate([meta_own, swap_cores(meta_own)])
+    own_local, own_halo = local_tiles[0, 0], halo_tiles[0, 0]
+    other_local, other_halo = swap_cores(own_local), swap_cores(own_halo)
 
     def turn(array, axis):
         low, high = split(array, axis)
@@ -465,7 +476,7 @@
         near_values = values if last else values[:1]
         near = pl.pallas_call(
             functools.partial(near_kernel, stride, last),
-            out_shape=jax.ShapeDtypeStruct((rows, LANES), f32),
+            out_shape=value_type,
             in_specs=[smem(), vmem(), hbm(), hbm()] + [hbm()] * len(near_values),
             out_specs=hbm(),
             scratch_shapes=[
@@ -473,7 +484,8 @@
                 pltpu.VMEM((local_count, block, block), bf16),
                 pltpu.VMEM((local_count, block, block), bf16),
                 pltpu.VMEM((rows, LANES), f32),
-                pltpu.SemaphoreType.DMA((HOPS + 3,)),
+                pltpu.VMEM((rows, LANES), bf16),
+                pltpu.SemaphoreType.DMA((HOPS + 6,)),
             ],
             compiler_params=params(),
             cost_estimate=pl.CostEstimate(
@@ -482,20 +494,22 @@
             name="near_last" if last else "near",
         )(meta, degree_blocks, own_local, other_local, *near_values)
         if hop == 0:
-            x, first_w, second_w, _ = lax.optimization_barrier((features, first_weight, second_weight, value))
-            pre_first = jnp.dot(x, turn(first_w, 1), preferred_element_type=f32) + turn(first_bias, 0)
-            hidden_first, slope_first = gelu_parts(pre_first)
-            second_turned = turn(second_w, 0)
-            near, hidden_first, slope_first, second_turned = lax.optimization_barrier(
-                (near, hidden_first, slope_first, second_turned)
+            first_w, first_b, second_w, _ = lax.optimization_barrier(
+                (first_weight, first_bias, second_weight, value)
+            )
+            first_turned, bias_turned, second_turned = turn(first_w, 1), turn(first_b, 0), turn(second_w, 0)
+            near, first_turned, bias_turned, second_turned = lax.optimization_barrier(
+                (near, first_turned, bias_turned, second_turned)
             )
         if hop == 1:
+            x, _ = lax.optimization_barrier((features, value))
+            pre_first = jnp.dot(x, first_turned, preferred_element_type=f32) + bias_turned
+            hidden_first, slope_first = gelu_parts(pre_first)
+            near, hidden_first, slope_first = lax.optimization_barrier((near, hidden_first, slope_first))
+        if hop == 2:
             tied, _ = lax.optimization_barrier((hidden_first, value))
-            pre_second = jnp.dot(tied, second_turned, preferred_element_type=f32)
-            near, pre_second = lax.optimization_barrier((near, pre_second))
-        if hop == 2:
-            tied, _ = lax.optimization_barrier((pre_second, value))
-            hidden_second, slope_second = gelu_parts(tied + second_bias)
+            pre_second = jnp.dot(tied, second_turned, preferred_element_type=f32) + second_bias
+            hidden_second, slope_second = gelu_parts(pre_second)
             near, hidden_second, slope_second = lax.optimization_barrier((near, hidden_second, slope_second))
         if last:
             tied, _ = lax.optimization_barrier((third_weight, value))
@@ -512,6 +526,7 @@
                 pltpu.VMEM((peers, packed, LANES), bf16),
                 pltpu.VMEM((halo_count, block, block), bf16),
                 pltpu.VMEM((halo_count, block, block), bf16),
+                pltpu.VMEM((rows, LANES), bf16),
                 pltpu.VMEM((peers * slots, LANES), bf16),
                 acc,
             ]
@@ -539,6 +554,9 @@
     send_lead = contract(hidden_first[:, half : half + lead], second_delta)
     got_lead = swap_cores(send_lead)
     keep_lead = contract(hidden_first[:, :lead], second_delta)
+    lead_plan = halving_plan(keep_lead.shape)
+    lead_keep, lead_send = halves_of((keep_lead.astype(f32) + got_lead.astype(f32)).astype(bf16), lead_plan[0])
+    lead_send, lead_keep, second_delta, delta = lax.optimization_barrier((lead_send, lead_keep, second_delta, delta))
     send_tail = contract(hidden_first[:, half + lead :], second_delta)
     keep_tail = contract(hidden_first[:, lead:half], second_delta)
     third_grad = contract(delta, hidden_second)
@@ -567,8 +585,10 @@
     keep_rest = bundle(0, keep_tail, third_grad[:LANES], jnp.where(is_first, low_bias, high_bias))
     send_rest = bundle(1, send_tail, third_grad[LANES:], jnp.where(is_first, high_bias, low_bias))
     got_rest = swap_cores(send_rest)
-    mine_lead = sum_over_domains((keep_lead.astype(f32) + got_lead.astype(f32)).astype(bf16))
-    mine_rest = sum_over_domains((keep_rest.astype(f32) + got_rest.astype(f32)).astype(bf16))
+    mine_lead = sum_over_domains(lead_keep, lead_send, lead_plan)
+    rest_plan = halving_plan(keep_rest.shape)
+    rest = (keep_rest.astype(f32) + got_rest.astype(f32)).astype(bf16)
+    mine_rest = sum_over_domains(*halves_of(rest, rest_plan[0]), rest_plan)
     theirs_lead, theirs_rest = swap_cores(mine_lead), swap_cores(mine_rest)
     first_out, first_bias_out, second_out, second_bias_out, third_out = pl.pallas_call(
         functools.partial(finish_kernel, class_half),

time: 183 us -> 187 us (1.022)
  matrix products: 25.8 us -> 34.7 us
  other arithmetic: 13.4 us -> 6.95 us
  waiting for transfers between devices: 41.7 us -> 46.1 us
  local copies, waits for them, and re-layouts: 11.8 us -> 9.77 us
    all_to_all x4, waiting for transfers between devices: 1.58 us -> 8.64 us  [shards(): landed = lax.all_to_all(out, 'dom', split_axis=0, concat_axis=0, tiled=True)]
    convert_element_type x2 -> x1, other arithmetic: 6.98 us -> 0.22 us  [shards(): rest = (keep_rest.astype(f32) + got_rest.astype(f32)).astype(bf16)]
    dot_general x6, matrix products: 5.8 us -> 11.6 us  [contract(): lax.dot_general(a, b, (((0,), (0,)), ((), ())), preferred_element_type=f32)]
    ppermute x12, waiting for transfers between devices: 37.2 us -> 32.2 us  [exchange(): return lax.ppermute(x, ('dom', 'col'), pairs)]
    all_to_all x4, starting transfers between devices: 25 us -> 22.6 us  [shards(): landed = lax.all_to_all(out, 'dom', split_axis=0, concat_axis=0, tiled=True)]
    ppermute x8, waiting for transfers between devices: 2.98 us -> 5.32 us  [swap_cores(): return lax.ppermute(x, 'col', [(0, 1), (1, 0)])]
    ppermute x12, starting transfers between devices: 12.5 us -> 14.7 us  [exchange(): return lax.ppermute(x, ('dom', 'col'), pairs)]
    dot_general x2, matrix products: 14.2 us -> 16.2 us  [the longest x1 10.5 us: shards(): jnp.dot(tied, second_turned, preferred_element_type=f32) + second_bias]
  transfers between devices with their start and end apart: 24 -> 24, of which waited for: 13 -> 13; matrix products, arithmetic and copies ran while one was open for 19% -> 19% of each run, Pallas kernels for 12% -> 11%
where the time goes in v6:
time: 187 us; the launch traced here: 186 us
  Pallas kernels  48.3 us (26%)
  waiting for transfers between devices  46.1 us (25%)
  starting transfers between devices  38.2 us (20%)
  matrix products  34.7 us (19%)
  local copies, waits for them, and re-layouts  9.77 us (5%)
  other arithmetic  6.95 us (4%)
    ppermute x12, waiting for transfers between devices, exchange(): return lax.ppermute(x, ('dom', 'col'), pairs)  32.2 us
    pallas_call x4, Pallas kernels, shards(): pl.pallas_call(functools.partial(far_kernel, slots, class_half, 2 * local...  24 us
    all_to_all x4, starting transfers between devices, shards(): landed = lax.all_to_all(out, 'dom', split_axis=0, concat_axis=0, tiled=True)  22.6 us
    pallas_call x4, Pallas kernels, shards(): pl.pallas_call(functools.partial(near_kernel, stride, last), out_shape=va...  15.5 us
    ppermute x12, starting transfers between devices, exchange(): return lax.ppermute(x, ('dom', 'col'), pairs)  14.7 us
    dot_general x6, matrix products, contract(): lax.dot_general(a, b, (((0,), (0,)), ((), ())), preferred_element_type=f32)  11.6 us
    dot_general x1, matrix products, shards(): jnp.dot(tied, second_turned, preferred_element_type=f32) + second_bias  10.5 us
    all_to_all x4, waiting for transfers between devices, shards(): landed = lax.all_to_all(out, 'dom', split_axis=0, concat_axis=0, tiled=True)  8.64 us
  transfers between devices with their start and end apart: 24, of which 13 were waited for; matrix products, arithmetic and copies ran while one was open for 19% of the time, Pallas kernels for 11%

profile of v6, /device:TPU:0, one launch (start us, length us, event | category | flops | bytes accessed | tf_op | source)
XLA Modules:
  0.0 185.5 jit_solution(10995954538702141893)
XLA Ops:
  0.6 0.5 collective-permute-start.1
  1.2 5.6 %first.1 = (bf16[8,192,128]{2,1,0:T(8,128)(2,1)}, bf16[3072,128]{1,0:T(8,128)(2,1)}) custom-call(s32[1]{0:T(128)} %bitcast.core_ref, s32[8]{0:T(128)} %bitcast.58, s32[256]{0:T(256)} %bitcast.71, s32[8,256]{1,0:T(8,128)} %bitcast.56, s32[1,256]{1,0:T(1,128)} %labels_ref.1, f32[172,1,256]{2,1,0:T(1,128)} %bitcast.55, s32[24,128]{1,0:T(8,128)} %bitcast.42), custom_call_target="tpu_custom_call" | custom-call | tf_op jit(solution)/shard_map/first/pallas_call | solution.py:440
  6.9 7.2 %all-to-all-start = ((bf16[8,192,128]{2,1,0:T(8,128)(2,1)}), bf16[8,192,128]{2,1,0:T(8,128)(2,1)}, u32[]{:S(2)}, u32[]{:S(2)}) async-start(bf16[8,192,128]{2,1,0:T(8,128)(2,1)} %get-tuple-element.53), calls=%async_computation | async-start | bytes 786432 | tf_op jit(solution)/shard_map/all_to_all | solution.py:475
  14.1 1.3 pad_add_fusion
  15.4 1.0 fusion.9
  16.4 1.7 fusion.6
  18.2 0.8 maximum_select_fusion.6
  19.0 2.3 %maximum_select_fusion = bf16[1024,1024]{1,0:T(8,128)(2,1)} fusion(bf16[1024,1024]{1,0:T(8,128)(2,1)S(1)} %copy-done.2, bf16[512,1024]{1,0:T(8,128)(2,1)S(1)} %get-tuple-element.96, bf16[512,1024]{1,0:T(8,128)(2,1)S(1)} %get-tuple-element.95, pred[]{:T(512)S(6)} %eq.2), kind=kLoop, calls=%fused_computation.12 | loop fusion | flops 5242880 | bytes 6291457 | tf_op jit(solution)/shard_map/jit(_where)/select_n | solution.py:469
  21.3 0.6 copy.23
  21.9 1.3 concatenate.80.meta_ref
  23.2 0.8 copy-done.3
  24.0 3.6 %near.3.near_ref = bf16[3072,128]{1,0:T(8,128)(2,1)} custom-call(s32[128]{0:T(128)} %concatenate.80.meta_ref, s32[24,128]{1,0:T(8,128)} %bitcast.43, bf16[16,128,128]{2,1,0:T(8,128)(2,1)} %bitcast.38, bf16[16,128,128]{2,1,0:T(8,128)(2,1)} %copy-done.3, bf16[3072,128]{1,0:T(8,128)(2,1)} %get-tuple-element.47.rest_0_.rest_3_), custom_call_target="tpu_custom_call" | custom-call | flops 134217728 | bytes 4194304 | tf_op jit(solution)/shard_map/near/pallas_call | solution.py:477
  27.6 0.8 copy-done.1
  28.4 6.3 %far.3 = (bf16[8,192,128]{2,1,0:T(8,128)(2,1)}, bf16[3072,128]{1,0:T(8,128)(2,1)}) custom-call(s32[1]{0:T(128)} %bitcast.core_ref, s32[128]{0:T(128)} %concatenate.80.meta_ref, s32[8]{0:T(128)} %bitcast.59, s32[2048]{0:T(1024)} %bitcast.51, s32[24,128]{1,0:T(8,128)} %bitcast.44, bf16[8,192,128]{2,1,0:T(8,128)(2,1)} %all-to-all-done.recv_ref, ...), custom_call_target="tpu_custom_call" | custom-call | tf_op jit(solution)/shard_map/far/pallas_call | solution.py:520
  34.8 5.9 %all-to-all-start.1 = ((bf16[8,192,128]{2,1,0:T(8,128)(2,1)}), bf16[8,192,128]{2,1,0:T(8,128)(2,1)S(1)}, u32[]{:S(2)}, u32[]{:S(2)}) async-start(bf16[8,192,128]{2,1,0:T(8,128)(2,1)} %get-tuple-element.63), calls=%async_computation.1 | async-start | bytes 786432 | tf_op jit(solution)/shard_map/all_to_all | solution.py:475
  40.6 3.6 %near.4.near_ref = bf16[3072,128]{1,0:T(8,128)(2,1)} custom-call(s32[128]{0:T(128)} %concatenate.80.meta_ref, s32[24,128]{1,0:T(8,128)} %bitcast.45, bf16[16,128,128]{2,1,0:T(8,128)(2,1)} %bitcast.39, bf16[16,128,128]{2,1,0:T(8,128)(2,1)} %copy-done.3, bf16[3072,128]{1,0:T(8,128)(2,1)} %get-tuple-element.58.rest_0_.rest_2_), custom_call_target="tpu_custom_call" | custom-call | flops 134217728 | bytes 4194304 | tf_op jit(solution)/shard_map/near/pallas_call | solution.py:477
  44.3 5.7 %add_convert_fusion.1 = (bf16[1536,1024]{1,0:T(8,128)(2,1)}, bf16[1536,1024]{1,0:T(8,128)(2,1)}) fusion(f32[1024]{0:T(1024)S(1)} %maximum_select_fusion.9, bf16[1536,128]{1,0:T(8,128)(2,1)S(1)} %copy-done, bf16[128,1024]{1,0:T(8,128)(2,1)S(1)} %copy-done.15), kind=kOutput, calls=%fused_computation.7 | convolution fusion | flops 430964736 | bytes 6950912 | tf_op jit(solution)/shard_map/dot_general | solution.py:506
  49.9 3.0 %all-to-all-done.1.recv_ref = bf16[8,192,128]{2,1,0:T(8,128)(2,1)S(1)} async-done(((bf16[8,192,128]{2,1,0:T(8,128)(2,1)}), bf16[8,192,128]{2,1,0:T(8,128)(2,1)S(1)}, u32[]{:S(2)}, u32[]{:S(2)}) %all-to-all-start.1) | async-done | bytes 393248 | tf_op jit(solution)/shard_map/all_to_all | solution.py:475
  53.0 0.7 copy-done.11
  53.7 6.3 %far.4 = (bf16[8,192,128]{2,1,0:T(8,128)(2,1)}, bf16[3072,128]{1,0:T(8,128)(2,1)}) custom-call(s32[1]{0:T(128)} %bitcast.core_ref, s32[128]{0:T(128)} %concatenate.80.meta_ref, s32[8]{0:T(128)} %bitcast.60, s32[2048]{0:T(1024)} %bitcast.52, s32[24,128]{1,0:T(8,128)} %bitcast.46, bf16[8,192,128]{2,1,0:T(8,128)(2,1)} %copy-done.11, ...), custom_call_target="tpu_custom_call" | custom-call | tf_op jit(solution)/shard_map/far/pallas_call | solution.py:520
  60.0 3.6 %all-to-all-start.2 = ((bf16[8,192,128]{2,1,0:T(8,128)(2,1)}), bf16[8,192,128]{2,1,0:T(8,128)(2,1)S(1)}, u32[]{:S(2)}, u32[]{:S(2)}) async-start(bf16[8,192,128]{2,1,0:T(8,128)(2,1)} %get-tuple-element.69), calls=%async_computation.2 | async-start | bytes 786432 | tf_op jit(solution)/shard_map/all_to_all | solution.py:475
  63.7 3.7 %near.5.near_ref = bf16[3072,128]{1,0:T(8,128)(2,1)} custom-call(s32[128]{0:T(128)} %concatenate.80.meta_ref, s32[24,128]{1,0:T(8,128)} %bitcast.47, bf16[16,128,128]{2,1,0:T(8,128)(2,1)} %bitcast.40, bf16[16,128,128]{2,1,0:T(8,128)(2,1)} %copy-done.3, bf16[3072,128]{1,0:T(8,128)(2,1)} %get-tuple-element.65.rest_0_.rest_1_), custom_call_target="tpu_custom_call" | custom-call | flops 134217728 | bytes 4194304 | tf_op jit(solution)/shard_map/near/pallas_call | solution.py:477
  67.4 10.5 %add_convert_fusion = (bf16[1536,1024]{1,0:T(8,128)(2,1)}, bf16[1536,1024]{1,0:T(8,128)(2,1)}) fusion(f32[1024]{0:T(1024)S(1)} %copy-done.22, bf16[1536,1024]{1,0:T(8,128)(2,1)} %get-tuple-element.66, bf16[1024,1024]{1,0:T(8,128)(2,1)S(1)} %copy-done.5), kind=kOutput, calls=%fused_computation.2 | convolution fusion | flops 3249537024 | bytes 11538432 | tf_op jit(solution)/shard_map/dot_general | solution.py:511
  77.9 0.7 copy-done.12
  78.7 6.3 %far.5 = (bf16[8,192,128]{2,1,0:T(8,128)(2,1)}, bf16[3072,128]{1,0:T(8,128)(2,1)}) custom-call(s32[1]{0:T(128)} %bitcast.core_ref, s32[128]{0:T(128)} %concatenate.80.meta_ref, s32[8]{0:T(128)} %bitcast.61, s32[2048]{0:T(1024)} %bitcast.53, s32[24,128]{1,0:T(8,128)} %bitcast.48, bf16[8,192,128]{2,1,0:T(8,128)(2,1)} %copy-done.12, ...), custom_call_target="tpu_custom_call" | custom-call | tf_op jit(solution)/shard_map/far/pallas_call | solution.py:520
  85.0 5.8 %all-to-all-start.3 = ((bf16[8,192,128]{2,1,0:T(8,128)(2,1)}), bf16[8,192,128]{2,1,0:T(8,128)(2,1)S(1)}, u32[]{:S(2)}, u32[]{:S(2)}) async-start(bf16[8,192,128]{2,1,0:T(8,128)(2,1)} %get-tuple-element.71), calls=%async_computation.3 | async-start | bytes 786432 | tf_op jit(solution)/shard_map/all_to_all | solution.py:475
  90.9 4.7 %near_last.1.near_ref = bf16[3072,128]{1,0:T(8,128)(2,1)} custom-call(s32[128]{0:T(128)} %concatenate.80.meta_ref, s32[24,128]{1,0:T(8,128)} %bitcast.49, bf16[16,128,128]{2,1,0:T(8,128)(2,1)} %bitcast.41, bf16[16,128,128]{2,1,0:T(8,128)(2,1)} %copy-done.3, bf16[3072,128]{1,0:T(8,128)(2,1)} %get-tuple-element.72.rest_0_, ...), custom_call_target="tpu_custom_call" | custom-call | flops 134217728 | bytes 4194304 | tf_op jit(solution)/shard_map/near_last/pallas_call | solution.py:477
  95.7 0.9 maximum_select_fusion.3
  96.6 5.6 %all-to-all-done.3.recv_ref = bf16[8,192,128]{2,1,0:T(8,128)(2,1)S(1)} async-done(((bf16[8,192,128]{2,1,0:T(8,128)(2,1)}), bf16[8,192,128]{2,1,0:T(8,128)(2,1)S(1)}, u32[]{:S(2)}, u32[]{:S(2)}) %all-to-all-start.3) | async-done | bytes 393248 | tf_op jit(solution)/shard_map/all_to_all | solution.py:475
  102.2 0.8 copy-done.10
  103.0 5.0 %far_last.1 = (bf16[1536,128]{1,0:T(8,128)(2,1)}, bf16[1536,128]{1,0:T(8,128)(2,1)}) custom-call(s32[1]{0:T(128)} %bitcast.core_ref, s32[128]{0:T(128)} %concatenate.80.meta_ref, s32[8]{0:T(128)} %bitcast.62, s32[2048]{0:T(1024)} %bitcast.54, s32[24,128]{1,0:T(8,128)} %bitcast.50, bf16[8,192,128]{2,1,0:T(8,128)(2,1)} %copy-done.10, ...), custom_call_target="tpu_custom_call" | custom-call | tf_op jit(solution)/shard_map/far_last/pallas_call | solution.py:520
  108.0 1.1 constant_dynamic-update-slice_fusion.1
  109.1 0.9 collective-permute-done.3
  110.1 3.2 %fusion.5 = (bf16[1024]{0:T(1024)(128)(2,1)S(1)}, bf16[1536,1024]{1,0:T(8,128)(2,1)S(1)}) fusion(bf16[1536,1024]{1,0:T(8,128)(2,1)} %get-tuple-element.68, bf16[1536,256]{1,0:T(8,128)(2,1)S(1)} %constant_dynamic-update-slice_fusion, bf16[1024,256]{0,1:T(8,128)(2,1)S(1)} %copy-done.7), kind=kOutput, calls=%fused_computation.57 | convolution fusion | flops 811596800 | bytes 7604224 | tf_op jit(solution)/shard_map/dot_general | solution.py:551
  113.3 3.6 %convolution_convert_fusion = bf16[384,1024]{1,0:T(8,128)(2,1)} fusion(bf16[1536,1024]{1,0:T(8,128)(2,1)S(1)} %get-tuple-element.80, bf16[1536,1024]{1,0:T(8,128)(2,1)} %get-tuple-element.66), kind=kOutput, calls=%fused_computation.14 | convolution fusion | flops 1208352768 | bytes 5111808 | tf_op jit(solution)/shard_map/dot_general | solution.py:547
  117.0 2.5 %collective-permute-done.4 = bf16[384,1024]{1,0:T(8,128)(2,1)} collective-permute-done((bf16[384,1024]{1,0:T(8,128)(2,1)}, bf16[384,1024]{1,0:T(8,128)(2,1)}, u32[]{:S(2)}, u32[]{:S(2)}) %collective-permute-start.4) | collective-permute-done | bytes 786464 | tf_op jit(solution)/shard_map/ppermute | solution.py:335
  119.5 2.9 %add_convert_fusion.2 = bf16[384,1024]{1,0:T(8,128)(2,1)S(1)} fusion(bf16[384,1024]{1,0:T(8,128)(2,1)} %collective-permute-done.4, bf16[1536,1024]{1,0:T(8,128)(2,1)S(1)} %get-tuple-element.80, bf16[1536,1024]{1,0:T(8,128)(2,1)} %get-tuple-element.66), kind=kOutput, calls=%fused_computation.13 | convolution fusion | flops 1209925632 | bytes 5898240 | tf_op jit(solution)/shard_map/dot_general | solution.py:547
  122.5 1.0 convolution_convert_fusion.2
  123.5 1.8 convolution_convert_fusion.3
  125.3 1.5 collective-permute-start.5
  126.8 3.7 %fusion.4 = (bf16[1024]{0:T(1024)(128)(2,1)S(1)}, f32[1536,1024]{1,0:T(8,128)S(1)}) fusion(bf16[1536,1024]{1,0:T(8,128)(2,1)S(1)} %copy-done.4, bf16[1536,1024]{1,0:T(8,128)(2,1)S(1)} %get-tuple-element.80, bf16[1024,1024]{1,0:T(8,128)(2,1)S(1)} %copy-done.6), kind=kOutput, calls=%fused_computation.56 | convolution fusion | flops 3227515904 | bytes 14682112 | tf_op jit(solution)/shard_map/dot_general | solution.py:563
  130.5 0.8 convolution_convert_fusion.4
  131.5 1.6 convolution_convert_fusion.5
  133.3 1.0 collective-permute-start.6
  134.2 0.2 add_convert_fusion.3
  134.5 1.0 collective-permute-start.13
  135.5 5.4 %collective-permute-done.6 = bf16[384,256]{1,0:T(8,128)(2,1)S(1)} collective-permute-done((bf16[384,256]{1,0:T(8,128)(2,1)S(1)}, bf16[384,256]{1,0:T(8,128)(2,1)S(1)}, u32[]{:S(2)}, u32[]{:S(2)}) %collective-permute-start.6) | collective-permute-done | bytes 196640 | tf_op jit(solution)/shard_map/ppermute | solution.py:344
  141.0 1.0 collective-permute-start.7
  142.2 1.3 collective-permute-start.14
  143.5 5.1 %collective-permute-done.7 = bf16[384,128]{1,0:T(8,128)(2,1)S(1)} collective-permute-done((bf16[384,128]{1,0:T(8,128)(2,1)S(1)}, bf16[384,128]{1,0:T(8,128)(2,1)S(1)}, u32[]{:S(2)}, u32[]{:S(2)}) %collective-permute-start.7) | collective-permute-done | bytes 98336 | tf_op jit(solution)/shard_map/ppermute | solution.py:344
  148.8 3.0 %collective-permute-start.15 = (bf16[288,128]{1,0:T(8,128)(2,1)S(1)}, bf16[288,128]{1,0:T(8,128)(2,1)S(1)}, u32[]{:S(2)}, u32[]{:S(2)}) collective-permute-start(bf16[288,128]{1,0:T(8,128)(2,1)S(1)} %broadcast_select_fusion.6), channel_id=1, source_target_pairs={{0,8},{1,9},{2,10},{3,11},{4,12},{5,13},{6,14},{7,15},{8,0},{9,1},... | collective-permute-start | bytes 221192 | tf_op jit(solution)/shard_map/ppermute | solution.py:344
  151.8 2.5 %collective-permute-done.8 = bf16[384,128]{1,0:T(8,128)(2,1)S(1)} collective-permute-done((bf16[384,128]{1,0:T(8,128)(2,1)S(1)}, bf16[384,128]{1,0:T(8,128)(2,1)S(1)}, u32[]{:S(2)}, u32[]{:S(2)}) %collective-permute-start.8) | collective-permute-done | bytes 98336 | tf_op jit(solution)/shard_map/ppermute | solution.py:344
  154.4 2.2 %collective-permute-done.15 = bf16[288,128]{1,0:T(8,128)(2,1)S(1)} collective-permute-done((bf16[288,128]{1,0:T(8,128)(2,1)S(1)}, bf16[288,128]{1,0:T(8,128)(2,1)S(1)}, u32[]{:S(2)}, u32[]{:S(2)}) %collective-permute-start.15) | collective-permute-done | bytes 73760 | tf_op jit(solution)/shard_map/ppermute | solution.py:344
  156.7 0.9 collective-permute-start.16
  157.6 5.4 %collective-permute-done.9 = bf16[384,256]{1,0:T(8,128)(2,1)S(1)} collective-permute-done((bf16[384,256]{1,0:T(8,128)(2,1)S(1)}, bf16[384,256]{1,0:T(8,128)(2,1)S(1)}, u32[]{:S(2)}, u32[]{:S(2)}) %collective-permute-start.9) | collective-permute-done | bytes 196640 | tf_op jit(solution)/shard_map/ppermute | solution.py:344
  163.0 4.7 %collective-permute-start.10 = (bf16[384,512]{1,0:T(8,128)(2,1)S(1)}, bf16[384,512]{1,0:T(8,128)(2,1)S(1)}, u32[]{:S(2)}, u32[]{:S(2)}) collective-permute-start(bf16[384,512]{1,0:T(8,128)(2,1)S(1)} %maximum_select_fusion.4), channel_id=1, source_target_pairs={{0,2},{1,5},{2,0},{3,7},{4,6},{5,1},{6,4},{7,3},{8,10},{9,13},{10,... | collective-permute-start | bytes 1179656 | tf_op jit(solution)/shard_map/ppermute | solution.py:344
  167.9 5.1 %collective-permute-done.17 = bf16[288,256]{1,0:T(8,128)(2,1)S(1)} collective-permute-done((bf16[288,256]{1,0:T(8,128)(2,1)S(1)}, bf16[288,256]{1,0:T(8,128)(2,1)S(1)}, u32[]{:S(2)}, u32[]{:S(2)}) %collective-permute-start.17) | collective-permute-done | bytes 147488 | tf_op jit(solution)/shard_map/ppermute | solution.py:344
  173.0 0.1 maximum_select_fusion.5
  173.2 0.3 collective-permute-done.10
  173.5 0.2 maximum_select_fusion.1.mine_one
  173.8 6.1 %collective-permute-done.18 = bf16[288,512]{1,0:T(8,128)(2,1)S(1)} collective-permute-done((bf16[288,512]{1,0:T(8,128)(2,1)S(1)}, bf16[288,512]{1,0:T(8,128)(2,1)S(1)}, u32[]{:S(2)}, u32[]{:S(2)}) %collective-permute-start.18) | collective-permute-done | bytes 294944 | tf_op jit(solution)/shard_map/ppermute | solution.py:344
  179.9 0.2 maximum_select_fusion.2.mine_two
  180.2 2.0 %collective-permute-done.19.theirs_two = bf16[288,1024]{1,0:T(8,128)(2,1)S(1)} collective-permute-done((bf16[288,1024]{1,0:T(8,128)(2,1)S(1)}, bf16[288,1024]{1,0:T(8,128)(2,1)S(1)}, u32[]{:S(2)}, u32[]{:S(2)}) %collective-permute-start.19) | collective-permute-done | bytes 589856 | tf_op jit(solution)/shard_map/ppermute | solution.py:335
  182.2 3.2 %finish.1 = (f32[128,1024]{1,0:T(8,128)}, f32[1,1024]{1,0:T(1,128)}, f32[1024,1024]{1,0:T(8,128)}, f32[1,1024]{1,0:T(1,128)}, f32[172,1024]{1,0:T(8,128)}) custom-call(s32[1]{0:T(128)} %bitcast.core_ref, bf16[384,1024]{1,0:T(8,128)(2,1)S(1)} %maximum_select_fusion.1.mine_one, bf16[384,1024]{1,0:T(8,128)(2,1)S(1)} %collective-permute-done.11.theirs_one, ...), custom_call_target="tpu_custom_call" | custom-call | tf_op jit(solution)/shard_map/finish/pallas_call | solution.py:593
  (96 shorter events, 2.1 us)
Async XLA Ops:
  0.6 43.6 %copy-start = (bf16[1536,128]{1,0:T(8,128)(2,1)S(1)}, bf16[1536,128]{1,0:T(8,128)(2,1)}, u32[]{:S(2)}) copy-start(bf16[1536,128]{1,0:T(8,128)(2,1)} %param.18) | copy-start | bytes 1179652
  0.6 22.5 %collective-permute-start.1 = (bf16[16,128,128]{2,1,0:T(8,128)(2,1)}, bf16[16,128,128]{2,1,0:T(8,128)(2,1)S(1)}, u32[]{:S(2)}, u32[]{:S(2)}) collective-permute-start(bf16[16,128,128]{2,1,0:T(8,128)(2,1)} %bitcast.37), channel_id=1, source_target_pairs={{0,1},{1,0},{2,3},{3,2},{4,5},{5,4},{6,7},{7,6},{8,9},{9,8},{10,11... | collective-permute-start | bytes 1572872 | tf_op jit(solution)/shard_map/ppermute | solution.py:335
  1.2 26.4 %collective-permute-start.2 = (bf16[16,128,128]{2,1,0:T(8,128)(2,1)}, bf16[16,128,128]{2,1,0:T(8,128)(2,1)S(1)}, u32[]{:S(2)}, u32[]{:S(2)}) collective-permute-start(bf16[16,128,128]{2,1,0:T(8,128)(2,1)} %bitcast.32), channel_id=1, source_target_pairs={{0,1},{1,0},{2,3},{3,2},{4,5},{5,4},{6,7},{7,6},{8,9},{9,8},{10,11... | collective-permute-start | bytes 1572872 | tf_op jit(solution)/shard_map/ppermute | solution.py:335
  6.8 12.1 %copy-start.17 = (f32[1024]{0:T(1024)S(1)}, f32[1024]{0:T(1024)}, u32[]{:S(2)}) copy-start(f32[1024]{0:T(1024)} %param.20) | copy-start | bytes 12292
  6.9 12.1 %copy-start.2 = (bf16[1024,1024]{1,0:T(8,128)(2,1)S(1)}, bf16[1024,1024]{1,0:T(8,128)(2,1)}, u32[]{:S(2)}) copy-start(bf16[1024,1024]{1,0:T(8,128)(2,1)} %param.21) | copy-start | bytes 6291460
  6.9 20.7 %all-to-all-start = ((bf16[8,192,128]{2,1,0:T(8,128)(2,1)}), bf16[8,192,128]{2,1,0:T(8,128)(2,1)}, u32[]{:S(2)}, u32[]{:S(2)}) async-start(bf16[8,192,128]{2,1,0:T(8,128)(2,1)} %get-tuple-element.53), calls=%async_computation | async-start | bytes 786432 | tf_op jit(solution)/shard_map/all_to_all | solution.py:475
  15.4 6.5 %collective-permute-start = (s32[64]{0:T(128)}, s32[64]{0:T(128)}, u32[]{:S(2)}, u32[]{:S(2)}) collective-permute-start(s32[64]{0:T(128)} %pad_add_fusion), channel_id=1, source_target_pairs={{0,1},{1,0},{2,3},{3,2},{4,5},{5,4},{6,7},{7,6},{8,9},{9,8},{10,11... | collective-permute-start | bytes 776 | tf_op jit(solution)/shard_map/ppermute | solution.py:335
  15.4 2.8 %copy-start.13 = (bf16[128,1024]{1,0:T(8,128)(2,1)S(1)}, bf16[128,1024]{1,0:T(8,128)(2,1)}, u32[]{:S(2)}) copy-start(bf16[128,1024]{1,0:T(8,128)(2,1)} %param.19) | copy-start | bytes 786436
  18.9 2.4 %copy-start.16 = (s32[1,8,256]{2,1,0:T(8,128)S(1)}, s32[1,8,256]{2,1,0:T(8,128)}, u32[]{:S(2)}) copy-start(s32[1,8,256]{2,1,0:T(8,128)} %param.30) | copy-start | bytes 24580
  18.9 3.0 %copy-start.18 = (s32[1,1,16]{2,1,0:T(1,128)S(1)}, s32[1,1,16]{2,1,0:T(1,128)}, u32[]{:S(2)}) copy-start(s32[1,1,16]{2,1,0:T(1,128)} %param.25) | copy-start | bytes 196
  18.9 2.9 %copy-start.19 = (s32[1,1,16]{2,1,0:T(1,128)S(1)}, s32[1,1,16]{2,1,0:T(1,128)}, u32[]{:S(2)}) copy-start(s32[1,1,16]{2,1,0:T(1,128)} %param.26) | copy-start | bytes 196
  19.0 2.9 %copy-start.20 = (s32[1,1,16]{2,1,0:T(1,128)S(1)}, s32[1,1,16]{2,1,0:T(1,128)}, u32[]{:S(2)}) copy-start(s32[1,1,16]{2,1,0:T(1,128)} %param.28) | copy-start | bytes 196
  23.2 0.8 copy-start.3
  27.6 16.7 %copy-start.15 = (bf16[128,1024]{1,0:T(8,128)(2,1)S(1)}, bf16[128,1024]{1,0:T(8,128)(2,1)}, u32[]{:S(2)}) copy-start(bf16[128,1024]{1,0:T(8,128)(2,1)} %maximum_select_fusion.6) | copy-start | bytes 786436
  27.6 0.8 copy-start.1
  34.8 18.2 %all-to-all-start.1 = ((bf16[8,192,128]{2,1,0:T(8,128)(2,1)}), bf16[8,192,128]{2,1,0:T(8,128)(2,1)S(1)}, u32[]{:S(2)}, u32[]{:S(2)}) async-start(bf16[8,192,128]{2,1,0:T(8,128)(2,1)} %get-tuple-element.63), calls=%async_computation.1 | async-start | bytes 786432 | tf_op jit(solution)/shard_map/all_to_all | solution.py:475
  49.9 17.4 %copy-start.5 = (bf16[1024,1024]{1,0:T(8,128)(2,1)S(1)}, bf16[1024,1024]{1,0:T(8,128)(2,1)}, u32[]{:S(2)}) copy-start(bf16[1024,1024]{1,0:T(8,128)(2,1)} %maximum_select_fusion) | copy-start | bytes 6291460
  49.9 17.4 %copy-start.22 = (f32[1024]{0:T(1024)S(1)}, f32[1024]{0:T(1024)}, u32[]{:S(2)}) copy-start(f32[1024]{0:T(1024)} %param.22) | copy-start | bytes 12292
  53.0 0.7 copy-start.11
  60.0 17.9 %all-to-all-start.2 = ((bf16[8,192,128]{2,1,0:T(8,128)(2,1)}), bf16[8,192,128]{2,1,0:T(8,128)(2,1)S(1)}, u32[]{:S(2)}, u32[]{:S(2)}) async-start(bf16[8,192,128]{2,1,0:T(8,128)(2,1)} %get-tuple-element.69), calls=%async_computation.2 | async-start | bytes 786432 | tf_op jit(solution)/shard_map/all_to_all | solution.py:475
  77.9 13.0 %slice-start = ((bf16[1024,172]{0,1:T(8,128)(2,1)}), bf16[1024,84]{0,1:T(8,128)(2,1)S(1)}, s32[]{:S(2)}) async-start(bf16[1024,172]{0,1:T(8,128)(2,1)} %param.23), calls=%async_computation.4 | async-start | bytes 360448 | tf_op jit(solution)/shard_map/slice | solution.py:517
  77.9 0.7 copy-start.12
  85.0 10.6 %copy-start.14 = (bf16[1024,172]{0,1:T(8,128)(2,1)S(1)}, bf16[1024,172]{0,1:T(8,128)(2,1)}, u32[]{:S(2)}) copy-start(bf16[1024,172]{0,1:T(8,128)(2,1)} %param.23) | copy-start | bytes 1056772
  85.0 10.6 %copy-start.21 = (pred[128]{0:T(512)(128)(4,1)S(1)}, pred[128]{0:T(512)(128)(4,1)}, u32[]{:S(2)}) copy-start(pred[128]{0:T(512)(128)(4,1)} %constant.31.clone.1) | copy-start | bytes 388
  85.0 17.2 %all-to-all-start.3 = ((bf16[8,192,128]{2,1,0:T(8,128)(2,1)}), bf16[8,192,128]{2,1,0:T(8,128)(2,1)S(1)}, u32[]{:S(2)}, u32[]{:S(2)}) async-start(bf16[8,192,128]{2,1,0:T(8,128)(2,1)} %get-tuple-element.71), calls=%async_computation.3 | async-start | bytes 786432 | tf_op jit(solution)/shard_map/all_to_all | solution.py:475
  102.2 0.8 copy-start.10
  103.0 7.1 %copy-start.7 = (bf16[1024,256]{0,1:T(8,128)(2,1)S(1)}, bf16[1024,256]{0,1:T(8,128)(2,1)}, u32[]{:S(2)}) copy-start(bf16[1024,256]{0,1:T(8,128)(2,1)} %maximum_select_fusion.3) | copy-start | bytes 1572868
  108.0 2.0 %collective-permute-start.3 = (bf16[1536,128]{1,0:T(8,128)(2,1)}, bf16[1536,128]{1,0:T(8,128)(2,1)S(1)}, u32[]{:S(2)}, u32[]{:S(2)}) collective-permute-start(bf16[1536,128]{1,0:T(8,128)(2,1)} %get-tuple-element.76), channel_id=1, source_target_pairs={{0,1},{1,0},{2,3},{3,2},{4,5},{5,4},{6,7},{7,6},{8,9},{9,8},{10,11... | collective-permute-start | bytes 1179656 | tf_op jit(solution)/shard_map/ppermute | solution.py:335
  110.1 3.2 %copy-start.8 = (bf16[1536,256]{1,0:T(8,128)(2,1)}, bf16[1536,256]{1,0:T(8,128)(2,1)S(1)}, u32[]{:S(2)}) copy-start(bf16[1536,256]{1,0:T(8,128)(2,1)S(1)} %constant_dynamic-update-slice_fusion) | copy-start | bytes 2359300
  116.8 2.6 %collective-permute-start.4 = (bf16[384,1024]{1,0:T(8,128)(2,1)}, bf16[384,1024]{1,0:T(8,128)(2,1)}, u32[]{:S(2)}, u32[]{:S(2)}) collective-permute-start(bf16[384,1024]{1,0:T(8,128)(2,1)} %convolution_convert_fusion), channel_id=1, source_target_pairs={{0,1},{1,0},{2,3},{3,2},{4,5},{5,4},{6,7},{7,6},{8,9},{9,8},{10,11... | collective-permute-start | bytes 2359304 | tf_op jit(solution)/shard_map/ppermute | solution.py:335
  117.0 5.5 %copy-start.9 = (bf16[1536,256]{1,0:T(8,128)(2,1)S(1)}, bf16[1536,256]{1,0:T(8,128)(2,1)}, u32[]{:S(2)}) copy-start(bf16[1536,256]{1,0:T(8,128)(2,1)} %copy-done.8) | copy-start | bytes 2359300
  117.0 5.5 %copy-start.23 = (bf16[1536,1024]{1,0:T(8,128)(2,1)S(1)}, bf16[1536,1024]{1,0:T(8,128)(2,1)}, u32[]{:S(2)}) copy-start(bf16[1536,1024]{1,0:T(8,128)(2,1)} %get-tuple-element.83) | copy-start | bytes 9437188
  122.5 4.3 %copy-start.6 = (bf16[1024,1024]{1,0:T(8,128)(2,1)S(1)}, bf16[1024,1024]{1,0:T(8,128)(2,1)}, u32[]{:S(2)}) copy-start(bf16[1024,1024]{1,0:T(8,128)(2,1)} %maximum_select_fusion) | copy-start | bytes 6291460
  123.5 3.3 %copy-start.4 = (bf16[1536,1024]{1,0:T(8,128)(2,1)S(1)}, bf16[1536,1024]{1,0:T(8,128)(2,1)}, u32[]{:S(2)}) copy-start(bf16[1536,1024]{1,0:T(8,128)(2,1)} %get-tuple-element.81) | copy-start | bytes 9437188
  125.3 7.8 %collective-permute-start.5 = (bf16[384,512]{1,0:T(8,128)(2,1)S(1)}, bf16[384,512]{1,0:T(8,128)(2,1)S(1)}, u32[]{:S(2)}, u32[]{:S(2)}) collective-permute-start(bf16[384,512]{1,0:T(8,128)(2,1)S(1)} %get-tuple-element.79), channel_id=1, source_target_pairs={{0,2},{1,5},{2,0},{3,7},{4,6},{5,1},{6,4},{7,3},{8,10},{9,13},{10,... | collective-permute-start | bytes 1179656 | tf_op jit(solution)/shard_map/ppermute | solution.py:344
  131.4 2.8 %collective-permute-start.12 = (bf16[288,1024]{1,0:T(8,128)(2,1)S(1)}, bf16[288,1024]{1,0:T(8,128)(2,1)S(1)}, u32[]{:S(2)}, u32[]{:S(2)}) collective-permute-start(bf16[288,1024]{1,0:T(8,128)(2,1)S(1)} %pad_maximum_fusion), channel_id=1, source_target_pairs={{0,1},{1,0},{2,3},{3,2},{4,5},{5,4},{6,7},{7,6},{8,9},{9,8},{10,11... | collective-permute-start | bytes 1769480 | tf_op jit(solution)/shard_map/ppermute | solution.py:335
  133.3 7.7 %collective-permute-start.6 = (bf16[384,256]{1,0:T(8,128)(2,1)S(1)}, bf16[384,256]{1,0:T(8,128)(2,1)S(1)}, u32[]{:S(2)}, u32[]{:S(2)}) collective-permute-start(bf16[384,256]{1,0:T(8,128)(2,1)S(1)} %broadcast_select_fusion.3), channel_id=1, source_target_pairs={{0,4},{1,3},{2,6},{3,1},{4,0},{5,7},{6,2},{7,5},{8,12},{9,11},{10,... | collective-permute-start | bytes 589832 | tf_op jit(solution)/shard_map/ppermute | solution.py:344
  134.5 7.5 %collective-permute-start.13 = (bf16[288,512]{1,0:T(8,128)(2,1)S(1)}, bf16[288,512]{1,0:T(8,128)(2,1)S(1)}, u32[]{:S(2)}, u32[]{:S(2)}) collective-permute-start(bf16[288,512]{1,0:T(8,128)(2,1)S(1)} %broadcast_select_fusion.2), channel_id=1, source_target_pairs={{0,2},{1,5},{2,0},{3,7},{4,6},{5,1},{6,4},{7,3},{8,10},{9,13},{10,... | collective-permute-start | bytes 884744 | tf_op jit(solution)/shard_map/ppermute | solution.py:344
  141.0 7.6 %collective-permute-start.7 = (bf16[384,128]{1,0:T(8,128)(2,1)S(1)}, bf16[384,128]{1,0:T(8,128)(2,1)S(1)}, u32[]{:S(2)}, u32[]{:S(2)}) collective-permute-start(bf16[384,128]{1,0:T(8,128)(2,1)S(1)} %broadcast_select_fusion.5), channel_id=1, source_target_pairs={{0,8},{1,9},{2,10},{3,11},{4,12},{5,13},{6,14},{7,15},{8,0},{9,1},... | collective-permute-start | bytes 294920 | tf_op jit(solution)/shard_map/ppermute | solution.py:344
  142.2 6.6 %collective-permute-start.14 = (bf16[288,256]{1,0:T(8,128)(2,1)S(1)}, bf16[288,256]{1,0:T(8,128)(2,1)S(1)}, u32[]{:S(2)}, u32[]{:S(2)}) collective-permute-start(bf16[288,256]{1,0:T(8,128)(2,1)S(1)} %broadcast_select_fusion.4), channel_id=1, source_target_pairs={{0,4},{1,3},{2,6},{3,1},{4,0},{5,7},{6,2},{7,5},{8,12},{9,11},{10,... | collective-permute-start | bytes 442376 | tf_op jit(solution)/shard_map/ppermute | solution.py:344
  148.6 5.6 %collective-permute-start.8 = (bf16[384,128]{1,0:T(8,128)(2,1)S(1)}, bf16[384,128]{1,0:T(8,128)(2,1)S(1)}, u32[]{:S(2)}, u32[]{:S(2)}) collective-permute-start(bf16[384,128]{1,0:T(8,128)(2,1)S(1)} %add_convert_fusion.8), channel_id=1, source_target_pairs={{0,8},{1,9},{2,10},{3,11},{4,12},{5,13},{6,14},{7,15},{8,0},{9,1},... | collective-permute-start | bytes 294920 | tf_op jit(solution)/shard_map/ppermute | solution.py:344
  148.8 7.8 %collective-permute-start.15 = (bf16[288,128]{1,0:T(8,128)(2,1)S(1)}, bf16[288,128]{1,0:T(8,128)(2,1)S(1)}, u32[]{:S(2)}, u32[]{:S(2)}) collective-permute-start(bf16[288,128]{1,0:T(8,128)(2,1)S(1)} %broadcast_select_fusion.6), channel_id=1, source_target_pairs={{0,8},{1,9},{2,10},{3,11},{4,12},{5,13},{6,14},{7,15},{8,0},{9,1},... | collective-permute-start | bytes 221192 | tf_op jit(solution)/shard_map/ppermute | solution.py:344
  154.3 8.6 %collective-permute-start.9 = (bf16[384,256]{1,0:T(8,128)(2,1)S(1)}, bf16[384,256]{1,0:T(8,128)(2,1)S(1)}, u32[]{:S(2)}, u32[]{:S(2)}) collective-permute-start(bf16[384,256]{1,0:T(8,128)(2,1)S(1)} %maximum_select_fusion.7), channel_id=1, source_target_pairs={{0,4},{1,3},{2,6},{3,1},{4,0},{5,7},{6,2},{7,5},{8,12},{9,11},{10,... | collective-permute-start | bytes 589832 | tf_op jit(solution)/shard_map/ppermute | solution.py:344
  156.7 11.1 %collective-permute-start.16 = (bf16[288,128]{1,0:T(8,128)(2,1)S(1)}, bf16[288,128]{1,0:T(8,128)(2,1)S(1)}, u32[]{:S(2)}, u32[]{:S(2)}) collective-permute-start(bf16[288,128]{1,0:T(8,128)(2,1)S(1)} %add_convert_fusion.9), channel_id=1, source_target_pairs={{0,8},{1,9},{2,10},{3,11},{4,12},{5,13},{6,14},{7,15},{8,0},{9,1},... | collective-permute-start | bytes 221192 | tf_op jit(solution)/shard_map/ppermute | solution.py:344
  163.0 10.5 %collective-permute-start.10 = (bf16[384,512]{1,0:T(8,128)(2,1)S(1)}, bf16[384,512]{1,0:T(8,128)(2,1)S(1)}, u32[]{:S(2)}, u32[]{:S(2)}) collective-permute-start(bf16[384,512]{1,0:T(8,128)(2,1)S(1)} %maximum_select_fusion.4), channel_id=1, source_target_pairs={{0,2},{1,5},{2,0},{3,7},{4,6},{5,1},{6,4},{7,3},{8,10},{9,13},{10,... | collective-permute-start | bytes 1179656 | tf_op jit(solution)/shard_map/ppermute | solution.py:344
  167.8 5.2 %collective-permute-start.17 = (bf16[288,256]{1,0:T(8,128)(2,1)S(1)}, bf16[288,256]{1,0:T(8,128)(2,1)S(1)}, u32[]{:S(2)}, u32[]{:S(2)}) collective-permute-start(bf16[288,256]{1,0:T(8,128)(2,1)S(1)} %maximum_select_fusion.8), channel_id=1, source_target_pairs={{0,4},{1,3},{2,6},{3,1},{4,0},{5,7},{6,2},{7,5},{8,12},{9,11},{10,... | collective-permute-start | bytes 442376 | tf_op jit(solution)/shard_map/ppermute | solution.py:344
  173.1 6.8 %collective-permute-start.18 = (bf16[288,512]{1,0:T(8,128)(2,1)S(1)}, bf16[288,512]{1,0:T(8,128)(2,1)S(1)}, u32[]{:S(2)}, u32[]{:S(2)}) collective-permute-start(bf16[288,512]{1,0:T(8,128)(2,1)S(1)} %maximum_select_fusion.5), channel_id=1, source_target_pairs={{0,2},{1,5},{2,0},{3,7},{4,6},{5,1},{6,4},{7,3},{8,10},{9,13},{10,... | collective-permute-start | bytes 884744 | tf_op jit(solution)/shard_map/ppermute | solution.py:344
  173.7 6.5 %collective-permute-start.11 = (bf16[384,1024]{1,0:T(8,128)(2,1)S(1)}, bf16[384,1024]{1,0:T(8,128)(2,1)S(1)}, u32[]{:S(2)}, u32[]{:S(2)}) collective-permute-start(bf16[384,1024]{1,0:T(8,128)(2,1)S(1)} %maximum_select_fusion.1.mine_one), channel_id=1, source_target_pairs={{0,1},{1,0},{2,3},{3,2},{4,5},{5,4},{6,7},{7,6},{8,9},{9,8},{10,11... | collective-permute-start | bytes 2359304 | tf_op jit(solution)/shard_map/ppermute | solution.py:335
  180.1 2.1 %collective-permute-start.19 = (bf16[288,1024]{1,0:T(8,128)(2,1)S(1)}, bf16[288,1024]{1,0:T(8,128)(2,1)S(1)}, u32[]{:S(2)}, u32[]{:S(2)}) collective-permute-start(bf16[288,1024]{1,0:T(8,128)(2,1)S(1)} %maximum_select_fusion.2.mine_two), channel_id=1, source_target_pairs={{0,1},{1,0},{2,3},{3,2},{4,5},{5,4},{6,7},{7,6},{8,9},{9,8},{10,11... | collective-permute-start | bytes 1769480 | tf_op jit(solution)/shard_map/ppermute | solution.py:335

commit v7 on v5

--- a/solution.py
+++ b/solution.py
@@ -193,58 +193,55 @@
             acc_ref[at, :] = acc_ref[at, :] + product
 
 
-def near_kernel(stride, last, meta_ref, degree_ref, own_ref, other_ref, *rest):
-    count = own_ref.shape[0]
-    values = 1 if not last else HOPS
-    value_refs, rest = rest[:values], rest[values:]
-    near_ref, value_vs, own_v, other_v, acc_ref, sems = rest
-    copies = [pltpu.make_async_copy(value_refs[i], value_vs.at[i], sems.at[i]) for i in range(values)]
-    copies.append(pltpu.make_async_copy(own_ref, own_v, sems.at[HOPS]))
-    copies.append(pltpu.make_async_copy(other_ref, other_v, sems.at[HOPS + 1]))
-    for copy in copies:
-        copy.start()
-    blocks, block = degree_ref.shape
-    if not last:
-        acc_ref[...] = jnp.zeros_like(acc_ref)
-    for copy in copies:
-        copy.wait()
+def far_kernel(slots, class_half, stride, last, core_ref, meta_ref, count_ref, idx_ref, degree_ref, recv_ref,
+               own_halo_ref, other_halo_ref, value_in_ref, own_local_ref, other_local_ref, *rest):
     if last:
-        columns = root_columns(degree_ref, lambda degree: (teleport / (1.0 - teleport)) * degree)
-        for b in range(blocks):
-            at = slice(b * block, (b + 1) * block)
-            total = value_vs[0, at, :].astype(f32)
-            for i in range(1, values):
-                total = total + value_vs[i, at, :].astype(f32)
-            acc_ref[at, :] = over_lanes(columns, b) * total
-    add_tiles(acc_ref, value_vs.at[0], (own_v, other_v), meta_ref, 0, count, stride)
-    out = pltpu.make_async_copy(acc_ref, near_ref, sems.at[HOPS + 2])
-    out.start()
-    out.wait()
-
-
-def far_kernel(slots, class_half, base, stride, last, core_ref, meta_ref, count_ref, idx_ref, degree_ref, recv_ref,
-               own_ref, other_ref, near_ref, *rest):
-    if last:
-        keep_ref, send_ref, recv_v, own_v, other_v, rows_ref, acc_ref, own_sems = rest
+        total_ref, keep_ref, send_ref, recv_v, tiles_v, value_in_v, rows_ref, acc_ref, total_v, own_sems = rest
     else:
-        (out_ref, value_ref, recv_v, own_v, other_v, rows_ref, acc_ref, stage_ref, packed_ref, value_v, sems,
+        (out_ref, value_ref, recv_v, tiles_v, value_in_v, rows_ref, acc_ref, stage_ref, packed_ref, value_v, sems,
          own_sems) = rest
-    count, block = own_ref.shape[0], own_ref.shape[1]
+    local_count, block = own_local_ref.shape[0], own_local_ref.shape[1]
+    halo_count = own_halo_ref.shape[0]
     blocks = degree_ref.shape[0]
+    tiles = []
+    start = 0
+    for ref in (own_local_ref, other_local_ref, own_halo_ref, other_halo_ref):
+        tiles.append(tiles_v.at[pl.ds(start, ref.shape[0])])
+        start += ref.shape[0]
     copies = [
-        pltpu.make_async_copy(recv_ref, recv_v, own_sems.at[0]),
-        pltpu.make_async_copy(near_ref, acc_ref, own_sems.at[1]),
-        pltpu.make_async_copy(own_ref, own_v, own_sems.at[2]),
-        pltpu.make_async_copy(other_ref, other_v, own_sems.at[3]),
+        pltpu.make_async_copy(value_in_ref, value_in_v, own_sems.at[0]),
+        pltpu.make_async_copy(own_local_ref, tiles[0], own_sems.at[1]),
+        pltpu.make_async_copy(other_local_ref, tiles[1], own_sems.at[2]),
+        pltpu.make_async_copy(recv_ref, recv_v, own_sems.at[3]),
+        pltpu.make_async_copy(own_halo_ref, tiles[2], own_sems.at[4]),
+        pltpu.make_async_copy(other_halo_ref, tiles[3], own_sems.at[5]),
     ]
     for copy in copies:
         copy.start()
+    if last:
+        total_copy = pltpu.make_async_copy(total_ref, total_v, own_sems.at[6])
+        total_copy.start()
     roots = root_columns(degree_ref, lax.rsqrt)
-    copies[0].wait()
+    if last:
+        columns = root_columns(degree_ref, lambda degree: (teleport / (1.0 - teleport)) * degree)
+        total_copy.wait()
+        copies[0].wait()
+        for b in range(blocks):
+            at = slice(b * block, (b + 1) * block)
+            total = total_v[at, :].astype(f32) + value_in_v[at, :].astype(f32)
+            acc_ref[at, :] = over_lanes(columns, b) * total
+    else:
+        acc_ref[...] = jnp.zeros_like(acc_ref)
+        copies[0].wait()
+    for copy in copies[1:3]:
+        copy.wait()
+    add_tiles(acc_ref, value_in_v, (tiles[0], tiles[1]), meta_ref, 0, local_count, stride)
+    copies[3].wait()
     unpack_rows(recv_v, rows_ref, slots, class_half)
-    for copy in copies[1:]:
+    for copy in copies[4:]:
         copy.wait()
-    add_tiles(acc_ref, rows_ref, (own_v, other_v), meta_ref, base, base + count, stride)
+    base = 2 * local_count
+    add_tiles(acc_ref, rows_ref, (tiles[2], tiles[3]), meta_ref, base, base + halo_count, stride)
     rate = 1.0 - teleport
     if last:
         half_blocks = blocks // 2
@@ -264,7 +261,7 @@
         scaled = (rate * root * root) * acc_ref[at, :]
         value_v[at, :] = scaled.astype(bf16)
         acc_ref[at, :] = scaled
-    value_copy = pltpu.make_async_copy(value_v, value_ref, own_sems.at[4])
+    value_copy = pltpu.make_async_copy(value_v, value_ref, own_sems.at[6])
     value_copy.start()
     send_packed(acc_ref, count_ref, idx_ref, stage_ref, packed_ref, out_ref, sems, slots, class_half)
     value_copy.wait()
@@ -412,12 +409,7 @@
     packed = packed_rows(slots, class_half)
     local_count, halo_count = local_tiles.shape[2], halo_tiles.shape[2]
 
-    meta_own = jnp.concatenate([local_target[0, 0], local_source[0, 0], halo_target[0, 0], halo_block[0, 0]])
-    stride = meta_own.shape[0]
-    meta = jnp.concatenate([meta_own, swap_cores(meta_own)])
-    own_local, own_halo = local_tiles[0, 0], halo_tiles[0, 0]
-    other_local, other_halo = swap_cores(own_local), swap_cores(own_halo)
-
+    stride = 2 * (local_count + halo_count)
     degree_blocks = degree.reshape(blocks, block)
     out_type = jax.ShapeDtypeStruct((peers, packed, LANES), bf16)
     value_type = jax.ShapeDtypeStruct((rows, LANES), bf16)
@@ -451,7 +443,14 @@
         compiler_params=params(),
         name="first",
     )(core_arg, counts, batch_nodes[0], first_rows, labels, jnp.transpose(batch_logits, (2, 0, 1)), degree_blocks)
-    idx = lax.optimization_barrier((send_rows, value))[0].reshape(-1)
+    tied_rows, *lists, _ = lax.optimization_barrier(
+        (send_rows, local_target, local_source, halo_target, halo_block, value)
+    )
+    idx = tied_rows.reshape(-1)
+    meta_own = jnp.concatenate([part[0, 0] for part in lists])
+    meta = jnp.concatenate([meta_own, swap_cores(meta_own)])
+    own_local, own_halo = local_tiles[0, 0], halo_tiles[0, 0]
+    other_local, other_halo = swap_cores(own_local), swap_cores(own_halo)
 
     def turn(array, axis):
         low, high = split(array, axis)
@@ -462,64 +461,48 @@
         last = hop + 1 == HOPS
         values.insert(0, value)
         landed = lax.all_to_all(out, "dom", split_axis=0, concat_axis=0, tiled=True)
-        near_values = values if last else values[:1]
-        near = pl.pallas_call(
-            functools.partial(near_kernel, stride, last),
-            out_shape=jax.ShapeDtypeStruct((rows, LANES), f32),
-            in_specs=[smem(), vmem(), hbm(), hbm()] + [hbm()] * len(near_values),
-            out_specs=hbm(),
-            scratch_shapes=[
-                pltpu.VMEM((len(near_values), rows, LANES), bf16),
-                pltpu.VMEM((local_count, block, block), bf16),
-                pltpu.VMEM((local_count, block, block), bf16),
-                pltpu.VMEM((rows, LANES), f32),
-                pltpu.SemaphoreType.DMA((HOPS + 3,)),
-            ],
-            compiler_params=params(),
-            cost_estimate=pl.CostEstimate(
-                flops=4 * local_count * block**3, bytes_accessed=4 * 2**20, transcendentals=0
-            ),
-            name="near_last" if last else "near",
-        )(meta, degree_blocks, own_local, other_local, *near_values)
+        extra = []
         if hop == 0:
-            x, first_w, second_w, _ = lax.optimization_barrier((features, first_weight, second_weight, value))
-            pre_first = jnp.dot(x, turn(first_w, 1), preferred_element_type=f32) + turn(first_bias, 0)
-            hidden_first, slope_first = gelu_parts(pre_first)
-            second_turned = turn(second_w, 0)
-            near, hidden_first, slope_first, second_turned = lax.optimization_barrier(
-                (near, hidden_first, slope_first, second_turned)
+            first_w, first_b, second_w, _ = lax.optimization_barrier(
+                (first_weight, first_bias, second_weight, value)
             )
+            held = (turn(first_w, 1), turn(first_b, 0), turn(second_w, 0))
+            value, first_turned, bias_turned, second_turned = lax.optimization_barrier((value, *held))
         if hop == 1:
+            x, third_w, _ = lax.optimization_barrier((features, third_weight, value))
+            pre_first = jnp.dot(x, first_turned, preferred_element_type=f32) + bias_turned
+            low = jnp.pad(third_w[:, :class_half], ((0, 0), (0, LANES - class_half)))
+            high = jnp.pad(third_w[:, class_half:], ((0, 0), (0, LANES - classes + class_half)))
+            third = jnp.where(core == 0, jnp.concatenate([low, high], 1), jnp.concatenate([high, low], 1))
+            value, hidden_first, slope_first, third = lax.optimization_barrier((value, *gelu_parts(pre_first), third))
+        if hop == 2:
             tied, _ = lax.optimization_barrier((hidden_first, value))
             pre_second = jnp.dot(tied, second_turned, preferred_element_type=f32)
-            near, pre_second = lax.optimization_barrier((near, pre_second))
-        if hop == 2:
-            tied, _ = lax.optimization_barrier((pre_second, value))
-            hidden_second, slope_second = gelu_parts(tied + second_bias)
-            near, hidden_second, slope_second = lax.optimization_barrier((near, hidden_second, slope_second))
+            value, pre_second = lax.optimization_barrier((value, pre_second))
         if last:
-            tied, _ = lax.optimization_barrier((third_weight, value))
-            low = jnp.pad(tied[:, :class_half], ((0, 0), (0, LANES - class_half)))
-            high = jnp.pad(tied[:, class_half:], ((0, 0), (0, LANES - classes + class_half)))
-            third = jnp.where(core == 0, jnp.concatenate([low, high], 1), jnp.concatenate([high, low], 1))
-            near, third = lax.optimization_barrier((near, third))
+            tied, *earlier, _ = lax.optimization_barrier((pre_second, *values[1:], value))
+            total = sum(part.astype(f32) for part in earlier).astype(bf16)
+            value, hidden_second, slope_second, total = lax.optimization_barrier(
+                (value, *gelu_parts(tied + second_bias), total)
+            )
+            extra = [total]
         result = pl.pallas_call(
-            functools.partial(far_kernel, slots, class_half, 2 * local_count, stride, last),
+            functools.partial(far_kernel, slots, class_half, stride, last),
             out_shape=(half_type, half_type) if last else (out_type, value_type),
-            in_specs=[smem()] * 4 + [vmem()] + [hbm()] * 4,
+            in_specs=[smem()] * 4 + [vmem()] + [hbm()] * (6 + len(extra)),
             out_specs=(vmem(), vmem()) if last else (hbm(), hbm()),
             scratch_shapes=[
                 pltpu.VMEM((peers, packed, LANES), bf16),
-                pltpu.VMEM((halo_count, block, block), bf16),
-                pltpu.VMEM((halo_count, block, block), bf16),
+                pltpu.VMEM((2 * (local_count + halo_count), block, block), bf16),
+                pltpu.VMEM((rows, LANES), bf16),
                 pltpu.VMEM((peers * slots, LANES), bf16),
                 acc,
             ]
-            + ([] if last else sending + [peer_sems])
-            + [pltpu.SemaphoreType.DMA((5,))],
+            + ([pltpu.VMEM((rows, LANES), bf16)] if last else sending + [peer_sems])
+            + [pltpu.SemaphoreType.DMA((7,))],
             compiler_params=params(),
             name="far_last" if last else "far",
-        )(core_arg, meta, counts, idx, degree_blocks, landed, own_halo, other_halo, near)
+        )(core_arg, meta, counts, idx, degree_blocks, landed, own_halo, other_halo, value, own_local, other_local, *extra)
         if last:
             keep, send = result
         else:

time: 183 us -> 182 us (level)
  Pallas kernels: 48.9 us -> 35.9 us
  waiting for transfers between devices: 41.7 us -> 54.2 us
  starting transfers between devices: 38.8 us -> 33.4 us
  other arithmetic: 13.4 us -> 17.6 us
    pallas_call x8 -> x4, Pallas kernels: 39.9 us -> 27.2 us  [shards(): pl.pallas_call(functools.partial(far_kernel, slots, class_half, stride, l...]
    all_to_all x4, waiting for transfers between devices: 1.58 us -> 11.1 us  [shards(): landed = lax.all_to_all(out, 'dom', split_axis=0, concat_axis=0, tiled=True)]
    select_n x2 -> x3, other arithmetic: 1.69 us -> 5.58 us  [turn(): return jnp.where(core == 0, array, jnp.concatenate([high, low], axis))]
    all_to_all x4, starting transfers between devices: 25 us -> 21.2 us  [shards(): landed = lax.all_to_all(out, 'dom', split_axis=0, concat_axis=0, tiled=True)]
    ppermute x12, waiting for transfers between devices: 37.2 us -> 40.1 us  [exchange(): return lax.ppermute(x, ('dom', 'col'), pairs)]
    ppermute x12, starting transfers between devices: 12.5 us -> 10.3 us  [exchange(): return lax.ppermute(x, ('dom', 'col'), pairs)]
    slice x3, local copies, waits for them, and re-layouts: 1.93 us -> 4.07 us  [split(): lax.slice_in_dim(x, half, 2 * half, axis=axis)]
    unnamed x36 -> x48, local copies, waits for them, and re-layouts: 6.56 us -> 6.34 us
  transfers between devices with their start and end apart: 24 -> 24, of which waited for: 13 -> 17; matrix products, arithmetic and copies ran while one was open for 19% -> 22% of each run, Pallas kernels for 12% -> 0%
where the time goes in v7:
time: 182 us; the launch traced here: 180 us
  waiting for transfers between devices  54.2 us (30%)
  Pallas kernels  35.9 us (20%)
  starting transfers between devices  33.4 us (18%)
  matrix products  24.5 us (13%)
  other arithmetic  17.6 us (10%)
  local copies, waits for them, and re-layouts  12.8 us (7%)
    ppermute x12, waiting for transfers between devices, exchange(): return lax.ppermute(x, ('dom', 'col'), pairs)  40.1 us
    pallas_call x4, Pallas kernels, shards(): pl.pallas_call(functools.partial(far_kernel, slots, class_half, stride, l...  27.2 us
    all_to_all x4, starting transfers between devices, shards(): landed = lax.all_to_all(out, 'dom', split_axis=0, concat_axis=0, tiled=True)  21.2 us
    all_to_all x4, waiting for transfers between devices, shards(): landed = lax.all_to_all(out, 'dom', split_axis=0, concat_axis=0, tiled=True)  11.1 us
    ppermute x12, starting transfers between devices, exchange(): return lax.ppermute(x, ('dom', 'col'), pairs)  10.3 us
    dot_general x1, matrix products, shards(): pre_second = jnp.dot(tied, second_turned, preferred_element_type=f32)  7.25 us
    convert_element_type x1, other arithmetic, gelu_parts(): return ((x * half_up).astype(bf16), slope.astype(bf16))  6.92 us
    unnamed x48, local copies, waits for them, and re-layouts  6.34 us
  transfers between devices with their start and end apart: 24, of which 17 were waited for; matrix products, arithmetic and copies ran while one was open for 22% of the time, Pallas kernels for 0%

profile of v7, /device:TPU:0, one launch (start us, length us, event | category | flops | bytes accessed | tf_op | source)
XLA Modules:
  0.0 179.9 jit_solution(12852909428081619836)
XLA Ops:
  0.7 5.5 %first.1 = (bf16[8,192,128]{2,1,0:T(8,128)(2,1)}, bf16[3072,128]{1,0:T(8,128)(2,1)}) custom-call(s32[1]{0:T(128)} %bitcast.core_ref, s32[8]{0:T(128)} %bitcast.54, s32[256]{0:T(256)} %bitcast.67, s32[8,256]{1,0:T(8,128)} %bitcast.52, s32[1,256]{1,0:T(1,128)} %labels_ref.1, f32[172,1,256]{2,1,0:T(1,128)} %bitcast.51, s32[24,128]{1,0:T(8,128)} %bitcast.42), custom_call_target="tpu_custom_call" | custom-call | tf_op jit(solution)/shard_map/first/pallas_call | solution.py:428
  6.1 1.3 pad_add_fusion
  7.4 0.5 collective-permute-start
  7.9 7.0 %all-to-all-start = ((bf16[8,192,128]{2,1,0:T(8,128)(2,1)}), bf16[8,192,128]{2,1,0:T(8,128)(2,1)}, u32[]{:S(2)}, u32[]{:S(2)}) async-start(bf16[8,192,128]{2,1,0:T(8,128)(2,1)} %get-tuple-element.55), calls=%async_computation | async-start | bytes 786432 | tf_op jit(solution)/shard_map/all_to_all | solution.py:463
  15.2 0.3 collective-permute-start.2
  15.5 3.1 %fusion.5 = (bf16[512,1024]{1,0:T(8,128)(2,1)}, bf16[512,1024]{1,0:T(8,128)(2,1)}) fusion(bf16[1024,1024]{1,0:T(8,128)(2,1)} %param.21), kind=kLoop, calls=%fused_computation.57 | loop fusion | bytes 4194304 | tf_op jit(solution)/shard_map/slice | solution.py:346
  18.5 1.0 fusion.8
  19.5 1.7 maximum_select_fusion.6
  21.3 3.9 %maximum_select_fusion = bf16[1024,1024]{1,0:T(8,128)(2,1)} fusion(bf16[1024,1024]{1,0:T(8,128)(2,1)S(1)} %copy-done.1, bf16[512,1024]{1,0:T(8,128)(2,1)} %get-tuple-element.98, bf16[512,1024]{1,0:T(8,128)(2,1)} %get-tuple-element.97, pred[]{:T(512)S(6)} %eq.2), kind=kLoop, calls=%fused_computation.12 | loop fusion | flops 5242880 | bytes 6291457 | tf_op jit(solution)/shard_map/jit(_where)/select_n | solution.py:457
  25.2 0.6 copy.23
  25.8 1.3 concatenate.80.meta_ref
  27.1 0.3 all-to-all-done.recv_ref
  27.4 0.5 copy-done.2
  28.0 7.0 %far.3 = (bf16[8,192,128]{2,1,0:T(8,128)(2,1)}, bf16[3072,128]{1,0:T(8,128)(2,1)}) custom-call(s32[1]{0:T(128)} %bitcast.core_ref, s32[128]{0:T(128)} %concatenate.80.meta_ref, s32[8]{0:T(128)} %bitcast.55, s32[2048]{0:T(1024)} %bitcast.47, s32[24,128]{1,0:T(8,128)} %bitcast.43, bf16[8,192,128]{2,1,0:T(8,128)(2,1)} %all-to-all-done.recv_ref, ...), custom_call_target="tpu_custom_call" | custom-call | tf_op jit(solution)/shard_map/far/pallas_call | solution.py:489
  35.1 6.1 %all-to-all-start.1 = ((bf16[8,192,128]{2,1,0:T(8,128)(2,1)}), bf16[8,192,128]{2,1,0:T(8,128)(2,1)S(1)}, u32[]{:S(2)}, u32[]{:S(2)}) async-start(bf16[8,192,128]{2,1,0:T(8,128)(2,1)} %get-tuple-element.66), calls=%async_computation.1 | async-start | bytes 786432 | tf_op jit(solution)/shard_map/all_to_all | solution.py:463
  41.3 0.9 maximum_select_fusion.3
  42.2 5.7 %add_convert_fusion.1 = (bf16[1536,1024]{1,0:T(8,128)(2,1)}, bf16[1536,1024]{1,0:T(8,128)(2,1)}) fusion(f32[1024]{0:T(1024)S(1)} %maximum_select_fusion.9, bf16[1536,128]{1,0:T(8,128)(2,1)S(1)} %copy-done, bf16[128,1024]{1,0:T(8,128)(2,1)S(1)} %copy-done.14), kind=kOutput, calls=%fused_computation.7 | convolution fusion | flops 430964736 | bytes 6950912 | tf_op jit(solution)/shard_map/dot_general | solution.py:473
  47.9 4.3 %all-to-all-done.1.recv_ref = bf16[8,192,128]{2,1,0:T(8,128)(2,1)S(1)} async-done(((bf16[8,192,128]{2,1,0:T(8,128)(2,1)}), bf16[8,192,128]{2,1,0:T(8,128)(2,1)S(1)}, u32[]{:S(2)}, u32[]{:S(2)}) %all-to-all-start.1) | async-done | bytes 393248 | tf_op jit(solution)/shard_map/all_to_all | solution.py:463
  52.2 0.7 copy-done.11
  52.9 6.9 %far.4 = (bf16[8,192,128]{2,1,0:T(8,128)(2,1)}, bf16[3072,128]{1,0:T(8,128)(2,1)}) custom-call(s32[1]{0:T(128)} %bitcast.core_ref, s32[128]{0:T(128)} %concatenate.80.meta_ref, s32[8]{0:T(128)} %bitcast.56, s32[2048]{0:T(1024)} %bitcast.48, s32[24,128]{1,0:T(8,128)} %bitcast.44, bf16[8,192,128]{2,1,0:T(8,128)(2,1)} %copy-done.11, ...), custom_call_target="tpu_custom_call" | custom-call | tf_op jit(solution)/shard_map/far/pallas_call | solution.py:489
  59.8 3.8 %all-to-all-start.2 = ((bf16[8,192,128]{2,1,0:T(8,128)(2,1)}), bf16[8,192,128]{2,1,0:T(8,128)(2,1)S(1)}, u32[]{:S(2)}, u32[]{:S(2)}) async-start(bf16[8,192,128]{2,1,0:T(8,128)(2,1)} %get-tuple-element.68), calls=%async_computation.2 | async-start | bytes 786432 | tf_op jit(solution)/shard_map/all_to_all | solution.py:463
  63.6 7.2 %fusion.12 = f32[1536,1024]{1,0:T(8,128)} fusion(bf16[1536,1024]{1,0:T(8,128)(2,1)} %get-tuple-element.70, bf16[1024,1024]{1,0:T(8,128)(2,1)S(1)} %copy-done.9), kind=kOutput, calls=%fused_computation.64 | convolution fusion | flops 3221225472 | bytes 11534336 | tf_op jit(solution)/shard_map/dot_general | solution.py:480
  70.8 3.9 %all-to-all-done.2.recv_ref = bf16[8,192,128]{2,1,0:T(8,128)(2,1)S(1)} async-done(((bf16[8,192,128]{2,1,0:T(8,128)(2,1)}), bf16[8,192,128]{2,1,0:T(8,128)(2,1)S(1)}, u32[]{:S(2)}, u32[]{:S(2)}) %all-to-all-start.2) | async-done | bytes 393248 | tf_op jit(solution)/shard_map/all_to_all | solution.py:463
  74.7 0.7 copy-done.12
  75.4 6.9 %far.5 = (bf16[8,192,128]{2,1,0:T(8,128)(2,1)}, bf16[3072,128]{1,0:T(8,128)(2,1)}) custom-call(s32[1]{0:T(128)} %bitcast.core_ref, s32[128]{0:T(128)} %concatenate.80.meta_ref, s32[8]{0:T(128)} %bitcast.57, s32[2048]{0:T(1024)} %bitcast.49, s32[24,128]{1,0:T(8,128)} %bitcast.45, bf16[8,192,128]{2,1,0:T(8,128)(2,1)} %copy-done.12, ...), custom_call_target="tpu_custom_call" | custom-call | tf_op jit(solution)/shard_map/far/pallas_call | solution.py:489
  82.3 4.3 %all-to-all-start.3 = ((bf16[8,192,128]{2,1,0:T(8,128)(2,1)}), bf16[8,192,128]{2,1,0:T(8,128)(2,1)}, u32[]{:S(2)}, u32[]{:S(2)}) async-start(bf16[8,192,128]{2,1,0:T(8,128)(2,1)} %get-tuple-element.80), calls=%async_computation.3 | async-start | bytes 786432 | tf_op jit(solution)/shard_map/all_to_all | solution.py:463
  86.7 6.9 %add_convert_fusion = (bf16[1536,1024]{1,0:T(8,128)(2,1)S(1)}, bf16[1536,1024]{1,0:T(8,128)(2,1)}) fusion(f32[1536,1024]{1,0:T(8,128)} %fusion.12, f32[1024]{0:T(1024)S(1)} %copy-done.18), kind=kLoop, calls=%fused_computation.2 | loop fusion | flops 28311552 | bytes 12587008 | tf_op jit(solution)/shard_map/convert_element_type | solution.py:319
  93.6 1.2 add_convert_fusion.3.rest_0_
  94.8 2.7 %all-to-all-done.3.recv_ref = bf16[8,192,128]{2,1,0:T(8,128)(2,1)} async-done(((bf16[8,192,128]{2,1,0:T(8,128)(2,1)}), bf16[8,192,128]{2,1,0:T(8,128)(2,1)}, u32[]{:S(2)}, u32[]{:S(2)}) %all-to-all-start.3) | async-done | bytes 393248 | tf_op jit(solution)/shard_map/all_to_all | solution.py:463
  97.5 6.5 %far_last.1 = (bf16[1536,128]{1,0:T(8,128)(2,1)}, bf16[1536,128]{1,0:T(8,128)(2,1)}) custom-call(s32[1]{0:T(128)} %bitcast.core_ref, s32[128]{0:T(128)} %concatenate.80.meta_ref, s32[8]{0:T(128)} %bitcast.58, s32[2048]{0:T(1024)} %bitcast.50, s32[24,128]{1,0:T(8,128)} %bitcast.46, bf16[8,192,128]{2,1,0:T(8,128)(2,1)} %all-to-all-done.3.recv_ref, ...), custom_call_target="tpu_custom_call" | custom-call | tf_op jit(solution)/shard_map/far_last/pallas_call | solution.py:489
  104.1 1.1 constant_dynamic-update-slice_fusion.1
  105.2 1.0 collective-permute-done.3
  106.1 1.1 constant_dynamic-update-slice_fusion
  107.2 2.2 %fusion.11 = (bf16[1024]{0:T(1024)(128)(2,1)S(1)}, bf16[1536,1024]{1,0:T(8,128)(2,1)S(1)}) fusion(bf16[1536,256]{1,0:T(8,128)(2,1)S(1)} %constant_dynamic-update-slice_fusion, bf16[1024,256]{0,1:T(8,128)(2,1)} %maximum_select_fusion.3, bf16[1536,1024]{1,0:T(8,128)(2,1)S(1)} %get-tuple-element.79), kind=kOutput, calls=%fused_computation.63 | convolution fusion | flops 811596800 | bytes 7604224 | tf_op jit(solution)/shard_map/dot_general | solution.py:519
  109.5 0.6 convolution_convert_fusion.3
  110.1 1.4 copy-done.4
  111.5 3.6 %fusion.4 = (bf16[1024]{0:T(1024)(128)(2,1)S(1)}, f32[1536,1024]{1,0:T(8,128)S(1)}) fusion(bf16[1536,1024]{1,0:T(8,128)(2,1)S(1)} %copy-done.4, bf16[1536,1024]{1,0:T(8,128)(2,1)S(1)} %get-tuple-element.114, bf16[1024,1024]{1,0:T(8,128)(2,1)S(1)} %copy-done.10), kind=kOutput, calls=%fused_computation.56 | convolution fusion | flops 3227515904 | bytes 14682112 | tf_op jit(solution)/shard_map/dot_general | solution.py:528
  115.1 0.8 convolution_convert_fusion.4
  115.9 1.1 copy-done.5
  117.0 1.0 convolution_convert_fusion.2
  118.3 1.4 convolution_convert_fusion
  119.8 0.4 collective-permute-start.4
  120.2 0.6 convolution_convert_fusion.5
  121.1 1.5 collective-permute-start.13
  122.6 1.4 add_convert_fusion.2
  124.1 1.0 collective-permute-start.5
  125.1 2.8 %collective-permute-done.13 = bf16[288,512]{1,0:T(8,128)(2,1)S(1)} collective-permute-done((bf16[288,512]{1,0:T(8,128)(2,1)S(1)}, bf16[288,512]{1,0:T(8,128)(2,1)S(1)}, u32[]{:S(2)}, u32[]{:S(2)}) %collective-permute-start.13) | collective-permute-done | bytes 294944 | tf_op jit(solution)/shard_map/ppermute | solution.py:332
  128.0 4.1 %collective-permute-done.5 = bf16[384,512]{1,0:T(8,128)(2,1)S(1)} collective-permute-done((bf16[384,512]{1,0:T(8,128)(2,1)S(1)}, bf16[384,512]{1,0:T(8,128)(2,1)S(1)}, u32[]{:S(2)}, u32[]{:S(2)}) %collective-permute-start.5) | collective-permute-done | bytes 393248 | tf_op jit(solution)/shard_map/ppermute | solution.py:332
  132.3 1.0 collective-permute-start.6
  133.3 1.1 collective-permute-start.14
  134.5 3.6 %collective-permute-done.6 = bf16[384,256]{1,0:T(8,128)(2,1)S(1)} collective-permute-done((bf16[384,256]{1,0:T(8,128)(2,1)S(1)}, bf16[384,256]{1,0:T(8,128)(2,1)S(1)}, u32[]{:S(2)}, u32[]{:S(2)}) %collective-permute-start.6) | collective-permute-done | bytes 196640 | tf_op jit(solution)/shard_map/ppermute | solution.py:332
  138.1 1.0 collective-permute-start.7
  139.2 0.4 collective-permute-done.14
  139.7 5.1 %collective-permute-done.7 = bf16[384,128]{1,0:T(8,128)(2,1)S(1)} collective-permute-done((bf16[384,128]{1,0:T(8,128)(2,1)S(1)}, bf16[384,128]{1,0:T(8,128)(2,1)S(1)}, u32[]{:S(2)}, u32[]{:S(2)}) %collective-permute-start.7) | collective-permute-done | bytes 98336 | tf_op jit(solution)/shard_map/ppermute | solution.py:332
  144.9 3.0 %collective-permute-start.15 = (bf16[288,128]{1,0:T(8,128)(2,1)S(1)}, bf16[288,128]{1,0:T(8,128)(2,1)S(1)}, u32[]{:S(2)}, u32[]{:S(2)}) collective-permute-start(bf16[288,128]{1,0:T(8,128)(2,1)S(1)} %broadcast_select_fusion.5), channel_id=1, source_target_pairs={{0,8},{1,9},{2,10},{3,11},{4,12},{5,13},{6,14},{7,15},{8,0},{9,1},... | collective-permute-start | bytes 221192 | tf_op jit(solution)/shard_map/ppermute | solution.py:332
  147.9 4.6 %collective-permute-done.8 = bf16[384,128]{1,0:T(8,128)(2,1)S(1)} collective-permute-done((bf16[384,128]{1,0:T(8,128)(2,1)S(1)}, bf16[384,128]{1,0:T(8,128)(2,1)S(1)}, u32[]{:S(2)}, u32[]{:S(2)}) %collective-permute-start.8) | collective-permute-done | bytes 98336 | tf_op jit(solution)/shard_map/ppermute | solution.py:332
  152.6 1.4 collective-permute-done.15
  154.1 7.0 %collective-permute-done.9 = bf16[384,256]{1,0:T(8,128)(2,1)S(1)} collective-permute-done((bf16[384,256]{1,0:T(8,128)(2,1)S(1)}, bf16[384,256]{1,0:T(8,128)(2,1)S(1)}, u32[]{:S(2)}, u32[]{:S(2)}) %collective-permute-start.9) | collective-permute-done | bytes 196640 | tf_op jit(solution)/shard_map/ppermute | solution.py:332
  161.4 5.9 %collective-permute-done.17 = bf16[288,256]{1,0:T(8,128)(2,1)S(1)} collective-permute-done((bf16[288,256]{1,0:T(8,128)(2,1)S(1)}, bf16[288,256]{1,0:T(8,128)(2,1)S(1)}, u32[]{:S(2)}, u32[]{:S(2)}) %collective-permute-start.17) | collective-permute-done | bytes 147488 | tf_op jit(solution)/shard_map/ppermute | solution.py:332
  167.5 1.3 collective-permute-start.18
  168.8 0.3 collective-permute-done.10
  169.3 4.9 %collective-permute-done.18 = bf16[288,512]{1,0:T(8,128)(2,1)S(1)} collective-permute-done((bf16[288,512]{1,0:T(8,128)(2,1)S(1)}, bf16[288,512]{1,0:T(8,128)(2,1)S(1)}, u32[]{:S(2)}, u32[]{:S(2)}) %collective-permute-start.18) | collective-permute-done | bytes 294944 | tf_op jit(solution)/shard_map/ppermute | solution.py:332
  174.5 2.0 %collective-permute-done.19.theirs_two = bf16[288,1024]{1,0:T(8,128)(2,1)S(1)} collective-permute-done((bf16[288,1024]{1,0:T(8,128)(2,1)S(1)}, bf16[288,1024]{1,0:T(8,128)(2,1)S(1)}, u32[]{:S(2)}, u32[]{:S(2)}) %collective-permute-start.19) | collective-permute-done | bytes 589856 | tf_op jit(solution)/shard_map/ppermute | solution.py:323
  176.5 3.2 %finish.1 = (f32[128,1024]{1,0:T(8,128)}, f32[1,1024]{1,0:T(1,128)}, f32[1024,1024]{1,0:T(8,128)}, f32[1,1024]{1,0:T(1,128)}, f32[172,1024]{1,0:T(8,128)}) custom-call(s32[1]{0:T(128)} %bitcast.core_ref, bf16[384,1024]{1,0:T(8,128)(2,1)S(1)} %maximum_select_fusion.1.mine_one, bf16[384,1024]{1,0:T(8,128)(2,1)S(1)} %collective-permute-done.11.theirs_one, ...), custom_call_target="tpu_custom_call" | custom-call | tf_op jit(solution)/shard_map/finish/pallas_call | solution.py:556
  (92 shorter events, 3.1 us)
Async XLA Ops:
  0.6 41.6 %copy-start = (bf16[1536,128]{1,0:T(8,128)(2,1)S(1)}, bf16[1536,128]{1,0:T(8,128)(2,1)}, u32[]{:S(2)}) copy-start(bf16[1536,128]{1,0:T(8,128)(2,1)} %param.18) | copy-start | bytes 1179652
  7.4 18.4 %collective-permute-start = (s32[64]{0:T(128)}, s32[64]{0:T(128)}, u32[]{:S(2)}, u32[]{:S(2)}) collective-permute-start(s32[64]{0:T(128)} %pad_add_fusion), channel_id=1, source_target_pairs={{0,1},{1,0},{2,3},{3,2},{4,5},{5,4},{6,7},{7,6},{8,9},{9,8},{10,11... | collective-permute-start | bytes 776 | tf_op jit(solution)/shard_map/ppermute | solution.py:323
  7.9 13.4 %copy-start.17 = (f32[1024]{0:T(1024)S(1)}, f32[1024]{0:T(1024)}, u32[]{:S(2)}) copy-start(f32[1024]{0:T(1024)} %param.20) | copy-start | bytes 12292
  7.9 13.4 %copy-start.1 = (bf16[1024,1024]{1,0:T(8,128)(2,1)S(1)}, bf16[1024,1024]{1,0:T(8,128)(2,1)}, u32[]{:S(2)}) copy-start(bf16[1024,1024]{1,0:T(8,128)(2,1)} %param.21) | copy-start | bytes 6291460
  7.9 19.5 %all-to-all-start = ((bf16[8,192,128]{2,1,0:T(8,128)(2,1)}), bf16[8,192,128]{2,1,0:T(8,128)(2,1)}, u32[]{:S(2)}, u32[]{:S(2)}) async-start(bf16[8,192,128]{2,1,0:T(8,128)(2,1)} %get-tuple-element.55), calls=%async_computation | async-start | bytes 786432 | tf_op jit(solution)/shard_map/all_to_all | solution.py:463
  14.9 12.1 %collective-permute-start.1 = (bf16[16,128,128]{2,1,0:T(8,128)(2,1)}, bf16[16,128,128]{2,1,0:T(8,128)(2,1)S(1)}, u32[]{:S(2)}, u32[]{:S(2)}) collective-permute-start(bf16[16,128,128]{2,1,0:T(8,128)(2,1)} %bitcast.32), channel_id=1, source_target_pairs={{0,1},{1,0},{2,3},{3,2},{4,5},{5,4},{6,7},{7,6},{8,9},{9,8},{10,11... | collective-permute-start | bytes 1572872 | tf_op jit(solution)/shard_map/ppermute | solution.py:323
  15.2 11.9 %collective-permute-start.2 = (bf16[16,128,128]{2,1,0:T(8,128)(2,1)}, bf16[16,128,128]{2,1,0:T(8,128)(2,1)S(1)}, u32[]{:S(2)}, u32[]{:S(2)}) collective-permute-start(bf16[16,128,128]{2,1,0:T(8,128)(2,1)} %bitcast.37), channel_id=1, source_target_pairs={{0,1},{1,0},{2,3},{3,2},{4,5},{5,4},{6,7},{7,6},{8,9},{9,8},{10,11... | collective-permute-start | bytes 1572872 | tf_op jit(solution)/shard_map/ppermute | solution.py:323
  21.3 3.9 %copy-start.16 = (s32[1,8,256]{2,1,0:T(8,128)S(1)}, s32[1,8,256]{2,1,0:T(8,128)}, u32[]{:S(2)}) copy-start(s32[1,8,256]{2,1,0:T(8,128)} %param.30) | copy-start | bytes 24580
  21.3 4.5 %copy-start.19 = (s32[1,1,16]{2,1,0:T(1,128)S(1)}, s32[1,1,16]{2,1,0:T(1,128)}, u32[]{:S(2)}) copy-start(s32[1,1,16]{2,1,0:T(1,128)} %param.25) | copy-start | bytes 196
  21.3 4.5 %copy-start.20 = (s32[1,1,16]{2,1,0:T(1,128)S(1)}, s32[1,1,16]{2,1,0:T(1,128)}, u32[]{:S(2)}) copy-start(s32[1,1,16]{2,1,0:T(1,128)} %param.26) | copy-start | bytes 196
  21.3 4.5 %copy-start.21 = (s32[1,1,16]{2,1,0:T(1,128)S(1)}, s32[1,1,16]{2,1,0:T(1,128)}, u32[]{:S(2)}) copy-start(s32[1,1,16]{2,1,0:T(1,128)} %param.28) | copy-start | bytes 196
  25.2 9.9 %copy-start.13 = (bf16[1024,172]{0,1:T(8,128)(2,1)S(1)}, bf16[1024,172]{0,1:T(8,128)(2,1)}, u32[]{:S(2)}) copy-start(bf16[1024,172]{0,1:T(8,128)(2,1)} %param.23) | copy-start | bytes 1056772
  25.2 9.9 %copy-start.22 = (pred[128]{0:T(512)(128)(4,1)S(1)}, pred[128]{0:T(512)(128)(4,1)}, u32[]{:S(2)}) copy-start(pred[128]{0:T(512)(128)(4,1)} %constant.31.clone.1) | copy-start | bytes 388
  25.2 16.1 %slice-start = ((bf16[1024,172]{0,1:T(8,128)(2,1)}), bf16[1024,84]{0,1:T(8,128)(2,1)S(1)}, s32[]{:S(2)}) async-start(bf16[1024,172]{0,1:T(8,128)(2,1)} %param.23), calls=%async_computation.4 | async-start | bytes 360448 | tf_op jit(solution)/shard_map/slice | solution.py:475
  27.1 0.8 copy-start.2
  27.1 1.0 copy-start.3
  28.0 14.2 %copy-start.14 = (bf16[128,1024]{1,0:T(8,128)(2,1)S(1)}, bf16[128,1024]{1,0:T(8,128)(2,1)}, u32[]{:S(2)}) copy-start(bf16[128,1024]{1,0:T(8,128)(2,1)} %maximum_select_fusion.6) | copy-start | bytes 786436
  35.1 17.0 %all-to-all-start.1 = ((bf16[8,192,128]{2,1,0:T(8,128)(2,1)}), bf16[8,192,128]{2,1,0:T(8,128)(2,1)S(1)}, u32[]{:S(2)}, u32[]{:S(2)}) async-start(bf16[8,192,128]{2,1,0:T(8,128)(2,1)} %get-tuple-element.66), calls=%async_computation.1 | async-start | bytes 786432 | tf_op jit(solution)/shard_map/all_to_all | solution.py:463
  47.9 15.7 %copy-start.9 = (bf16[1024,1024]{1,0:T(8,128)(2,1)S(1)}, bf16[1024,1024]{1,0:T(8,128)(2,1)}, u32[]{:S(2)}) copy-start(bf16[1024,1024]{1,0:T(8,128)(2,1)} %maximum_select_fusion) | copy-start | bytes 6291460
  52.2 0.7 copy-start.11
  59.8 14.9 %all-to-all-start.2 = ((bf16[8,192,128]{2,1,0:T(8,128)(2,1)}), bf16[8,192,128]{2,1,0:T(8,128)(2,1)S(1)}, u32[]{:S(2)}, u32[]{:S(2)}) async-start(bf16[8,192,128]{2,1,0:T(8,128)(2,1)} %get-tuple-element.68), calls=%async_computation.2 | async-start | bytes 786432 | tf_op jit(solution)/shard_map/all_to_all | solution.py:463
  70.8 15.8 %copy-start.18 = (f32[1024]{0:T(1024)S(1)}, f32[1024]{0:T(1024)}, u32[]{:S(2)}) copy-start(f32[1024]{0:T(1024)} %param.22) | copy-start | bytes 12292
  74.7 0.7 copy-start.12
  82.3 15.2 %all-to-all-start.3 = ((bf16[8,192,128]{2,1,0:T(8,128)(2,1)}), bf16[8,192,128]{2,1,0:T(8,128)(2,1)}, u32[]{:S(2)}, u32[]{:S(2)}) async-start(bf16[8,192,128]{2,1,0:T(8,128)(2,1)} %get-tuple-element.80), calls=%async_computation.3 | async-start | bytes 786432 | tf_op jit(solution)/shard_map/all_to_all | solution.py:463
  86.6 7.0 %copy-start.6 = (bf16[3072,128]{1,0:T(8,128)(2,1)S(1)}, bf16[3072,128]{1,0:T(8,128)(2,1)}, u32[]{:S(2)}) copy-start(bf16[3072,128]{1,0:T(8,128)(2,1)} %get-tuple-element.78.value_in_ref) | copy-start | bytes 2359300
  86.6 6.9 %copy-start.7 = (bf16[3072,128]{1,0:T(8,128)(2,1)S(1)}, bf16[3072,128]{1,0:T(8,128)(2,1)}, u32[]{:S(2)}) copy-start(bf16[3072,128]{1,0:T(8,128)(2,1)} %get-tuple-element.77.value_in_ref) | copy-start | bytes 2359300
  86.6 6.9 %copy-start.8 = (bf16[3072,128]{1,0:T(8,128)(2,1)S(1)}, bf16[3072,128]{1,0:T(8,128)(2,1)}, u32[]{:S(2)}) copy-start(bf16[3072,128]{1,0:T(8,128)(2,1)} %get-tuple-element.76.value_in_ref) | copy-start | bytes 2359300
  104.0 2.1 %collective-permute-start.3 = (bf16[1536,128]{1,0:T(8,128)(2,1)}, bf16[1536,128]{1,0:T(8,128)(2,1)}, u32[]{:S(2)}, u32[]{:S(2)}) collective-permute-start(bf16[1536,128]{1,0:T(8,128)(2,1)} %get-tuple-element.84), channel_id=1, source_target_pairs={{0,1},{1,0},{2,3},{3,2},{4,5},{5,4},{6,7},{7,6},{8,9},{9,8},{10,11... | collective-permute-start | bytes 1179656 | tf_op jit(solution)/shard_map/ppermute | solution.py:323
  107.2 2.3 %copy-start.15 = (bf16[1536,1024]{1,0:T(8,128)(2,1)S(1)}, bf16[1536,1024]{1,0:T(8,128)(2,1)}, u32[]{:S(2)}) copy-start(bf16[1536,1024]{1,0:T(8,128)(2,1)} %get-tuple-element.70) | copy-start | bytes 9437188
  107.2 2.9 %copy-start.10 = (bf16[1024,1024]{1,0:T(8,128)(2,1)S(1)}, bf16[1024,1024]{1,0:T(8,128)(2,1)}, u32[]{:S(2)}) copy-start(bf16[1024,1024]{1,0:T(8,128)(2,1)} %maximum_select_fusion) | copy-start | bytes 6291460
  109.5 2.0 %copy-start.4 = (bf16[1536,1024]{1,0:T(8,128)(2,1)S(1)}, bf16[1536,1024]{1,0:T(8,128)(2,1)}, u32[]{:S(2)}) copy-start(bf16[1536,1024]{1,0:T(8,128)(2,1)} %get-tuple-element.86) | copy-start | bytes 9437188
  115.1 1.9 %copy-start.5 = (bf16[1536,1024]{1,0:T(8,128)(2,1)S(1)}, bf16[1536,1024]{1,0:T(8,128)(2,1)}, u32[]{:S(2)}) copy-start(bf16[1536,1024]{1,0:T(8,128)(2,1)} %get-tuple-element.87) | copy-start | bytes 9437188
  118.1 2.7 %collective-permute-start.12 = (bf16[288,1024]{1,0:T(8,128)(2,1)S(1)}, bf16[288,1024]{1,0:T(8,128)(2,1)S(1)}, u32[]{:S(2)}, u32[]{:S(2)}) collective-permute-start(bf16[288,1024]{1,0:T(8,128)(2,1)S(1)} %pad_maximum_fusion), channel_id=1, source_target_pairs={{0,1},{1,0},{2,3},{3,2},{4,5},{5,4},{6,7},{7,6},{8,9},{9,8},{10,11... | collective-permute-start | bytes 1769480 | tf_op jit(solution)/shard_map/ppermute | solution.py:323
  119.8 2.9 %collective-permute-start.4 = (bf16[384,1024]{1,0:T(8,128)(2,1)S(1)}, bf16[384,1024]{1,0:T(8,128)(2,1)S(1)}, u32[]{:S(2)}, u32[]{:S(2)}) collective-permute-start(bf16[384,1024]{1,0:T(8,128)(2,1)S(1)} %convolution_convert_fusion), channel_id=1, source_target_pairs={{0,1},{1,0},{2,3},{3,2},{4,5},{5,4},{6,7},{7,6},{8,9},{9,8},{10,11... | collective-permute-start | bytes 2359304 | tf_op jit(solution)/shard_map/ppermute | solution.py:323
  121.1 6.8 %collective-permute-start.13 = (bf16[288,512]{1,0:T(8,128)(2,1)S(1)}, bf16[288,512]{1,0:T(8,128)(2,1)S(1)}, u32[]{:S(2)}, u32[]{:S(2)}) collective-permute-start(bf16[288,512]{1,0:T(8,128)(2,1)S(1)} %broadcast_select_fusion.1), channel_id=1, source_target_pairs={{0,2},{1,5},{2,0},{3,7},{4,6},{5,1},{6,4},{7,3},{8,10},{9,13},{10,... | collective-permute-start | bytes 884744 | tf_op jit(solution)/shard_map/ppermute | solution.py:332
  124.1 8.0 %collective-permute-start.5 = (bf16[384,512]{1,0:T(8,128)(2,1)S(1)}, bf16[384,512]{1,0:T(8,128)(2,1)S(1)}, u32[]{:S(2)}, u32[]{:S(2)}) collective-permute-start(bf16[384,512]{1,0:T(8,128)(2,1)S(1)} %broadcast_select_fusion), channel_id=1, source_target_pairs={{0,2},{1,5},{2,0},{3,7},{4,6},{5,1},{6,4},{7,3},{8,10},{9,13},{10,... | collective-permute-start | bytes 1179656 | tf_op jit(solution)/shard_map/ppermute | solution.py:332
  132.3 5.7 %collective-permute-start.6 = (bf16[384,256]{1,0:T(8,128)(2,1)S(1)}, bf16[384,256]{1,0:T(8,128)(2,1)S(1)}, u32[]{:S(2)}, u32[]{:S(2)}) collective-permute-start(bf16[384,256]{1,0:T(8,128)(2,1)S(1)} %broadcast_select_fusion.2), channel_id=1, source_target_pairs={{0,4},{1,3},{2,6},{3,1},{4,0},{5,7},{6,2},{7,5},{8,12},{9,11},{10,... | collective-permute-start | bytes 589832 | tf_op jit(solution)/shard_map/ppermute | solution.py:332
  133.3 6.3 %collective-permute-start.14 = (bf16[288,256]{1,0:T(8,128)(2,1)S(1)}, bf16[288,256]{1,0:T(8,128)(2,1)S(1)}, u32[]{:S(2)}, u32[]{:S(2)}) collective-permute-start(bf16[288,256]{1,0:T(8,128)(2,1)S(1)} %broadcast_select_fusion.3), channel_id=1, source_target_pairs={{0,4},{1,3},{2,6},{3,1},{4,0},{5,7},{6,2},{7,5},{8,12},{9,11},{10,... | collective-permute-start | bytes 442376 | tf_op jit(solution)/shard_map/ppermute | solution.py:332
  138.1 6.6 %collective-permute-start.7 = (bf16[384,128]{1,0:T(8,128)(2,1)S(1)}, bf16[384,128]{1,0:T(8,128)(2,1)S(1)}, u32[]{:S(2)}, u32[]{:S(2)}) collective-permute-start(bf16[384,128]{1,0:T(8,128)(2,1)S(1)} %broadcast_select_fusion.4), channel_id=1, source_target_pairs={{0,8},{1,9},{2,10},{3,11},{4,12},{5,13},{6,14},{7,15},{8,0},{9,1},... | collective-permute-start | bytes 294920 | tf_op jit(solution)/shard_map/ppermute | solution.py:332
  144.8 7.6 %collective-permute-start.8 = (bf16[384,128]{1,0:T(8,128)(2,1)S(1)}, bf16[384,128]{1,0:T(8,128)(2,1)S(1)}, u32[]{:S(2)}, u32[]{:S(2)}) collective-permute-start(bf16[384,128]{1,0:T(8,128)(2,1)S(1)} %add_convert_fusion.9), channel_id=1, source_target_pairs={{0,8},{1,9},{2,10},{3,11},{4,12},{5,13},{6,14},{7,15},{8,0},{9,1},... | collective-permute-start | bytes 294920 | tf_op jit(solution)/shard_map/ppermute | solution.py:332
  144.9 9.1 %collective-permute-start.15 = (bf16[288,128]{1,0:T(8,128)(2,1)S(1)}, bf16[288,128]{1,0:T(8,128)(2,1)S(1)}, u32[]{:S(2)}, u32[]{:S(2)}) collective-permute-start(bf16[288,128]{1,0:T(8,128)(2,1)S(1)} %broadcast_select_fusion.5), channel_id=1, source_target_pairs={{0,8},{1,9},{2,10},{3,11},{4,12},{5,13},{6,14},{7,15},{8,0},{9,1},... | collective-permute-start | bytes 221192 | tf_op jit(solution)/shard_map/ppermute | solution.py:332
  152.5 8.6 %collective-permute-start.9 = (bf16[384,256]{1,0:T(8,128)(2,1)S(1)}, bf16[384,256]{1,0:T(8,128)(2,1)S(1)}, u32[]{:S(2)}, u32[]{:S(2)}) collective-permute-start(bf16[384,256]{1,0:T(8,128)(2,1)S(1)} %maximum_select_fusion.7), channel_id=1, source_target_pairs={{0,4},{1,3},{2,6},{3,1},{4,0},{5,7},{6,2},{7,5},{8,12},{9,11},{10,... | collective-permute-start | bytes 589832 | tf_op jit(solution)/shard_map/ppermute | solution.py:332
  154.1 7.2 %collective-permute-start.16 = (bf16[288,128]{1,0:T(8,128)(2,1)S(1)}, bf16[288,128]{1,0:T(8,128)(2,1)S(1)}, u32[]{:S(2)}, u32[]{:S(2)}) collective-permute-start(bf16[288,128]{1,0:T(8,128)(2,1)S(1)} %add_convert_fusion.10), channel_id=1, source_target_pairs={{0,8},{1,9},{2,10},{3,11},{4,12},{5,13},{6,14},{7,15},{8,0},{9,1},... | collective-permute-start | bytes 221192 | tf_op jit(solution)/shard_map/ppermute | solution.py:332
  161.2 7.8 %collective-permute-start.10 = (bf16[384,512]{1,0:T(8,128)(2,1)S(1)}, bf16[384,512]{1,0:T(8,128)(2,1)S(1)}, u32[]{:S(2)}, u32[]{:S(2)}) collective-permute-start(bf16[384,512]{1,0:T(8,128)(2,1)S(1)} %maximum_select_fusion.4), channel_id=1, source_target_pairs={{0,2},{1,5},{2,0},{3,7},{4,6},{5,1},{6,4},{7,3},{8,10},{9,13},{10,... | collective-permute-start | bytes 1179656 | tf_op jit(solution)/shard_map/ppermute | solution.py:332
  161.4 6.0 %collective-permute-start.17 = (bf16[288,256]{1,0:T(8,128)(2,1)S(1)}, bf16[288,256]{1,0:T(8,128)(2,1)S(1)}, u32[]{:S(2)}, u32[]{:S(2)}) collective-permute-start(bf16[288,256]{1,0:T(8,128)(2,1)S(1)} %maximum_select_fusion.8), channel_id=1, source_target_pairs={{0,4},{1,3},{2,6},{3,1},{4,0},{5,7},{6,2},{7,5},{8,12},{9,11},{10,... | collective-permute-start | bytes 442376 | tf_op jit(solution)/shard_map/ppermute | solution.py:332
  167.5 6.8 %collective-permute-start.18 = (bf16[288,512]{1,0:T(8,128)(2,1)S(1)}, bf16[288,512]{1,0:T(8,128)(2,1)S(1)}, u32[]{:S(2)}, u32[]{:S(2)}) collective-permute-start(bf16[288,512]{1,0:T(8,128)(2,1)S(1)} %maximum_select_fusion.5), channel_id=1, source_target_pairs={{0,2},{1,5},{2,0},{3,7},{4,6},{5,1},{6,4},{7,3},{8,10},{9,13},{10,... | collective-permute-start | bytes 884744 | tf_op jit(solution)/shard_map/ppermute | solution.py:332
  169.3 7.3 %collective-permute-start.11 = (bf16[384,1024]{1,0:T(8,128)(2,1)S(1)}, bf16[384,1024]{1,0:T(8,128)(2,1)S(1)}, u32[]{:S(2)}, u32[]{:S(2)}) collective-permute-start(bf16[384,1024]{1,0:T(8,128)(2,1)S(1)} %maximum_select_fusion.1.mine_one), channel_id=1, source_target_pairs={{0,1},{1,0},{2,3},{3,2},{4,5},{5,4},{6,7},{7,6},{8,9},{9,8},{10,11... | collective-permute-start | bytes 2359304 | tf_op jit(solution)/shard_map/ppermute | solution.py:323
  174.5 2.1 %collective-permute-start.19 = (bf16[288,1024]{1,0:T(8,128)(2,1)S(1)}, bf16[288,1024]{1,0:T(8,128)(2,1)S(1)}, u32[]{:S(2)}, u32[]{:S(2)}) collective-permute-start(bf16[288,1024]{1,0:T(8,128)(2,1)S(1)} %maximum_select_fusion.2.mine_two), channel_id=1, source_target_pairs={{0,1},{1,0},{2,3},{3,2},{4,5},{5,4},{6,7},{7,6},{8,9},{9,8},{10,11... | collective-permute-start | bytes 1769480 | tf_op jit(solution)/shard_map/ppermute | solution.py:323

commit v8 on v7

--- a/solution.py
+++ b/solution.py
@@ -193,13 +193,46 @@
             acc_ref[at, :] = acc_ref[at, :] + product
 
 
-def far_kernel(slots, class_half, stride, last, core_ref, meta_ref, count_ref, idx_ref, degree_ref, recv_ref,
+class Part:
+    def __init__(self, ref, offset):
+        self.ref, self.offset = ref, offset
+
+    def __getitem__(self, i):
+        return self.ref[self.offset + i]
+
+
+def turn_kernel(core_ref, first_ref, bias_ref, second_ref, first_out, bias_out, second_out, sems):
+    core = core_ref[0]
+    half = second_ref.shape[0] // 2
+    copies = []
+    for i in range(2):
+        source = pl.ds(pl.multiple_of((core ^ i) * half, half), half)
+        to = pl.ds(i * half, half)
+        copies += [
+            pltpu.make_async_copy(second_ref.at[source], second_out.at[to], sems.at[3 * i]),
+            pltpu.make_async_copy(first_ref.at[:, source], first_out.at[:, to], sems.at[3 * i + 1]),
+            pltpu.make_async_copy(bias_ref.at[:, source], bias_out.at[:, to], sems.at[3 * i + 2]),
+        ]
+    for copy in copies:
+        copy.start()
+    for copy in copies:
+        copy.wait()
+
+
+def far_kernel(slots, class_half, stride, last, ints_ref, degree_in_ref, recv_ref,
                own_halo_ref, other_halo_ref, value_in_ref, own_local_ref, other_local_ref, *rest):
     if last:
-        total_ref, keep_ref, send_ref, recv_v, tiles_v, value_in_v, rows_ref, acc_ref, total_v, own_sems = rest
+        (total_ref, keep_ref, send_ref, ints, degree_ref, recv_v, tiles_v, value_in_v, rows_ref, acc_ref, total_v,
+         own_sems) = rest
     else:
-        (out_ref, value_ref, recv_v, tiles_v, value_in_v, rows_ref, acc_ref, stage_ref, packed_ref, value_v, sems,
-         own_sems) = rest
+        (out_ref, value_ref, ints, degree_ref, recv_v, tiles_v, value_in_v, rows_ref, acc_ref, stage_ref, packed_ref,
+         value_v, sems, own_sems) = rest
+    core_ref, count_ref = Part(ints, 0), Part(ints, 1)
+    meta_ref, idx_ref = Part(ints, LANES), Part(ints, LANES + 2 * stride)
+    degree_copy = pltpu.make_async_copy(degree_in_ref, degree_ref, own_sems.at[7])
+    degree_copy.start()
+    ints_copy = pltpu.make_async_copy(ints_ref, ints, own_sems.at[8])
+    ints_copy.start()
     local_count, block = own_local_ref.shape[0], own_local_ref.shape[1]
     halo_count = own_halo_ref.shape[0]
     blocks = degree_ref.shape[0]
@@ -221,6 +254,7 @@
     if last:
         total_copy = pltpu.make_async_copy(total_ref, total_v, own_sems.at[6])
         total_copy.start()
+    degree_copy.wait()
     roots = root_columns(degree_ref, lax.rsqrt)
     if last:
         columns = root_columns(degree_ref, lambda degree: (teleport / (1.0 - teleport)) * degree)
@@ -235,6 +269,7 @@
         copies[0].wait()
     for copy in copies[1:3]:
         copy.wait()
+    ints_copy.wait()
     add_tiles(acc_ref, value_in_v, (tiles[0], tiles[1]), meta_ref, 0, local_count, stride)
     copies[3].wait()
     unpack_rows(recv_v, rows_ref, slots, class_half)
@@ -443,18 +478,38 @@
         compiler_params=params(),
         name="first",
     )(core_arg, counts, batch_nodes[0], first_rows, labels, jnp.transpose(batch_logits, (2, 0, 1)), degree_blocks)
-    tied_rows, *lists, _ = lax.optimization_barrier(
-        (send_rows, local_target, local_source, halo_target, halo_block, value)
+    first_w, first_b, second_w, _ = lax.optimization_barrier((first_weight, first_bias, second_weight, value))
+    first_turned, bias_turned, second_turned = pl.pallas_call(
+        turn_kernel,
+        out_shape=(
+            jax.ShapeDtypeStruct(first_w.shape, bf16),
+            jax.ShapeDtypeStruct((1, hidden), f32),
+            jax.ShapeDtypeStruct(second_w.shape, bf16),
+        ),
+        in_specs=[smem(), hbm(), hbm(), hbm()],
+        out_specs=(hbm(), hbm(), hbm()),
+        scratch_shapes=[pltpu.SemaphoreType.DMA((6,))],
+        compiler_params=params(),
+        name="turn",
+    )(core_arg, first_w, first_b.reshape(1, hidden), second_w)
+    tied_rows, *lists, first_turned = lax.optimization_barrier(
+        (send_rows, local_target, local_source, halo_target, halo_block, first_turned)
     )
-    idx = tied_rows.reshape(-1)
     meta_own = jnp.concatenate([part[0, 0] for part in lists])
-    meta = jnp.concatenate([meta_own, swap_cores(meta_own)])
+    total_ints = LANES + 2 * stride + peers * slots
+    ints = jnp.concatenate(
+        [
+            core_arg,
+            counts,
+            jnp.zeros((LANES - 1 - peers,), jnp.int32),
+            meta_own,
+            swap_cores(meta_own),
+            tied_rows.reshape(-1),
+            jnp.zeros((-total_ints % 1024,), jnp.int32),
+        ]
+    )
     own_local, own_halo = local_tiles[0, 0], halo_tiles[0, 0]
     other_local, other_halo = swap_cores(own_local), swap_cores(own_halo)
-
-    def turn(array, axis):
-        low, high = split(array, axis)
-        return jnp.where(core == 0, array, jnp.concatenate([high, low], axis))
 
     values = []
     for hop in range(HOPS):
@@ -463,11 +518,9 @@
         landed = lax.all_to_all(out, "dom", split_axis=0, concat_axis=0, tiled=True)
         extra = []
         if hop == 0:
-            first_w, first_b, second_w, _ = lax.optimization_barrier(
-                (first_weight, first_bias, second_weight, value)
+            value, first_turned, bias_turned, second_turned = lax.optimization_barrier(
+                (value, first_turned, bias_turned, second_turned)
             )
-            held = (turn(first_w, 1), turn(first_b, 0), turn(second_w, 0))
-            value, first_turned, bias_turned, second_turned = lax.optimization_barrier((value, *held))
         if hop == 1:
             x, third_w, _ = lax.optimization_barrier((features, third_weight, value))
             pre_first = jnp.dot(x, first_turned, preferred_element_type=f32) + bias_turned
@@ -489,9 +542,11 @@
         result = pl.pallas_call(
             functools.partial(far_kernel, slots, class_half, stride, last),
             out_shape=(half_type, half_type) if last else (out_type, value_type),
-            in_specs=[smem()] * 4 + [vmem()] + [hbm()] * (6 + len(extra)),
+            in_specs=[hbm()] * (8 + len(extra)),
             out_specs=(vmem(), vmem()) if last else (hbm(), hbm()),
             scratch_shapes=[
+                pltpu.SMEM(ints.shape, jnp.int32),
+                pltpu.VMEM((blocks, block), jnp.int32),
                 pltpu.VMEM((peers, packed, LANES), bf16),
                 pltpu.VMEM((2 * (local_count + halo_count), block, block), bf16),
                 pltpu.VMEM((rows, LANES), bf16),
@@ -499,10 +554,10 @@
                 acc,
             ]
             + ([pltpu.VMEM((rows, LANES), bf16)] if last else sending + [peer_sems])
-            + [pltpu.SemaphoreType.DMA((7,))],
+            + [pltpu.SemaphoreType.DMA((9,))],
             compiler_params=params(),
             name="far_last" if last else "far",
-        )(core_arg, meta, counts, idx, degree_blocks, landed, own_halo, other_halo, value, own_local, other_local, *extra)
+        )(ints, degree_blocks, landed, own_halo, other_halo, value, own_local, other_local, *extra)
         if last:
             keep, send = result
         else:

time: 182 us -> 242 us (1.33)
  Pallas kernels: 35.9 us -> 106 us
  other arithmetic: 17.6 us -> 10.9 us
  local copies, waits for them, and re-layouts: 12.8 us -> 8.62 us
  waiting for transfers between devices: 54.2 us -> 57.3 us
    pallas_call x0 -> x1, Pallas kernels: none -> 72.7 us  [shards(): pl.pallas_call(turn_kernel, out_shape=(jax.ShapeDtypeStruct(first_w.shape...]
    select_n x3 -> x0, other arithmetic: 5.58 us -> none  [turn(): return jnp.where(core == 0, array, jnp.concatenate([high, low], axis))]
    slice x3 -> x0, local copies, waits for them, and re-layouts: 4.07 us -> none  [split(): lax.slice_in_dim(x, half, 2 * half, axis=axis)]
    pallas_call x4, Pallas kernels: 27.2 us -> 24.2 us  [shards(): pl.pallas_call(functools.partial(far_kernel, slots, class_half, stride, l...]
    unnamed x48 -> x52, local copies, waits for them, and re-layouts: 6.34 us -> 6.77 us
  transfers between devices with their start and end apart: 24 -> 24, of which waited for: 17 -> 17; matrix products, arithmetic and copies ran while one was open for 22% -> 12% of each run, Pallas kernels for 0% -> 30%
where the time goes in v8:
time: 242 us
  Pallas kernels  106 us (44%)
  waiting for transfers between devices  57.3 us (24%)
  starting transfers between devices  33.1 us (14%)
  matrix products  24.6 us (10%)
  other arithmetic  10.9 us (5%)
  local copies, waits for them, and re-layouts  8.62 us (4%)
    pallas_call x1, Pallas kernels, shards(): pl.pallas_call(turn_kernel, out_shape=(jax.ShapeDtypeStruct(first_w.shape...  72.7 us
    ppermute x12, waiting for transfers between devices, exchange(): return lax.ppermute(x, ('dom', 'col'), pairs)  40.1 us
    pallas_call x4, Pallas kernels, shards(): pl.pallas_call(functools.partial(far_kernel, slots, class_half, stride, l...  24.2 us
    all_to_all x4, starting transfers between devices, shards(): landed = lax.all_to_all(out, 'dom', split_axis=0, concat_axis=0, tiled=True)  21.4 us
    all_to_all x4, waiting for transfers between devices, shards(): landed = lax.all_to_all(out, 'dom', split_axis=0, concat_axis=0, tiled=True)  13.2 us
    ppermute x12, starting transfers between devices, exchange(): return lax.ppermute(x, ('dom', 'col'), pairs)  10.2 us
    dot_general x1, matrix products, shards(): pre_second = jnp.dot(tied, second_turned, preferred_element_type=f32)  7.25 us
    convert_element_type x1, other arithmetic, gelu_parts(): return ((x * half_up).astype(bf16), slope.astype(bf16))  6.92 us
  transfers between devices with their start and end apart: 24, of which 17 were waited for; matrix products, arithmetic and copies ran while one was open for 12% of the time, Pallas kernels for 30%

profile of v8, /device:TPU:0, one launch (start us, length us, event | category | flops | bytes accessed | tf_op | source)
XLA Modules:
  0.0 241.6 jit_solution(16678217356912211627)
XLA Ops:
  0.7 5.5 %first.1 = (bf16[8,192,128]{2,1,0:T(8,128)(2,1)}, bf16[3072,128]{1,0:T(8,128)(2,1)}) custom-call(s32[1]{0:T(128)} %bitcast.core_ref, s32[8]{0:T(128)} %bitcast.54, s32[256]{0:T(256)} %bitcast.64, s32[8,256]{1,0:T(8,128)} %bitcast.50, s32[1,256]{1,0:T(1,128)} %labels_ref.1, f32[172,1,256]{2,1,0:T(1,128)} %bitcast.49, s32[24,128]{1,0:T(8,128)} %bitcast.44), custom_call_target="tpu_custom_call" | custom-call | tf_op jit(solution)/shard_map/first/pallas_call | solution.py:463
  6.2 7.4 %all-to-all-start = ((bf16[8,192,128]{2,1,0:T(8,128)(2,1)}), bf16[8,192,128]{2,1,0:T(8,128)(2,1)S(1)}, u32[]{:S(2)}, u32[]{:S(2)}) async-start(bf16[8,192,128]{2,1,0:T(8,128)(2,1)} %get-tuple-element.63), calls=%async_computation | async-start | bytes 786432 | tf_op jit(solution)/shard_map/all_to_all | solution.py:518
  13.7 0.5 collective-permute-start.2
  14.2 72.7 %turn.1 = (bf16[128,1024]{1,0:T(8,128)(2,1)}, f32[1,1024]{1,0:T(1,128)}, bf16[1024,1024]{1,0:T(8,128)(2,1)}) custom-call(s32[1]{0:T(128)} %bitcast.core_ref, bf16[128,1024]{1,0:T(8,128)(2,1)} %first_ref, f32[1,1024]{1,0:T(1,128)} %bitcast.53, bf16[1024,1024]{1,0:T(8,128)(2,1)} %second_ref), custom_call_target="tpu_custom_call" | custom-call | tf_op jit(solution)/shard_map/turn/pallas_call | solution.py:482
  87.1 1.0 collective-permute-done
  88.2 0.7 concatenate.71.ints_ref
  88.9 0.8 copy-done.1
  89.7 0.2 copy-done.2
  89.8 0.7 copy-done.8
  90.6 6.2 %far.3 = (bf16[8,192,128]{2,1,0:T(8,128)(2,1)}, bf16[3072,128]{1,0:T(8,128)(2,1)}) custom-call(s32[3072]{0:T(1024)} %concatenate.71.ints_ref, s32[24,128]{1,0:T(8,128)} %bitcast.45, bf16[8,192,128]{2,1,0:T(8,128)(2,1)} %copy-done.8, bf16[16,128,128]{2,1,0:T(8,128)(2,1)} %bitcast.35, bf16[16,128,128]{2,1,0:T(8,128)(2,1)} %copy-done.1, ...), custom_call_target="tpu_custom_call" | custom-call | tf_op jit(solution)/shard_map/far/pallas_call | solution.py:542
  96.9 6.0 %all-to-all-start.1 = ((bf16[8,192,128]{2,1,0:T(8,128)(2,1)}), bf16[8,192,128]{2,1,0:T(8,128)(2,1)S(1)}, u32[]{:S(2)}, u32[]{:S(2)}) async-start(bf16[8,192,128]{2,1,0:T(8,128)(2,1)} %get-tuple-element.74), calls=%async_computation.1 | async-start | bytes 786432 | tf_op jit(solution)/shard_map/all_to_all | solution.py:518
  102.9 0.9 maximum_select_fusion.2
  103.9 5.7 %add_convert_fusion.1 = (bf16[1536,1024]{1,0:T(8,128)(2,1)}, bf16[1536,1024]{1,0:T(8,128)(2,1)}) fusion(f32[1024]{0:T(1024)S(1)} %bitcast.66, bf16[1536,128]{1,0:T(8,128)(2,1)S(1)} %copy-done, bf16[128,1024]{1,0:T(8,128)(2,1)S(1)} %copy-done.23), kind=kOutput, calls=%fused_computation.7 | convolution fusion | flops 430964736 | bytes 6950912 | tf_op jit(solution)/shard_map/dot_general | solution.py:526
  109.5 5.4 %all-to-all-done.1.recv_ref = bf16[8,192,128]{2,1,0:T(8,128)(2,1)S(1)} async-done(((bf16[8,192,128]{2,1,0:T(8,128)(2,1)}), bf16[8,192,128]{2,1,0:T(8,128)(2,1)S(1)}, u32[]{:S(2)}, u32[]{:S(2)}) %all-to-all-start.1) | async-done | bytes 393248 | tf_op jit(solution)/shard_map/all_to_all | solution.py:518
  114.9 0.7 copy-done.9
  115.7 6.2 %far.4 = (bf16[8,192,128]{2,1,0:T(8,128)(2,1)}, bf16[3072,128]{1,0:T(8,128)(2,1)}) custom-call(s32[3072]{0:T(1024)} %concatenate.71.ints_ref, s32[24,128]{1,0:T(8,128)} %bitcast.46, bf16[8,192,128]{2,1,0:T(8,128)(2,1)} %copy-done.9, bf16[16,128,128]{2,1,0:T(8,128)(2,1)} %bitcast.36, bf16[16,128,128]{2,1,0:T(8,128)(2,1)} %copy-done.1, ...), custom_call_target="tpu_custom_call" | custom-call | tf_op jit(solution)/shard_map/far/pallas_call | solution.py:542
  121.8 3.7 %all-to-all-start.2 = ((bf16[8,192,128]{2,1,0:T(8,128)(2,1)}), bf16[8,192,128]{2,1,0:T(8,128)(2,1)S(1)}, u32[]{:S(2)}, u32[]{:S(2)}) async-start(bf16[8,192,128]{2,1,0:T(8,128)(2,1)} %get-tuple-element.76), calls=%async_computation.2 | async-start | bytes 786432 | tf_op jit(solution)/shard_map/all_to_all | solution.py:518
  125.6 7.2 %fusion.9 = f32[1536,1024]{1,0:T(8,128)} fusion(bf16[1536,1024]{1,0:T(8,128)(2,1)} %get-tuple-element.78, bf16[1024,1024]{1,0:T(8,128)(2,1)S(1)} %copy-done.21), kind=kOutput, calls=%fused_computation.58 | convolution fusion | flops 3221225472 | bytes 11534336 | tf_op jit(solution)/shard_map/dot_general | solution.py:533
  132.8 4.6 %all-to-all-done.2.recv_ref = bf16[8,192,128]{2,1,0:T(8,128)(2,1)S(1)} async-done(((bf16[8,192,128]{2,1,0:T(8,128)(2,1)}), bf16[8,192,128]{2,1,0:T(8,128)(2,1)S(1)}, u32[]{:S(2)}, u32[]{:S(2)}) %all-to-all-start.2) | async-done | bytes 393248 | tf_op jit(solution)/shard_map/all_to_all | solution.py:518
  137.4 0.7 copy-done.10
  138.2 6.1 %far.5 = (bf16[8,192,128]{2,1,0:T(8,128)(2,1)}, bf16[3072,128]{1,0:T(8,128)(2,1)}) custom-call(s32[3072]{0:T(1024)} %concatenate.71.ints_ref, s32[24,128]{1,0:T(8,128)} %bitcast.47, bf16[8,192,128]{2,1,0:T(8,128)(2,1)} %copy-done.10, bf16[16,128,128]{2,1,0:T(8,128)(2,1)} %bitcast.37, bf16[16,128,128]{2,1,0:T(8,128)(2,1)} %copy-done.1, ...), custom_call_target="tpu_custom_call" | custom-call | tf_op jit(solution)/shard_map/far/pallas_call | solution.py:542
  144.3 4.3 %all-to-all-start.3 = ((bf16[8,192,128]{2,1,0:T(8,128)(2,1)}), bf16[8,192,128]{2,1,0:T(8,128)(2,1)}, u32[]{:S(2)}, u32[]{:S(2)}) async-start(bf16[8,192,128]{2,1,0:T(8,128)(2,1)} %get-tuple-element.88), calls=%async_computation.3 | async-start | bytes 786432 | tf_op jit(solution)/shard_map/all_to_all | solution.py:518
  148.7 6.9 %add_convert_fusion = (bf16[1536,1024]{1,0:T(8,128)(2,1)S(1)}, bf16[1536,1024]{1,0:T(8,128)(2,1)}) fusion(f32[1536,1024]{1,0:T(8,128)} %fusion.9, f32[1024]{0:T(1024)S(1)} %copy-done.14), kind=kLoop, calls=%fused_computation.2 | loop fusion | flops 28311552 | bytes 12587008 | tf_op jit(solution)/shard_map/convert_element_type | solution.py:354
  155.6 1.2 add_convert_fusion.3.rest_0_
  156.8 3.2 %all-to-all-done.3.recv_ref = bf16[8,192,128]{2,1,0:T(8,128)(2,1)} async-done(((bf16[8,192,128]{2,1,0:T(8,128)(2,1)}), bf16[8,192,128]{2,1,0:T(8,128)(2,1)}, u32[]{:S(2)}, u32[]{:S(2)}) %all-to-all-start.3) | async-done | bytes 393248 | tf_op jit(solution)/shard_map/all_to_all | solution.py:518
  160.0 5.8 %far_last.1 = (bf16[1536,128]{1,0:T(8,128)(2,1)}, bf16[1536,128]{1,0:T(8,128)(2,1)}) custom-call(s32[3072]{0:T(1024)} %concatenate.71.ints_ref, s32[24,128]{1,0:T(8,128)} %bitcast.48, bf16[8,192,128]{2,1,0:T(8,128)(2,1)} %all-to-all-done.3.recv_ref, bf16[16,128,128]{2,1,0:T(8,128)(2,1)} %bitcast.38, bf16[16,128,128]{2,1,0:T(8,128)(2,1)} %copy-done.1, ...), custom_call_target="tpu_custom_call" | custom-call | tf_op jit(solution)/shard_map/far_last/pallas_call | solution.py:542
  165.9 1.1 constant_dynamic-update-slice_fusion.1
  167.0 1.0 collective-permute-done.3
  167.9 1.1 constant_dynamic-update-slice_fusion
  169.0 2.2 fusion.8
  171.3 0.6 convolution_convert_fusion.3
  171.9 1.4 copy-done.3
  173.3 3.6 %fusion.4 = (bf16[1024]{0:T(1024)(128)(2,1)S(1)}, f32[1536,1024]{1,0:T(8,128)S(1)}) fusion(bf16[1536,1024]{1,0:T(8,128)(2,1)S(1)} %copy-done.3, bf16[1536,1024]{1,0:T(8,128)(2,1)S(1)} %get-tuple-element.116, bf16[1024,1024]{1,0:T(8,128)(2,1)S(1)} %copy-done.22), kind=kOutput, calls=%fused_computation.53 | convolution fusion | flops 3227515904 | bytes 14682112 | tf_op jit(solution)/shard_map/dot_general | solution.py:583
  176.9 0.8 convolution_convert_fusion.4
  177.7 1.1 copy-done.4
  178.8 1.0 convolution_convert_fusion.2
  179.9 0.2 collective-permute-start.12
  180.2 1.4 convolution_convert_fusion
  181.6 0.4 collective-permute-start.4
  182.0 0.6 convolution_convert_fusion.5
  182.7 0.2 add_convert_fusion.4
  182.9 1.5 collective-permute-start.13
  184.4 1.4 add_convert_fusion.2
  185.9 1.0 collective-permute-start.5
  186.9 2.9 %collective-permute-done.13 = bf16[288,512]{1,0:T(8,128)(2,1)S(1)} collective-permute-done((bf16[288,512]{1,0:T(8,128)(2,1)S(1)}, bf16[288,512]{1,0:T(8,128)(2,1)S(1)}, u32[]{:S(2)}, u32[]{:S(2)}) %collective-permute-start.13) | collective-permute-done | bytes 294944 | tf_op jit(solution)/shard_map/ppermute | solution.py:367
  189.8 4.1 %collective-permute-done.5 = bf16[384,512]{1,0:T(8,128)(2,1)S(1)} collective-permute-done((bf16[384,512]{1,0:T(8,128)(2,1)S(1)}, bf16[384,512]{1,0:T(8,128)(2,1)S(1)}, u32[]{:S(2)}, u32[]{:S(2)}) %collective-permute-start.5) | collective-permute-done | bytes 393248 | tf_op jit(solution)/shard_map/ppermute | solution.py:367
  194.1 1.0 collective-permute-start.6
  195.1 1.2 collective-permute-start.14
  196.3 3.6 %collective-permute-done.6 = bf16[384,256]{1,0:T(8,128)(2,1)S(1)} collective-permute-done((bf16[384,256]{1,0:T(8,128)(2,1)S(1)}, bf16[384,256]{1,0:T(8,128)(2,1)S(1)}, u32[]{:S(2)}, u32[]{:S(2)}) %collective-permute-start.6) | collective-permute-done | bytes 196640 | tf_op jit(solution)/shard_map/ppermute | solution.py:367
  200.0 1.0 collective-permute-start.7
  201.0 0.5 collective-permute-done.14
  201.5 5.1 %collective-permute-done.7 = bf16[384,128]{1,0:T(8,128)(2,1)S(1)} collective-permute-done((bf16[384,128]{1,0:T(8,128)(2,1)S(1)}, bf16[384,128]{1,0:T(8,128)(2,1)S(1)}, u32[]{:S(2)}, u32[]{:S(2)}) %collective-permute-start.7) | collective-permute-done | bytes 98336 | tf_op jit(solution)/shard_map/ppermute | solution.py:367
  206.7 3.0 %collective-permute-start.15 = (bf16[288,128]{1,0:T(8,128)(2,1)S(1)}, bf16[288,128]{1,0:T(8,128)(2,1)S(1)}, u32[]{:S(2)}, u32[]{:S(2)}) collective-permute-start(bf16[288,128]{1,0:T(8,128)(2,1)S(1)} %broadcast_select_fusion.5), channel_id=1, source_target_pairs={{0,8},{1,9},{2,10},{3,11},{4,12},{5,13},{6,14},{7,15},{8,0},{9,1},... | collective-permute-start | bytes 221192 | tf_op jit(solution)/shard_map/ppermute | solution.py:367
  209.7 4.5 %collective-permute-done.8 = bf16[384,128]{1,0:T(8,128)(2,1)S(1)} collective-permute-done((bf16[384,128]{1,0:T(8,128)(2,1)S(1)}, bf16[384,128]{1,0:T(8,128)(2,1)S(1)}, u32[]{:S(2)}, u32[]{:S(2)}) %collective-permute-start.8) | collective-permute-done | bytes 98336 | tf_op jit(solution)/shard_map/ppermute | solution.py:367
  214.4 1.4 collective-permute-done.15
  215.9 7.0 %collective-permute-done.9 = bf16[384,256]{1,0:T(8,128)(2,1)S(1)} collective-permute-done((bf16[384,256]{1,0:T(8,128)(2,1)S(1)}, bf16[384,256]{1,0:T(8,128)(2,1)S(1)}, u32[]{:S(2)}, u32[]{:S(2)}) %collective-permute-start.9) | collective-permute-done | bytes 196640 | tf_op jit(solution)/shard_map/ppermute | solution.py:367
  223.2 5.9 %collective-permute-done.17 = bf16[288,256]{1,0:T(8,128)(2,1)S(1)} collective-permute-done((bf16[288,256]{1,0:T(8,128)(2,1)S(1)}, bf16[288,256]{1,0:T(8,128)(2,1)S(1)}, u32[]{:S(2)}, u32[]{:S(2)}) %collective-permute-start.17) | collective-permute-done | bytes 147488 | tf_op jit(solution)/shard_map/ppermute | solution.py:367
  229.2 1.3 collective-permute-start.18
  230.5 0.3 collective-permute-done.10
  230.8 0.2 maximum_select_fusion.mine_one
  231.1 4.9 %collective-permute-done.18 = bf16[288,512]{1,0:T(8,128)(2,1)S(1)} collective-permute-done((bf16[288,512]{1,0:T(8,128)(2,1)S(1)}, bf16[288,512]{1,0:T(8,128)(2,1)S(1)}, u32[]{:S(2)}, u32[]{:S(2)}) %collective-permute-start.18) | collective-permute-done | bytes 294944 | tf_op jit(solution)/shard_map/ppermute | solution.py:367
  236.0 0.2 maximum_select_fusion.1.mine_two
  236.3 2.0 collective-permute-done.19.theirs_two
  238.3 3.2 %finish.1 = (f32[128,1024]{1,0:T(8,128)}, f32[1,1024]{1,0:T(1,128)}, f32[1024,1024]{1,0:T(8,128)}, f32[1,1024]{1,0:T(1,128)}, f32[172,1024]{1,0:T(8,128)}) custom-call(s32[1]{0:T(128)} %bitcast.core_ref, bf16[384,1024]{1,0:T(8,128)(2,1)S(1)} %maximum_select_fusion.mine_one, bf16[384,1024]{1,0:T(8,128)(2,1)S(1)} %collective-permute-done.11.theirs_one, ...), custom_call_target="tpu_custom_call" | custom-call | tf_op jit(solution)/shard_map/finish/pallas_call | solution.py:611
  (93 shorter events, 2.1 us)
Async XLA Ops:
  0.6 103.2 %copy-start = (bf16[1536,128]{1,0:T(8,128)(2,1)S(1)}, bf16[1536,128]{1,0:T(8,128)(2,1)}, u32[]{:S(2)}) copy-start(bf16[1536,128]{1,0:T(8,128)(2,1)} %param.18) | copy-start | bytes 1179652
  0.7 87.5 %copy-start.15 = (s32[1,8]{1,0:T(1,128)S(1)}, s32[1,8]{1,0:T(1,128)}, u32[]{:S(2)}) copy-start(s32[1,8]{1,0:T(1,128)} %param.31) | copy-start | bytes 100
  0.7 86.5 %copy-start.13 = (s32[1,8,256]{2,1,0:T(8,128)S(1)}, s32[1,8,256]{2,1,0:T(8,128)}, u32[]{:S(2)}) copy-start(s32[1,8,256]{2,1,0:T(8,128)} %param.30) | copy-start | bytes 24580
  0.7 86.3 %copy-start.16 = (s32[1,1,16]{2,1,0:T(1,128)S(1)}, s32[1,1,16]{2,1,0:T(1,128)}, u32[]{:S(2)}) copy-start(s32[1,1,16]{2,1,0:T(1,128)} %param.25) | copy-start | bytes 196
  0.7 86.3 %copy-start.17 = (s32[1,1,16]{2,1,0:T(1,128)S(1)}, s32[1,1,16]{2,1,0:T(1,128)}, u32[]{:S(2)}) copy-start(s32[1,1,16]{2,1,0:T(1,128)} %param.26) | copy-start | bytes 196
  0.7 86.3 %copy-start.18 = (s32[1,1,16]{2,1,0:T(1,128)S(1)}, s32[1,1,16]{2,1,0:T(1,128)}, u32[]{:S(2)}) copy-start(s32[1,1,16]{2,1,0:T(1,128)} %param.28) | copy-start | bytes 196
  0.7 86.3 %copy-start.19 = (s32[1,1,16]{2,1,0:T(1,128)S(1)}, s32[1,1,16]{2,1,0:T(1,128)}, u32[]{:S(2)}) copy-start(s32[1,1,16]{2,1,0:T(1,128)} %param.29) | copy-start | bytes 196
  6.2 82.7 %all-to-all-start = ((bf16[8,192,128]{2,1,0:T(8,128)(2,1)}), bf16[8,192,128]{2,1,0:T(8,128)(2,1)S(1)}, u32[]{:S(2)}, u32[]{:S(2)}) async-start(bf16[8,192,128]{2,1,0:T(8,128)(2,1)} %get-tuple-element.63), calls=%async_computation | async-start | bytes 786432 | tf_op jit(solution)/shard_map/all_to_all | solution.py:518
  13.6 83.2 %copy-start.11 = (bf16[1024,172]{0,1:T(8,128)(2,1)S(1)}, bf16[1024,172]{0,1:T(8,128)(2,1)}, u32[]{:S(2)}) copy-start(bf16[1024,172]{0,1:T(8,128)(2,1)} %param.23) | copy-start | bytes 1056772
  13.6 83.2 %copy-start.20 = (pred[128]{0:T(512)(128)(4,1)S(1)}, pred[128]{0:T(512)(128)(4,1)}, u32[]{:S(2)}) copy-start(pred[128]{0:T(512)(128)(4,1)} %constant.33.clone.1) | copy-start | bytes 388
  13.6 75.3 %collective-permute-start.1 = (bf16[16,128,128]{2,1,0:T(8,128)(2,1)}, bf16[16,128,128]{2,1,0:T(8,128)(2,1)S(1)}, u32[]{:S(2)}, u32[]{:S(2)}) collective-permute-start(bf16[16,128,128]{2,1,0:T(8,128)(2,1)} %bitcast.34), channel_id=1, source_target_pairs={{0,1},{1,0},{2,3},{3,2},{4,5},{5,4},{6,7},{7,6},{8,9},{9,8},{10,11... | collective-permute-start | bytes 1572872 | tf_op jit(solution)/shard_map/ppermute | solution.py:358
  13.7 75.2 %collective-permute-start.2 = (bf16[16,128,128]{2,1,0:T(8,128)(2,1)}, bf16[16,128,128]{2,1,0:T(8,128)(2,1)S(1)}, u32[]{:S(2)}, u32[]{:S(2)}) collective-permute-start(bf16[16,128,128]{2,1,0:T(8,128)(2,1)} %bitcast.39), channel_id=1, source_target_pairs={{0,1},{1,0},{2,3},{3,2},{4,5},{5,4},{6,7},{7,6},{8,9},{9,8},{10,11... | collective-permute-start | bytes 1572872 | tf_op jit(solution)/shard_map/ppermute | solution.py:358
  14.2 88.7 %slice-start = ((bf16[1024,172]{0,1:T(8,128)(2,1)}), bf16[1024,84]{0,1:T(8,128)(2,1)S(1)}, s32[]{:S(2)}) async-start(bf16[1024,172]{0,1:T(8,128)(2,1)} %param.23), calls=%async_computation.4 | async-start | bytes 360448 | tf_op jit(solution)/shard_map/slice | solution.py:528
  87.0 1.1 collective-permute-start
  88.9 15.0 %copy-start.23 = (bf16[128,1024]{1,0:T(8,128)(2,1)S(1)}, bf16[128,1024]{1,0:T(8,128)(2,1)}, u32[]{:S(2)}) copy-start(bf16[128,1024]{1,0:T(8,128)(2,1)} %get-tuple-element.70) | copy-start | bytes 786436
  88.9 15.0 %copy-start.24 = (f32[1,1024]{1,0:T(1,128)S(1)}, f32[1,1024]{1,0:T(1,128)}, u32[]{:S(2)}) copy-start(f32[1,1024]{1,0:T(1,128)} %get-tuple-element.71) | copy-start | bytes 12292
  88.9 0.8 copy-start.1
  88.9 0.9 copy-start.2
  89.8 0.7 copy-start.8
  96.9 18.1 %all-to-all-start.1 = ((bf16[8,192,128]{2,1,0:T(8,128)(2,1)}), bf16[8,192,128]{2,1,0:T(8,128)(2,1)S(1)}, u32[]{:S(2)}, u32[]{:S(2)}) async-start(bf16[8,192,128]{2,1,0:T(8,128)(2,1)} %get-tuple-element.74), calls=%async_computation.1 | async-start | bytes 786432 | tf_op jit(solution)/shard_map/all_to_all | solution.py:518
  109.5 16.1 %copy-start.21 = (bf16[1024,1024]{1,0:T(8,128)(2,1)S(1)}, bf16[1024,1024]{1,0:T(8,128)(2,1)}, u32[]{:S(2)}) copy-start(bf16[1024,1024]{1,0:T(8,128)(2,1)} %get-tuple-element.79) | copy-start | bytes 6291460
  114.9 0.7 copy-start.9
  121.8 15.6 %all-to-all-start.2 = ((bf16[8,192,128]{2,1,0:T(8,128)(2,1)}), bf16[8,192,128]{2,1,0:T(8,128)(2,1)S(1)}, u32[]{:S(2)}, u32[]{:S(2)}) async-start(bf16[8,192,128]{2,1,0:T(8,128)(2,1)} %get-tuple-element.76), calls=%async_computation.2 | async-start | bytes 786432 | tf_op jit(solution)/shard_map/all_to_all | solution.py:518
  132.8 15.8 %copy-start.14 = (f32[1024]{0:T(1024)S(1)}, f32[1024]{0:T(1024)}, u32[]{:S(2)}) copy-start(f32[1024]{0:T(1024)} %param.22) | copy-start | bytes 12292
  137.4 0.7 copy-start.10
  144.3 15.7 %all-to-all-start.3 = ((bf16[8,192,128]{2,1,0:T(8,128)(2,1)}), bf16[8,192,128]{2,1,0:T(8,128)(2,1)}, u32[]{:S(2)}, u32[]{:S(2)}) async-start(bf16[8,192,128]{2,1,0:T(8,128)(2,1)} %get-tuple-element.88), calls=%async_computation.3 | async-start | bytes 786432 | tf_op jit(solution)/shard_map/all_to_all | solution.py:518
  148.6 7.0 %copy-start.5 = (bf16[3072,128]{1,0:T(8,128)(2,1)S(1)}, bf16[3072,128]{1,0:T(8,128)(2,1)}, u32[]{:S(2)}) copy-start(bf16[3072,128]{1,0:T(8,128)(2,1)} %get-tuple-element.86.value_in_ref) | copy-start | bytes 2359300
  148.6 6.9 %copy-start.6 = (bf16[3072,128]{1,0:T(8,128)(2,1)S(1)}, bf16[3072,128]{1,0:T(8,128)(2,1)}, u32[]{:S(2)}) copy-start(bf16[3072,128]{1,0:T(8,128)(2,1)} %get-tuple-element.85.value_in_ref) | copy-start | bytes 2359300
  148.7 6.9 %copy-start.7 = (bf16[3072,128]{1,0:T(8,128)(2,1)S(1)}, bf16[3072,128]{1,0:T(8,128)(2,1)}, u32[]{:S(2)}) copy-start(bf16[3072,128]{1,0:T(8,128)(2,1)} %get-tuple-element.84.value_in_ref) | copy-start | bytes 2359300
  165.8 2.1 collective-permute-start.3
  169.0 2.3 copy-start.12
  169.0 2.9 %copy-start.22 = (bf16[1024,1024]{1,0:T(8,128)(2,1)S(1)}, bf16[1024,1024]{1,0:T(8,128)(2,1)}, u32[]{:S(2)}) copy-start(bf16[1024,1024]{1,0:T(8,128)(2,1)} %get-tuple-element.79) | copy-start | bytes 6291460
  171.3 2.0 copy-start.3
  176.9 1.9 copy-start.4
  179.9 2.7 %collective-permute-start.12 = (bf16[288,1024]{1,0:T(8,128)(2,1)S(1)}, bf16[288,1024]{1,0:T(8,128)(2,1)S(1)}, u32[]{:S(2)}, u32[]{:S(2)}) collective-permute-start(bf16[288,1024]{1,0:T(8,128)(2,1)S(1)} %pad_maximum_fusion), channel_id=1, source_target_pairs={{0,1},{1,0},{2,3},{3,2},{4,5},{5,4},{6,7},{7,6},{8,9},{9,8},{10,11... | collective-permute-start | bytes 1769480 | tf_op jit(solution)/shard_map/ppermute | solution.py:358
  181.6 2.8 %collective-permute-start.4 = (bf16[384,1024]{1,0:T(8,128)(2,1)S(1)}, bf16[384,1024]{1,0:T(8,128)(2,1)S(1)}, u32[]{:S(2)}, u32[]{:S(2)}) collective-permute-start(bf16[384,1024]{1,0:T(8,128)(2,1)S(1)} %convolution_convert_fusion), channel_id=1, source_target_pairs={{0,1},{1,0},{2,3},{3,2},{4,5},{5,4},{6,7},{7,6},{8,9},{9,8},{10,11... | collective-permute-start | bytes 2359304 | tf_op jit(solution)/shard_map/ppermute | solution.py:358
  182.9 6.8 %collective-permute-start.13 = (bf16[288,512]{1,0:T(8,128)(2,1)S(1)}, bf16[288,512]{1,0:T(8,128)(2,1)S(1)}, u32[]{:S(2)}, u32[]{:S(2)}) collective-permute-start(bf16[288,512]{1,0:T(8,128)(2,1)S(1)} %broadcast_select_fusion.1), channel_id=1, source_target_pairs={{0,2},{1,5},{2,0},{3,7},{4,6},{5,1},{6,4},{7,3},{8,10},{9,13},{10,... | collective-permute-start | bytes 884744 | tf_op jit(solution)/shard_map/ppermute | solution.py:367
  185.9 8.1 %collective-permute-start.5 = (bf16[384,512]{1,0:T(8,128)(2,1)S(1)}, bf16[384,512]{1,0:T(8,128)(2,1)S(1)}, u32[]{:S(2)}, u32[]{:S(2)}) collective-permute-start(bf16[384,512]{1,0:T(8,128)(2,1)S(1)} %broadcast_select_fusion), channel_id=1, source_target_pairs={{0,2},{1,5},{2,0},{3,7},{4,6},{5,1},{6,4},{7,3},{8,10},{9,13},{10,... | collective-permute-start | bytes 1179656 | tf_op jit(solution)/shard_map/ppermute | solution.py:367
  194.1 5.7 %collective-permute-start.6 = (bf16[384,256]{1,0:T(8,128)(2,1)S(1)}, bf16[384,256]{1,0:T(8,128)(2,1)S(1)}, u32[]{:S(2)}, u32[]{:S(2)}) collective-permute-start(bf16[384,256]{1,0:T(8,128)(2,1)S(1)} %broadcast_select_fusion.2), channel_id=1, source_target_pairs={{0,4},{1,3},{2,6},{3,1},{4,0},{5,7},{6,2},{7,5},{8,12},{9,11},{10,... | collective-permute-start | bytes 589832 | tf_op jit(solution)/shard_map/ppermute | solution.py:367
  195.1 6.3 %collective-permute-start.14 = (bf16[288,256]{1,0:T(8,128)(2,1)S(1)}, bf16[288,256]{1,0:T(8,128)(2,1)S(1)}, u32[]{:S(2)}, u32[]{:S(2)}) collective-permute-start(bf16[288,256]{1,0:T(8,128)(2,1)S(1)} %broadcast_select_fusion.3), channel_id=1, source_target_pairs={{0,4},{1,3},{2,6},{3,1},{4,0},{5,7},{6,2},{7,5},{8,12},{9,11},{10,... | collective-permute-start | bytes 442376 | tf_op jit(solution)/shard_map/ppermute | solution.py:367
  200.0 6.6 %collective-permute-start.7 = (bf16[384,128]{1,0:T(8,128)(2,1)S(1)}, bf16[384,128]{1,0:T(8,128)(2,1)S(1)}, u32[]{:S(2)}, u32[]{:S(2)}) collective-permute-start(bf16[384,128]{1,0:T(8,128)(2,1)S(1)} %broadcast_select_fusion.4), channel_id=1, source_target_pairs={{0,8},{1,9},{2,10},{3,11},{4,12},{5,13},{6,14},{7,15},{8,0},{9,1},... | collective-permute-start | bytes 294920 | tf_op jit(solution)/shard_map/ppermute | solution.py:367
  206.6 7.6 %collective-permute-start.8 = (bf16[384,128]{1,0:T(8,128)(2,1)S(1)}, bf16[384,128]{1,0:T(8,128)(2,1)S(1)}, u32[]{:S(2)}, u32[]{:S(2)}) collective-permute-start(bf16[384,128]{1,0:T(8,128)(2,1)S(1)} %add_convert_fusion.9), channel_id=1, source_target_pairs={{0,8},{1,9},{2,10},{3,11},{4,12},{5,13},{6,14},{7,15},{8,0},{9,1},... | collective-permute-start | bytes 294920 | tf_op jit(solution)/shard_map/ppermute | solution.py:367
  206.7 9.0 %collective-permute-start.15 = (bf16[288,128]{1,0:T(8,128)(2,1)S(1)}, bf16[288,128]{1,0:T(8,128)(2,1)S(1)}, u32[]{:S(2)}, u32[]{:S(2)}) collective-permute-start(bf16[288,128]{1,0:T(8,128)(2,1)S(1)} %broadcast_select_fusion.5), channel_id=1, source_target_pairs={{0,8},{1,9},{2,10},{3,11},{4,12},{5,13},{6,14},{7,15},{8,0},{9,1},... | collective-permute-start | bytes 221192 | tf_op jit(solution)/shard_map/ppermute | solution.py:367
  214.3 8.6 %collective-permute-start.9 = (bf16[384,256]{1,0:T(8,128)(2,1)S(1)}, bf16[384,256]{1,0:T(8,128)(2,1)S(1)}, u32[]{:S(2)}, u32[]{:S(2)}) collective-permute-start(bf16[384,256]{1,0:T(8,128)(2,1)S(1)} %maximum_select_fusion.5), channel_id=1, source_target_pairs={{0,4},{1,3},{2,6},{3,1},{4,0},{5,7},{6,2},{7,5},{8,12},{9,11},{10,... | collective-permute-start | bytes 589832 | tf_op jit(solution)/shard_map/ppermute | solution.py:367
  215.8 7.2 %collective-permute-start.16 = (bf16[288,128]{1,0:T(8,128)(2,1)S(1)}, bf16[288,128]{1,0:T(8,128)(2,1)S(1)}, u32[]{:S(2)}, u32[]{:S(2)}) collective-permute-start(bf16[288,128]{1,0:T(8,128)(2,1)S(1)} %add_convert_fusion.10), channel_id=1, source_target_pairs={{0,8},{1,9},{2,10},{3,11},{4,12},{5,13},{6,14},{7,15},{8,0},{9,1},... | collective-permute-start | bytes 221192 | tf_op jit(solution)/shard_map/ppermute | solution.py:367
  223.0 7.8 %collective-permute-start.10 = (bf16[384,512]{1,0:T(8,128)(2,1)S(1)}, bf16[384,512]{1,0:T(8,128)(2,1)S(1)}, u32[]{:S(2)}, u32[]{:S(2)}) collective-permute-start(bf16[384,512]{1,0:T(8,128)(2,1)S(1)} %maximum_select_fusion.3), channel_id=1, source_target_pairs={{0,2},{1,5},{2,0},{3,7},{4,6},{5,1},{6,4},{7,3},{8,10},{9,13},{10,... | collective-permute-start | bytes 1179656 | tf_op jit(solution)/shard_map/ppermute | solution.py:367
  223.1 6.0 %collective-permute-start.17 = (bf16[288,256]{1,0:T(8,128)(2,1)S(1)}, bf16[288,256]{1,0:T(8,128)(2,1)S(1)}, u32[]{:S(2)}, u32[]{:S(2)}) collective-permute-start(bf16[288,256]{1,0:T(8,128)(2,1)S(1)} %maximum_select_fusion.6), channel_id=1, source_target_pairs={{0,4},{1,3},{2,6},{3,1},{4,0},{5,7},{6,2},{7,5},{8,12},{9,11},{10,... | collective-permute-start | bytes 442376 | tf_op jit(solution)/shard_map/ppermute | solution.py:367
  229.2 6.8 %collective-permute-start.18 = (bf16[288,512]{1,0:T(8,128)(2,1)S(1)}, bf16[288,512]{1,0:T(8,128)(2,1)S(1)}, u32[]{:S(2)}, u32[]{:S(2)}) collective-permute-start(bf16[288,512]{1,0:T(8,128)(2,1)S(1)} %maximum_select_fusion.4), channel_id=1, source_target_pairs={{0,2},{1,5},{2,0},{3,7},{4,6},{5,1},{6,4},{7,3},{8,10},{9,13},{10,... | collective-permute-start | bytes 884744 | tf_op jit(solution)/shard_map/ppermute | solution.py:367
  231.0 7.3 %collective-permute-start.11 = (bf16[384,1024]{1,0:T(8,128)(2,1)S(1)}, bf16[384,1024]{1,0:T(8,128)(2,1)S(1)}, u32[]{:S(2)}, u32[]{:S(2)}) collective-permute-start(bf16[384,1024]{1,0:T(8,128)(2,1)S(1)} %maximum_select_fusion.mine_one), channel_id=1, source_target_pairs={{0,1},{1,0},{2,3},{3,2},{4,5},{5,4},{6,7},{7,6},{8,9},{9,8},{10,11... | collective-permute-start | bytes 2359304 | tf_op jit(solution)/shard_map/ppermute | solution.py:358
  236.2 2.1 collective-permute-start.19

commit v9 on v8

--- a/solution.py
+++ b/solution.py
@@ -201,22 +201,34 @@
         return self.ref[self.offset + i]
 
 
-def turn_kernel(core_ref, first_ref, bias_ref, second_ref, first_out, bias_out, second_out, sems):
+def turn_kernel(core_ref, first_ref, bias_ref, second_ref, first_out, bias_out, second_out, first_v, bias_v, second_v,
+                in_sems, out_sems):
     core = core_ref[0]
     half = second_ref.shape[0] // 2
-    copies = []
+    steps = []
     for i in range(2):
         source = pl.ds(pl.multiple_of((core ^ i) * half, half), half)
         to = pl.ds(i * half, half)
-        copies += [
-            pltpu.make_async_copy(second_ref.at[source], second_out.at[to], sems.at[3 * i]),
-            pltpu.make_async_copy(first_ref.at[:, source], first_out.at[:, to], sems.at[3 * i + 1]),
-            pltpu.make_async_copy(bias_ref.at[:, source], bias_out.at[:, to], sems.at[3 * i + 2]),
-        ]
-    for copy in copies:
-        copy.start()
-    for copy in copies:
-        copy.wait()
+        for k, (array, held, out) in enumerate(
+            (
+                (second_ref.at[source], second_v.at[to], second_out.at[to]),
+                (first_ref.at[:, source], first_v.at[:, to], first_out.at[:, to]),
+                (bias_ref.at[:, source], bias_v.at[:, to], bias_out.at[:, to]),
+            )
+        ):
+            steps.append(
+                (
+                    pltpu.make_async_copy(array, held, in_sems.at[3 * i + k]),
+                    pltpu.make_async_copy(held, out, out_sems.at[3 * i + k]),
+                )
+            )
+    for copy_in, unused in steps:
+        copy_in.start()
+    for copy_in, copy_out in steps:
+        copy_in.wait()
+        copy_out.start()
+    for unused, copy_out in steps:
+        copy_out.wait()
 
 
 def far_kernel(slots, class_half, stride, last, ints_ref, degree_in_ref, recv_ref,
@@ -488,7 +500,13 @@
         ),
         in_specs=[smem(), hbm(), hbm(), hbm()],
         out_specs=(hbm(), hbm(), hbm()),
-        scratch_shapes=[pltpu.SemaphoreType.DMA((6,))],
+        scratch_shapes=[
+            pltpu.VMEM(first_w.shape, bf16),
+            pltpu.VMEM((1, hidden), f32),
+            pltpu.VMEM(second_w.shape, bf16),
+            pltpu.SemaphoreType.DMA((6,)),
+            pltpu.SemaphoreType.DMA((6,)),
+        ],
         compiler_params=params(),
         name="turn",
     )(core_arg, first_w, first_b.reshape(1, hidden), second_w)

time: 242 us -> 174 us (0.72)
  Pallas kernels: 106 us -> 35.8 us
  waiting for transfers between devices: 57.3 us -> 61.7 us
    pallas_call x1, Pallas kernels: 72.7 us -> 2.79 us  [shards(): pl.pallas_call(turn_kernel, out_shape=(jax.ShapeDtypeStruct(first_w.shape...]
    all_to_all x4, waiting for transfers between devices: 13.2 us -> 17.6 us  [shards(): landed = lax.all_to_all(out, 'dom', split_axis=0, concat_axis=0, tiled=True)]
  transfers between devices with their start and end apart: 24 -> 24, of which waited for: 17 -> 18; matrix products, arithmetic and copies ran while one was open for 12% -> 17% of each run, Pallas kernels for 30% -> 2%
where the time goes in v9:
time: 174 us; the launch traced here: 173 us
  waiting for transfers between devices  61.7 us (35%)
  Pallas kernels  35.8 us (21%)
  starting transfers between devices  30.9 us (18%)
  matrix products  24.6 us (14%)
  other arithmetic  10.9 us (6%)
  local copies, waits for them, and re-layouts  7.7 us (4%)
    ppermute x12, waiting for transfers between devices, exchange(): return lax.ppermute(x, ('dom', 'col'), pairs)  40.1 us
    pallas_call x4, Pallas kernels, shards(): pl.pallas_call(functools.partial(far_kernel, slots, class_half, stride, l...  24.3 us
    all_to_all x4, starting transfers between devices, shards(): landed = lax.all_to_all(out, 'dom', split_axis=0, concat_axis=0, tiled=True)  19 us
    all_to_all x4, waiting for transfers between devices, shards(): landed = lax.all_to_all(out, 'dom', split_axis=0, concat_axis=0, tiled=True)  17.6 us
    ppermute x12, starting transfers between devices, exchange(): return lax.ppermute(x, ('dom', 'col'), pairs)  10.3 us
    dot_general x1, matrix products, shards(): pre_second = jnp.dot(tied, second_turned, preferred_element_type=f32)  7.25 us
    convert_element_type x1, other arithmetic, gelu_parts(): return ((x * half_up).astype(bf16), slope.astype(bf16))  6.92 us
    unnamed x52, local copies, waits for them, and re-layouts  5.85 us
  transfers between devices with their start and end apart: 24, of which 18 were waited for; matrix products, arithmetic and copies ran while one was open for 17% of the time, Pallas kernels for 2%

profile of v9, /device:TPU:0, one launch (start us, length us, event | category | flops | bytes accessed | tf_op | source)
XLA Modules:
  0.0 172.9 jit_solution(9831286770810380670)
XLA Ops:
  0.7 5.5 %first.1 = (bf16[8,192,128]{2,1,0:T(8,128)(2,1)}, bf16[3072,128]{1,0:T(8,128)(2,1)}) custom-call(s32[1]{0:T(128)} %bitcast.core_ref, s32[8]{0:T(128)} %bitcast.54, s32[256]{0:T(256)} %bitcast.64, s32[8,256]{1,0:T(8,128)} %bitcast.50, s32[1,256]{1,0:T(1,128)} %labels_ref.1, f32[172,1,256]{2,1,0:T(1,128)} %bitcast.49, s32[24,128]{1,0:T(8,128)} %bitcast.44), custom_call_target="tpu_custom_call" | custom-call | tf_op jit(solution)/shard_map/first/pallas_call | solution.py:475
  6.2 7.3 %all-to-all-start = ((bf16[8,192,128]{2,1,0:T(8,128)(2,1)}), bf16[8,192,128]{2,1,0:T(8,128)(2,1)S(1)}, u32[]{:S(2)}, u32[]{:S(2)}) async-start(bf16[8,192,128]{2,1,0:T(8,128)(2,1)} %get-tuple-element.63), calls=%async_computation | async-start | bytes 786432 | tf_op jit(solution)/shard_map/all_to_all | solution.py:536
  13.7 0.5 collective-permute-start.2
  14.2 2.8 %turn.1 = (bf16[128,1024]{1,0:T(8,128)(2,1)}, f32[1,1024]{1,0:T(1,128)}, bf16[1024,1024]{1,0:T(8,128)(2,1)}) custom-call(s32[1]{0:T(128)} %bitcast.core_ref, bf16[128,1024]{1,0:T(8,128)(2,1)} %first_ref, f32[1,1024]{1,0:T(1,128)} %bitcast.53, bf16[1024,1024]{1,0:T(8,128)(2,1)} %second_ref), custom_call_target="tpu_custom_call" | custom-call | tf_op jit(solution)/shard_map/turn/pallas_call | solution.py:494
  17.2 1.0 collective-permute-done
  18.2 0.7 concatenate.71.ints_ref
  18.9 6.3 %all-to-all-done.recv_ref = bf16[8,192,128]{2,1,0:T(8,128)(2,1)S(1)} async-done(((bf16[8,192,128]{2,1,0:T(8,128)(2,1)}), bf16[8,192,128]{2,1,0:T(8,128)(2,1)S(1)}, u32[]{:S(2)}, u32[]{:S(2)}) %all-to-all-start) | async-done | bytes 393248 | tf_op jit(solution)/shard_map/all_to_all | solution.py:536
  25.3 0.7 copy-done.8
  26.0 6.2 %far.3 = (bf16[8,192,128]{2,1,0:T(8,128)(2,1)}, bf16[3072,128]{1,0:T(8,128)(2,1)}) custom-call(s32[3072]{0:T(1024)} %concatenate.71.ints_ref, s32[24,128]{1,0:T(8,128)} %bitcast.45, bf16[8,192,128]{2,1,0:T(8,128)(2,1)} %copy-done.8, bf16[16,128,128]{2,1,0:T(8,128)(2,1)} %bitcast.35, bf16[16,128,128]{2,1,0:T(8,128)(2,1)} %copy-done.1, ...), custom_call_target="tpu_custom_call" | custom-call | tf_op jit(solution)/shard_map/far/pallas_call | solution.py:560
  32.3 3.7 %all-to-all-start.1 = ((bf16[8,192,128]{2,1,0:T(8,128)(2,1)}), bf16[8,192,128]{2,1,0:T(8,128)(2,1)S(1)}, u32[]{:S(2)}, u32[]{:S(2)}) async-start(bf16[8,192,128]{2,1,0:T(8,128)(2,1)} %get-tuple-element.74), calls=%async_computation.1 | async-start | bytes 786432 | tf_op jit(solution)/shard_map/all_to_all | solution.py:536
  36.1 0.9 maximum_select_fusion.2
  37.0 5.7 %add_convert_fusion.1 = (bf16[1536,1024]{1,0:T(8,128)(2,1)}, bf16[1536,1024]{1,0:T(8,128)(2,1)}) fusion(f32[1024]{0:T(1024)S(1)} %bitcast.66, bf16[1536,128]{1,0:T(8,128)(2,1)S(1)} %copy-done, bf16[128,1024]{1,0:T(8,128)(2,1)S(1)} %copy-done.23), kind=kOutput, calls=%fused_computation.7 | convolution fusion | flops 430964736 | bytes 6950912 | tf_op jit(solution)/shard_map/dot_general | solution.py:544
  42.7 4.9 %all-to-all-done.1.recv_ref = bf16[8,192,128]{2,1,0:T(8,128)(2,1)S(1)} async-done(((bf16[8,192,128]{2,1,0:T(8,128)(2,1)}), bf16[8,192,128]{2,1,0:T(8,128)(2,1)S(1)}, u32[]{:S(2)}, u32[]{:S(2)}) %all-to-all-start.1) | async-done | bytes 393248 | tf_op jit(solution)/shard_map/all_to_all | solution.py:536
  47.6 0.7 copy-done.9
  48.4 6.2 %far.4 = (bf16[8,192,128]{2,1,0:T(8,128)(2,1)}, bf16[3072,128]{1,0:T(8,128)(2,1)}) custom-call(s32[3072]{0:T(1024)} %concatenate.71.ints_ref, s32[24,128]{1,0:T(8,128)} %bitcast.46, bf16[8,192,128]{2,1,0:T(8,128)(2,1)} %copy-done.9, bf16[16,128,128]{2,1,0:T(8,128)(2,1)} %bitcast.36, bf16[16,128,128]{2,1,0:T(8,128)(2,1)} %copy-done.1, ...), custom_call_target="tpu_custom_call" | custom-call | tf_op jit(solution)/shard_map/far/pallas_call | solution.py:560
  54.6 3.7 %all-to-all-start.2 = ((bf16[8,192,128]{2,1,0:T(8,128)(2,1)}), bf16[8,192,128]{2,1,0:T(8,128)(2,1)S(1)}, u32[]{:S(2)}, u32[]{:S(2)}) async-start(bf16[8,192,128]{2,1,0:T(8,128)(2,1)} %get-tuple-element.76), calls=%async_computation.2 | async-start | bytes 786432 | tf_op jit(solution)/shard_map/all_to_all | solution.py:536
  58.3 7.3 %fusion.9 = f32[1536,1024]{1,0:T(8,128)} fusion(bf16[1536,1024]{1,0:T(8,128)(2,1)} %get-tuple-element.78, bf16[1024,1024]{1,0:T(8,128)(2,1)S(1)} %copy-done.21), kind=kOutput, calls=%fused_computation.58 | convolution fusion | flops 3221225472 | bytes 11534336 | tf_op jit(solution)/shard_map/dot_general | solution.py:551
  65.5 3.8 %all-to-all-done.2.recv_ref = bf16[8,192,128]{2,1,0:T(8,128)(2,1)S(1)} async-done(((bf16[8,192,128]{2,1,0:T(8,128)(2,1)}), bf16[8,192,128]{2,1,0:T(8,128)(2,1)S(1)}, u32[]{:S(2)}, u32[]{:S(2)}) %all-to-all-start.2) | async-done | bytes 393248 | tf_op jit(solution)/shard_map/all_to_all | solution.py:536
  69.4 0.7 copy-done.10
  70.1 6.2 %far.5 = (bf16[8,192,128]{2,1,0:T(8,128)(2,1)}, bf16[3072,128]{1,0:T(8,128)(2,1)}) custom-call(s32[3072]{0:T(1024)} %concatenate.71.ints_ref, s32[24,128]{1,0:T(8,128)} %bitcast.47, bf16[8,192,128]{2,1,0:T(8,128)(2,1)} %copy-done.10, bf16[16,128,128]{2,1,0:T(8,128)(2,1)} %bitcast.37, bf16[16,128,128]{2,1,0:T(8,128)(2,1)} %copy-done.1, ...), custom_call_target="tpu_custom_call" | custom-call | tf_op jit(solution)/shard_map/far/pallas_call | solution.py:560
  76.3 4.3 %all-to-all-start.3 = ((bf16[8,192,128]{2,1,0:T(8,128)(2,1)}), bf16[8,192,128]{2,1,0:T(8,128)(2,1)}, u32[]{:S(2)}, u32[]{:S(2)}) async-start(bf16[8,192,128]{2,1,0:T(8,128)(2,1)} %get-tuple-element.88), calls=%async_computation.3 | async-start | bytes 786432 | tf_op jit(solution)/shard_map/all_to_all | solution.py:536
  80.6 6.9 %add_convert_fusion = (bf16[1536,1024]{1,0:T(8,128)(2,1)S(1)}, bf16[1536,1024]{1,0:T(8,128)(2,1)}) fusion(f32[1536,1024]{1,0:T(8,128)} %fusion.9, f32[1024]{0:T(1024)S(1)} %copy-done.14), kind=kLoop, calls=%fused_computation.2 | loop fusion | flops 28311552 | bytes 12587008 | tf_op jit(solution)/shard_map/convert_element_type | solution.py:366
  87.6 1.2 add_convert_fusion.3.rest_0_
  88.8 2.5 %all-to-all-done.3.recv_ref = bf16[8,192,128]{2,1,0:T(8,128)(2,1)} async-done(((bf16[8,192,128]{2,1,0:T(8,128)(2,1)}), bf16[8,192,128]{2,1,0:T(8,128)(2,1)}, u32[]{:S(2)}, u32[]{:S(2)}) %all-to-all-start.3) | async-done | bytes 393248 | tf_op jit(solution)/shard_map/all_to_all | solution.py:536
  91.3 5.8 %far_last.1 = (bf16[1536,128]{1,0:T(8,128)(2,1)}, bf16[1536,128]{1,0:T(8,128)(2,1)}) custom-call(s32[3072]{0:T(1024)} %concatenate.71.ints_ref, s32[24,128]{1,0:T(8,128)} %bitcast.48, bf16[8,192,128]{2,1,0:T(8,128)(2,1)} %all-to-all-done.3.recv_ref, bf16[16,128,128]{2,1,0:T(8,128)(2,1)} %bitcast.38, bf16[16,128,128]{2,1,0:T(8,128)(2,1)} %copy-done.1, ...), custom_call_target="tpu_custom_call" | custom-call | tf_op jit(solution)/shard_map/far_last/pallas_call | solution.py:560
  97.2 1.1 constant_dynamic-update-slice_fusion.1
  98.2 1.0 collective-permute-done.3
  99.2 1.1 constant_dynamic-update-slice_fusion
  100.3 2.2 %fusion.8 = (bf16[1024]{0:T(1024)(128)(2,1)S(1)}, bf16[1536,1024]{1,0:T(8,128)(2,1)S(1)}) fusion(bf16[1536,256]{1,0:T(8,128)(2,1)S(1)} %constant_dynamic-update-slice_fusion, bf16[1024,256]{0,1:T(8,128)(2,1)} %maximum_select_fusion.2, bf16[1536,1024]{1,0:T(8,128)(2,1)S(1)} %get-tuple-element.87), kind=kOutput, calls=%fused_computation.57 | convolution fusion | flops 811596800 | bytes 7604224 | tf_op jit(solution)/shard_map/dot_general | solution.py:592
  102.6 0.6 convolution_convert_fusion.3
  103.2 1.4 copy-done.3
  104.5 3.6 %fusion.4 = (bf16[1024]{0:T(1024)(128)(2,1)S(1)}, f32[1536,1024]{1,0:T(8,128)S(1)}) fusion(bf16[1536,1024]{1,0:T(8,128)(2,1)S(1)} %copy-done.3, bf16[1536,1024]{1,0:T(8,128)(2,1)S(1)} %get-tuple-element.116, bf16[1024,1024]{1,0:T(8,128)(2,1)S(1)} %copy-done.22), kind=kOutput, calls=%fused_computation.53 | convolution fusion | flops 3227515904 | bytes 14682112 | tf_op jit(solution)/shard_map/dot_general | solution.py:601
  108.2 0.8 convolution_convert_fusion.4
  109.0 1.1 copy-done.4
  110.1 1.0 convolution_convert_fusion.2
  111.2 0.2 collective-permute-start.12
  111.4 1.4 convolution_convert_fusion
  112.8 0.4 collective-permute-start.4
  113.3 0.6 convolution_convert_fusion.5
  113.9 0.2 add_convert_fusion.4
  114.2 1.5 collective-permute-start.13
  115.7 1.4 add_convert_fusion.2
  117.2 1.0 collective-permute-start.5
  118.2 2.8 %collective-permute-done.13 = bf16[288,512]{1,0:T(8,128)(2,1)S(1)} collective-permute-done((bf16[288,512]{1,0:T(8,128)(2,1)S(1)}, bf16[288,512]{1,0:T(8,128)(2,1)S(1)}, u32[]{:S(2)}, u32[]{:S(2)}) %collective-permute-start.13) | collective-permute-done | bytes 294944 | tf_op jit(solution)/shard_map/ppermute | solution.py:379
  121.1 4.1 %collective-permute-done.5 = bf16[384,512]{1,0:T(8,128)(2,1)S(1)} collective-permute-done((bf16[384,512]{1,0:T(8,128)(2,1)S(1)}, bf16[384,512]{1,0:T(8,128)(2,1)S(1)}, u32[]{:S(2)}, u32[]{:S(2)}) %collective-permute-start.5) | collective-permute-done | bytes 393248 | tf_op jit(solution)/shard_map/ppermute | solution.py:379
  125.2 0.1 add_convert_fusion.5
  125.4 1.0 collective-permute-start.6
  126.4 1.2 collective-permute-start.14
  127.6 3.6 %collective-permute-done.6 = bf16[384,256]{1,0:T(8,128)(2,1)S(1)} collective-permute-done((bf16[384,256]{1,0:T(8,128)(2,1)S(1)}, bf16[384,256]{1,0:T(8,128)(2,1)S(1)}, u32[]{:S(2)}, u32[]{:S(2)}) %collective-permute-start.6) | collective-permute-done | bytes 196640 | tf_op jit(solution)/shard_map/ppermute | solution.py:379
  131.2 1.0 collective-permute-start.7
  132.3 0.4 collective-permute-done.14
  132.8 5.1 %collective-permute-done.7 = bf16[384,128]{1,0:T(8,128)(2,1)S(1)} collective-permute-done((bf16[384,128]{1,0:T(8,128)(2,1)S(1)}, bf16[384,128]{1,0:T(8,128)(2,1)S(1)}, u32[]{:S(2)}, u32[]{:S(2)}) %collective-permute-start.7) | collective-permute-done | bytes 98336 | tf_op jit(solution)/shard_map/ppermute | solution.py:379
  138.0 3.0 %collective-permute-start.15 = (bf16[288,128]{1,0:T(8,128)(2,1)S(1)}, bf16[288,128]{1,0:T(8,128)(2,1)S(1)}, u32[]{:S(2)}, u32[]{:S(2)}) collective-permute-start(bf16[288,128]{1,0:T(8,128)(2,1)S(1)} %broadcast_select_fusion.5), channel_id=1, source_target_pairs={{0,8},{1,9},{2,10},{3,11},{4,12},{5,13},{6,14},{7,15},{8,0},{9,1},... | collective-permute-start | bytes 221192 | tf_op jit(solution)/shard_map/ppermute | solution.py:379
  141.0 4.6 %collective-permute-done.8 = bf16[384,128]{1,0:T(8,128)(2,1)S(1)} collective-permute-done((bf16[384,128]{1,0:T(8,128)(2,1)S(1)}, bf16[384,128]{1,0:T(8,128)(2,1)S(1)}, u32[]{:S(2)}, u32[]{:S(2)}) %collective-permute-start.8) | collective-permute-done | bytes 98336 | tf_op jit(solution)/shard_map/ppermute | solution.py:379
  145.7 1.4 collective-permute-done.15
  147.2 7.0 %collective-permute-done.9 = bf16[384,256]{1,0:T(8,128)(2,1)S(1)} collective-permute-done((bf16[384,256]{1,0:T(8,128)(2,1)S(1)}, bf16[384,256]{1,0:T(8,128)(2,1)S(1)}, u32[]{:S(2)}, u32[]{:S(2)}) %collective-permute-start.9) | collective-permute-done | bytes 196640 | tf_op jit(solution)/shard_map/ppermute | solution.py:379
  154.5 5.9 %collective-permute-done.17 = bf16[288,256]{1,0:T(8,128)(2,1)S(1)} collective-permute-done((bf16[288,256]{1,0:T(8,128)(2,1)S(1)}, bf16[288,256]{1,0:T(8,128)(2,1)S(1)}, u32[]{:S(2)}, u32[]{:S(2)}) %collective-permute-start.17) | collective-permute-done | bytes 147488 | tf_op jit(solution)/shard_map/ppermute | solution.py:379
  160.6 1.3 collective-permute-start.18
  161.8 0.3 collective-permute-done.10
  162.1 0.2 maximum_select_fusion.mine_one
  162.4 4.9 %collective-permute-done.18 = bf16[288,512]{1,0:T(8,128)(2,1)S(1)} collective-permute-done((bf16[288,512]{1,0:T(8,128)(2,1)S(1)}, bf16[288,512]{1,0:T(8,128)(2,1)S(1)}, u32[]{:S(2)}, u32[]{:S(2)}) %collective-permute-start.18) | collective-permute-done | bytes 294944 | tf_op jit(solution)/shard_map/ppermute | solution.py:379
  167.4 0.2 maximum_select_fusion.1.mine_two
  167.6 2.0 %collective-permute-done.19.theirs_two = bf16[288,1024]{1,0:T(8,128)(2,1)S(1)} collective-permute-done((bf16[288,1024]{1,0:T(8,128)(2,1)S(1)}, bf16[288,1024]{1,0:T(8,128)(2,1)S(1)}, u32[]{:S(2)}, u32[]{:S(2)}) %collective-permute-start.19) | collective-permute-done | bytes 589856 | tf_op jit(solution)/shard_map/ppermute | solution.py:370
  169.6 3.2 %finish.1 = (f32[128,1024]{1,0:T(8,128)}, f32[1,1024]{1,0:T(1,128)}, f32[1024,1024]{1,0:T(8,128)}, f32[1,1024]{1,0:T(1,128)}, f32[172,1024]{1,0:T(8,128)}) custom-call(s32[1]{0:T(128)} %bitcast.core_ref, bf16[384,1024]{1,0:T(8,128)(2,1)S(1)} %maximum_select_fusion.mine_one, bf16[384,1024]{1,0:T(8,128)(2,1)S(1)} %collective-permute-done.11.theirs_one, ...), custom_call_target="tpu_custom_call" | custom-call | tf_op jit(solution)/shard_map/finish/pallas_call | solution.py:629
  (93 shorter events, 2.0 us)
Async XLA Ops:
  0.6 36.4 %copy-start = (bf16[1536,128]{1,0:T(8,128)(2,1)S(1)}, bf16[1536,128]{1,0:T(8,128)(2,1)}, u32[]{:S(2)}) copy-start(bf16[1536,128]{1,0:T(8,128)(2,1)} %param.18) | copy-start | bytes 1179652
  0.7 17.6 %copy-start.15 = (s32[1,8]{1,0:T(1,128)S(1)}, s32[1,8]{1,0:T(1,128)}, u32[]{:S(2)}) copy-start(s32[1,8]{1,0:T(1,128)} %param.31) | copy-start | bytes 100
  0.7 16.5 %copy-start.13 = (s32[1,8,256]{2,1,0:T(8,128)S(1)}, s32[1,8,256]{2,1,0:T(8,128)}, u32[]{:S(2)}) copy-start(s32[1,8,256]{2,1,0:T(8,128)} %param.30) | copy-start | bytes 24580
  0.7 16.3 %copy-start.16 = (s32[1,1,16]{2,1,0:T(1,128)S(1)}, s32[1,1,16]{2,1,0:T(1,128)}, u32[]{:S(2)}) copy-start(s32[1,1,16]{2,1,0:T(1,128)} %param.25) | copy-start | bytes 196
  0.7 16.3 %copy-start.17 = (s32[1,1,16]{2,1,0:T(1,128)S(1)}, s32[1,1,16]{2,1,0:T(1,128)}, u32[]{:S(2)}) copy-start(s32[1,1,16]{2,1,0:T(1,128)} %param.26) | copy-start | bytes 196
  0.7 16.3 %copy-start.18 = (s32[1,1,16]{2,1,0:T(1,128)S(1)}, s32[1,1,16]{2,1,0:T(1,128)}, u32[]{:S(2)}) copy-start(s32[1,1,16]{2,1,0:T(1,128)} %param.28) | copy-start | bytes 196
  0.7 16.3 %copy-start.19 = (s32[1,1,16]{2,1,0:T(1,128)S(1)}, s32[1,1,16]{2,1,0:T(1,128)}, u32[]{:S(2)}) copy-start(s32[1,1,16]{2,1,0:T(1,128)} %param.29) | copy-start | bytes 196
  6.2 19.0 %all-to-all-start = ((bf16[8,192,128]{2,1,0:T(8,128)(2,1)}), bf16[8,192,128]{2,1,0:T(8,128)(2,1)S(1)}, u32[]{:S(2)}, u32[]{:S(2)}) async-start(bf16[8,192,128]{2,1,0:T(8,128)(2,1)} %get-tuple-element.63), calls=%async_computation | async-start | bytes 786432 | tf_op jit(solution)/shard_map/all_to_all | solution.py:536
  13.6 18.6 %copy-start.11 = (bf16[1024,172]{0,1:T(8,128)(2,1)S(1)}, bf16[1024,172]{0,1:T(8,128)(2,1)}, u32[]{:S(2)}) copy-start(bf16[1024,172]{0,1:T(8,128)(2,1)} %param.23) | copy-start | bytes 1056772
  13.6 18.6 %copy-start.20 = (pred[128]{0:T(512)(128)(4,1)S(1)}, pred[128]{0:T(512)(128)(4,1)}, u32[]{:S(2)}) copy-start(pred[128]{0:T(512)(128)(4,1)} %constant.33.clone.1) | copy-start | bytes 388
  13.6 5.3 %collective-permute-start.1 = (bf16[16,128,128]{2,1,0:T(8,128)(2,1)}, bf16[16,128,128]{2,1,0:T(8,128)(2,1)S(1)}, u32[]{:S(2)}, u32[]{:S(2)}) collective-permute-start(bf16[16,128,128]{2,1,0:T(8,128)(2,1)} %bitcast.34), channel_id=1, source_target_pairs={{0,1},{1,0},{2,3},{3,2},{4,5},{5,4},{6,7},{7,6},{8,9},{9,8},{10,11... | collective-permute-start | bytes 1572872 | tf_op jit(solution)/shard_map/ppermute | solution.py:370
  13.7 5.2 %collective-permute-start.2 = (bf16[16,128,128]{2,1,0:T(8,128)(2,1)}, bf16[16,128,128]{2,1,0:T(8,128)(2,1)S(1)}, u32[]{:S(2)}, u32[]{:S(2)}) collective-permute-start(bf16[16,128,128]{2,1,0:T(8,128)(2,1)} %bitcast.39), channel_id=1, source_target_pairs={{0,1},{1,0},{2,3},{3,2},{4,5},{5,4},{6,7},{7,6},{8,9},{9,8},{10,11... | collective-permute-start | bytes 1572872 | tf_op jit(solution)/shard_map/ppermute | solution.py:370
  14.2 21.9 %slice-start = ((bf16[1024,172]{0,1:T(8,128)(2,1)}), bf16[1024,84]{0,1:T(8,128)(2,1)S(1)}, s32[]{:S(2)}) async-start(bf16[1024,172]{0,1:T(8,128)(2,1)} %param.23), calls=%async_computation.4 | async-start | bytes 360448 | tf_op jit(solution)/shard_map/slice | solution.py:546
  17.1 1.1 collective-permute-start
  18.9 18.1 %copy-start.23 = (bf16[128,1024]{1,0:T(8,128)(2,1)S(1)}, bf16[128,1024]{1,0:T(8,128)(2,1)}, u32[]{:S(2)}) copy-start(bf16[128,1024]{1,0:T(8,128)(2,1)} %get-tuple-element.70) | copy-start | bytes 786436
  18.9 18.1 %copy-start.24 = (f32[1,1024]{1,0:T(1,128)S(1)}, f32[1,1024]{1,0:T(1,128)}, u32[]{:S(2)}) copy-start(f32[1,1024]{1,0:T(1,128)} %get-tuple-element.71) | copy-start | bytes 12292
  18.9 6.4 %copy-start.1 = (bf16[16,128,128]{2,1,0:T(8,128)(2,1)}, bf16[16,128,128]{2,1,0:T(8,128)(2,1)S(1)}, u32[]{:S(2)}) copy-start(bf16[16,128,128]{2,1,0:T(8,128)(2,1)S(1)} %collective-permute-done.1.other_halo_ref) | copy-start | bytes 1572868
  18.9 6.4 %copy-start.2 = (bf16[16,128,128]{2,1,0:T(8,128)(2,1)}, bf16[16,128,128]{2,1,0:T(8,128)(2,1)S(1)}, u32[]{:S(2)}) copy-start(bf16[16,128,128]{2,1,0:T(8,128)(2,1)S(1)} %collective-permute-done.2.other_local_ref) | copy-start | bytes 1572868
  25.3 0.7 copy-start.8
  32.3 15.3 %all-to-all-start.1 = ((bf16[8,192,128]{2,1,0:T(8,128)(2,1)}), bf16[8,192,128]{2,1,0:T(8,128)(2,1)S(1)}, u32[]{:S(2)}, u32[]{:S(2)}) async-start(bf16[8,192,128]{2,1,0:T(8,128)(2,1)} %get-tuple-element.74), calls=%async_computation.1 | async-start | bytes 786432 | tf_op jit(solution)/shard_map/all_to_all | solution.py:536
  42.7 15.6 %copy-start.21 = (bf16[1024,1024]{1,0:T(8,128)(2,1)S(1)}, bf16[1024,1024]{1,0:T(8,128)(2,1)}, u32[]{:S(2)}) copy-start(bf16[1024,1024]{1,0:T(8,128)(2,1)} %get-tuple-element.79) | copy-start | bytes 6291460
  47.6 0.7 copy-start.9
  54.6 14.8 %all-to-all-start.2 = ((bf16[8,192,128]{2,1,0:T(8,128)(2,1)}), bf16[8,192,128]{2,1,0:T(8,128)(2,1)S(1)}, u32[]{:S(2)}, u32[]{:S(2)}) async-start(bf16[8,192,128]{2,1,0:T(8,128)(2,1)} %get-tuple-element.76), calls=%async_computation.2 | async-start | bytes 786432 | tf_op jit(solution)/shard_map/all_to_all | solution.py:536
  65.5 15.1 %copy-start.14 = (f32[1024]{0:T(1024)S(1)}, f32[1024]{0:T(1024)}, u32[]{:S(2)}) copy-start(f32[1024]{0:T(1024)} %param.22) | copy-start | bytes 12292
  69.4 0.7 copy-start.10
  76.3 15.0 %all-to-all-start.3 = ((bf16[8,192,128]{2,1,0:T(8,128)(2,1)}), bf16[8,192,128]{2,1,0:T(8,128)(2,1)}, u32[]{:S(2)}, u32[]{:S(2)}) async-start(bf16[8,192,128]{2,1,0:T(8,128)(2,1)} %get-tuple-element.88), calls=%async_computation.3 | async-start | bytes 786432 | tf_op jit(solution)/shard_map/all_to_all | solution.py:536
  80.6 7.0 %copy-start.5 = (bf16[3072,128]{1,0:T(8,128)(2,1)S(1)}, bf16[3072,128]{1,0:T(8,128)(2,1)}, u32[]{:S(2)}) copy-start(bf16[3072,128]{1,0:T(8,128)(2,1)} %get-tuple-element.86.value_in_ref) | copy-start | bytes 2359300
  80.6 6.9 %copy-start.6 = (bf16[3072,128]{1,0:T(8,128)(2,1)S(1)}, bf16[3072,128]{1,0:T(8,128)(2,1)}, u32[]{:S(2)}) copy-start(bf16[3072,128]{1,0:T(8,128)(2,1)} %get-tuple-element.85.value_in_ref) | copy-start | bytes 2359300
  80.6 6.9 %copy-start.7 = (bf16[3072,128]{1,0:T(8,128)(2,1)S(1)}, bf16[3072,128]{1,0:T(8,128)(2,1)}, u32[]{:S(2)}) copy-start(bf16[3072,128]{1,0:T(8,128)(2,1)} %get-tuple-element.84.value_in_ref) | copy-start | bytes 2359300
  97.1 2.1 %collective-permute-start.3 = (bf16[1536,128]{1,0:T(8,128)(2,1)}, bf16[1536,128]{1,0:T(8,128)(2,1)}, u32[]{:S(2)}, u32[]{:S(2)}) collective-permute-start(bf16[1536,128]{1,0:T(8,128)(2,1)} %get-tuple-element.92), channel_id=1, source_target_pairs={{0,1},{1,0},{2,3},{3,2},{4,5},{5,4},{6,7},{7,6},{8,9},{9,8},{10,11... | collective-permute-start | bytes 1179656 | tf_op jit(solution)/shard_map/ppermute | solution.py:370
  100.3 2.3 %copy-start.12 = (bf16[1536,1024]{1,0:T(8,128)(2,1)S(1)}, bf16[1536,1024]{1,0:T(8,128)(2,1)}, u32[]{:S(2)}) copy-start(bf16[1536,1024]{1,0:T(8,128)(2,1)} %get-tuple-element.78) | copy-start | bytes 9437188
  100.3 2.9 %copy-start.22 = (bf16[1024,1024]{1,0:T(8,128)(2,1)S(1)}, bf16[1024,1024]{1,0:T(8,128)(2,1)}, u32[]{:S(2)}) copy-start(bf16[1024,1024]{1,0:T(8,128)(2,1)} %get-tuple-element.79) | copy-start | bytes 6291460
  102.5 2.0 %copy-start.3 = (bf16[1536,1024]{1,0:T(8,128)(2,1)S(1)}, bf16[1536,1024]{1,0:T(8,128)(2,1)}, u32[]{:S(2)}) copy-start(bf16[1536,1024]{1,0:T(8,128)(2,1)} %get-tuple-element.94) | copy-start | bytes 9437188
  108.2 1.9 %copy-start.4 = (bf16[1536,1024]{1,0:T(8,128)(2,1)S(1)}, bf16[1536,1024]{1,0:T(8,128)(2,1)}, u32[]{:S(2)}) copy-start(bf16[1536,1024]{1,0:T(8,128)(2,1)} %get-tuple-element.95) | copy-start | bytes 9437188
  111.2 2.7 %collective-permute-start.12 = (bf16[288,1024]{1,0:T(8,128)(2,1)S(1)}, bf16[288,1024]{1,0:T(8,128)(2,1)S(1)}, u32[]{:S(2)}, u32[]{:S(2)}) collective-permute-start(bf16[288,1024]{1,0:T(8,128)(2,1)S(1)} %pad_maximum_fusion), channel_id=1, source_target_pairs={{0,1},{1,0},{2,3},{3,2},{4,5},{5,4},{6,7},{7,6},{8,9},{9,8},{10,11... | collective-permute-start | bytes 1769480 | tf_op jit(solution)/shard_map/ppermute | solution.py:370
  112.8 2.9 %collective-permute-start.4 = (bf16[384,1024]{1,0:T(8,128)(2,1)S(1)}, bf16[384,1024]{1,0:T(8,128)(2,1)S(1)}, u32[]{:S(2)}, u32[]{:S(2)}) collective-permute-start(bf16[384,1024]{1,0:T(8,128)(2,1)S(1)} %convolution_convert_fusion), channel_id=1, source_target_pairs={{0,1},{1,0},{2,3},{3,2},{4,5},{5,4},{6,7},{7,6},{8,9},{9,8},{10,11... | collective-permute-start | bytes 2359304 | tf_op jit(solution)/shard_map/ppermute | solution.py:370
  114.2 6.8 %collective-permute-start.13 = (bf16[288,512]{1,0:T(8,128)(2,1)S(1)}, bf16[288,512]{1,0:T(8,128)(2,1)S(1)}, u32[]{:S(2)}, u32[]{:S(2)}) collective-permute-start(bf16[288,512]{1,0:T(8,128)(2,1)S(1)} %broadcast_select_fusion.1), channel_id=1, source_target_pairs={{0,2},{1,5},{2,0},{3,7},{4,6},{5,1},{6,4},{7,3},{8,10},{9,13},{10,... | collective-permute-start | bytes 884744 | tf_op jit(solution)/shard_map/ppermute | solution.py:379
  117.2 8.0 %collective-permute-start.5 = (bf16[384,512]{1,0:T(8,128)(2,1)S(1)}, bf16[384,512]{1,0:T(8,128)(2,1)S(1)}, u32[]{:S(2)}, u32[]{:S(2)}) collective-permute-start(bf16[384,512]{1,0:T(8,128)(2,1)S(1)} %broadcast_select_fusion), channel_id=1, source_target_pairs={{0,2},{1,5},{2,0},{3,7},{4,6},{5,1},{6,4},{7,3},{8,10},{9,13},{10,... | collective-permute-start | bytes 1179656 | tf_op jit(solution)/shard_map/ppermute | solution.py:379
  125.4 5.7 %collective-permute-start.6 = (bf16[384,256]{1,0:T(8,128)(2,1)S(1)}, bf16[384,256]{1,0:T(8,128)(2,1)S(1)}, u32[]{:S(2)}, u32[]{:S(2)}) collective-permute-start(bf16[384,256]{1,0:T(8,128)(2,1)S(1)} %broadcast_select_fusion.2), channel_id=1, source_target_pairs={{0,4},{1,3},{2,6},{3,1},{4,0},{5,7},{6,2},{7,5},{8,12},{9,11},{10,... | collective-permute-start | bytes 589832 | tf_op jit(solution)/shard_map/ppermute | solution.py:379
  126.4 6.3 %collective-permute-start.14 = (bf16[288,256]{1,0:T(8,128)(2,1)S(1)}, bf16[288,256]{1,0:T(8,128)(2,1)S(1)}, u32[]{:S(2)}, u32[]{:S(2)}) collective-permute-start(bf16[288,256]{1,0:T(8,128)(2,1)S(1)} %broadcast_select_fusion.3), channel_id=1, source_target_pairs={{0,4},{1,3},{2,6},{3,1},{4,0},{5,7},{6,2},{7,5},{8,12},{9,11},{10,... | collective-permute-start | bytes 442376 | tf_op jit(solution)/shard_map/ppermute | solution.py:379
  131.2 6.6 %collective-permute-start.7 = (bf16[384,128]{1,0:T(8,128)(2,1)S(1)}, bf16[384,128]{1,0:T(8,128)(2,1)S(1)}, u32[]{:S(2)}, u32[]{:S(2)}) collective-permute-start(bf16[384,128]{1,0:T(8,128)(2,1)S(1)} %broadcast_select_fusion.4), channel_id=1, source_target_pairs={{0,8},{1,9},{2,10},{3,11},{4,12},{5,13},{6,14},{7,15},{8,0},{9,1},... | collective-permute-start | bytes 294920 | tf_op jit(solution)/shard_map/ppermute | solution.py:379
  137.9 7.6 %collective-permute-start.8 = (bf16[384,128]{1,0:T(8,128)(2,1)S(1)}, bf16[384,128]{1,0:T(8,128)(2,1)S(1)}, u32[]{:S(2)}, u32[]{:S(2)}) collective-permute-start(bf16[384,128]{1,0:T(8,128)(2,1)S(1)} %add_convert_fusion.9), channel_id=1, source_target_pairs={{0,8},{1,9},{2,10},{3,11},{4,12},{5,13},{6,14},{7,15},{8,0},{9,1},... | collective-permute-start | bytes 294920 | tf_op jit(solution)/shard_map/ppermute | solution.py:379
  138.0 9.1 %collective-permute-start.15 = (bf16[288,128]{1,0:T(8,128)(2,1)S(1)}, bf16[288,128]{1,0:T(8,128)(2,1)S(1)}, u32[]{:S(2)}, u32[]{:S(2)}) collective-permute-start(bf16[288,128]{1,0:T(8,128)(2,1)S(1)} %broadcast_select_fusion.5), channel_id=1, source_target_pairs={{0,8},{1,9},{2,10},{3,11},{4,12},{5,13},{6,14},{7,15},{8,0},{9,1},... | collective-permute-start | bytes 221192 | tf_op jit(solution)/shard_map/ppermute | solution.py:379
  145.6 8.6 %collective-permute-start.9 = (bf16[384,256]{1,0:T(8,128)(2,1)S(1)}, bf16[384,256]{1,0:T(8,128)(2,1)S(1)}, u32[]{:S(2)}, u32[]{:S(2)}) collective-permute-start(bf16[384,256]{1,0:T(8,128)(2,1)S(1)} %maximum_select_fusion.5), channel_id=1, source_target_pairs={{0,4},{1,3},{2,6},{3,1},{4,0},{5,7},{6,2},{7,5},{8,12},{9,11},{10,... | collective-permute-start | bytes 589832 | tf_op jit(solution)/shard_map/ppermute | solution.py:379
  147.1 7.3 %collective-permute-start.16 = (bf16[288,128]{1,0:T(8,128)(2,1)S(1)}, bf16[288,128]{1,0:T(8,128)(2,1)S(1)}, u32[]{:S(2)}, u32[]{:S(2)}) collective-permute-start(bf16[288,128]{1,0:T(8,128)(2,1)S(1)} %add_convert_fusion.10), channel_id=1, source_target_pairs={{0,8},{1,9},{2,10},{3,11},{4,12},{5,13},{6,14},{7,15},{8,0},{9,1},... | collective-permute-start | bytes 221192 | tf_op jit(solution)/shard_map/ppermute | solution.py:379
  154.3 7.8 %collective-permute-start.10 = (bf16[384,512]{1,0:T(8,128)(2,1)S(1)}, bf16[384,512]{1,0:T(8,128)(2,1)S(1)}, u32[]{:S(2)}, u32[]{:S(2)}) collective-permute-start(bf16[384,512]{1,0:T(8,128)(2,1)S(1)} %maximum_select_fusion.3), channel_id=1, source_target_pairs={{0,2},{1,5},{2,0},{3,7},{4,6},{5,1},{6,4},{7,3},{8,10},{9,13},{10,... | collective-permute-start | bytes 1179656 | tf_op jit(solution)/shard_map/ppermute | solution.py:379
  154.4 6.0 %collective-permute-start.17 = (bf16[288,256]{1,0:T(8,128)(2,1)S(1)}, bf16[288,256]{1,0:T(8,128)(2,1)S(1)}, u32[]{:S(2)}, u32[]{:S(2)}) collective-permute-start(bf16[288,256]{1,0:T(8,128)(2,1)S(1)} %maximum_select_fusion.6), channel_id=1, source_target_pairs={{0,4},{1,3},{2,6},{3,1},{4,0},{5,7},{6,2},{7,5},{8,12},{9,11},{10,... | collective-permute-start | bytes 442376 | tf_op jit(solution)/shard_map/ppermute | solution.py:379
  160.6 6.8 %collective-permute-start.18 = (bf16[288,512]{1,0:T(8,128)(2,1)S(1)}, bf16[288,512]{1,0:T(8,128)(2,1)S(1)}, u32[]{:S(2)}, u32[]{:S(2)}) collective-permute-start(bf16[288,512]{1,0:T(8,128)(2,1)S(1)} %maximum_select_fusion.4), channel_id=1, source_target_pairs={{0,2},{1,5},{2,0},{3,7},{4,6},{5,1},{6,4},{7,3},{8,10},{9,13},{10,... | collective-permute-start | bytes 884744 | tf_op jit(solution)/shard_map/ppermute | solution.py:379
  162.3 7.3 %collective-permute-start.11 = (bf16[384,1024]{1,0:T(8,128)(2,1)S(1)}, bf16[384,1024]{1,0:T(8,128)(2,1)S(1)}, u32[]{:S(2)}, u32[]{:S(2)}) collective-permute-start(bf16[384,1024]{1,0:T(8,128)(2,1)S(1)} %maximum_select_fusion.mine_one), channel_id=1, source_target_pairs={{0,1},{1,0},{2,3},{3,2},{4,5},{5,4},{6,7},{7,6},{8,9},{9,8},{10,11... | collective-permute-start | bytes 2359304 | tf_op jit(solution)/shard_map/ppermute | solution.py:370
  167.5 2.1 %collective-permute-start.19 = (bf16[288,1024]{1,0:T(8,128)(2,1)S(1)}, bf16[288,1024]{1,0:T(8,128)(2,1)S(1)}, u32[]{:S(2)}, u32[]{:S(2)}) collective-permute-start(bf16[288,1024]{1,0:T(8,128)(2,1)S(1)} %maximum_select_fusion.1.mine_two), channel_id=1, source_target_pairs={{0,1},{1,0},{2,3},{3,2},{4,5},{5,4},{6,7},{7,6},{8,9},{9,8},{10,11... | collective-permute-start | bytes 1769480 | tf_op jit(solution)/shard_map/ppermute | solution.py:370

commit v10 on v9

--- a/solution.py
+++ b/solution.py
@@ -129,10 +129,18 @@
     return jnp.broadcast_to(columns[:, b : b + 1], columns.shape)
 
 
-def first_kernel(class_half, core_ref, count_ref, nodes_ref, rows_ref, labels_ref, logits_ref, degree_ref,
-                 out_ref, value_ref, wide_ref, diff_ref, v_ref, stage_ref, packed_ref, value_v, idx_ref, idx_sems,
-                 sems, own_sems):
+def first_kernel(class_half, core_ref, count_ref, nodes_ref, rows_ref, labels_in_ref, logits_in_ref, degree_in_ref,
+                 out_ref, value_ref, labels_ref, logits_ref, degree_ref, wide_ref, diff_ref, v_ref, stage_ref,
+                 packed_ref, value_v, idx_ref, idx_sems, sems, own_sems):
     classes, unused, batch = logits_ref.shape
+    entries = [
+        pltpu.make_async_copy(source, target, own_sems.at[1 + i])
+        for i, (source, target) in enumerate(
+            ((logits_in_ref, logits_ref), (labels_in_ref, labels_ref), (degree_in_ref, degree_ref))
+        )
+    ]
+    for copy in entries:
+        copy.start()
     peers = packed_ref.shape[0]
     slots = stage_ref.shape[0] // peers
     flat = []
@@ -146,16 +154,18 @@
         copy.start()
     blocks, block = degree_ref.shape
     core = core_ref[0]
+    v_ref[...] = jnp.zeros_like(v_ref)
+    wide_ref[...] = jnp.zeros_like(wide_ref)
+    for copy in entries:
+        copy.wait()
     logits = logits_ref[...].reshape(classes, batch)
     shifted = jnp.exp(logits - jnp.max(logits, axis=0, keepdims=True))
     hot = lax.broadcasted_iota(jnp.int32, (classes, batch), 0) == labels_ref[...]
     probs = shifted / jnp.sum(shifted, axis=0, keepdims=True)
-    wide_ref[...] = jnp.zeros_like(wide_ref)
     wide_ref[0:classes, :] = probs - jnp.where(hot, 1.0, 0.0)
     chosen = wide_ref[pl.ds(pl.multiple_of(core * class_half, 8), LANES), :]
     lane = lax.broadcasted_iota(jnp.int32, (batch, LANES), 1)
     diff_ref[...] = jnp.where(lane < class_half, jnp.transpose(chosen), 0.0)
-    v_ref[...] = jnp.zeros_like(v_ref)
 
     def add_row(i, carry):
         at = pl.ds(nodes_ref[i], 1)
@@ -475,9 +485,12 @@
     out, value = pl.pallas_call(
         functools.partial(first_kernel, class_half),
         out_shape=(out_type, value_type),
-        in_specs=[smem()] * 3 + [vmem() if whole_tiles else smem()] + [vmem()] * 3,
+        in_specs=[smem()] * 3 + [vmem() if whole_tiles else smem()] + [hbm()] * 3,
         out_specs=(hbm(), hbm()),
         scratch_shapes=[
+            pltpu.VMEM((1, batch), jnp.int32),
+            pltpu.VMEM((classes, 1, batch), f32),
+            pltpu.VMEM((blocks, block), jnp.int32),
             pltpu.VMEM((2 * LANES, batch), f32),
             pltpu.VMEM((batch, LANES), f32),
             acc,
@@ -485,7 +498,7 @@
             pltpu.SMEM((peers * slots,), jnp.int32),
             peer_sems,
             peer_sems,
-            pltpu.SemaphoreType.DMA((1,)),
+            pltpu.SemaphoreType.DMA((4,)),
         ],
         compiler_params=params(),
         name="first",

time: 174 us -> 175 us (level)
  transfers between devices with their start and end apart: 24 -> 24, of which waited for: 18 -> 18; matrix products, arithmetic and copies ran while one was open for 17% -> 16% of each run, Pallas kernels for 2% -> 2%
where the time goes in v10:
time: 175 us; the launch traced here: 173 us
  waiting for transfers between devices  61.7 us (35%)
  Pallas kernels  36.5 us (21%)
  starting transfers between devices  30.7 us (18%)
  matrix products  24.6 us (14%)
  other arithmetic  10.9 us (6%)
  local copies, waits for them, and re-layouts  7.7 us (4%)
    ppermute x12, waiting for transfers between devices, exchange(): return lax.ppermute(x, ('dom', 'col'), pairs)  40.1 us
    pallas_call x4, Pallas kernels, shards(): pl.pallas_call(functools.partial(far_kernel, slots, class_half, stride, l...  24.4 us
    all_to_all x4, starting transfers between devices, shards(): landed = lax.all_to_all(out, 'dom', split_axis=0, concat_axis=0, tiled=True)  18.8 us
    all_to_all x4, waiting for transfers between devices, shards(): landed = lax.all_to_all(out, 'dom', split_axis=0, concat_axis=0, tiled=True)  17.6 us
    ppermute x12, starting transfers between devices, exchange(): return lax.ppermute(x, ('dom', 'col'), pairs)  10.3 us
    dot_general x1, matrix products, shards(): pre_second = jnp.dot(tied, second_turned, preferred_element_type=f32)  7.25 us
    convert_element_type x1, other arithmetic, gelu_parts(): return ((x * half_up).astype(bf16), slope.astype(bf16))  6.92 us
    pallas_call x1, Pallas kernels, shards(): pl.pallas_call(functools.partial(first_kernel, class_half), out_shape=(ou...  6.17 us
  transfers between devices with their start and end apart: 24, of which 18 were waited for; matrix products, arithmetic and copies ran while one was open for 16% of the time, Pallas kernels for 2%

profile of v10, /device:TPU:0, one launch (start us, length us, event | category | flops | bytes accessed | tf_op | source)
XLA Modules:
  0.0 173.4 jit_solution(4072863965195299123)
XLA Ops:
  0.7 6.2 %first.1 = (bf16[8,192,128]{2,1,0:T(8,128)(2,1)}, bf16[3072,128]{1,0:T(8,128)(2,1)}) custom-call(s32[1]{0:T(128)} %bitcast.core_ref, s32[8]{0:T(128)} %bitcast.54, s32[256]{0:T(256)} %bitcast.64, s32[8,256]{1,0:T(8,128)} %bitcast.50, s32[1,256]{1,0:T(1,128)} %labels_in_ref.1, f32[172,1,256]{2,1,0:T(1,128)} %bitcast.49, s32[24,128]{1,0:T(8,128)} %bitcast.44), custom_call_target="tpu_custom_call" | custom-call | tf_op jit(solution)/shard_map/first/pallas_call | solution.py:485
  6.9 7.3 %all-to-all-start = ((bf16[8,192,128]{2,1,0:T(8,128)(2,1)}), bf16[8,192,128]{2,1,0:T(8,128)(2,1)S(1)}, u32[]{:S(2)}, u32[]{:S(2)}) async-start(bf16[8,192,128]{2,1,0:T(8,128)(2,1)} %get-tuple-element.63), calls=%async_computation | async-start | bytes 786432 | tf_op jit(solution)/shard_map/all_to_all | solution.py:549
  14.3 0.5 collective-permute-start.2
  14.8 2.8 %turn.1 = (bf16[128,1024]{1,0:T(8,128)(2,1)}, f32[1,1024]{1,0:T(1,128)}, bf16[1024,1024]{1,0:T(8,128)(2,1)}) custom-call(s32[1]{0:T(128)} %bitcast.core_ref, bf16[128,1024]{1,0:T(8,128)(2,1)} %first_ref, f32[1,1024]{1,0:T(1,128)} %bitcast.53, bf16[1024,1024]{1,0:T(8,128)(2,1)} %second_ref), custom_call_target="tpu_custom_call" | custom-call | tf_op jit(solution)/shard_map/turn/pallas_call | solution.py:507
  17.8 1.0 collective-permute-done
  18.8 0.7 concatenate.71.ints_ref
  19.5 6.3 %all-to-all-done.recv_ref = bf16[8,192,128]{2,1,0:T(8,128)(2,1)S(1)} async-done(((bf16[8,192,128]{2,1,0:T(8,128)(2,1)}), bf16[8,192,128]{2,1,0:T(8,128)(2,1)S(1)}, u32[]{:S(2)}, u32[]{:S(2)}) %all-to-all-start) | async-done | bytes 393248 | tf_op jit(solution)/shard_map/all_to_all | solution.py:549
  25.9 0.7 copy-done.8
  26.6 6.2 %far.3 = (bf16[8,192,128]{2,1,0:T(8,128)(2,1)}, bf16[3072,128]{1,0:T(8,128)(2,1)}) custom-call(s32[3072]{0:T(1024)} %concatenate.71.ints_ref, s32[24,128]{1,0:T(8,128)} %bitcast.45, bf16[8,192,128]{2,1,0:T(8,128)(2,1)} %copy-done.8, bf16[16,128,128]{2,1,0:T(8,128)(2,1)} %bitcast.35, bf16[16,128,128]{2,1,0:T(8,128)(2,1)} %copy-done.1, ...), custom_call_target="tpu_custom_call" | custom-call | tf_op jit(solution)/shard_map/far/pallas_call | solution.py:573
  32.9 3.6 %all-to-all-start.1 = ((bf16[8,192,128]{2,1,0:T(8,128)(2,1)}), bf16[8,192,128]{2,1,0:T(8,128)(2,1)S(1)}, u32[]{:S(2)}, u32[]{:S(2)}) async-start(bf16[8,192,128]{2,1,0:T(8,128)(2,1)} %get-tuple-element.74), calls=%async_computation.1 | async-start | bytes 786432 | tf_op jit(solution)/shard_map/all_to_all | solution.py:549
  36.6 0.9 maximum_select_fusion.2
  37.5 5.7 %add_convert_fusion.1 = (bf16[1536,1024]{1,0:T(8,128)(2,1)}, bf16[1536,1024]{1,0:T(8,128)(2,1)}) fusion(f32[1024]{0:T(1024)S(1)} %bitcast.66, bf16[1536,128]{1,0:T(8,128)(2,1)S(1)} %copy-done, bf16[128,1024]{1,0:T(8,128)(2,1)S(1)} %copy-done.23), kind=kOutput, calls=%fused_computation.7 | convolution fusion | flops 430964736 | bytes 6950912 | tf_op jit(solution)/shard_map/dot_general | solution.py:557
  43.2 4.9 %all-to-all-done.1.recv_ref = bf16[8,192,128]{2,1,0:T(8,128)(2,1)S(1)} async-done(((bf16[8,192,128]{2,1,0:T(8,128)(2,1)}), bf16[8,192,128]{2,1,0:T(8,128)(2,1)S(1)}, u32[]{:S(2)}, u32[]{:S(2)}) %all-to-all-start.1) | async-done | bytes 393248 | tf_op jit(solution)/shard_map/all_to_all | solution.py:549
  48.2 0.7 copy-done.9
  48.9 6.2 %far.4 = (bf16[8,192,128]{2,1,0:T(8,128)(2,1)}, bf16[3072,128]{1,0:T(8,128)(2,1)}) custom-call(s32[3072]{0:T(1024)} %concatenate.71.ints_ref, s32[24,128]{1,0:T(8,128)} %bitcast.46, bf16[8,192,128]{2,1,0:T(8,128)(2,1)} %copy-done.9, bf16[16,128,128]{2,1,0:T(8,128)(2,1)} %bitcast.36, bf16[16,128,128]{2,1,0:T(8,128)(2,1)} %copy-done.1, ...), custom_call_target="tpu_custom_call" | custom-call | tf_op jit(solution)/shard_map/far/pallas_call | solution.py:573
  55.1 3.6 %all-to-all-start.2 = ((bf16[8,192,128]{2,1,0:T(8,128)(2,1)}), bf16[8,192,128]{2,1,0:T(8,128)(2,1)S(1)}, u32[]{:S(2)}, u32[]{:S(2)}) async-start(bf16[8,192,128]{2,1,0:T(8,128)(2,1)} %get-tuple-element.76), calls=%async_computation.2 | async-start | bytes 786432 | tf_op jit(solution)/shard_map/all_to_all | solution.py:549
  58.8 7.2 %fusion.9 = f32[1536,1024]{1,0:T(8,128)} fusion(bf16[1536,1024]{1,0:T(8,128)(2,1)} %get-tuple-element.78, bf16[1024,1024]{1,0:T(8,128)(2,1)S(1)} %copy-done.21), kind=kOutput, calls=%fused_computation.58 | convolution fusion | flops 3221225472 | bytes 11534336 | tf_op jit(solution)/shard_map/dot_general | solution.py:564
  66.0 3.8 %all-to-all-done.2.recv_ref = bf16[8,192,128]{2,1,0:T(8,128)(2,1)S(1)} async-done(((bf16[8,192,128]{2,1,0:T(8,128)(2,1)}), bf16[8,192,128]{2,1,0:T(8,128)(2,1)S(1)}, u32[]{:S(2)}, u32[]{:S(2)}) %all-to-all-start.2) | async-done | bytes 393248 | tf_op jit(solution)/shard_map/all_to_all | solution.py:549
  69.9 0.7 copy-done.10
  70.6 6.2 %far.5 = (bf16[8,192,128]{2,1,0:T(8,128)(2,1)}, bf16[3072,128]{1,0:T(8,128)(2,1)}) custom-call(s32[3072]{0:T(1024)} %concatenate.71.ints_ref, s32[24,128]{1,0:T(8,128)} %bitcast.47, bf16[8,192,128]{2,1,0:T(8,128)(2,1)} %copy-done.10, bf16[16,128,128]{2,1,0:T(8,128)(2,1)} %bitcast.37, bf16[16,128,128]{2,1,0:T(8,128)(2,1)} %copy-done.1, ...), custom_call_target="tpu_custom_call" | custom-call | tf_op jit(solution)/shard_map/far/pallas_call | solution.py:573
  76.8 4.3 %all-to-all-start.3 = ((bf16[8,192,128]{2,1,0:T(8,128)(2,1)}), bf16[8,192,128]{2,1,0:T(8,128)(2,1)}, u32[]{:S(2)}, u32[]{:S(2)}) async-start(bf16[8,192,128]{2,1,0:T(8,128)(2,1)} %get-tuple-element.88), calls=%async_computation.3 | async-start | bytes 786432 | tf_op jit(solution)/shard_map/all_to_all | solution.py:549
  81.1 6.9 %add_convert_fusion = (bf16[1536,1024]{1,0:T(8,128)(2,1)S(1)}, bf16[1536,1024]{1,0:T(8,128)(2,1)}) fusion(f32[1536,1024]{1,0:T(8,128)} %fusion.9, f32[1024]{0:T(1024)S(1)} %copy-done.14), kind=kLoop, calls=%fused_computation.2 | loop fusion | flops 28311552 | bytes 12587008 | tf_op jit(solution)/shard_map/convert_element_type | solution.py:376
  88.1 1.2 add_convert_fusion.3.rest_0_
  89.3 2.4 %all-to-all-done.3.recv_ref = bf16[8,192,128]{2,1,0:T(8,128)(2,1)} async-done(((bf16[8,192,128]{2,1,0:T(8,128)(2,1)}), bf16[8,192,128]{2,1,0:T(8,128)(2,1)}, u32[]{:S(2)}, u32[]{:S(2)}) %all-to-all-start.3) | async-done | bytes 393248 | tf_op jit(solution)/shard_map/all_to_all | solution.py:549
  91.7 5.8 %far_last.1 = (bf16[1536,128]{1,0:T(8,128)(2,1)}, bf16[1536,128]{1,0:T(8,128)(2,1)}) custom-call(s32[3072]{0:T(1024)} %concatenate.71.ints_ref, s32[24,128]{1,0:T(8,128)} %bitcast.48, bf16[8,192,128]{2,1,0:T(8,128)(2,1)} %all-to-all-done.3.recv_ref, bf16[16,128,128]{2,1,0:T(8,128)(2,1)} %bitcast.38, bf16[16,128,128]{2,1,0:T(8,128)(2,1)} %copy-done.1, ...), custom_call_target="tpu_custom_call" | custom-call | tf_op jit(solution)/shard_map/far_last/pallas_call | solution.py:573
  97.6 1.1 constant_dynamic-update-slice_fusion.1
  98.7 1.0 collective-permute-done.3
  99.6 1.1 constant_dynamic-update-slice_fusion
  100.7 2.2 %fusion.8 = (bf16[1024]{0:T(1024)(128)(2,1)S(1)}, bf16[1536,1024]{1,0:T(8,128)(2,1)S(1)}) fusion(bf16[1536,256]{1,0:T(8,128)(2,1)S(1)} %constant_dynamic-update-slice_fusion, bf16[1024,256]{0,1:T(8,128)(2,1)} %maximum_select_fusion.2, bf16[1536,1024]{1,0:T(8,128)(2,1)S(1)} %get-tuple-element.87), kind=kOutput, calls=%fused_computation.57 | convolution fusion | flops 811596800 | bytes 7604224 | tf_op jit(solution)/shard_map/dot_general | solution.py:605
  103.0 0.6 convolution_convert_fusion.3
  103.6 1.4 copy-done.3
  105.0 3.6 %fusion.4 = (bf16[1024]{0:T(1024)(128)(2,1)S(1)}, f32[1536,1024]{1,0:T(8,128)S(1)}) fusion(bf16[1536,1024]{1,0:T(8,128)(2,1)S(1)} %copy-done.3, bf16[1536,1024]{1,0:T(8,128)(2,1)S(1)} %get-tuple-element.116, bf16[1024,1024]{1,0:T(8,128)(2,1)S(1)} %copy-done.22), kind=kOutput, calls=%fused_computation.53 | convolution fusion | flops 3227515904 | bytes 14682112 | tf_op jit(solution)/shard_map/dot_general | solution.py:614
  108.6 0.8 convolution_convert_fusion.4
  109.4 1.1 copy-done.4
  110.5 1.0 convolution_convert_fusion.2
  111.7 0.2 collective-permute-start.12
  111.9 1.4 convolution_convert_fusion
  113.3 0.4 collective-permute-start.4
  113.7 0.6 convolution_convert_fusion.5
  114.4 0.2 add_convert_fusion.4
  114.6 1.5 collective-permute-start.13
  116.2 1.4 add_convert_fusion.2
  117.6 1.0 collective-permute-start.5
  118.6 2.8 %collective-permute-done.13 = bf16[288,512]{1,0:T(8,128)(2,1)S(1)} collective-permute-done((bf16[288,512]{1,0:T(8,128)(2,1)S(1)}, bf16[288,512]{1,0:T(8,128)(2,1)S(1)}, u32[]{:S(2)}, u32[]{:S(2)}) %collective-permute-start.13) | collective-permute-done | bytes 294944 | tf_op jit(solution)/shard_map/ppermute | solution.py:389
  121.5 4.1 %collective-permute-done.5 = bf16[384,512]{1,0:T(8,128)(2,1)S(1)} collective-permute-done((bf16[384,512]{1,0:T(8,128)(2,1)S(1)}, bf16[384,512]{1,0:T(8,128)(2,1)S(1)}, u32[]{:S(2)}, u32[]{:S(2)}) %collective-permute-start.5) | collective-permute-done | bytes 393248 | tf_op jit(solution)/shard_map/ppermute | solution.py:389
  125.6 0.1 add_convert_fusion.5
  125.8 1.0 collective-permute-start.6
  126.8 1.2 collective-permute-start.14
  128.0 3.6 %collective-permute-done.6 = bf16[384,256]{1,0:T(8,128)(2,1)S(1)} collective-permute-done((bf16[384,256]{1,0:T(8,128)(2,1)S(1)}, bf16[384,256]{1,0:T(8,128)(2,1)S(1)}, u32[]{:S(2)}, u32[]{:S(2)}) %collective-permute-start.6) | collective-permute-done | bytes 196640 | tf_op jit(solution)/shard_map/ppermute | solution.py:389
  131.7 1.0 collective-permute-start.7
  132.7 0.4 collective-permute-done.14
  133.2 5.1 %collective-permute-done.7 = bf16[384,128]{1,0:T(8,128)(2,1)S(1)} collective-permute-done((bf16[384,128]{1,0:T(8,128)(2,1)S(1)}, bf16[384,128]{1,0:T(8,128)(2,1)S(1)}, u32[]{:S(2)}, u32[]{:S(2)}) %collective-permute-start.7) | collective-permute-done | bytes 98336 | tf_op jit(solution)/shard_map/ppermute | solution.py:389
  138.4 3.0 %collective-permute-start.15 = (bf16[288,128]{1,0:T(8,128)(2,1)S(1)}, bf16[288,128]{1,0:T(8,128)(2,1)S(1)}, u32[]{:S(2)}, u32[]{:S(2)}) collective-permute-start(bf16[288,128]{1,0:T(8,128)(2,1)S(1)} %broadcast_select_fusion.5), channel_id=1, source_target_pairs={{0,8},{1,9},{2,10},{3,11},{4,12},{5,13},{6,14},{7,15},{8,0},{9,1},... | collective-permute-start | bytes 221192 | tf_op jit(solution)/shard_map/ppermute | solution.py:389
  141.4 4.6 %collective-permute-done.8 = bf16[384,128]{1,0:T(8,128)(2,1)S(1)} collective-permute-done((bf16[384,128]{1,0:T(8,128)(2,1)S(1)}, bf16[384,128]{1,0:T(8,128)(2,1)S(1)}, u32[]{:S(2)}, u32[]{:S(2)}) %collective-permute-start.8) | collective-permute-done | bytes 98336 | tf_op jit(solution)/shard_map/ppermute | solution.py:389
  146.1 1.4 collective-permute-done.15
  147.6 7.0 %collective-permute-done.9 = bf16[384,256]{1,0:T(8,128)(2,1)S(1)} collective-permute-done((bf16[384,256]{1,0:T(8,128)(2,1)S(1)}, bf16[384,256]{1,0:T(8,128)(2,1)S(1)}, u32[]{:S(2)}, u32[]{:S(2)}) %collective-permute-start.9) | collective-permute-done | bytes 196640 | tf_op jit(solution)/shard_map/ppermute | solution.py:389
  154.9 5.9 %collective-permute-done.17 = bf16[288,256]{1,0:T(8,128)(2,1)S(1)} collective-permute-done((bf16[288,256]{1,0:T(8,128)(2,1)S(1)}, bf16[288,256]{1,0:T(8,128)(2,1)S(1)}, u32[]{:S(2)}, u32[]{:S(2)}) %collective-permute-start.17) | collective-permute-done | bytes 147488 | tf_op jit(solution)/shard_map/ppermute | solution.py:389
  161.0 1.3 collective-permute-start.18
  162.3 0.3 collective-permute-done.10
  162.6 0.2 maximum_select_fusion.mine_one
  162.9 4.9 %collective-permute-done.18 = bf16[288,512]{1,0:T(8,128)(2,1)S(1)} collective-permute-done((bf16[288,512]{1,0:T(8,128)(2,1)S(1)}, bf16[288,512]{1,0:T(8,128)(2,1)S(1)}, u32[]{:S(2)}, u32[]{:S(2)}) %collective-permute-start.18) | collective-permute-done | bytes 294944 | tf_op jit(solution)/shard_map/ppermute | solution.py:389
  167.8 0.2 maximum_select_fusion.1.mine_two
  168.0 2.0 %collective-permute-done.19.theirs_two = bf16[288,1024]{1,0:T(8,128)(2,1)S(1)} collective-permute-done((bf16[288,1024]{1,0:T(8,128)(2,1)S(1)}, bf16[288,1024]{1,0:T(8,128)(2,1)S(1)}, u32[]{:S(2)}, u32[]{:S(2)}) %collective-permute-start.19) | collective-permute-done | bytes 589856 | tf_op jit(solution)/shard_map/ppermute | solution.py:380
  170.0 3.2 %finish.1 = (f32[128,1024]{1,0:T(8,128)}, f32[1,1024]{1,0:T(1,128)}, f32[1024,1024]{1,0:T(8,128)}, f32[1,1024]{1,0:T(1,128)}, f32[172,1024]{1,0:T(8,128)}) custom-call(s32[1]{0:T(128)} %bitcast.core_ref, bf16[384,1024]{1,0:T(8,128)(2,1)S(1)} %maximum_select_fusion.mine_one, bf16[384,1024]{1,0:T(8,128)(2,1)S(1)} %collective-permute-done.11.theirs_one, ...), custom_call_target="tpu_custom_call" | custom-call | tf_op jit(solution)/shard_map/finish/pallas_call | solution.py:642
  (93 shorter events, 2.0 us)
Async XLA Ops:
  0.6 36.9 %copy-start = (bf16[1536,128]{1,0:T(8,128)(2,1)S(1)}, bf16[1536,128]{1,0:T(8,128)(2,1)}, u32[]{:S(2)}) copy-start(bf16[1536,128]{1,0:T(8,128)(2,1)} %param.18) | copy-start | bytes 1179652
  0.7 18.2 %copy-start.15 = (s32[1,8]{1,0:T(1,128)S(1)}, s32[1,8]{1,0:T(1,128)}, u32[]{:S(2)}) copy-start(s32[1,8]{1,0:T(1,128)} %param.31) | copy-start | bytes 100
  0.7 17.1 %copy-start.13 = (s32[1,8,256]{2,1,0:T(8,128)S(1)}, s32[1,8,256]{2,1,0:T(8,128)}, u32[]{:S(2)}) copy-start(s32[1,8,256]{2,1,0:T(8,128)} %param.30) | copy-start | bytes 24580
  0.7 16.9 %copy-start.16 = (s32[1,1,16]{2,1,0:T(1,128)S(1)}, s32[1,1,16]{2,1,0:T(1,128)}, u32[]{:S(2)}) copy-start(s32[1,1,16]{2,1,0:T(1,128)} %param.25) | copy-start | bytes 196
  0.7 16.9 %copy-start.17 = (s32[1,1,16]{2,1,0:T(1,128)S(1)}, s32[1,1,16]{2,1,0:T(1,128)}, u32[]{:S(2)}) copy-start(s32[1,1,16]{2,1,0:T(1,128)} %param.26) | copy-start | bytes 196
  0.7 16.9 %copy-start.18 = (s32[1,1,16]{2,1,0:T(1,128)S(1)}, s32[1,1,16]{2,1,0:T(1,128)}, u32[]{:S(2)}) copy-start(s32[1,1,16]{2,1,0:T(1,128)} %param.28) | copy-start | bytes 196
  0.7 16.9 %copy-start.19 = (s32[1,1,16]{2,1,0:T(1,128)S(1)}, s32[1,1,16]{2,1,0:T(1,128)}, u32[]{:S(2)}) copy-start(s32[1,1,16]{2,1,0:T(1,128)} %param.29) | copy-start | bytes 196
  6.9 19.0 %all-to-all-start = ((bf16[8,192,128]{2,1,0:T(8,128)(2,1)}), bf16[8,192,128]{2,1,0:T(8,128)(2,1)S(1)}, u32[]{:S(2)}, u32[]{:S(2)}) async-start(bf16[8,192,128]{2,1,0:T(8,128)(2,1)} %get-tuple-element.63), calls=%async_computation | async-start | bytes 786432 | tf_op jit(solution)/shard_map/all_to_all | solution.py:549
  14.2 18.7 %copy-start.11 = (bf16[1024,172]{0,1:T(8,128)(2,1)S(1)}, bf16[1024,172]{0,1:T(8,128)(2,1)}, u32[]{:S(2)}) copy-start(bf16[1024,172]{0,1:T(8,128)(2,1)} %param.23) | copy-start | bytes 1056772
  14.2 18.7 %copy-start.20 = (pred[128]{0:T(512)(128)(4,1)S(1)}, pred[128]{0:T(512)(128)(4,1)}, u32[]{:S(2)}) copy-start(pred[128]{0:T(512)(128)(4,1)} %constant.33.clone.1) | copy-start | bytes 388
  14.2 5.3 %collective-permute-start.1 = (bf16[16,128,128]{2,1,0:T(8,128)(2,1)}, bf16[16,128,128]{2,1,0:T(8,128)(2,1)S(1)}, u32[]{:S(2)}, u32[]{:S(2)}) collective-permute-start(bf16[16,128,128]{2,1,0:T(8,128)(2,1)} %bitcast.34), channel_id=1, source_target_pairs={{0,1},{1,0},{2,3},{3,2},{4,5},{5,4},{6,7},{7,6},{8,9},{9,8},{10,11... | collective-permute-start | bytes 1572872 | tf_op jit(solution)/shard_map/ppermute | solution.py:380
  14.3 5.2 %collective-permute-start.2 = (bf16[16,128,128]{2,1,0:T(8,128)(2,1)}, bf16[16,128,128]{2,1,0:T(8,128)(2,1)S(1)}, u32[]{:S(2)}, u32[]{:S(2)}) collective-permute-start(bf16[16,128,128]{2,1,0:T(8,128)(2,1)} %bitcast.39), channel_id=1, source_target_pairs={{0,1},{1,0},{2,3},{3,2},{4,5},{5,4},{6,7},{7,6},{8,9},{9,8},{10,11... | collective-permute-start | bytes 1572872 | tf_op jit(solution)/shard_map/ppermute | solution.py:380
  14.8 21.8 %slice-start = ((bf16[1024,172]{0,1:T(8,128)(2,1)}), bf16[1024,84]{0,1:T(8,128)(2,1)S(1)}, s32[]{:S(2)}) async-start(bf16[1024,172]{0,1:T(8,128)(2,1)} %param.23), calls=%async_computation.4 | async-start | bytes 360448 | tf_op jit(solution)/shard_map/slice | solution.py:559
  17.7 1.1 collective-permute-start
  19.5 18.1 %copy-start.23 = (bf16[128,1024]{1,0:T(8,128)(2,1)S(1)}, bf16[128,1024]{1,0:T(8,128)(2,1)}, u32[]{:S(2)}) copy-start(bf16[128,1024]{1,0:T(8,128)(2,1)} %get-tuple-element.70) | copy-start | bytes 786436
  19.5 18.1 %copy-start.24 = (f32[1,1024]{1,0:T(1,128)S(1)}, f32[1,1024]{1,0:T(1,128)}, u32[]{:S(2)}) copy-start(f32[1,1024]{1,0:T(1,128)} %get-tuple-element.71) | copy-start | bytes 12292
  19.5 6.4 %copy-start.1 = (bf16[16,128,128]{2,1,0:T(8,128)(2,1)}, bf16[16,128,128]{2,1,0:T(8,128)(2,1)S(1)}, u32[]{:S(2)}) copy-start(bf16[16,128,128]{2,1,0:T(8,128)(2,1)S(1)} %collective-permute-done.1.other_halo_ref) | copy-start | bytes 1572868
  19.5 6.4 %copy-start.2 = (bf16[16,128,128]{2,1,0:T(8,128)(2,1)}, bf16[16,128,128]{2,1,0:T(8,128)(2,1)S(1)}, u32[]{:S(2)}) copy-start(bf16[16,128,128]{2,1,0:T(8,128)(2,1)S(1)} %collective-permute-done.2.other_local_ref) | copy-start | bytes 1572868
  25.9 0.7 copy-start.8
  32.9 15.2 %all-to-all-start.1 = ((bf16[8,192,128]{2,1,0:T(8,128)(2,1)}), bf16[8,192,128]{2,1,0:T(8,128)(2,1)S(1)}, u32[]{:S(2)}, u32[]{:S(2)}) async-start(bf16[8,192,128]{2,1,0:T(8,128)(2,1)} %get-tuple-element.74), calls=%async_computation.1 | async-start | bytes 786432 | tf_op jit(solution)/shard_map/all_to_all | solution.py:549
  43.2 15.5 %copy-start.21 = (bf16[1024,1024]{1,0:T(8,128)(2,1)S(1)}, bf16[1024,1024]{1,0:T(8,128)(2,1)}, u32[]{:S(2)}) copy-start(bf16[1024,1024]{1,0:T(8,128)(2,1)} %get-tuple-element.79) | copy-start | bytes 6291460
  48.2 0.7 copy-start.9
  55.1 14.7 %all-to-all-start.2 = ((bf16[8,192,128]{2,1,0:T(8,128)(2,1)}), bf16[8,192,128]{2,1,0:T(8,128)(2,1)S(1)}, u32[]{:S(2)}, u32[]{:S(2)}) async-start(bf16[8,192,128]{2,1,0:T(8,128)(2,1)} %get-tuple-element.76), calls=%async_computation.2 | async-start | bytes 786432 | tf_op jit(solution)/shard_map/all_to_all | solution.py:549
  66.0 15.1 %copy-start.14 = (f32[1024]{0:T(1024)S(1)}, f32[1024]{0:T(1024)}, u32[]{:S(2)}) copy-start(f32[1024]{0:T(1024)} %param.22) | copy-start | bytes 12292
  69.9 0.7 copy-start.10
  76.8 14.9 %all-to-all-start.3 = ((bf16[8,192,128]{2,1,0:T(8,128)(2,1)}), bf16[8,192,128]{2,1,0:T(8,128)(2,1)}, u32[]{:S(2)}, u32[]{:S(2)}) async-start(bf16[8,192,128]{2,1,0:T(8,128)(2,1)} %get-tuple-element.88), calls=%async_computation.3 | async-start | bytes 786432 | tf_op jit(solution)/shard_map/all_to_all | solution.py:549
  81.1 7.0 %copy-start.5 = (bf16[3072,128]{1,0:T(8,128)(2,1)S(1)}, bf16[3072,128]{1,0:T(8,128)(2,1)}, u32[]{:S(2)}) copy-start(bf16[3072,128]{1,0:T(8,128)(2,1)} %get-tuple-element.86.value_in_ref) | copy-start | bytes 2359300
  81.1 6.9 %copy-start.6 = (bf16[3072,128]{1,0:T(8,128)(2,1)S(1)}, bf16[3072,128]{1,0:T(8,128)(2,1)}, u32[]{:S(2)}) copy-start(bf16[3072,128]{1,0:T(8,128)(2,1)} %get-tuple-element.85.value_in_ref) | copy-start | bytes 2359300
  81.1 6.9 %copy-start.7 = (bf16[3072,128]{1,0:T(8,128)(2,1)S(1)}, bf16[3072,128]{1,0:T(8,128)(2,1)}, u32[]{:S(2)}) copy-start(bf16[3072,128]{1,0:T(8,128)(2,1)} %get-tuple-element.84.value_in_ref) | copy-start | bytes 2359300
  97.5 2.1 %collective-permute-start.3 = (bf16[1536,128]{1,0:T(8,128)(2,1)}, bf16[1536,128]{1,0:T(8,128)(2,1)}, u32[]{:S(2)}, u32[]{:S(2)}) collective-permute-start(bf16[1536,128]{1,0:T(8,128)(2,1)} %get-tuple-element.92), channel_id=1, source_target_pairs={{0,1},{1,0},{2,3},{3,2},{4,5},{5,4},{6,7},{7,6},{8,9},{9,8},{10,11... | collective-permute-start | bytes 1179656 | tf_op jit(solution)/shard_map/ppermute | solution.py:380
  100.7 2.3 %copy-start.12 = (bf16[1536,1024]{1,0:T(8,128)(2,1)S(1)}, bf16[1536,1024]{1,0:T(8,128)(2,1)}, u32[]{:S(2)}) copy-start(bf16[1536,1024]{1,0:T(8,128)(2,1)} %get-tuple-element.78) | copy-start | bytes 9437188
  100.7 2.9 %copy-start.22 = (bf16[1024,1024]{1,0:T(8,128)(2,1)S(1)}, bf16[1024,1024]{1,0:T(8,128)(2,1)}, u32[]{:S(2)}) copy-start(bf16[1024,1024]{1,0:T(8,128)(2,1)} %get-tuple-element.79) | copy-start | bytes 6291460
  103.0 2.0 %copy-start.3 = (bf16[1536,1024]{1,0:T(8,128)(2,1)S(1)}, bf16[1536,1024]{1,0:T(8,128)(2,1)}, u32[]{:S(2)}) copy-start(bf16[1536,1024]{1,0:T(8,128)(2,1)} %get-tuple-element.94) | copy-start | bytes 9437188
  108.6 1.9 %copy-start.4 = (bf16[1536,1024]{1,0:T(8,128)(2,1)S(1)}, bf16[1536,1024]{1,0:T(8,128)(2,1)}, u32[]{:S(2)}) copy-start(bf16[1536,1024]{1,0:T(8,128)(2,1)} %get-tuple-element.95) | copy-start | bytes 9437188
  111.7 2.7 %collective-permute-start.12 = (bf16[288,1024]{1,0:T(8,128)(2,1)S(1)}, bf16[288,1024]{1,0:T(8,128)(2,1)S(1)}, u32[]{:S(2)}, u32[]{:S(2)}) collective-permute-start(bf16[288,1024]{1,0:T(8,128)(2,1)S(1)} %pad_maximum_fusion), channel_id=1, source_target_pairs={{0,1},{1,0},{2,3},{3,2},{4,5},{5,4},{6,7},{7,6},{8,9},{9,8},{10,11... | collective-permute-start | bytes 1769480 | tf_op jit(solution)/shard_map/ppermute | solution.py:380
  113.3 2.9 %collective-permute-start.4 = (bf16[384,1024]{1,0:T(8,128)(2,1)S(1)}, bf16[384,1024]{1,0:T(8,128)(2,1)S(1)}, u32[]{:S(2)}, u32[]{:S(2)}) collective-permute-start(bf16[384,1024]{1,0:T(8,128)(2,1)S(1)} %convolution_convert_fusion), channel_id=1, source_target_pairs={{0,1},{1,0},{2,3},{3,2},{4,5},{5,4},{6,7},{7,6},{8,9},{9,8},{10,11... | collective-permute-start | bytes 2359304 | tf_op jit(solution)/shard_map/ppermute | solution.py:380
  114.6 6.8 %collective-permute-start.13 = (bf16[288,512]{1,0:T(8,128)(2,1)S(1)}, bf16[288,512]{1,0:T(8,128)(2,1)S(1)}, u32[]{:S(2)}, u32[]{:S(2)}) collective-permute-start(bf16[288,512]{1,0:T(8,128)(2,1)S(1)} %broadcast_select_fusion.1), channel_id=1, source_target_pairs={{0,2},{1,5},{2,0},{3,7},{4,6},{5,1},{6,4},{7,3},{8,10},{9,13},{10,... | collective-permute-start | bytes 884744 | tf_op jit(solution)/shard_map/ppermute | solution.py:389
  117.6 8.0 %collective-permute-start.5 = (bf16[384,512]{1,0:T(8,128)(2,1)S(1)}, bf16[384,512]{1,0:T(8,128)(2,1)S(1)}, u32[]{:S(2)}, u32[]{:S(2)}) collective-permute-start(bf16[384,512]{1,0:T(8,128)(2,1)S(1)} %broadcast_select_fusion), channel_id=1, source_target_pairs={{0,2},{1,5},{2,0},{3,7},{4,6},{5,1},{6,4},{7,3},{8,10},{9,13},{10,... | collective-permute-start | bytes 1179656 | tf_op jit(solution)/shard_map/ppermute | solution.py:389
  125.8 5.7 %collective-permute-start.6 = (bf16[384,256]{1,0:T(8,128)(2,1)S(1)}, bf16[384,256]{1,0:T(8,128)(2,1)S(1)}, u32[]{:S(2)}, u32[]{:S(2)}) collective-permute-start(bf16[384,256]{1,0:T(8,128)(2,1)S(1)} %broadcast_select_fusion.2), channel_id=1, source_target_pairs={{0,4},{1,3},{2,6},{3,1},{4,0},{5,7},{6,2},{7,5},{8,12},{9,11},{10,... | collective-permute-start | bytes 589832 | tf_op jit(solution)/shard_map/ppermute | solution.py:389
  126.8 6.3 %collective-permute-start.14 = (bf16[288,256]{1,0:T(8,128)(2,1)S(1)}, bf16[288,256]{1,0:T(8,128)(2,1)S(1)}, u32[]{:S(2)}, u32[]{:S(2)}) collective-permute-start(bf16[288,256]{1,0:T(8,128)(2,1)S(1)} %broadcast_select_fusion.3), channel_id=1, source_target_pairs={{0,4},{1,3},{2,6},{3,1},{4,0},{5,7},{6,2},{7,5},{8,12},{9,11},{10,... | collective-permute-start | bytes 442376 | tf_op jit(solution)/shard_map/ppermute | solution.py:389
  131.7 6.6 %collective-permute-start.7 = (bf16[384,128]{1,0:T(8,128)(2,1)S(1)}, bf16[384,128]{1,0:T(8,128)(2,1)S(1)}, u32[]{:S(2)}, u32[]{:S(2)}) collective-permute-start(bf16[384,128]{1,0:T(8,128)(2,1)S(1)} %broadcast_select_fusion.4), channel_id=1, source_target_pairs={{0,8},{1,9},{2,10},{3,11},{4,12},{5,13},{6,14},{7,15},{8,0},{9,1},... | collective-permute-start | bytes 294920 | tf_op jit(solution)/shard_map/ppermute | solution.py:389
  138.3 7.6 %collective-permute-start.8 = (bf16[384,128]{1,0:T(8,128)(2,1)S(1)}, bf16[384,128]{1,0:T(8,128)(2,1)S(1)}, u32[]{:S(2)}, u32[]{:S(2)}) collective-permute-start(bf16[384,128]{1,0:T(8,128)(2,1)S(1)} %add_convert_fusion.9), channel_id=1, source_target_pairs={{0,8},{1,9},{2,10},{3,11},{4,12},{5,13},{6,14},{7,15},{8,0},{9,1},... | collective-permute-start | bytes 294920 | tf_op jit(solution)/shard_map/ppermute | solution.py:389
  138.4 9.1 %collective-permute-start.15 = (bf16[288,128]{1,0:T(8,128)(2,1)S(1)}, bf16[288,128]{1,0:T(8,128)(2,1)S(1)}, u32[]{:S(2)}, u32[]{:S(2)}) collective-permute-start(bf16[288,128]{1,0:T(8,128)(2,1)S(1)} %broadcast_select_fusion.5), channel_id=1, source_target_pairs={{0,8},{1,9},{2,10},{3,11},{4,12},{5,13},{6,14},{7,15},{8,0},{9,1},... | collective-permute-start | bytes 221192 | tf_op jit(solution)/shard_map/ppermute | solution.py:389
  146.0 8.6 %collective-permute-start.9 = (bf16[384,256]{1,0:T(8,128)(2,1)S(1)}, bf16[384,256]{1,0:T(8,128)(2,1)S(1)}, u32[]{:S(2)}, u32[]{:S(2)}) collective-permute-start(bf16[384,256]{1,0:T(8,128)(2,1)S(1)} %maximum_select_fusion.5), channel_id=1, source_target_pairs={{0,4},{1,3},{2,6},{3,1},{4,0},{5,7},{6,2},{7,5},{8,12},{9,11},{10,... | collective-permute-start | bytes 589832 | tf_op jit(solution)/shard_map/ppermute | solution.py:389
  147.5 7.3 %collective-permute-start.16 = (bf16[288,128]{1,0:T(8,128)(2,1)S(1)}, bf16[288,128]{1,0:T(8,128)(2,1)S(1)}, u32[]{:S(2)}, u32[]{:S(2)}) collective-permute-start(bf16[288,128]{1,0:T(8,128)(2,1)S(1)} %add_convert_fusion.10), channel_id=1, source_target_pairs={{0,8},{1,9},{2,10},{3,11},{4,12},{5,13},{6,14},{7,15},{8,0},{9,1},... | collective-permute-start | bytes 221192 | tf_op jit(solution)/shard_map/ppermute | solution.py:389
  154.7 7.8 %collective-permute-start.10 = (bf16[384,512]{1,0:T(8,128)(2,1)S(1)}, bf16[384,512]{1,0:T(8,128)(2,1)S(1)}, u32[]{:S(2)}, u32[]{:S(2)}) collective-permute-start(bf16[384,512]{1,0:T(8,128)(2,1)S(1)} %maximum_select_fusion.3), channel_id=1, source_target_pairs={{0,2},{1,5},{2,0},{3,7},{4,6},{5,1},{6,4},{7,3},{8,10},{9,13},{10,... | collective-permute-start | bytes 1179656 | tf_op jit(solution)/shard_map/ppermute | solution.py:389
  154.9 6.0 %collective-permute-start.17 = (bf16[288,256]{1,0:T(8,128)(2,1)S(1)}, bf16[288,256]{1,0:T(8,128)(2,1)S(1)}, u32[]{:S(2)}, u32[]{:S(2)}) collective-permute-start(bf16[288,256]{1,0:T(8,128)(2,1)S(1)} %maximum_select_fusion.6), channel_id=1, source_target_pairs={{0,4},{1,3},{2,6},{3,1},{4,0},{5,7},{6,2},{7,5},{8,12},{9,11},{10,... | collective-permute-start | bytes 442376 | tf_op jit(solution)/shard_map/ppermute | solution.py:389
  161.0 6.8 %collective-permute-start.18 = (bf16[288,512]{1,0:T(8,128)(2,1)S(1)}, bf16[288,512]{1,0:T(8,128)(2,1)S(1)}, u32[]{:S(2)}, u32[]{:S(2)}) collective-permute-start(bf16[288,512]{1,0:T(8,128)(2,1)S(1)} %maximum_select_fusion.4), channel_id=1, source_target_pairs={{0,2},{1,5},{2,0},{3,7},{4,6},{5,1},{6,4},{7,3},{8,10},{9,13},{10,... | collective-permute-start | bytes 884744 | tf_op jit(solution)/shard_map/ppermute | solution.py:389
  162.8 7.3 %collective-permute-start.11 = (bf16[384,1024]{1,0:T(8,128)(2,1)S(1)}, bf16[384,1024]{1,0:T(8,128)(2,1)S(1)}, u32[]{:S(2)}, u32[]{:S(2)}) collective-permute-start(bf16[384,1024]{1,0:T(8,128)(2,1)S(1)} %maximum_select_fusion.mine_one), channel_id=1, source_target_pairs={{0,1},{1,0},{2,3},{3,2},{4,5},{5,4},{6,7},{7,6},{8,9},{9,8},{10,11... | collective-permute-start | bytes 2359304 | tf_op jit(solution)/shard_map/ppermute | solution.py:380
  168.0 2.1 %collective-permute-start.19 = (bf16[288,1024]{1,0:T(8,128)(2,1)S(1)}, bf16[288,1024]{1,0:T(8,128)(2,1)S(1)}, u32[]{:S(2)}, u32[]{:S(2)}) collective-permute-start(bf16[288,1024]{1,0:T(8,128)(2,1)S(1)} %maximum_select_fusion.1.mine_two), channel_id=1, source_target_pairs={{0,1},{1,0},{2,3},{3,2},{4,5},{5,4},{6,7},{7,6},{8,9},{9,8},{10,11... | collective-permute-start | bytes 1769480 | tf_op jit(solution)/shard_map/ppermute | solution.py:380

commit v11 on v9

--- a/solution.py
+++ b/solution.py
@@ -315,38 +315,52 @@
     wait_packed(packed_ref, out_ref, sems)
 
 
-def finish_kernel(class_half, core_ref, mine_one, theirs_one, mine_two, theirs_two, first_ref, first_bias_ref,
-                  second_ref, second_bias_ref, third_ref, wide_v, out_sems):
-    one = mine_one.shape[0]
-    hidden = second_ref.shape[0]
-    feat = first_ref.shape[0]
-    classes = third_ref.shape[0]
-    half, feat_half = hidden // 2, feat // 2
+def write_rows(core_ref, mine_ref, theirs_ref, second_ref, wide_v, out_sems, start, count, step):
+    half = second_ref.shape[0] // 2
     is_first = core_ref[0] == 0
-
-    def both(start, count):
-        mine_ref, theirs_ref = (mine_one, theirs_one) if start < one else (mine_two, theirs_two)
-        at = start if start < one else start - one
-        mine = mine_ref[at : at + count, :].astype(f32)
-        theirs = theirs_ref[at : at + count, :].astype(f32)
-        return jnp.where(is_first, mine, theirs), jnp.where(is_first, theirs, mine)
-
-    step = math.gcd(one, half)
     outs = []
-    for start in range(0, half, step):
-        for k, value in enumerate(both(start, step)):
-            at = k * half + start
-            wide_v[at : at + step, :] = value
+    for at in range(0, count, step):
+        mine = mine_ref[at : at + step, :].astype(f32)
+        theirs = theirs_ref[at : at + step, :].astype(f32)
+        pair = jnp.where(is_first, mine, theirs), jnp.where(is_first, theirs, mine)
+        for k in range(2):
+            here = pl.ds(k * count + at, step)
+            wide_v[here, :] = pair[k]
             out = pltpu.make_async_copy(
-                wide_v.at[pl.ds(at, step)], second_ref.at[pl.ds(at, step)], out_sems.at[2 * (start // step) + k]
+                wide_v.at[here],
+                second_ref.at[pl.ds(k * half + start + at, step)],
+                out_sems.at[2 * (at // step) + k],
             )
             out.start()
             outs.append(out)
-    low, high = both(half + feat_half, class_half)
+    return outs
+
+
+def finish_lead_kernel(step, core_ref, mine_ref, theirs_ref, second_ref, wide_v, out_sems):
+    count = mine_ref.shape[0]
+    for out in write_rows(core_ref, mine_ref, theirs_ref, second_ref, wide_v, out_sems, 0, count, step):
+        out.wait()
+
+
+def finish_kernel(class_half, lead, step, core_ref, mine_ref, theirs_ref, unused_ref, first_ref, first_bias_ref,
+                  second_ref, second_bias_ref, third_ref, wide_v, out_sems):
+    half, feat = second_ref.shape[0] // 2, first_ref.shape[0]
+    classes = third_ref.shape[0]
+    feat_half = feat // 2
+    count = half - lead
+    outs = write_rows(core_ref, mine_ref, theirs_ref, second_ref, wide_v, out_sems, lead, count, step)
+    is_first = core_ref[0] == 0
+
+    def both(start, size):
+        mine = mine_ref[start : start + size, :].astype(f32)
+        theirs = theirs_ref[start : start + size, :].astype(f32)
+        return jnp.where(is_first, mine, theirs), jnp.where(is_first, theirs, mine)
+
+    low, high = both(count + feat_half, class_half)
     third_ref[0:class_half, :] = low
     third_ref[class_half:classes, :] = high[: classes - class_half]
-    firsts = both(half, feat_half)
-    biases = both(half + feat_half + class_half, 8)
+    firsts = both(count, feat_half)
+    biases = both(count + feat_half + class_half, 8)
     for k in range(2):
         at = slice(k * half, (k + 1) * half)
         first_ref[0:feat_half, at] = firsts[k][:, :half]
@@ -626,24 +640,38 @@
     mine_lead = sum_over_domains((keep_lead.astype(f32) + got_lead.astype(f32)).astype(bf16))
     mine_rest = sum_over_domains((keep_rest.astype(f32) + got_rest.astype(f32)).astype(bf16))
     theirs_lead, theirs_rest = swap_cores(mine_lead), swap_cores(mine_rest)
+    step = math.gcd(lead, half)
+    second_type = jax.ShapeDtypeStruct((hidden, hidden), f32)
+    small_grant = pltpu.CompilerParams(vmem_limit_bytes=24 * 1024 * 1024)
+    second_lead = pl.pallas_call(
+        functools.partial(finish_lead_kernel, step),
+        out_shape=second_type,
+        in_specs=[smem(), vmem(), vmem()],
+        out_specs=hbm(),
+        scratch_shapes=[pltpu.VMEM((2 * lead, hidden), f32), pltpu.SemaphoreType.DMA((2 * (lead // step),))],
+        compiler_params=small_grant,
+        cost_estimate=pl.CostEstimate(flops=2 * lead * hidden, bytes_accessed=12 * lead * hidden, transcendentals=0),
+        name="finish_lead",
+    )(core_arg, mine_lead, theirs_lead)
     first_out, first_bias_out, second_out, second_bias_out, third_out = pl.pallas_call(
-        functools.partial(finish_kernel, class_half),
+        functools.partial(finish_kernel, class_half, lead, step),
         out_shape=(
             jax.ShapeDtypeStruct((feat, hidden), f32),
             jax.ShapeDtypeStruct((1, hidden), f32),
-            jax.ShapeDtypeStruct((hidden, hidden), f32),
+            second_type,
             jax.ShapeDtypeStruct((1, hidden), f32),
             jax.ShapeDtypeStruct((classes, hidden), f32),
         ),
-        in_specs=[smem()] + [vmem()] * 4,
+        in_specs=[smem(), vmem(), vmem(), hbm()],
         out_specs=(vmem(), vmem(), hbm(), vmem(), vmem()),
         scratch_shapes=[
-            pltpu.VMEM((hidden, hidden), f32),
-            pltpu.SemaphoreType.DMA((2 * (half // math.gcd(lead, half)),)),
+            pltpu.VMEM((2 * (half - lead), hidden), f32),
+            pltpu.SemaphoreType.DMA((2 * ((half - lead) // step),)),
         ],
-        compiler_params=pltpu.CompilerParams(vmem_limit_bytes=24 * 1024 * 1024),
+        input_output_aliases={3: 2},
+        compiler_params=small_grant,
         name="finish",
-    )(core_arg, mine_lead, theirs_lead, mine_rest, theirs_rest)
+    )(core_arg, mine_rest, theirs_rest, second_lead)
     return first_out, first_bias_out.reshape(hidden), second_out, second_bias_out.reshape(hidden), third_out.T
 
 

time: 174 us -> 173 us (level)
  waiting for transfers between devices: 61.7 us -> 59.8 us
    dot_general x6, matrix products: 5.8 us -> 7.76 us  [contract(): lax.dot_general(a, b, (((0,), (0,)), ((), ())), preferred_element_type=f32)]
    ppermute x8, waiting for transfers between devices: 4.01 us -> 2.21 us  [swap_cores(): return lax.ppermute(x, 'col', [(0, 1), (1, 0)])]
    pallas_call x1 -> x2, Pallas kernels: 3.18 us -> 3.88 us  [the longest x1 2.09 us: shards(): pl.pallas_call(functools.partial(finish_kernel, class_half, lead, step),...]
  transfers between devices with their start and end apart: 24 -> 24, of which waited for: 18 -> 18; matrix products, arithmetic and copies ran while one was open for 17% -> 17% of each run, Pallas kernels for 2% -> 3%
where the time goes in v11:
time: 173 us; the launch traced here: 172 us
  waiting for transfers between devices  59.8 us (35%)
  Pallas kernels  36.7 us (21%)
  starting transfers between devices  30.6 us (18%)
  matrix products  25.4 us (15%)
  other arithmetic  10.8 us (6%)
  local copies, waits for them, and re-layouts  7.26 us (4%)
    ppermute x12, waiting for transfers between devices, exchange(): return lax.ppermute(x, ('dom', 'col'), pairs)  40.1 us
    pallas_call x4, Pallas kernels, shards(): pl.pallas_call(functools.partial(far_kernel, slots, class_half, stride, l...  24.4 us
    all_to_all x4, starting transfers between devices, shards(): landed = lax.all_to_all(out, 'dom', split_axis=0, concat_axis=0, tiled=True)  18.8 us
    all_to_all x4, waiting for transfers between devices, shards(): landed = lax.all_to_all(out, 'dom', split_axis=0, concat_axis=0, tiled=True)  17.5 us
    ppermute x12, starting transfers between devices, exchange(): return lax.ppermute(x, ('dom', 'col'), pairs)  10.4 us
    dot_general x6, matrix products, contract(): lax.dot_general(a, b, (((0,), (0,)), ((), ())), preferred_element_type=f32)  7.76 us
    dot_general x1, matrix products, shards(): pre_second = jnp.dot(tied, second_turned, preferred_element_type=f32)  7.25 us
    convert_element_type x1, other arithmetic, gelu_parts(): return ((x * half_up).astype(bf16), slope.astype(bf16))  6.92 us
  transfers between devices with their start and end apart: 24, of which 18 were waited for; matrix products, arithmetic and copies ran while one was open for 17% of the time, Pallas kernels for 3%

profile of v11, /device:TPU:0, one launch (start us, length us, event | category | flops | bytes accessed | tf_op | source)
XLA Modules:
  0.0 171.9 jit_solution(14807082270457199374)
XLA Ops:
  0.7 5.5 %first.1 = (bf16[8,192,128]{2,1,0:T(8,128)(2,1)}, bf16[3072,128]{1,0:T(8,128)(2,1)}) custom-call(s32[1]{0:T(128)} %bitcast.core_ref, s32[8]{0:T(128)} %bitcast.54, s32[256]{0:T(256)} %bitcast.64, s32[8,256]{1,0:T(8,128)} %bitcast.50, s32[1,256]{1,0:T(1,128)} %labels_ref.1, f32[172,1,256]{2,1,0:T(1,128)} %bitcast.49, s32[24,128]{1,0:T(8,128)} %bitcast.44), custom_call_target="tpu_custom_call" | custom-call | tf_op jit(solution)/shard_map/first/pallas_call | solution.py:489
  6.3 7.2 %all-to-all-start = ((bf16[8,192,128]{2,1,0:T(8,128)(2,1)}), bf16[8,192,128]{2,1,0:T(8,128)(2,1)S(1)}, u32[]{:S(2)}, u32[]{:S(2)}) async-start(bf16[8,192,128]{2,1,0:T(8,128)(2,1)} %get-tuple-element.63), calls=%async_computation | async-start | bytes 786432 | tf_op jit(solution)/shard_map/all_to_all | solution.py:550
  13.5 0.5 collective-permute-start.1
  14.0 2.8 %turn.1 = (bf16[128,1024]{1,0:T(8,128)(2,1)}, f32[1,1024]{1,0:T(1,128)}, bf16[1024,1024]{1,0:T(8,128)(2,1)}) custom-call(s32[1]{0:T(128)} %bitcast.core_ref, bf16[128,1024]{1,0:T(8,128)(2,1)} %first_ref, f32[1,1024]{1,0:T(1,128)} %bitcast.53, bf16[1024,1024]{1,0:T(8,128)(2,1)} %second_ref), custom_call_target="tpu_custom_call" | custom-call | tf_op jit(solution)/shard_map/turn/pallas_call | solution.py:508
  17.1 1.0 collective-permute-done
  18.1 0.7 concatenate.71.ints_ref
  18.8 6.4 %all-to-all-done.recv_ref = bf16[8,192,128]{2,1,0:T(8,128)(2,1)S(1)} async-done(((bf16[8,192,128]{2,1,0:T(8,128)(2,1)}), bf16[8,192,128]{2,1,0:T(8,128)(2,1)S(1)}, u32[]{:S(2)}, u32[]{:S(2)}) %all-to-all-start) | async-done | bytes 393248 | tf_op jit(solution)/shard_map/all_to_all | solution.py:550
  25.2 0.7 copy-done.8
  26.0 6.2 %far.3 = (bf16[8,192,128]{2,1,0:T(8,128)(2,1)}, bf16[3072,128]{1,0:T(8,128)(2,1)}) custom-call(s32[3072]{0:T(1024)} %concatenate.71.ints_ref, s32[24,128]{1,0:T(8,128)} %bitcast.45, bf16[8,192,128]{2,1,0:T(8,128)(2,1)} %copy-done.8, bf16[16,128,128]{2,1,0:T(8,128)(2,1)} %bitcast.35, bf16[16,128,128]{2,1,0:T(8,128)(2,1)} %copy-done.2, ...), custom_call_target="tpu_custom_call" | custom-call | tf_op jit(solution)/shard_map/far/pallas_call | solution.py:574
  32.2 3.6 %all-to-all-start.1 = ((bf16[8,192,128]{2,1,0:T(8,128)(2,1)}), bf16[8,192,128]{2,1,0:T(8,128)(2,1)S(1)}, u32[]{:S(2)}, u32[]{:S(2)}) async-start(bf16[8,192,128]{2,1,0:T(8,128)(2,1)} %get-tuple-element.74), calls=%async_computation.1 | async-start | bytes 786432 | tf_op jit(solution)/shard_map/all_to_all | solution.py:550
  36.0 0.9 maximum_select_fusion.2
  36.9 5.7 %add_convert_fusion.1 = (bf16[1536,1024]{1,0:T(8,128)(2,1)}, bf16[1536,1024]{1,0:T(8,128)(2,1)}) fusion(f32[1024]{0:T(1024)S(1)} %bitcast.66, bf16[1536,128]{1,0:T(8,128)(2,1)S(1)} %copy-done, bf16[128,1024]{1,0:T(8,128)(2,1)S(1)} %copy-done.23), kind=kOutput, calls=%fused_computation.7 | convolution fusion | flops 430964736 | bytes 6950912 | tf_op jit(solution)/shard_map/dot_general | solution.py:558
  42.6 4.8 %all-to-all-done.1.recv_ref = bf16[8,192,128]{2,1,0:T(8,128)(2,1)S(1)} async-done(((bf16[8,192,128]{2,1,0:T(8,128)(2,1)}), bf16[8,192,128]{2,1,0:T(8,128)(2,1)S(1)}, u32[]{:S(2)}, u32[]{:S(2)}) %all-to-all-start.1) | async-done | bytes 393248 | tf_op jit(solution)/shard_map/all_to_all | solution.py:550
  47.4 0.7 copy-done.9
  48.2 6.2 %far.4 = (bf16[8,192,128]{2,1,0:T(8,128)(2,1)}, bf16[3072,128]{1,0:T(8,128)(2,1)}) custom-call(s32[3072]{0:T(1024)} %concatenate.71.ints_ref, s32[24,128]{1,0:T(8,128)} %bitcast.46, bf16[8,192,128]{2,1,0:T(8,128)(2,1)} %copy-done.9, bf16[16,128,128]{2,1,0:T(8,128)(2,1)} %bitcast.36, bf16[16,128,128]{2,1,0:T(8,128)(2,1)} %copy-done.2, ...), custom_call_target="tpu_custom_call" | custom-call | tf_op jit(solution)/shard_map/far/pallas_call | solution.py:574
  54.4 3.6 %all-to-all-start.2 = ((bf16[8,192,128]{2,1,0:T(8,128)(2,1)}), bf16[8,192,128]{2,1,0:T(8,128)(2,1)S(1)}, u32[]{:S(2)}, u32[]{:S(2)}) async-start(bf16[8,192,128]{2,1,0:T(8,128)(2,1)} %get-tuple-element.76), calls=%async_computation.2 | async-start | bytes 786432 | tf_op jit(solution)/shard_map/all_to_all | solution.py:550
  58.0 7.2 %fusion.9 = f32[1536,1024]{1,0:T(8,128)} fusion(bf16[1536,1024]{1,0:T(8,128)(2,1)} %get-tuple-element.78, bf16[1024,1024]{1,0:T(8,128)(2,1)S(1)} %copy-done.21), kind=kOutput, calls=%fused_computation.58 | convolution fusion | flops 3221225472 | bytes 11534336 | tf_op jit(solution)/shard_map/dot_general | solution.py:565
  65.3 3.8 %all-to-all-done.2.recv_ref = bf16[8,192,128]{2,1,0:T(8,128)(2,1)S(1)} async-done(((bf16[8,192,128]{2,1,0:T(8,128)(2,1)}), bf16[8,192,128]{2,1,0:T(8,128)(2,1)S(1)}, u32[]{:S(2)}, u32[]{:S(2)}) %all-to-all-start.2) | async-done | bytes 393248 | tf_op jit(solution)/shard_map/all_to_all | solution.py:550
  69.1 0.7 copy-done.10
  69.9 6.2 %far.5 = (bf16[8,192,128]{2,1,0:T(8,128)(2,1)}, bf16[3072,128]{1,0:T(8,128)(2,1)}) custom-call(s32[3072]{0:T(1024)} %concatenate.71.ints_ref, s32[24,128]{1,0:T(8,128)} %bitcast.47, bf16[8,192,128]{2,1,0:T(8,128)(2,1)} %copy-done.10, bf16[16,128,128]{2,1,0:T(8,128)(2,1)} %bitcast.37, bf16[16,128,128]{2,1,0:T(8,128)(2,1)} %copy-done.2, ...), custom_call_target="tpu_custom_call" | custom-call | tf_op jit(solution)/shard_map/far/pallas_call | solution.py:574
  76.1 4.3 %all-to-all-start.3 = ((bf16[8,192,128]{2,1,0:T(8,128)(2,1)}), bf16[8,192,128]{2,1,0:T(8,128)(2,1)}, u32[]{:S(2)}, u32[]{:S(2)}) async-start(bf16[8,192,128]{2,1,0:T(8,128)(2,1)} %get-tuple-element.88), calls=%async_computation.3 | async-start | bytes 786432 | tf_op jit(solution)/shard_map/all_to_all | solution.py:550
  80.4 6.9 %add_convert_fusion = (bf16[1536,1024]{1,0:T(8,128)(2,1)S(1)}, bf16[1536,1024]{1,0:T(8,128)(2,1)}) fusion(f32[1536,1024]{1,0:T(8,128)} %fusion.9, f32[1024]{0:T(1024)S(1)} %copy-done.14), kind=kLoop, calls=%fused_computation.2 | loop fusion | flops 28311552 | bytes 12587008 | tf_op jit(solution)/shard_map/convert_element_type | solution.py:380
  87.3 1.2 add_convert_fusion.3.rest_0_
  88.5 2.4 %all-to-all-done.3.recv_ref = bf16[8,192,128]{2,1,0:T(8,128)(2,1)} async-done(((bf16[8,192,128]{2,1,0:T(8,128)(2,1)}), bf16[8,192,128]{2,1,0:T(8,128)(2,1)}, u32[]{:S(2)}, u32[]{:S(2)}) %all-to-all-start.3) | async-done | bytes 393248 | tf_op jit(solution)/shard_map/all_to_all | solution.py:550
  91.0 5.8 %far_last.1 = (bf16[1536,128]{1,0:T(8,128)(2,1)}, bf16[1536,128]{1,0:T(8,128)(2,1)}) custom-call(s32[3072]{0:T(1024)} %concatenate.71.ints_ref, s32[24,128]{1,0:T(8,128)} %bitcast.48, bf16[8,192,128]{2,1,0:T(8,128)(2,1)} %all-to-all-done.3.recv_ref, bf16[16,128,128]{2,1,0:T(8,128)(2,1)} %bitcast.38, bf16[16,128,128]{2,1,0:T(8,128)(2,1)} %copy-done.2, ...), custom_call_target="tpu_custom_call" | custom-call | tf_op jit(solution)/shard_map/far_last/pallas_call | solution.py:574
  96.8 1.1 constant_dynamic-update-slice_fusion.1
  97.9 1.0 collective-permute-done.3
  98.9 1.1 constant_dynamic-update-slice_fusion
  100.0 3.0 %convolution_convert_fusion.2 = bf16[256,1024]{1,0:T(8,128)(2,1)S(1)} fusion(bf16[1536,256]{1,0:T(8,128)(2,1)S(1)} %constant_dynamic-update-slice_fusion, bf16[1536,1024]{1,0:T(8,128)(2,1)} %get-tuple-element.95), kind=kOutput, calls=%fused_computation.16 | convolution fusion | flops 805568512 | bytes 4456448 | tf_op jit(solution)/shard_map/dot_general | solution.py:602
  103.0 1.0 fusion.8
  104.1 0.8 copy-done.12
  104.9 0.6 convolution_convert_fusion.3
  105.5 1.1 copy-done.3
  106.7 3.7 %fusion.4 = (bf16[1024]{0:T(1024)(128)(2,1)S(1)}, f32[1536,1024]{1,0:T(8,128)S(1)}) fusion(bf16[1536,1024]{1,0:T(8,128)(2,1)S(1)} %copy-done.3, bf16[1536,1024]{1,0:T(8,128)(2,1)S(1)} %get-tuple-element.116, bf16[1024,1024]{1,0:T(8,128)(2,1)S(1)} %copy-done.22), kind=kOutput, calls=%fused_computation.53 | convolution fusion | flops 3227515904 | bytes 14682112 | tf_op jit(solution)/shard_map/dot_general | solution.py:615
  110.3 0.8 convolution_convert_fusion.4
  111.2 0.2 collective-permute-start.4
  111.5 1.4 convolution_convert_fusion
  112.9 0.4 collective-permute-start.12
  113.3 0.6 convolution_convert_fusion.5
  114.0 0.2 add_convert_fusion.4
  114.2 1.5 collective-permute-start.5
  115.7 1.4 add_convert_fusion.2
  117.2 1.0 collective-permute-start.13
  118.2 2.8 %collective-permute-done.5 = bf16[288,512]{1,0:T(8,128)(2,1)S(1)} collective-permute-done((bf16[288,512]{1,0:T(8,128)(2,1)S(1)}, bf16[288,512]{1,0:T(8,128)(2,1)S(1)}, u32[]{:S(2)}, u32[]{:S(2)}) %collective-permute-start.5) | collective-permute-done | bytes 294944 | tf_op jit(solution)/shard_map/ppermute | solution.py:393
  121.1 4.1 %collective-permute-done.13 = bf16[384,512]{1,0:T(8,128)(2,1)S(1)} collective-permute-done((bf16[384,512]{1,0:T(8,128)(2,1)S(1)}, bf16[384,512]{1,0:T(8,128)(2,1)S(1)}, u32[]{:S(2)}, u32[]{:S(2)}) %collective-permute-start.13) | collective-permute-done | bytes 393248 | tf_op jit(solution)/shard_map/ppermute | solution.py:393
  125.4 1.0 collective-permute-start.14
  126.4 1.1 collective-permute-start.6
  127.6 3.6 %collective-permute-done.14 = bf16[384,256]{1,0:T(8,128)(2,1)S(1)} collective-permute-done((bf16[384,256]{1,0:T(8,128)(2,1)S(1)}, bf16[384,256]{1,0:T(8,128)(2,1)S(1)}, u32[]{:S(2)}, u32[]{:S(2)}) %collective-permute-start.14) | collective-permute-done | bytes 196640 | tf_op jit(solution)/shard_map/ppermute | solution.py:393
  131.2 1.1 collective-permute-start.15
  132.3 0.4 collective-permute-done.6
  132.8 5.1 %collective-permute-done.15 = bf16[384,128]{1,0:T(8,128)(2,1)S(1)} collective-permute-done((bf16[384,128]{1,0:T(8,128)(2,1)S(1)}, bf16[384,128]{1,0:T(8,128)(2,1)S(1)}, u32[]{:S(2)}, u32[]{:S(2)}) %collective-permute-start.15) | collective-permute-done | bytes 98336 | tf_op jit(solution)/shard_map/ppermute | solution.py:393
  138.0 2.9 %collective-permute-start.7 = (bf16[288,128]{1,0:T(8,128)(2,1)S(1)}, bf16[288,128]{1,0:T(8,128)(2,1)S(1)}, u32[]{:S(2)}, u32[]{:S(2)}) collective-permute-start(bf16[288,128]{1,0:T(8,128)(2,1)S(1)} %broadcast_select_fusion.5), channel_id=1, source_target_pairs={{0,8},{1,9},{2,10},{3,11},{4,12},{5,13},{6,14},{7,15},{8,0},{9,1},... | collective-permute-start | bytes 221192 | tf_op jit(solution)/shard_map/ppermute | solution.py:393
  141.0 4.6 %collective-permute-done.16 = bf16[384,128]{1,0:T(8,128)(2,1)S(1)} collective-permute-done((bf16[384,128]{1,0:T(8,128)(2,1)S(1)}, bf16[384,128]{1,0:T(8,128)(2,1)S(1)}, u32[]{:S(2)}, u32[]{:S(2)}) %collective-permute-start.16) | collective-permute-done | bytes 98336 | tf_op jit(solution)/shard_map/ppermute | solution.py:393
  145.7 1.4 collective-permute-done.7
  147.2 7.0 %collective-permute-done.17 = bf16[384,256]{1,0:T(8,128)(2,1)S(1)} collective-permute-done((bf16[384,256]{1,0:T(8,128)(2,1)S(1)}, bf16[384,256]{1,0:T(8,128)(2,1)S(1)}, u32[]{:S(2)}, u32[]{:S(2)}) %collective-permute-start.17) | collective-permute-done | bytes 196640 | tf_op jit(solution)/shard_map/ppermute | solution.py:393
  154.5 5.9 %collective-permute-done.9 = bf16[288,256]{1,0:T(8,128)(2,1)S(1)} collective-permute-done((bf16[288,256]{1,0:T(8,128)(2,1)S(1)}, bf16[288,256]{1,0:T(8,128)(2,1)S(1)}, u32[]{:S(2)}, u32[]{:S(2)}) %collective-permute-start.9) | collective-permute-done | bytes 147488 | tf_op jit(solution)/shard_map/ppermute | solution.py:393
  160.6 1.3 collective-permute-start.10
  161.9 0.3 collective-permute-done.18
  162.2 0.2 maximum_select_fusion.mine_ref
  162.5 4.9 %collective-permute-done.10 = bf16[288,512]{1,0:T(8,128)(2,1)S(1)} collective-permute-done((bf16[288,512]{1,0:T(8,128)(2,1)S(1)}, bf16[288,512]{1,0:T(8,128)(2,1)S(1)}, u32[]{:S(2)}, u32[]{:S(2)}) %collective-permute-start.10) | collective-permute-done | bytes 294944 | tf_op jit(solution)/shard_map/ppermute | solution.py:393
  167.4 0.2 maximum_select_fusion.1.mine_ref
  167.7 1.8 %finish_lead.1.unused_ref = f32[1024,1024]{1,0:T(8,128)} custom-call(s32[1]{0:T(128)} %bitcast.core_ref, bf16[384,1024]{1,0:T(8,128)(2,1)S(1)} %maximum_select_fusion.mine_ref, bf16[384,1024]{1,0:T(8,128)(2,1)S(1)} %collective-permute-done.19.theirs_ref), custom_call_target="tpu_custom_call" | custom-call | flops 786432 | bytes 4718592 | tf_op jit(solution)/shard_map/finish_lead/pallas_call | solution.py:646
  169.4 0.2 collective-permute-done.11.theirs_ref
  169.6 2.1 %finish.1 = (f32[128,1024]{1,0:T(8,128)}, f32[1,1024]{1,0:T(1,128)}, f32[1024,1024]{1,0:T(8,128)}, f32[1,1024]{1,0:T(1,128)}, f32[172,1024]{1,0:T(8,128)}) custom-call(s32[1]{0:T(128)} %bitcast.core_ref, bf16[288,1024]{1,0:T(8,128)(2,1)S(1)} %maximum_select_fusion.1.mine_ref, ...), custom_call_target="tpu_custom_call", output_to_operand_aliasing={{2}: (3, {})} | custom-call | tf_op jit(solution)/shard_map/finish/pallas_call | solution.py:656
  (94 shorter events, 2.1 us)
Async XLA Ops:
  0.6 36.3 %copy-start = (bf16[1536,128]{1,0:T(8,128)(2,1)S(1)}, bf16[1536,128]{1,0:T(8,128)(2,1)}, u32[]{:S(2)}) copy-start(bf16[1536,128]{1,0:T(8,128)(2,1)} %param.18) | copy-start | bytes 1179652
  0.7 16.4 %copy-start.13 = (s32[1,8,256]{2,1,0:T(8,128)S(1)}, s32[1,8,256]{2,1,0:T(8,128)}, u32[]{:S(2)}) copy-start(s32[1,8,256]{2,1,0:T(8,128)} %param.30) | copy-start | bytes 24580
  0.7 17.4 %copy-start.15 = (s32[1,8]{1,0:T(1,128)S(1)}, s32[1,8]{1,0:T(1,128)}, u32[]{:S(2)}) copy-start(s32[1,8]{1,0:T(1,128)} %param.31) | copy-start | bytes 100
  0.7 16.2 %copy-start.19 = (s32[1,1,16]{2,1,0:T(1,128)S(1)}, s32[1,1,16]{2,1,0:T(1,128)}, u32[]{:S(2)}) copy-start(s32[1,1,16]{2,1,0:T(1,128)} %param.29) | copy-start | bytes 196
  0.7 16.2 %copy-start.18 = (s32[1,1,16]{2,1,0:T(1,128)S(1)}, s32[1,1,16]{2,1,0:T(1,128)}, u32[]{:S(2)}) copy-start(s32[1,1,16]{2,1,0:T(1,128)} %param.28) | copy-start | bytes 196
  0.7 16.2 %copy-start.17 = (s32[1,1,16]{2,1,0:T(1,128)S(1)}, s32[1,1,16]{2,1,0:T(1,128)}, u32[]{:S(2)}) copy-start(s32[1,1,16]{2,1,0:T(1,128)} %param.26) | copy-start | bytes 196
  0.7 16.2 %copy-start.16 = (s32[1,1,16]{2,1,0:T(1,128)S(1)}, s32[1,1,16]{2,1,0:T(1,128)}, u32[]{:S(2)}) copy-start(s32[1,1,16]{2,1,0:T(1,128)} %param.25) | copy-start | bytes 196
  6.3 18.9 %all-to-all-start = ((bf16[8,192,128]{2,1,0:T(8,128)(2,1)}), bf16[8,192,128]{2,1,0:T(8,128)(2,1)S(1)}, u32[]{:S(2)}, u32[]{:S(2)}) async-start(bf16[8,192,128]{2,1,0:T(8,128)(2,1)} %get-tuple-element.63), calls=%async_computation | async-start | bytes 786432 | tf_op jit(solution)/shard_map/all_to_all | solution.py:550
  13.5 5.3 %collective-permute-start.2 = (bf16[16,128,128]{2,1,0:T(8,128)(2,1)}, bf16[16,128,128]{2,1,0:T(8,128)(2,1)S(1)}, u32[]{:S(2)}, u32[]{:S(2)}) collective-permute-start(bf16[16,128,128]{2,1,0:T(8,128)(2,1)} %bitcast.39), channel_id=1, source_target_pairs={{0,1},{1,0},{2,3},{3,2},{4,5},{5,4},{6,7},{7,6},{8,9},{9,8},{10,11... | collective-permute-start | bytes 1572872 | tf_op jit(solution)/shard_map/ppermute | solution.py:384
  13.5 5.3 %collective-permute-start.1 = (bf16[16,128,128]{2,1,0:T(8,128)(2,1)}, bf16[16,128,128]{2,1,0:T(8,128)(2,1)S(1)}, u32[]{:S(2)}, u32[]{:S(2)}) collective-permute-start(bf16[16,128,128]{2,1,0:T(8,128)(2,1)} %bitcast.34), channel_id=1, source_target_pairs={{0,1},{1,0},{2,3},{3,2},{4,5},{5,4},{6,7},{7,6},{8,9},{9,8},{10,11... | collective-permute-start | bytes 1572872 | tf_op jit(solution)/shard_map/ppermute | solution.py:384
  14.0 21.8 %copy-start.11 = (bf16[1024,172]{0,1:T(8,128)(2,1)S(1)}, bf16[1024,172]{0,1:T(8,128)(2,1)}, u32[]{:S(2)}) copy-start(bf16[1024,172]{0,1:T(8,128)(2,1)} %param.23) | copy-start | bytes 1056772
  14.0 21.8 %copy-start.20 = (pred[128]{0:T(512)(128)(4,1)S(1)}, pred[128]{0:T(512)(128)(4,1)}, u32[]{:S(2)}) copy-start(pred[128]{0:T(512)(128)(4,1)} %constant.33.clone.1) | copy-start | bytes 388
  14.0 21.9 %slice-start = ((bf16[1024,172]{0,1:T(8,128)(2,1)}), bf16[1024,84]{0,1:T(8,128)(2,1)S(1)}, s32[]{:S(2)}) async-start(bf16[1024,172]{0,1:T(8,128)(2,1)} %param.23), calls=%async_computation.4 | async-start | bytes 360448 | tf_op jit(solution)/shard_map/slice | solution.py:560
  17.0 1.1 collective-permute-start
  18.8 18.1 %copy-start.23 = (bf16[128,1024]{1,0:T(8,128)(2,1)S(1)}, bf16[128,1024]{1,0:T(8,128)(2,1)}, u32[]{:S(2)}) copy-start(bf16[128,1024]{1,0:T(8,128)(2,1)} %get-tuple-element.70) | copy-start | bytes 786436
  18.8 18.1 %copy-start.24 = (f32[1,1024]{1,0:T(1,128)S(1)}, f32[1,1024]{1,0:T(1,128)}, u32[]{:S(2)}) copy-start(f32[1,1024]{1,0:T(1,128)} %get-tuple-element.71) | copy-start | bytes 12292
  18.8 6.4 %copy-start.1 = (bf16[16,128,128]{2,1,0:T(8,128)(2,1)}, bf16[16,128,128]{2,1,0:T(8,128)(2,1)S(1)}, u32[]{:S(2)}) copy-start(bf16[16,128,128]{2,1,0:T(8,128)(2,1)S(1)} %collective-permute-done.2.other_local_ref) | copy-start | bytes 1572868
  18.8 6.4 %copy-start.2 = (bf16[16,128,128]{2,1,0:T(8,128)(2,1)}, bf16[16,128,128]{2,1,0:T(8,128)(2,1)S(1)}, u32[]{:S(2)}) copy-start(bf16[16,128,128]{2,1,0:T(8,128)(2,1)S(1)} %collective-permute-done.1.other_halo_ref) | copy-start | bytes 1572868
  25.2 0.7 copy-start.8
  32.2 15.2 %all-to-all-start.1 = ((bf16[8,192,128]{2,1,0:T(8,128)(2,1)}), bf16[8,192,128]{2,1,0:T(8,128)(2,1)S(1)}, u32[]{:S(2)}, u32[]{:S(2)}) async-start(bf16[8,192,128]{2,1,0:T(8,128)(2,1)} %get-tuple-element.74), calls=%async_computation.1 | async-start | bytes 786432 | tf_op jit(solution)/shard_map/all_to_all | solution.py:550
  42.6 15.4 %copy-start.21 = (bf16[1024,1024]{1,0:T(8,128)(2,1)S(1)}, bf16[1024,1024]{1,0:T(8,128)(2,1)}, u32[]{:S(2)}) copy-start(bf16[1024,1024]{1,0:T(8,128)(2,1)} %get-tuple-element.79) | copy-start | bytes 6291460
  47.4 0.7 copy-start.9
  54.4 14.7 %all-to-all-start.2 = ((bf16[8,192,128]{2,1,0:T(8,128)(2,1)}), bf16[8,192,128]{2,1,0:T(8,128)(2,1)S(1)}, u32[]{:S(2)}, u32[]{:S(2)}) async-start(bf16[8,192,128]{2,1,0:T(8,128)(2,1)} %get-tuple-element.76), calls=%async_computation.2 | async-start | bytes 786432 | tf_op jit(solution)/shard_map/all_to_all | solution.py:550
  65.3 15.1 %copy-start.14 = (f32[1024]{0:T(1024)S(1)}, f32[1024]{0:T(1024)}, u32[]{:S(2)}) copy-start(f32[1024]{0:T(1024)} %param.22) | copy-start | bytes 12292
  69.1 0.7 copy-start.10
  76.1 14.9 %all-to-all-start.3 = ((bf16[8,192,128]{2,1,0:T(8,128)(2,1)}), bf16[8,192,128]{2,1,0:T(8,128)(2,1)}, u32[]{:S(2)}, u32[]{:S(2)}) async-start(bf16[8,192,128]{2,1,0:T(8,128)(2,1)} %get-tuple-element.88), calls=%async_computation.3 | async-start | bytes 786432 | tf_op jit(solution)/shard_map/all_to_all | solution.py:550
  80.4 7.0 %copy-start.4 = (bf16[3072,128]{1,0:T(8,128)(2,1)S(1)}, bf16[3072,128]{1,0:T(8,128)(2,1)}, u32[]{:S(2)}) copy-start(bf16[3072,128]{1,0:T(8,128)(2,1)} %get-tuple-element.86.value_in_ref) | copy-start | bytes 2359300
  80.4 6.9 %copy-start.5 = (bf16[3072,128]{1,0:T(8,128)(2,1)S(1)}, bf16[3072,128]{1,0:T(8,128)(2,1)}, u32[]{:S(2)}) copy-start(bf16[3072,128]{1,0:T(8,128)(2,1)} %get-tuple-element.85.value_in_ref) | copy-start | bytes 2359300
  80.4 6.9 %copy-start.6 = (bf16[3072,128]{1,0:T(8,128)(2,1)S(1)}, bf16[3072,128]{1,0:T(8,128)(2,1)}, u32[]{:S(2)}) copy-start(bf16[3072,128]{1,0:T(8,128)(2,1)} %get-tuple-element.84.value_in_ref) | copy-start | bytes 2359300
  96.7 2.1 %collective-permute-start.3 = (bf16[1536,128]{1,0:T(8,128)(2,1)}, bf16[1536,128]{1,0:T(8,128)(2,1)}, u32[]{:S(2)}, u32[]{:S(2)}) collective-permute-start(bf16[1536,128]{1,0:T(8,128)(2,1)} %get-tuple-element.92), channel_id=1, source_target_pairs={{0,1},{1,0},{2,3},{3,2},{4,5},{5,4},{6,7},{7,6},{8,9},{9,8},{10,11... | collective-permute-start | bytes 1179656 | tf_op jit(solution)/shard_map/ppermute | solution.py:384
  100.0 3.0 %copy-start.7 = (bf16[1024,256]{0,1:T(8,128)(2,1)S(1)}, bf16[1024,256]{0,1:T(8,128)(2,1)}, u32[]{:S(2)}) copy-start(bf16[1024,256]{0,1:T(8,128)(2,1)} %maximum_select_fusion.2) | copy-start | bytes 1572868
  103.0 1.9 %copy-start.12 = (bf16[1536,1024]{1,0:T(8,128)(2,1)S(1)}, bf16[1536,1024]{1,0:T(8,128)(2,1)}, u32[]{:S(2)}) copy-start(bf16[1536,1024]{1,0:T(8,128)(2,1)} %get-tuple-element.78) | copy-start | bytes 9437188
  103.0 2.5 %copy-start.22 = (bf16[1024,1024]{1,0:T(8,128)(2,1)S(1)}, bf16[1024,1024]{1,0:T(8,128)(2,1)}, u32[]{:S(2)}) copy-start(bf16[1024,1024]{1,0:T(8,128)(2,1)} %get-tuple-element.79) | copy-start | bytes 6291460
  104.0 2.6 %copy-start.3 = (bf16[1536,1024]{1,0:T(8,128)(2,1)S(1)}, bf16[1536,1024]{1,0:T(8,128)(2,1)}, u32[]{:S(2)}) copy-start(bf16[1536,1024]{1,0:T(8,128)(2,1)} %get-tuple-element.94) | copy-start | bytes 9437188
  111.2 2.7 %collective-permute-start.4 = (bf16[288,1024]{1,0:T(8,128)(2,1)S(1)}, bf16[288,1024]{1,0:T(8,128)(2,1)S(1)}, u32[]{:S(2)}, u32[]{:S(2)}) collective-permute-start(bf16[288,1024]{1,0:T(8,128)(2,1)S(1)} %pad_maximum_fusion), channel_id=1, source_target_pairs={{0,1},{1,0},{2,3},{3,2},{4,5},{5,4},{6,7},{7,6},{8,9},{9,8},{10,11... | collective-permute-start | bytes 1769480 | tf_op jit(solution)/shard_map/ppermute | solution.py:384
  112.9 2.9 %collective-permute-start.12 = (bf16[384,1024]{1,0:T(8,128)(2,1)S(1)}, bf16[384,1024]{1,0:T(8,128)(2,1)S(1)}, u32[]{:S(2)}, u32[]{:S(2)}) collective-permute-start(bf16[384,1024]{1,0:T(8,128)(2,1)S(1)} %convolution_convert_fusion), channel_id=1, source_target_pairs={{0,1},{1,0},{2,3},{3,2},{4,5},{5,4},{6,7},{7,6},{8,9},{9,8},{10,11... | collective-permute-start | bytes 2359304 | tf_op jit(solution)/shard_map/ppermute | solution.py:384
  114.2 6.8 %collective-permute-start.5 = (bf16[288,512]{1,0:T(8,128)(2,1)S(1)}, bf16[288,512]{1,0:T(8,128)(2,1)S(1)}, u32[]{:S(2)}, u32[]{:S(2)}) collective-permute-start(bf16[288,512]{1,0:T(8,128)(2,1)S(1)} %broadcast_select_fusion.1), channel_id=1, source_target_pairs={{0,2},{1,5},{2,0},{3,7},{4,6},{5,1},{6,4},{7,3},{8,10},{9,13},{10,... | collective-permute-start | bytes 884744 | tf_op jit(solution)/shard_map/ppermute | solution.py:393
  117.2 8.0 %collective-permute-start.13 = (bf16[384,512]{1,0:T(8,128)(2,1)S(1)}, bf16[384,512]{1,0:T(8,128)(2,1)S(1)}, u32[]{:S(2)}, u32[]{:S(2)}) collective-permute-start(bf16[384,512]{1,0:T(8,128)(2,1)S(1)} %broadcast_select_fusion), channel_id=1, source_target_pairs={{0,2},{1,5},{2,0},{3,7},{4,6},{5,1},{6,4},{7,3},{8,10},{9,13},{10,... | collective-permute-start | bytes 1179656 | tf_op jit(solution)/shard_map/ppermute | solution.py:393
  125.4 5.7 %collective-permute-start.14 = (bf16[384,256]{1,0:T(8,128)(2,1)S(1)}, bf16[384,256]{1,0:T(8,128)(2,1)S(1)}, u32[]{:S(2)}, u32[]{:S(2)}) collective-permute-start(bf16[384,256]{1,0:T(8,128)(2,1)S(1)} %broadcast_select_fusion.2), channel_id=1, source_target_pairs={{0,4},{1,3},{2,6},{3,1},{4,0},{5,7},{6,2},{7,5},{8,12},{9,11},{10,... | collective-permute-start | bytes 589832 | tf_op jit(solution)/shard_map/ppermute | solution.py:393
  126.4 6.3 %collective-permute-start.6 = (bf16[288,256]{1,0:T(8,128)(2,1)S(1)}, bf16[288,256]{1,0:T(8,128)(2,1)S(1)}, u32[]{:S(2)}, u32[]{:S(2)}) collective-permute-start(bf16[288,256]{1,0:T(8,128)(2,1)S(1)} %broadcast_select_fusion.3), channel_id=1, source_target_pairs={{0,4},{1,3},{2,6},{3,1},{4,0},{5,7},{6,2},{7,5},{8,12},{9,11},{10,... | collective-permute-start | bytes 442376 | tf_op jit(solution)/shard_map/ppermute | solution.py:393
  131.2 6.6 %collective-permute-start.15 = (bf16[384,128]{1,0:T(8,128)(2,1)S(1)}, bf16[384,128]{1,0:T(8,128)(2,1)S(1)}, u32[]{:S(2)}, u32[]{:S(2)}) collective-permute-start(bf16[384,128]{1,0:T(8,128)(2,1)S(1)} %broadcast_select_fusion.4), channel_id=1, source_target_pairs={{0,8},{1,9},{2,10},{3,11},{4,12},{5,13},{6,14},{7,15},{8,0},{9,1},... | collective-permute-start | bytes 294920 | tf_op jit(solution)/shard_map/ppermute | solution.py:393
  137.9 7.6 %collective-permute-start.16 = (bf16[384,128]{1,0:T(8,128)(2,1)S(1)}, bf16[384,128]{1,0:T(8,128)(2,1)S(1)}, u32[]{:S(2)}, u32[]{:S(2)}) collective-permute-start(bf16[384,128]{1,0:T(8,128)(2,1)S(1)} %add_convert_fusion.9), channel_id=1, source_target_pairs={{0,8},{1,9},{2,10},{3,11},{4,12},{5,13},{6,14},{7,15},{8,0},{9,1},... | collective-permute-start | bytes 294920 | tf_op jit(solution)/shard_map/ppermute | solution.py:393
  138.0 9.1 %collective-permute-start.7 = (bf16[288,128]{1,0:T(8,128)(2,1)S(1)}, bf16[288,128]{1,0:T(8,128)(2,1)S(1)}, u32[]{:S(2)}, u32[]{:S(2)}) collective-permute-start(bf16[288,128]{1,0:T(8,128)(2,1)S(1)} %broadcast_select_fusion.5), channel_id=1, source_target_pairs={{0,8},{1,9},{2,10},{3,11},{4,12},{5,13},{6,14},{7,15},{8,0},{9,1},... | collective-permute-start | bytes 221192 | tf_op jit(solution)/shard_map/ppermute | solution.py:393
  145.6 8.6 %collective-permute-start.17 = (bf16[384,256]{1,0:T(8,128)(2,1)S(1)}, bf16[384,256]{1,0:T(8,128)(2,1)S(1)}, u32[]{:S(2)}, u32[]{:S(2)}) collective-permute-start(bf16[384,256]{1,0:T(8,128)(2,1)S(1)} %maximum_select_fusion.5), channel_id=1, source_target_pairs={{0,4},{1,3},{2,6},{3,1},{4,0},{5,7},{6,2},{7,5},{8,12},{9,11},{10,... | collective-permute-start | bytes 589832 | tf_op jit(solution)/shard_map/ppermute | solution.py:393
  147.2 7.2 %collective-permute-start.8 = (bf16[288,128]{1,0:T(8,128)(2,1)S(1)}, bf16[288,128]{1,0:T(8,128)(2,1)S(1)}, u32[]{:S(2)}, u32[]{:S(2)}) collective-permute-start(bf16[288,128]{1,0:T(8,128)(2,1)S(1)} %add_convert_fusion.10), channel_id=1, source_target_pairs={{0,8},{1,9},{2,10},{3,11},{4,12},{5,13},{6,14},{7,15},{8,0},{9,1},... | collective-permute-start | bytes 221192 | tf_op jit(solution)/shard_map/ppermute | solution.py:393
  154.3 7.8 %collective-permute-start.18 = (bf16[384,512]{1,0:T(8,128)(2,1)S(1)}, bf16[384,512]{1,0:T(8,128)(2,1)S(1)}, u32[]{:S(2)}, u32[]{:S(2)}) collective-permute-start(bf16[384,512]{1,0:T(8,128)(2,1)S(1)} %maximum_select_fusion.3), channel_id=1, source_target_pairs={{0,2},{1,5},{2,0},{3,7},{4,6},{5,1},{6,4},{7,3},{8,10},{9,13},{10,... | collective-permute-start | bytes 1179656 | tf_op jit(solution)/shard_map/ppermute | solution.py:393
  154.5 6.0 %collective-permute-start.9 = (bf16[288,256]{1,0:T(8,128)(2,1)S(1)}, bf16[288,256]{1,0:T(8,128)(2,1)S(1)}, u32[]{:S(2)}, u32[]{:S(2)}) collective-permute-start(bf16[288,256]{1,0:T(8,128)(2,1)S(1)} %maximum_select_fusion.6), channel_id=1, source_target_pairs={{0,4},{1,3},{2,6},{3,1},{4,0},{5,7},{6,2},{7,5},{8,12},{9,11},{10,... | collective-permute-start | bytes 442376 | tf_op jit(solution)/shard_map/ppermute | solution.py:393
  160.6 6.8 %collective-permute-start.10 = (bf16[288,512]{1,0:T(8,128)(2,1)S(1)}, bf16[288,512]{1,0:T(8,128)(2,1)S(1)}, u32[]{:S(2)}, u32[]{:S(2)}) collective-permute-start(bf16[288,512]{1,0:T(8,128)(2,1)S(1)} %maximum_select_fusion.4), channel_id=1, source_target_pairs={{0,2},{1,5},{2,0},{3,7},{4,6},{5,1},{6,4},{7,3},{8,10},{9,13},{10,... | collective-permute-start | bytes 884744 | tf_op jit(solution)/shard_map/ppermute | solution.py:393
  162.4 5.3 %collective-permute-start.19 = (bf16[384,1024]{1,0:T(8,128)(2,1)S(1)}, bf16[384,1024]{1,0:T(8,128)(2,1)S(1)}, u32[]{:S(2)}, u32[]{:S(2)}) collective-permute-start(bf16[384,1024]{1,0:T(8,128)(2,1)S(1)} %maximum_select_fusion.mine_ref), channel_id=1, source_target_pairs={{0,1},{1,0},{2,3},{3,2},{4,5},{5,4},{6,7},{7,6},{8,9},{9,8},{10,11... | collective-permute-start | bytes 2359304 | tf_op jit(solution)/shard_map/ppermute | solution.py:384
  167.6 2.1 %collective-permute-start.11 = (bf16[288,1024]{1,0:T(8,128)(2,1)S(1)}, bf16[288,1024]{1,0:T(8,128)(2,1)S(1)}, u32[]{:S(2)}, u32[]{:S(2)}) collective-permute-start(bf16[288,1024]{1,0:T(8,128)(2,1)S(1)} %maximum_select_fusion.1.mine_ref), channel_id=1, source_target_pairs={{0,1},{1,0},{2,3},{3,2},{4,5},{5,4},{6,7},{7,6},{8,9},{9,8},{10,11... | collective-permute-start | bytes 1769480 | tf_op jit(solution)/shard_map/ppermute | solution.py:384
